TPU v7x, 32 devices: a whole 2x2x4 slice. The times are simulated.
32 devices in a mesh: dp: 8 (over z, x), crop: 4 (over y, core).
Axes of the slice: x: 2, y: 2, z: 4, core: 2. Of those that a mesh axis runs over, the one named last changes fastest.
Arguments:
- query_crops: bfloat16 [16384, 2048], P(('dp', 'crop')), may hold values from -6 to 6
- key_crops: bfloat16 [16384, 2048], P(('dp', 'crop')), may hold values from -43 to 43
- shuffle: int32 [16384], P(('dp', 'crop')), may hold values from 0 to 16383, as said below
- distractor_bank: bfloat16 [16384, 128], replicated, may hold values from -2.5 to 2.5
- query_inner: bfloat16 [2048, 2048], replicated, may hold values from -0.125 to 0.125
- query_outer: bfloat16 [2048, 128], replicated, may hold values from -0.125 to 0.125
- key_inner: bfloat16 [2048, 2048], replicated, may hold values from -0.125 to 0.125
- key_outer: bfloat16 [2048, 128], replicated, may hold values from -0.125 to 0.125
Outputs:
- grad_inner: float32 [2048, 2048], P(('dp', 'crop'))
- grad_outer: float32 [2048, 128], P(('dp', 'crop'))
Inputs may be any that keep to these rules, and one draw needn't show every extreme that they name: `shuffle`: a permutation of the 16384 key crops; shuffled position t * 512 + s * 16 + j, for j below 16, takes a crop from rows s * 512 up to (s + 1) * 512 - 1.
All inputs are finite; a program needn't handle non-finite values.
Results may differ from a plain program's by a relative error of at most 0.008.
Values may be sent and summed in bfloat16 or wider, within the bound.
No kernel may reach another device: no remote copies, remote signals or barrier semaphores. Data moves between devices by JAX's collectives and lax.ppermute only.
A program may use at most 192 MiB of HBM per device.

v0:
```python
import jax
import jax.numpy as jnp
from jax import lax
from jax.sharding import PartitionSpec as P

sharpness_divisor = 0.2
loss_scale = 4096.0
bn_eps = 1e-05
norm_eps = 1e-06


def batch_stats(hidden):
    average = jnp.mean(hidden, axis=0)
    variance = jnp.mean(hidden * hidden, axis=0) - average * average
    return (average, lax.rsqrt(variance + bn_eps))


def head_tail(normed, w_out):
    active = jnp.maximum(normed, 0.0).astype(jnp.bfloat16)
    projected = jnp.dot(active, w_out, preferred_element_type=jnp.float32)
    return projected * lax.rsqrt(jnp.sum(projected * projected, axis=-1, keepdims=True) + norm_eps)


def key_embed(crop_rows, w_in, w_out):
    hidden = jnp.dot(crop_rows, w_in, preferred_element_type=jnp.float32)
    average, inv_std = batch_stats(hidden)
    return head_tail((hidden - average) * inv_std, w_out)


def query_grads(crop_rows, matching_targets, distractor_bank, w_in, w_out, all_rows):
    hidden = jnp.dot(crop_rows, w_in, preferred_element_type=jnp.float32)
    average, inv_std = batch_stats(hidden)
    normed = (hidden - average) * inv_std
    active = jnp.maximum(normed, 0.0).astype(jnp.bfloat16)
    projected = jnp.dot(active, w_out, preferred_element_type=jnp.float32)
    inv_len = lax.rsqrt(jnp.sum(projected * projected, axis=-1, keepdims=True) + norm_eps)
    probe_features = projected * inv_len
    matching_similarity = (
        jnp.sum(probe_features * matching_targets, axis=-1, keepdims=True) / sharpness_divisor
    )
    distractor_similarities = (
        lax.dot_general(
            probe_features.astype(jnp.bfloat16),
            distractor_bank,
            (((1,), (1,)), ((), ())),
            preferred_element_type=jnp.float32,
        )
        / sharpness_divisor
    )
    exp_pos = jnp.exp(matching_similarity)
    exp_neg = jnp.exp(distractor_similarities)
    total_exp = exp_pos + jnp.sum(exp_neg, axis=-1, keepdims=True)
    scale_coef = loss_scale / all_rows
    matching_similarity_slope = scale_coef * (exp_pos / total_exp - 1.0)
    distractor_similarity_slope = (scale_coef * exp_neg / total_exp).astype(jnp.bfloat16)
    probe_feature_slope = (
        matching_similarity_slope * matching_targets
        + jnp.dot(distractor_similarity_slope, distractor_bank, preferred_element_type=jnp.float32)
    ) / sharpness_divisor
    d_proj = (
        (
            probe_feature_slope
            - probe_features * jnp.sum(probe_feature_slope * probe_features, axis=-1, keepdims=True)
        )
        * inv_len
    ).astype(jnp.bfloat16)
    grad_out = lax.dot_general(
        active, d_proj, (((0,), (0,)), ((), ())), preferred_element_type=jnp.float32
    )
    d_act = lax.dot_general(
        d_proj, w_out, (((1,), (1,)), ((), ())), preferred_element_type=jnp.float32
    )
    d_norm = jnp.where(normed > 0.0, d_act, 0.0)
    d_hidden = inv_std * (
        d_norm - jnp.mean(d_norm, axis=0) - normed * jnp.mean(d_norm * normed, axis=0)
    )
    grad_in = lax.dot_general(
        crop_rows,
        d_hidden.astype(jnp.bfloat16),
        (((0,), (0,)), ((), ())),
        preferred_element_type=jnp.float32,
    )
    return (grad_in, grad_out)


def per_device(
    query_crops, key_crops, shuffle, distractor_bank, query_inner, query_outer, key_inner, key_outer
):
    group_count = lax.axis_size(("dp", "crop"))
    row_count = query_crops.shape[0]
    per_peer = row_count // group_count
    all_rows = float(row_count * group_count)
    wanted = (shuffle % row_count).reshape(group_count, per_peer)
    requested = lax.all_to_all(wanted, ("dp", "crop"), split_axis=0, concat_axis=0, tiled=True)
    flat_req = requested.reshape(-1)
    outgoing = key_crops[flat_req].reshape(group_count, per_peer, key_crops.shape[1])
    incoming = lax.all_to_all(
        outgoing, ("dp", "crop"), split_axis=0, concat_axis=0, tiled=True
    ).reshape(row_count, key_crops.shape[1])
    embedded = key_embed(incoming, key_inner, key_outer).reshape(
        group_count, per_peer, key_outer.shape[1]
    )
    returned = lax.all_to_all(
        embedded, ("dp", "crop"), split_axis=0, concat_axis=0, tiled=True
    ).reshape(row_count, key_outer.shape[1])
    matching_targets = (
        jnp.zeros((row_count, returned.shape[1]), jnp.float32).at[flat_req].set(returned)
    )
    grad_in, grad_out = query_grads(
        query_crops, matching_targets, distractor_bank, query_inner, query_outer, all_rows
    )
    grad_in, grad_out = (
        lax.psum_scatter(grad_in, ("dp", "crop"), scatter_dimension=0, tiled=True),
        lax.psum_scatter(grad_out, ("dp", "crop"), scatter_dimension=0, tiled=True),
    )
    return (grad_in, grad_out)


def solution(mesh):
    placed = (
        P(("dp", "crop"), None),
        P(("dp", "crop"), None),
        P(("dp", "crop")),
        P(),
        P(),
        P(),
        P(),
        P(),
    )
    return jax.shard_map(
        per_device,
        mesh=mesh,
        in_specs=placed,
        out_specs=(P(("dp", "crop"), None), P(("dp", "crop"), None)),
        check_vma=False,
    )
```

profile of v0, /device:TPU:0, one launch (start us, length us, event | category | flops | bytes accessed | tf_op | source)
XLA Modules:
  0.0 464.1 jit_solution(4945937192021879088)
XLA Ops:
  7.2 0.0 copy-start
  7.2 0.8 add_select_fusion
  8.0 0.1 all_to_all.12
  8.1 14.2 %all_to_all.19 = s32[32,1,16]{2,1,0:T(1,128)S(1)} all-to-all(s32[32,1,16]{2,1,0:T(1,128)S(1)} %bitcast.24), channel_id=1, replica_groups=mesh['dp'=8,'crop'=4] {'dp','crop'}, dimensions={0} | all-to-all | bytes 4096 | tf_op jit(solution)/shard_map/all_to_all | solution.py:94
  22.3 0.5 broadcast.154
  22.9 0.7 reduce.3
  23.6 0.1 reshape.115
  23.7 7.1 %gather_fusion = bf16[512,2048]{1,0:T(8,128)(2,1)} fusion(bf16[512,2048]{1,0:T(8,128)(2,1)} %param.9, s32[1024]{0:T(1024)S(1)} %pad_clamp_fusion), kind=kCustom, calls=%fused_computation | custom fusion | bytes 4196352 | tf_op jit(solution)/shard_map/gather | solution.py:96
  30.8 3.5 all-to-all-start.1
  34.2 0.0 copy-done
  34.2 0.0 copy-start.2
  34.3 7.0 %multiply_reduce_fusion.2 = (f32[2048]{0:T(1024)S(1)}, f32[2048]{0:T(1024)S(1)}, f32[512,2048]{1,0:T(8,128)S(1)}) fusion(bf16[512,2048]{1,0:T(8,128)(2,1)S(1)} %copy-done, bf16[2048,2048]{1,0:T(8,128)(2,1)} %param.12), kind=kOutput, calls=%fused_computation.13 | convolution fusion | flops 4298108928 | bytes 14696448 | tf_op jit(solution)/shard_map/dot_general | solution.py:31
  41.3 0.0 copy-start.1
  41.3 2.0 copy-done.1
  43.3 0.0 copy-done.2
  43.3 0.8 multiply_reduce_fusion.6
  44.2 38.8 %all-to-all-done.1 = bf16[32,16,2048]{2,1,0:T(8,128)(2,1)} async-done(((bf16[32,16,2048]{2,1,0:T(8,128)(2,1)}), bf16[32,16,2048]{2,1,0:T(8,128)(2,1)}, u32[]{:S(2)}, u32[]{:S(2)}) %all-to-all-start.1) | async-done | bytes 2097184 | tf_op jit(solution)/shard_map/all_to_all | solution.py:97
  83.0 0.0 copy-start.3
  83.0 7.7 %fusion.26 = (f32[2048]{0:T(1024)S(1)}, f32[2048]{0:T(1024)S(1)}, f32[512,2048]{1,0:T(8,128)S(1)}) fusion(bf16[512,2048]{1,0:T(8,128)(2,1)} %bitcast.3, bf16[2048,2048]{1,0:T(8,128)(2,1)} %param.14), kind=kOutput, calls=%fused_computation.61 | convolution fusion | flops 4298108928 | bytes 14696448 | tf_op jit(solution)/shard_map/dot_general | solution.py:25
  90.6 0.0 copy-done.3
  90.7 0.8 multiply_reduce_fusion.5
  91.5 0.8 broadcast_multiply_fusion
  92.3 4.0 all-to-all-start.2
  96.3 0.2 reduce-scatter.5.cloned.1.call-start
  96.5 15.6 %fusion = (f32[512]{0:T(512)S(1)}, f32[512,16384]{1,0:T(8,128)}) fusion(bf16[16384,128]{1,0:T(8,128)(2,1)} %param.11, f32[512,128]{0,1:T(8,128)S(1)} %get-tuple-element.22, f32[512]{0:T(512)S(1)} %add_rsqrt_fusion.3), kind=kOutput, calls=%fused_computation.4 | convolution fusion | flops 2164391424 | bytes 38014976 | tf_op jit(solution)/shard_map/dot_general | solution.py:42
  112.1 0.0 all-to-all-done.2
  112.1 1.8 scatter_custom_fusion
  113.9 0.1 copy.16
  114.0 0.1 multiply_reduce_fusion.4
  114.1 15.9 %multiply_reduce_fusion.3 = (f32[512]{0:T(512)S(1)}, f32[512,128]{0,1:T(8,128)S(1)}) fusion(f32[512,128]{0,1:T(8,128)S(1)} %get-tuple-element.22, f32[512]{0:T(512)S(1)} %add_rsqrt_fusion.3, bf16[16384,128]{1,0:T(8,128)(2,1)} %param.11, f32[512,16384]{1,0:T(8,128)} %get-tuple-element.27, f32[512]{0:T(512)S(1)} %get-tuple-element.19, ...), kind=kOutput, calls=%fused_computation.28 | convolution fusion | flops 2181430784 | bytes 38543360 | tf_op jit(solution)/shard_map/dot_general | solution.py:58
  130.0 0.1 multiply_convert_fusion.2
  130.1 3.9 fusion.12
  134.0 5.3 %fusion.25 = (f32[2048]{0:T(1024)S(1)}, f32[2048]{0:T(1024)S(1)}, f32[512,2048]{1,0:T(8,128)}) fusion(f32[2048]{0:T(1024)S(1)} %get-tuple-element.16, f32[512,2048]{1,0:T(8,128)} %copy-done.1, f32[2048]{0:T(1024)S(1)} %get-tuple-element.17, bf16[512,128]{0,1:T(8,128)(2,1)S(1)} %multiply_convert_fusion.2, bf16[2048,128]{1,0:T(8,128)(2,1)S(1)} %copy-done.2), kind=kOutput, calls=%fused_computation.60 | convolution fusion | flops 275771392 | bytes 9076736 | tf_op jit(solution)/shard_map/dot_general | solution.py:70
  139.2 0.0 reduce-scatter.5.cloned.1.call-update
  139.2 0.0 reduce-scatter.7.cloned.1.call-start
  139.3 11.8 %convolution_bitcast_fusion = f32[2048,2048]{0,1:T(8,128)} fusion(bf16[512,2048]{1,0:T(8,128)(2,1)S(1)} %copy-done, f32[512,2048]{1,0:T(8,128)} %get-tuple-element.30, f32[512,2048]{1,0:T(8,128)} %copy-done.1, f32[2048]{0:T(1024)S(1)} %get-tuple-element.31, f32[2048]{0:T(1024)S(1)} %get-tuple-element.32, f32[2048]{0:T(1024)S(1)} %get-tuple-element.17, ...), kind=kOutput, calls=%fused_computation.6 | convolution fusion | flops 4302307328 | bytes 27295744 | tf_op jit(solution)/shard_map/dot_general | solution.py:77
  151.1 17.6 %copy.19 = f32[2048,2048]{1,0:T(8,128)} copy(f32[2048,2048]{0,1:T(8,128)} %convolution_bitcast_fusion) | data formatting | bytes 33554432
  168.7 0.0 reduce-scatter.7.cloned.1.call-update
  168.7 106.7 %reduce-scatter.5.cloned.1.call-done = f32[64,128]{1,0:T(8,128)} async-done(((f32[2048,128]{1,0:T(8,128)}), f32[64,128]{1,0:T(8,128)}) %reduce-scatter.5.cloned.1.call-update) | async-done | bytes 32784 | tf_op jit(solution)/shard_map/reduce_scatter | solution.py:114
  275.4 181.9 %reduce-scatter.7.cloned.1.call-done = f32[64,2048]{1,0:T(8,128)} async-done(((f32[2048,2048]{1,0:T(8,128)}), f32[64,2048]{1,0:T(8,128)}) %reduce-scatter.7.cloned.1.call-update) | async-done | bytes 524304
  (8 shorter events, 0.1 us)
Async XLA Ops:
  7.2 27.1 %copy-start = (bf16[512,2048]{1,0:T(8,128)(2,1)S(1)}, bf16[512,2048]{1,0:T(8,128)(2,1)}, u32[]{:S(2)}) copy-start(bf16[512,2048]{1,0:T(8,128)(2,1)} %param.8) | copy-start | bytes 6291460
  30.8 52.2 %all-to-all-start.1 = ((bf16[32,16,2048]{2,1,0:T(8,128)(2,1)}), bf16[32,16,2048]{2,1,0:T(8,128)(2,1)}, u32[]{:S(2)}, u32[]{:S(2)}) async-start(bf16[32,16,2048]{2,1,0:T(8,128)(2,1)} %bitcast.22), calls=%async_computation.1 | async-start | bytes 4194304 | tf_op jit(solution)/shard_map/all_to_all | solution.py:97
  34.2 9.1 %copy-start.2 = (bf16[2048,128]{1,0:T(8,128)(2,1)S(1)}, bf16[2048,128]{1,0:T(8,128)(2,1)}, u32[]{:S(2)}) copy-start(bf16[2048,128]{1,0:T(8,128)(2,1)} %param.13) | copy-start | bytes 1572868
  41.3 2.0 copy-start.1
  83.0 7.7 %copy-start.3 = (bf16[2048,128]{1,0:T(8,128)(2,1)S(1)}, bf16[2048,128]{1,0:T(8,128)(2,1)}, u32[]{:S(2)}) copy-start(bf16[2048,128]{1,0:T(8,128)(2,1)} %param.15) | copy-start | bytes 1572868
  92.3 19.8 %all-to-all-start.2 = ((f32[32,16,128]{2,1,0:T(8,128)}), f32[32,16,128]{2,1,0:T(8,128)S(1)}, u32[]{:S(2)}, u32[]{:S(2)}) async-start(f32[32,16,128]{2,1,0:T(8,128)} %bitcast.4), calls=%async_computation.2 | async-start | bytes 524288 | tf_op jit(solution)/shard_map/all_to_all | solution.py:103
  96.3 179.1 %reduce-scatter.5.cloned.1.call-start = ((), (), s32[]{:S(2)}) async-start(), calls=%async_computation.5 | async-start | bytes 1081344 | tf_op jit(solution)/shard_map/reduce_scatter | solution.py:114
  139.2 318.0 %reduce-scatter.7.cloned.1.call-start = ((), (), s32[]{:S(2)}) async-start(), calls=%async_computation.6 | async-start | bytes 17301504
Sparse Core Ops, SparseCore 0:
  139.4 135.9 reduce-scatter.4
  278.4 178.8 reduce-scatter.6
where the time goes:
time: 466 us; the launch traced here: 464 us
  waiting for transfers between devices  327 us (70%)
  matrix products  68.7 us (15%)
  local copies, waits for them, and re-layouts  29.3 us (6%)
  blocking collectives  14.2 us (3%)
  between operations  14.2 us (3%)
  starting transfers between devices  7.73 us (2%)
    unnamed x3, waiting for transfers between devices  182 us
    reduce_scatter x1, waiting for transfers between devices, per_device(): lax.psum_scatter(grad_out, ('dp', 'crop'), scatter_dimension=0, tiled=True)  107 us
    all_to_all x1, waiting for transfers between devices, per_device(): lax.all_to_all(outgoing, ('dp', 'crop'), split_axis=0, concat_axis=0, til...  38.8 us
    unnamed x9, local copies, waits for them, and re-layouts  19.6 us
    dot_general x1, matrix products, query_grads(): jnp.dot(distractor_similarity_slope, distractor_bank, preferred_element_t...  15.9 us
    dot_general x1, matrix products, query_grads(): lax.dot_general(probe_features.astype(jnp.bfloat16), distractor_bank, (((...  15.6 us
    all_to_all x1, blocking collectives, per_device(): lax.all_to_all(wanted, ('dp', 'crop'), split_axis=0, concat_axis=0, tiled...  14.2 us
    dot_general x1, matrix products, query_grads(): lax.dot_general(crop_rows, d_hidden.astype(jnp.bfloat16), (((0,), (0,)),...  11.8 us
  transfers between devices with their start and end apart: 4, of which 3 were waited for; matrix products, arithmetic and copies ran while one was open for 11% of the time, Pallas kernels for 0%

commit v1 on v0

v1 whole, which is shorter than its diff:
```python
import math
import jax
import jax.numpy as jnp
from jax import lax
from jax.experimental import pallas as pl
from jax.experimental.pallas import tpu as pltpu
from jax.sharding import PartitionSpec as P

sharpness_divisor = 0.2
loss_scale = 4096.0
bn_eps = 1e-05
norm_eps = 1e-06
AXES = ("dp", "crop")
QUARTER = 0.25


def neg_kernel(q_ref, bank_ref, sum_ref, u_ref):
    @pl.when(pl.program_id(0) == 0)
    def _():
        sum_ref[...] = jnp.zeros_like(sum_ref)
        u_ref[...] = jnp.zeros_like(u_ref)

    q = q_ref[...]
    step = 256
    total = sum_ref[...]
    u = u_ref[...]
    for j in range(bank_ref.shape[0] // step):
        bank = bank_ref[j * step:(j + 1) * step, :]
        s = lax.dot_general(q, bank, (((1,), (1,)), ((), ())), preferred_element_type=jnp.float32)
        e = jnp.exp2(s * (1.0 / (sharpness_divisor * math.log(2.0))) - 2.0)
        for i in range(step // 128):
            total = total + e[:, i * 128:(i + 1) * 128]
        u = u + jnp.dot(e.astype(jnp.bfloat16), bank, preferred_element_type=jnp.float32)
    sum_ref[...] = total
    u_ref[...] = u


def negatives(q, bank):
    rows, emb = q.shape
    tile = 2048
    return pl.pallas_call(
        neg_kernel,
        grid=(bank.shape[0] // tile,),
        in_specs=[
            pl.BlockSpec((rows, emb), lambda i: (0, 0)),
            pl.BlockSpec((tile, emb), lambda i: (i, 0)),
        ],
        out_specs=[
            pl.BlockSpec((rows, 128), lambda i: (0, 0)),
            pl.BlockSpec((rows, emb), lambda i: (0, 0)),
        ],
        out_shape=[
            jax.ShapeDtypeStruct((rows, 128), jnp.float32),
            jax.ShapeDtypeStruct((rows, emb), jnp.float32),
        ],
        cost_estimate=pl.CostEstimate(
            flops=4 * rows * bank.shape[0] * emb,
            bytes_accessed=bank.shape[0] * emb * 2,
            transcendentals=rows * bank.shape[0],
        ),
        compiler_params=pltpu.CompilerParams(vmem_limit_bytes=32 * 1024 * 1024),
        name="negatives",
    )(q, bank)


def swap(x, axis, bit):
    size = lax.axis_size(axis)
    return lax.ppermute(x, axis, [(i, i ^ bit) for i in range(size)])


def halve(x, dim, mine):
    keep = lax.dynamic_index_in_dim(x, mine, dim, keepdims=False)
    send = lax.dynamic_index_in_dim(x, 1 - mine, dim, keepdims=False)
    return keep, send


def add(a, b):
    return (a.astype(jnp.float32) + b.astype(jnp.float32)).astype(jnp.bfloat16)


def line_scatter(x, place, length):
    own = lax.dynamic_index_in_dim(x, place, 0, keepdims=False).astype(jnp.float32)
    right = jnp.zeros(x.shape[1:], x.dtype)
    left = right
    for k in range(1, length):
        d = jnp.clip(length - k + place, 0, length - 1)
        out = lax.dynamic_index_in_dim(x, d, 0, keepdims=False)
        out = out if k == 1 else add(out, right)
        right = lax.ppermute(
            out, "dp", [(2 * p + b, 2 * p + 2 + b) for p in range(k) for b in range(2)]
        )
        d = jnp.clip(k - length + place, 0, length - 1)
        out = lax.dynamic_index_in_dim(x, d, 0, keepdims=False)
        out = out if k == 1 else add(out, left)
        left = lax.ppermute(
            out,
            "dp",
            [
                (2 * p + b, 2 * p - 2 + b)
                for p in range(length - k, length)
                for b in range(2)
            ],
        )
    return own + right.astype(jnp.float32) + left.astype(jnp.float32)


def scatter_sum(grads):
    n_dp, n_crop = lax.axis_size("dp"), lax.axis_size("crop")
    length, half_crop = n_dp // 2, n_crop // 2
    dp, crop = lax.axis_index("dp"), lax.axis_index("crop")
    z, x, y, core = dp // 2, dp % 2, crop // 2, crop % 2
    parts = []
    for part, g in enumerate(grads):
        rows = g.shape[0] // (n_dp * n_crop)
        g = g.reshape(length, 2, half_crop, 2, rows, g.shape[1])
        keep, send = halve(g, 3, core)
        g = add(keep, swap(send, "crop", 1))
        if part % 2 == 0:
            keep, send = halve(g, 1, x)
            g = add(keep, swap(send, "dp", 1))
            keep, send = halve(g, 1, y)
            g = add(keep, swap(send, "crop", 2))
        else:
            keep, send = halve(g, 2, y)
            g = add(keep, swap(send, "crop", 2))
            keep, send = halve(g, 1, x)
            g = add(keep, swap(send, "dp", 1))
        parts.append(line_scatter(g, z, length))
    return parts


def per_device(
    query_crops, key_crops, shuffle, distractor_bank, query_inner, query_outer, key_inner, key_outer
):
    group_count = lax.axis_size(AXES)
    row_count = query_crops.shape[0]
    hid = query_inner.shape[1]
    per_peer = row_count // group_count
    all_rows = float(row_count * group_count)

    wanted = (shuffle % row_count).reshape(group_count, per_peer)
    requested = lax.all_to_all(wanted, AXES, split_axis=0, concat_axis=0, tiled=True)
    flat_req = requested.reshape(-1)
    pick = (flat_req[:, None] == lax.iota(jnp.int32, row_count)[None, :]).astype(jnp.bfloat16)

    by_group = jnp.dot(pick, key_crops, preferred_element_type=jnp.float32).astype(jnp.bfloat16)
    hidden_k = jnp.dot(by_group, key_inner, preferred_element_type=jnp.float32)
    hidden_k = hidden_k.reshape(group_count, per_peer, hid)
    sums = jnp.concatenate(
        [jnp.sum(hidden_k, axis=1), jnp.sum(hidden_k * hidden_k, axis=1)], axis=1
    )
    mine = lax.all_to_all(sums, AXES, split_axis=0, concat_axis=0, tiled=True)
    mine = jnp.sum(mine, axis=0) / row_count
    mu = mine[:hid]
    inv_std = lax.rsqrt(mine[hid:] - mu * mu + bn_eps)
    told = jnp.broadcast_to(jnp.concatenate([mu, inv_std])[None, :], (group_count, 2 * hid))
    told = lax.all_to_all(told, AXES, split_axis=0, concat_axis=0, tiled=True)

    hidden = jnp.dot(query_crops, query_inner, preferred_element_type=jnp.float32)
    average = jnp.mean(hidden, axis=0)
    inv_q = lax.rsqrt(jnp.mean(hidden * hidden, axis=0) - average * average + bn_eps)
    normed = (hidden - average) * inv_q
    active = jnp.maximum(normed, 0.0).astype(jnp.bfloat16)
    projected = jnp.dot(active, query_outer, preferred_element_type=jnp.float32)
    inv_len = lax.rsqrt(jnp.sum(projected * projected, axis=-1, keepdims=True) + norm_eps)
    q = projected * inv_len
    neg_sum, weighted = negatives(q.astype(jnp.bfloat16), distractor_bank)
    neg_sum = jnp.sum(neg_sum, axis=-1, keepdims=True)

    normed_k = (hidden_k - told[:, None, :hid]) * told[:, None, hid:]
    active_k = jnp.maximum(normed_k, 0.0).astype(jnp.bfloat16).reshape(row_count, hid)
    z_k = jnp.dot(active_k, key_outer, preferred_element_type=jnp.float32)
    z_k = z_k * lax.rsqrt(jnp.sum(z_k * z_k, axis=-1, keepdims=True) + norm_eps)
    positives = jnp.zeros_like(z_k).at[flat_req].set(z_k)

    scale_coef = loss_scale / all_rows
    pos = jnp.sum(q * positives, axis=-1, keepdims=True) / sharpness_divisor
    exp_pos = jnp.exp(pos) * QUARTER
    total = exp_pos + neg_sum
    d_pos = scale_coef * (exp_pos / total - 1.0)
    d_q = (d_pos * positives + weighted * (scale_coef / total)) / sharpness_divisor
    d_z = ((d_q - q * jnp.sum(d_q * q, axis=-1, keepdims=True)) * inv_len).astype(jnp.bfloat16)

    grad_out = lax.dot_general(
        active, d_z, (((0,), (0,)), ((), ())), preferred_element_type=jnp.float32
    ).astype(jnp.bfloat16)
    grads = []
    cols = hid // 2
    for part in range(2):
        cut = slice(part * cols, (part + 1) * cols)
        n_cut = normed[:, cut]
        d_act = lax.dot_general(
            d_z, query_outer[cut], (((1,), (1,)), ((), ())), preferred_element_type=jnp.float32
        )
        d_norm = jnp.where(n_cut > 0.0, d_act, 0.0)
        d_hidden = inv_q[cut] * (
            d_norm - jnp.mean(d_norm, axis=0) - n_cut * jnp.mean(d_norm * n_cut, axis=0)
        )
        g = lax.dot_general(
            query_crops,
            d_hidden.astype(jnp.bfloat16),
            (((0,), (0,)), ((), ())),
            preferred_element_type=jnp.float32,
        ).astype(jnp.bfloat16)
        grads.append(g)
    grads[1] = jnp.concatenate([grads[1], grad_out], axis=1)
    left, right = scatter_sum(grads)
    return (jnp.concatenate([left, right[:, :cols]], axis=1), right[:, cols:])


def solution(mesh):
    placed = (
        P(AXES, None),
        P(AXES, None),
        P(AXES),
        P(),
        P(),
        P(),
        P(),
        P(),
    )
    return jax.shard_map(
        per_device,
        mesh=mesh,
        in_specs=placed,
        out_specs=(P(AXES, None), P(AXES, None)),
        check_vma=False,
    )
```

time: 466 us -> 218 us (0.47)
  waiting for transfers between devices: 327 us -> 47.6 us
  starting transfers between devices: 7.73 us -> 38.8 us
  matrix products: 68.7 us -> 39.1 us
  other arithmetic: 2.56 us -> 28.6 us
  between operations: 14.2 us -> 1.22 us
  Pallas kernels: 0 us -> 11 us
  local copies, waits for them, and re-layouts: 29.3 us -> 36 us
    unnamed x3 -> x0, waiting for transfers between devices: 182 us -> none
    reduce_scatter x1 -> x0, waiting for transfers between devices: 107 us -> none  [per_device(): lax.psum_scatter(grad_out, ('dp', 'crop'), scatter_dimension=0, tiled=True)]
    ppermute x0 -> x18, waiting for transfers between devices: none -> 37.2 us  [the longest x6 31.2 us: swap(): return lax.ppermute(x, axis, [(i, i ^ bit) for i in range(size)])]
    ppermute x0 -> x18, starting transfers between devices: none -> 31.3 us  [the longest x6 21 us: line_scatter(): lax.ppermute(out, 'dp', [(2 * p + b, 2 * p + 2 + b) for p in range(k) for...]
    dot_general x9, matrix products: 68.7 us -> 39.1 us  [the longest x1 12.4 us: per_device(): hidden_k = jnp.dot(by_group, key_inner, preferred_element_type=jnp.float32)]
    all_to_all x2, waiting for transfers between devices: 38.8 us -> 10.3 us  [the longest x1 9.2 us: per_device(): told = lax.all_to_all(told, AXES, split_axis=0, concat_axis=0, tiled=True)]
    convert_element_type x1 -> x14, other arithmetic: 0.06 us -> 15.5 us  [the longest x12 12.2 us: add(): return (a.astype(jnp.float32) + b.astype(jnp.float32)).astype(jnp.bfloat16)]
    unnamed x9 -> x27, local copies, waits for them, and re-layouts: 19.6 us -> 5.45 us
  transfers between devices with their start and end apart: 4 -> 20, of which waited for: 3 -> 10; matrix products, arithmetic and copies ran while one was open for 11% -> 25% of each run, Pallas kernels for 0% -> 0%
where the time goes in v1:
time: 218 us; the launch traced here: 217 us
  waiting for transfers between devices  47.6 us (22%)
  matrix products  39.1 us (18%)
  starting transfers between devices  38.8 us (18%)
  local copies, waits for them, and re-layouts  36 us (17%)
  other arithmetic  28.6 us (13%)
  blocking collectives  14.2 us (7%)
  Pallas kernels  11 us (5%)
    ppermute x6, waiting for transfers between devices, swap(): return lax.ppermute(x, axis, [(i, i ^ bit) for i in range(size)])  31.2 us
    ppermute x6, starting transfers between devices, line_scatter(): lax.ppermute(out, 'dp', [(2 * p + b, 2 * p + 2 + b) for p in range(k) for...  21 us
    all_to_all x1, blocking collectives, per_device(): lax.all_to_all(wanted, AXES, split_axis=0, concat_axis=0, tiled=True)  14.2 us
    dot_general x1, matrix products, per_device(): hidden_k = jnp.dot(by_group, key_inner, preferred_element_type=jnp.float32)  12.4 us
    convert_element_type x12, other arithmetic, add(): return (a.astype(jnp.float32) + b.astype(jnp.float32)).astype(jnp.bfloat16)  12.2 us
    pallas_call x1, Pallas kernels, negatives(): pl.pallas_call(neg_kernel, grid=(bank.shape[0] // tile,), in_specs=[pl.Bl...  11 us
    dot_general x1, matrix products, per_device(): jnp.dot(query_crops, query_inner, preferred_element_type=jnp.float32)  9.46 us
    all_to_all x1, waiting for transfers between devices, per_device(): told = lax.all_to_all(told, AXES, split_axis=0, concat_axis=0, tiled=True)  9.2 us
  transfers between devices with their start and end apart: 20, of which 10 were waited for; matrix products, arithmetic and copies ran while one was open for 25% of the time, Pallas kernels for 0%

profile of v1, /device:TPU:0, one launch (start us, length us, event | category | flops | bytes accessed | tf_op | source)
XLA Modules:
  0.0 216.5 jit_solution(3064209085772310826)
XLA Ops:
  1.6 14.2 %all_to_all.27 = s32[32,1,16]{2,1,0:T(1,128)S(1)} all-to-all(s32[32,1,16]{2,1,0:T(1,128)S(1)} %bitcast.115), channel_id=1, replica_groups=mesh['dp'=8,'crop'=4] {'dp','crop'}, dimensions={0} | all-to-all | bytes 4096 | tf_op jit(solution)/shard_map/all_to_all | solution.py:142
  15.9 12.4 %bitcast_reduce_fusion = (f32[32,2048]{1,0:T(8,128)S(1)}, f32[32,2048]{1,0:T(8,128)S(1)}, f32[512,2048]{1,0:T(8,128)}) fusion(bf16[2048,2048]{1,0:T(8,128)(2,1)} %param.14, bf16[512,2048]{1,0:T(8,128)(2,1)} %param.9, s32[512]{0:T(512)S(1)} %eq.20), kind=kOutput, calls=%fused_computation.11 | convolution fusion | flops 5373034496 | bytes 15206400 | tf_op jit(solution)/shard_map/dot_general | solution.py:147
  28.3 1.4 all_to_all.20
  29.7 2.6 %all-to-all-start.1 = ((f32[32,1,4096]{2,1,0:T(1,128)}), f32[32,1,4096]{2,1,0:T(1,128)S(1)}, u32[]{:S(2)}, u32[]{:S(2)}) async-start(f32[32,1,4096]{2,1,0:T(1,128)} %all_to_all.20), calls=%async_computation.1 | async-start | bytes 1048576 | tf_op jit(solution)/shard_map/all_to_all | solution.py:152
  32.3 9.5 %fusion.40 = (f32[2048]{0:T(1024)S(1)}, f32[2048]{0:T(1024)S(1)}, f32[512,2048]{1,0:T(8,128)}) fusion(bf16[512,2048]{1,0:T(8,128)(2,1)S(1)} %copy-done, bf16[2048,2048]{1,0:T(8,128)(2,1)} %param.12), kind=kOutput, calls=%fused_computation.116 | convolution fusion | flops 4298108928 | bytes 14696448 | tf_op jit(solution)/shard_map/dot_general | solution.py:159
  41.7 4.9 %subtract_multiply_fusion = f32[512,2048]{1,0:T(8,128)} fusion(f32[512,2048]{1,0:T(8,128)} %get-tuple-element.36, f32[2048]{0:T(1024)S(1)} %get-tuple-element.33, f32[2048]{0:T(1024)S(1)} %get-tuple-element.32), kind=kLoop, calls=%fused_computation.16 | loop fusion | flops 2097152 | bytes 8404992 | tf_op jit(solution)/shard_map/mul | solution.py:162
  46.7 1.1 all-to-all-done.1
  48.2 1.3 broadcast_in_dim.7
  49.5 4.9 %all-to-all-start.2 = ((f32[32,1,4096]{2,1,0:T(1,128)}), f32[32,1,4096]{2,1,0:T(1,128)S(1)}, u32[]{:S(2)}, u32[]{:S(2)}) async-start(f32[32,1,4096]{2,1,0:T(1,128)} %broadcast_in_dim.7), calls=%async_computation.2 | async-start | bytes 1048576 | tf_op jit(solution)/shard_map/all_to_all | solution.py:157
  54.4 3.7 %multiply_reduce_fusion.6 = (f32[512]{0:T(512)S(1)}, f32[512,128]{0,1:T(8,128)}) fusion(bf16[2048,128]{1,0:T(8,128)(2,1)S(1)} %copy-done.10, f32[512,2048]{1,0:T(8,128)} %subtract_multiply_fusion), kind=kOutput, calls=%fused_computation.83 | convolution fusion | flops 270663168 | bytes 4982784 | tf_op jit(solution)/shard_map/dot_general | solution.py:164
  60.5 9.2 %all-to-all-done.2 = f32[32,1,4096]{2,1,0:T(1,128)S(1)} async-done(((f32[32,1,4096]{2,1,0:T(1,128)}), f32[32,1,4096]{2,1,0:T(1,128)S(1)}, u32[]{:S(2)}, u32[]{:S(2)}) %all-to-all-start.2) | async-done | bytes 524320 | tf_op jit(solution)/shard_map/all_to_all | solution.py:157
  70.1 3.0 %fusion.3 = bf16[512,2048]{1,0:T(8,128)(2,1)S(1)} fusion(f32[512,2048]{1,0:T(8,128)} %get-tuple-element.39, f32[32,2048]{1,0:T(8,128)S(1)} %get-tuple-element.25, f32[32,2048]{1,0:T(8,128)S(1)} %get-tuple-element.24), kind=kLoop, calls=%fused_computation.8 | loop fusion | flops 4194304 | bytes 6815744 | tf_op jit(solution)/shard_map/convert_element_type | solution.py:171
  74.1 1.9 scatter_custom_fusion
  76.3 2.2 %copy-done.1 = bf16[16384,128]{1,0:T(8,128)(2,1)S(1)} copy-done((bf16[16384,128]{1,0:T(8,128)(2,1)S(1)}, bf16[16384,128]{1,0:T(8,128)(2,1)}, u32[]{:S(2)}) %copy-start.1) | copy-done | bytes 4194328
  78.4 11.0 %negatives.1 = (f32[512,128]{1,0:T(8,128)S(1)}, f32[512,128]{1,0:T(8,128)S(1)}) custom-call(bf16[512,128]{1,0:T(8,128)(2,1)S(1)} %get-tuple-element.27.q_ref, bf16[16384,128]{1,0:T(8,128)(2,1)S(1)} %copy-done.1), custom_call_target="tpu_custom_call" | custom-call | flops 4294967296 | bytes 4194304 | tf_op jit(solution)/shard_map/negatives/pallas_call | solution.py:41
  90.4 2.3 %compare_select_fusion = f32[512,1024]{1,0:T(8,128)S(1)} fusion(f32[512,2048]{1,0:T(8,128)} %subtract_multiply_fusion, bf16[512,128]{1,0:T(8,128)(2,1)S(1)} %multiply_convert_fusion.4, bf16[2048,128]{1,0:T(8,128)(2,1)} %param.13), kind=kOutput, calls=%fused_computation.31 | convolution fusion | flops 135266304 | bytes 4587520 | tf_op jit(solution)/shard_map/dot_general | solution.py:192
  94.6 1.2 multiply_reduce_fusion.2
  95.8 4.6 %convert_bitcast_fusion.1 = bf16[2048,1024]{0,1:T(8,128)(2,1)} fusion(bf16[512,2048]{1,0:T(8,128)(2,1)S(1)} %copy-done, f32[512,1024]{1,0:T(8,128)S(1)} %get-tuple-element.42, f32[512,2048]{1,0:T(8,128)S(1)} %copy-done.2, f32[1024]{0:T(1024)S(1)} %get-tuple-element.45, f32[1024]{0:T(1024)S(1)} %get-tuple-element.46, f32[1024]{0:T(1024)S(1)} %get-tuple-element.30), kind=kOutput, calls=%fused_computation.14 | convolution fusion | flops 2152202240 | bytes 10498048 | tf_op jit(solution)/shard_map/dot_general | solution.py:199
  100.4 6.4 %copy.25 = bf16[2048,1024]{1,0:T(8,128)(2,1)} copy(bf16[2048,1024]{0,1:T(8,128)(2,1)} %convert_bitcast_fusion.1) | data formatting | bytes 8388608 | tf_op jit(solution)/shard_map/convert_element_type | solution.py:204
  106.9 3.3 %dynamic-slice_bitcast_fusion = bf16[4,2,2,64,1024]{4,3,2,1,0:T(8,128)(2,1)} fusion(bf16[4,2,2,2,64,1024]{5,4,3,2,1,0:T(8,128)(2,1)} %bitcast.111, s32[]{:T(128)S(6)} %select_n.94), kind=kLoop, calls=%fused_computation.28 | loop fusion | bytes 4194308 | tf_op jit(solution)/shard_map/jit(dynamic_index_in_dim)/squeeze | solution.py:73
  110.1 4.2 %convert_bitcast_fusion = bf16[2048,1024]{0,1:T(8,128)(2,1)S(1)} fusion(bf16[512,2048]{1,0:T(8,128)(2,1)S(1)} %copy-done, f32[512,1024]{1,0:T(8,128)} %copy-done.8, f32[512,2048]{1,0:T(8,128)S(1)} %copy-done.3, f32[1024]{0:T(1024)S(1)} %get-tuple-element.43, f32[1024]{0:T(1024)S(1)} %get-tuple-element.44, f32[1024]{0:T(1024)S(1)} %get-tuple-element.31), kind=kOutput, calls=%fused_computation.13 | convolution fusion | flops 2152202240 | bytes 10498048 | tf_op jit(solution)/shard_map/dot_general | solution.py:199
  114.3 2.5 %pad_maximum_fusion = bf16[2048,1152]{0,1:T(8,128)(2,1)} fusion(bf16[2048,128]{0,1:T(8,128)(2,1)S(1)} %convolution_convert_fusion.1, bf16[2048,1024]{0,1:T(8,128)(2,1)S(1)} %convert_bitcast_fusion), kind=kLoop, calls=%fused_computation.1 | loop fusion | flops 9437184 | bytes 9437184 | tf_op jit(solution)/shard_map/concatenate | solution.py:206
  116.9 6.7 %copy.26 = bf16[2048,1152]{1,0:T(8,128)(2,1)} copy(bf16[2048,1152]{0,1:T(8,128)(2,1)} %pad_maximum_fusion) | data formatting | bytes 9437184 | tf_op jit(solution)/shard_map/concatenate | solution.py:206
  123.6 4.2 %constant_dynamic-slice_fusion.1 = (bf16[4,2,2,1,64,1152]{5,4,3,2,1,0:T(8,128)(2,1)}, bf16[4,2,2,1,64,1152]{5,4,3,2,1,0:T(8,128)(2,1)S(1)}) fusion(bf16[4,2,2,2,64,1152]{5,4,3,2,1,0:T(8,128)(2,1)} %bitcast.110, s32[]{:T(128)S(6)} %select_n.93, s32[]{:T(128)S(6)} %select_n.94), kind=kLoop, calls=%fused_computation.99 | loop fusion | bytes 9437192 | tf_op jit(solution)/shard_map/jit(dynamic_index_in_dim)/dynamic_slice | solution.py:72
  127.8 1.6 copy.36
  129.9 3.4 %fusion.1 = bf16[4,2,2,64,1024]{4,3,2,1,0:T(8,128)(2,1)S(1)} fusion(bf16[4,2,2,64,1024]{4,3,2,1,0:T(8,128)(2,1)} %collective-permute-done, bf16[4,2,2,2,64,1024]{5,4,3,2,1,0:T(8,128)(2,1)} %bitcast.112, s32[]{:T(128)S(6)} %select_n.93), kind=kLoop, calls=%fused_computation.5 | loop fusion | flops 4194304 | bytes 6291460 | tf_op jit(solution)/shard_map/convert_element_type | solution.py:78
  133.3 1.1 dynamic-slice_bitcast_fusion.2
  134.4 1.3 collective-permute-start.1
  135.7 2.4 %fusion = bf16[4,2,2,64,1152]{4,3,0,1,2:T(8,128)(2,1)S(1)} fusion(bf16[4,2,2,64,1152]{4,3,0,1,2:T(8,128)(2,1)} %collective-permute-done.9, bf16[4,2,2,1,64,1152]{5,4,3,2,1,0:T(8,128)(2,1)S(1)} %copy-done.4), kind=kLoop, calls=%fused_computation.3 | loop fusion | flops 4718592 | bytes 7077888 | tf_op jit(solution)/shard_map/convert_element_type | solution.py:78
  138.1 1.4 copy-done.5
  139.6 1.2 collective-permute-start.10
  140.8 19.0 %collective-permute-done.1 = bf16[4,2,64,1024]{3,2,1,0:T(8,128)(2,1)} collective-permute-done((bf16[4,2,64,1024]{3,2,1,0:T(8,128)(2,1)}, bf16[4,2,64,1024]{3,2,1,0:T(8,128)(2,1)}, u32[]{:S(2)}, u32[]{:S(2)}) %collective-permute-start.1) | collective-permute-done | bytes 1048608 | tf_op jit(solution)/shard_map/ppermute | solution.py:68
  159.8 1.9 fusion.6
  162.7 1.3 collective-permute-start.2
  164.0 4.6 %collective-permute-done.10 = bf16[4,2,64,1152]{3,2,0,1:T(8,128)(2,1)} collective-permute-done((bf16[4,2,64,1152]{3,2,0,1:T(8,128)(2,1)S(1)}, bf16[4,2,64,1152]{3,2,0,1:T(8,128)(2,1)}, u32[]{:S(2)}, u32[]{:S(2)}) %collective-permute-start.10) | collective-permute-done | bytes 1179680 | tf_op jit(solution)/shard_map/ppermute | solution.py:68
  168.6 1.6 fusion.5
  171.8 6.7 %collective-permute-done.2 = bf16[4,64,1024]{2,1,0:T(8,128)(2,1)} collective-permute-done((bf16[4,64,1024]{2,1,0:T(8,128)(2,1)}, bf16[4,64,1024]{2,1,0:T(8,128)(2,1)}, u32[]{:S(2)}, u32[]{:S(2)}) %collective-permute-start.2) | collective-permute-done | bytes 524320 | tf_op jit(solution)/shard_map/ppermute | solution.py:68
  178.6 1.4 fusion.8
  180.0 2.7 %collective-permute-start.3 = (bf16[64,1024]{1,0:T(8,128)(2,1)S(1)}, bf16[64,1024]{1,0:T(8,128)(2,1)S(1)}, u32[]{:S(2)}, u32[]{:S(2)}) collective-permute-start(bf16[64,1024]{1,0:T(8,128)(2,1)S(1)} %get-tuple-element.22), channel_id=1, source_target_pairs={{0,8},{4,12},{1,9},{5,13},{2,10},{6,14},{3,11},{7,15}} | collective-permute-start | bytes 393224 | tf_op jit(solution)/shard_map/ppermute | solution.py:89
  184.2 1.2 fusion.7
  185.5 2.8 %collective-permute-start.12 = (bf16[64,1152]{1,0:T(8,128)(2,1)S(1)}, bf16[64,1152]{1,0:T(8,128)(2,1)S(1)}, u32[]{:S(2)}, u32[]{:S(2)}) collective-permute-start(bf16[64,1152]{1,0:T(8,128)(2,1)S(1)} %get-tuple-element.18), channel_id=1, source_target_pairs={{0,8},{4,12},{1,9},{5,13},{2,10},{6,14},{3,11},{7,15}} | collective-permute-start | bytes 442376 | tf_op jit(solution)/shard_map/ppermute | solution.py:89
  188.3 1.5 collective-permute-start.4
  190.9 4.4 %collective-permute-start.13 = (bf16[64,1152]{1,0:T(8,128)(2,1)S(1)}, bf16[64,1152]{1,0:T(8,128)(2,1)S(1)}, u32[]{:S(2)}, u32[]{:S(2)}) collective-permute-start(bf16[64,1152]{1,0:T(8,128)(2,1)S(1)} %fusion.21), channel_id=1, source_target_pairs={{0,8},{4,12},{8,16},{12,20},{1,9},{5,13},{9,17},{13,21},{2,10},{6,... | collective-permute-start | bytes 442376 | tf_op jit(solution)/shard_map/ppermute | solution.py:89
  196.1 2.9 %collective-permute-start.5 = (bf16[64,1024]{1,0:T(8,128)(2,1)S(1)}, bf16[64,1024]{1,0:T(8,128)(2,1)S(1)}, u32[]{:S(2)}, u32[]{:S(2)}) collective-permute-start(bf16[64,1024]{1,0:T(8,128)(2,1)S(1)} %get-tuple-element.20), channel_id=1, source_target_pairs={{0,8},{4,12},{8,16},{12,20},{16,24},{20,28},{1,9},{5,13},{9,17},{1... | collective-permute-start | bytes 393224 | tf_op jit(solution)/shard_map/ppermute | solution.py:89
  199.9 1.3 collective-permute-start.8
  201.2 6.7 %collective-permute-start.14 = (bf16[64,1152]{1,0:T(8,128)(2,1)S(1)}, bf16[64,1152]{1,0:T(8,128)(2,1)S(1)}, u32[]{:S(2)}, u32[]{:S(2)}) collective-permute-start(bf16[64,1152]{1,0:T(8,128)(2,1)S(1)} %get-tuple-element.16), channel_id=1, source_target_pairs={{0,8},{4,12},{8,16},{12,20},{16,24},{20,28},{1,9},{5,13},{9,17},{1... | collective-permute-start | bytes 442376 | tf_op jit(solution)/shard_map/ppermute | solution.py:89
  208.0 1.3 collective-permute-start.17
  210.5 4.4 %collective-permute-done.17 = bf16[64,1152]{1,0:T(8,128)(2,1)S(1)} collective-permute-done((bf16[64,1152]{1,0:T(8,128)(2,1)S(1)}, bf16[64,1152]{1,0:T(8,128)(2,1)S(1)}, u32[]{:S(2)}, u32[]{:S(2)}) %collective-permute-start.17) | collective-permute-done | bytes 147488 | tf_op jit(solution)/shard_map/ppermute | solution.py:95
  (90 shorter events, 18.4 us)
Async XLA Ops:
  0.6 31.6 %copy-start = (bf16[512,2048]{1,0:T(8,128)(2,1)S(1)}, bf16[512,2048]{1,0:T(8,128)(2,1)}, u32[]{:S(2)}) copy-start(bf16[512,2048]{1,0:T(8,128)(2,1)} %param.8) | copy-start | bytes 6291460
  29.7 18.2 %all-to-all-start.1 = ((f32[32,1,4096]{2,1,0:T(1,128)}), f32[32,1,4096]{2,1,0:T(1,128)S(1)}, u32[]{:S(2)}, u32[]{:S(2)}) async-start(f32[32,1,4096]{2,1,0:T(1,128)} %all_to_all.20), calls=%async_computation.1 | async-start | bytes 1048576 | tf_op jit(solution)/shard_map/all_to_all | solution.py:152
  46.7 7.7 %copy-start.10 = (bf16[2048,128]{1,0:T(8,128)(2,1)S(1)}, bf16[2048,128]{1,0:T(8,128)(2,1)}, u32[]{:S(2)}) copy-start(bf16[2048,128]{1,0:T(8,128)(2,1)} %param.13) | copy-start | bytes 1572868
  49.5 20.2 %all-to-all-start.2 = ((f32[32,1,4096]{2,1,0:T(1,128)}), f32[32,1,4096]{2,1,0:T(1,128)S(1)}, u32[]{:S(2)}, u32[]{:S(2)}) async-start(f32[32,1,4096]{2,1,0:T(1,128)} %broadcast_in_dim.7), calls=%async_computation.2 | async-start | bytes 1048576 | tf_op jit(solution)/shard_map/all_to_all | solution.py:157
  70.1 3.0 %copy-start.12 = (bf16[2048,128]{1,0:T(8,128)(2,1)S(1)}, bf16[2048,128]{1,0:T(8,128)(2,1)}, u32[]{:S(2)}) copy-start(bf16[2048,128]{1,0:T(8,128)(2,1)} %param.15) | copy-start | bytes 1572868
  76.3 2.2 %copy-start.1 = (bf16[16384,128]{1,0:T(8,128)(2,1)S(1)}, bf16[16384,128]{1,0:T(8,128)(2,1)}, u32[]{:S(2)}) copy-start(bf16[16384,128]{1,0:T(8,128)(2,1)} %bank_ref.1) | copy-start | bytes 12582916
  90.3 2.9 %copy-start.2 = (f32[512,2048]{1,0:T(8,128)S(1)}, f32[512,2048]{1,0:T(8,128)}, u32[]{:S(2)}) copy-start(f32[512,2048]{1,0:T(8,128)} %subtract_multiply_fusion) | copy-start | bytes 12582916
  93.2 1.3 copy-start.8
  93.2 1.4 copy-start.11
  106.8 3.3 %copy-start.3 = (f32[512,2048]{1,0:T(8,128)S(1)}, f32[512,2048]{1,0:T(8,128)}, u32[]{:S(2)}) copy-start(f32[512,2048]{1,0:T(8,128)} %subtract_multiply_fusion) | copy-start | bytes 12582916
  110.1 19.8 %collective-permute-start = (bf16[4,2,2,64,1024]{4,3,2,1,0:T(8,128)(2,1)}, bf16[4,2,2,64,1024]{4,3,2,1,0:T(8,128)(2,1)}, u32[]{:S(2)}, u32[]{:S(2)}) collective-permute-start(bf16[4,2,2,64,1024]{4,3,2,1,0:T(8,128)(2,1)} %dynamic-slice_bitcast_fusion), channel_id=1, source_target_pairs={{0,1},{1,0},{2,3},{3,2},{4,5},{5,4},{6,7},{7,6},{8,9},{9,8},{10,11... | collective-permute-start | bytes 6291464 | tf_op jit(solution)/shard_map/ppermute | solution.py:68
  129.4 6.3 %collective-permute-start.9 = (bf16[4,2,2,64,1152]{4,3,0,1,2:T(8,128)(2,1)}, bf16[4,2,2,64,1152]{4,3,0,1,2:T(8,128)(2,1)}, u32[]{:S(2)}, u32[]{:S(2)}) collective-permute-start(bf16[4,2,2,64,1152]{4,3,0,1,2:T(8,128)(2,1)} %bitcast.108), channel_id=1, source_target_pairs={{0,1},{1,0},{2,3},{3,2},{4,5},{5,4},{6,7},{7,6},{8,9},{9,8},{10,11... | collective-permute-start | bytes 7077896 | tf_op jit(solution)/shard_map/ppermute | solution.py:68
  129.9 5.8 %copy-start.4 = (bf16[4,2,2,1,64,1152]{5,4,3,2,1,0:T(8,128)(2,1)S(1)}, bf16[4,2,2,1,64,1152]{5,4,3,2,1,0:T(8,128)(2,1)}, u32[]{:S(2)}) copy-start(bf16[4,2,2,1,64,1152]{5,4,3,2,1,0:T(8,128)(2,1)} %get-tuple-element.14) | copy-start | bytes 7077892
  133.3 2.4 %copy-start.7 = (bf16[4,2,2,64,1024]{4,3,2,1,0:T(8,128)(2,1)}, bf16[4,2,2,64,1024]{4,3,2,1,0:T(8,128)(2,1)S(1)}, u32[]{:S(2)}) copy-start(bf16[4,2,2,64,1024]{4,3,2,1,0:T(8,128)(2,1)S(1)} %fusion.1) | copy-start | bytes 6291460
  134.4 25.4 %collective-permute-start.1 = (bf16[4,2,64,1024]{3,2,1,0:T(8,128)(2,1)}, bf16[4,2,64,1024]{3,2,1,0:T(8,128)(2,1)}, u32[]{:S(2)}, u32[]{:S(2)}) collective-permute-start(bf16[4,2,64,1024]{3,2,1,0:T(8,128)(2,1)} %dynamic-slice_bitcast_fusion.2), channel_id=1, source_target_pairs={{0,4},{4,0},{8,12},{12,8},{16,20},{20,16},{24,28},{28,24},{1,5},{5... | collective-permute-start | bytes 3145736 | tf_op jit(solution)/shard_map/ppermute | solution.py:68
  138.1 1.4 copy-start.5
  139.6 29.0 %collective-permute-start.10 = (bf16[4,2,64,1152]{3,2,0,1:T(8,128)(2,1)S(1)}, bf16[4,2,64,1152]{3,2,0,1:T(8,128)(2,1)}, u32[]{:S(2)}, u32[]{:S(2)}) collective-permute-start(bf16[4,2,64,1152]{3,2,0,1:T(8,128)(2,1)S(1)} %dynamic-slice_bitcast_fusion.1), channel_id=1, source_target_pairs={{0,2},{1,3},{2,0},{3,1},{4,6},{5,7},{6,4},{7,5},{8,10},{9,11},{10,... | collective-permute-start | bytes 3538952 | tf_op jit(solution)/shard_map/ppermute | solution.py:68
  140.8 27.8 %copy-start.6 = (bf16[4,2,2,64,1152]{4,3,0,1,2:T(8,128)(2,1)S(1)}, bf16[4,2,2,64,1152]{4,3,0,1,2:T(8,128)(2,1)}, u32[]{:S(2)}) copy-start(bf16[4,2,2,64,1152]{4,3,0,1,2:T(8,128)(2,1)} %copy-done.5) | copy-start | bytes 7077892
  161.8 9.3 %copy-start.9 = (bf16[4,2,64,1024]{3,2,1,0:T(8,128)(2,1)}, bf16[4,2,64,1024]{3,2,1,0:T(8,128)(2,1)S(1)}, u32[]{:S(2)}) copy-start(bf16[4,2,64,1024]{3,2,1,0:T(8,128)(2,1)S(1)} %fusion.6) | copy-start | bytes 3145732
  162.7 15.9 %collective-permute-start.2 = (bf16[4,64,1024]{2,1,0:T(8,128)(2,1)}, bf16[4,64,1024]{2,1,0:T(8,128)(2,1)}, u32[]{:S(2)}, u32[]{:S(2)}) collective-permute-start(bf16[4,64,1024]{2,1,0:T(8,128)(2,1)} %dynamic-slice_bitcast_fusion.4), channel_id=1, source_target_pairs={{0,2},{1,3},{2,0},{3,1},{4,6},{5,7},{6,4},{7,5},{8,10},{9,11},{10,... | collective-permute-start | bytes 1572872 | tf_op jit(solution)/shard_map/ppermute | solution.py:68
  171.1 13.1 %collective-permute-start.11 = (bf16[4,64,1152]{2,1,0:T(8,128)(2,1)}, bf16[4,64,1152]{2,1,0:T(8,128)(2,1)}, u32[]{:S(2)}, u32[]{:S(2)}) collective-permute-start(bf16[4,64,1152]{2,1,0:T(8,128)(2,1)} %dynamic-slice_bitcast_fusion.3), channel_id=1, source_target_pairs={{0,4},{4,0},{8,12},{12,8},{16,20},{20,16},{24,28},{28,24},{1,5},{5... | collective-permute-start | bytes 1769480 | tf_op jit(solution)/shard_map/ppermute | solution.py:68
  180.0 8.2 %collective-permute-start.3 = (bf16[64,1024]{1,0:T(8,128)(2,1)S(1)}, bf16[64,1024]{1,0:T(8,128)(2,1)S(1)}, u32[]{:S(2)}, u32[]{:S(2)}) collective-permute-start(bf16[64,1024]{1,0:T(8,128)(2,1)S(1)} %get-tuple-element.22), channel_id=1, source_target_pairs={{0,8},{4,12},{1,9},{5,13},{2,10},{6,14},{3,11},{7,15}} | collective-permute-start | bytes 393224 | tf_op jit(solution)/shard_map/ppermute | solution.py:89
  182.8 12.6 %collective-permute-start.6 = (bf16[64,1024]{1,0:T(8,128)(2,1)S(1)}, bf16[64,1024]{1,0:T(8,128)(2,1)S(1)}, u32[]{:S(2)}, u32[]{:S(2)}) collective-permute-start(bf16[64,1024]{1,0:T(8,128)(2,1)S(1)} %get-tuple-element.23), channel_id=1, source_target_pairs={{24,16},{28,20},{25,17},{29,21},{26,18},{30,22},{27,19},{31,23}} | collective-permute-start | bytes 393224 | tf_op jit(solution)/shard_map/ppermute | solution.py:95
  185.5 5.4 %collective-permute-start.12 = (bf16[64,1152]{1,0:T(8,128)(2,1)S(1)}, bf16[64,1152]{1,0:T(8,128)(2,1)S(1)}, u32[]{:S(2)}, u32[]{:S(2)}) collective-permute-start(bf16[64,1152]{1,0:T(8,128)(2,1)S(1)} %get-tuple-element.18), channel_id=1, source_target_pairs={{0,8},{4,12},{1,9},{5,13},{2,10},{6,14},{3,11},{7,15}} | collective-permute-start | bytes 442376 | tf_op jit(solution)/shard_map/ppermute | solution.py:89
  188.3 7.0 %collective-permute-start.4 = (bf16[64,1024]{1,0:T(8,128)(2,1)S(1)}, bf16[64,1024]{1,0:T(8,128)(2,1)S(1)}, u32[]{:S(2)}, u32[]{:S(2)}) collective-permute-start(bf16[64,1024]{1,0:T(8,128)(2,1)S(1)} %fusion.26), channel_id=1, source_target_pairs={{0,8},{4,12},{8,16},{12,20},{1,9},{5,13},{9,17},{13,21},{2,10},{6,... | collective-permute-start | bytes 393224 | tf_op jit(solution)/shard_map/ppermute | solution.py:89
  189.8 9.2 %collective-permute-start.15 = (bf16[64,1152]{1,0:T(8,128)(2,1)S(1)}, bf16[64,1152]{1,0:T(8,128)(2,1)S(1)}, u32[]{:S(2)}, u32[]{:S(2)}) collective-permute-start(bf16[64,1152]{1,0:T(8,128)(2,1)S(1)} %get-tuple-element.19), channel_id=1, source_target_pairs={{24,16},{28,20},{25,17},{29,21},{26,18},{30,22},{27,19},{31,23}} | collective-permute-start | bytes 442376 | tf_op jit(solution)/shard_map/ppermute | solution.py:95
  190.9 8.1 %collective-permute-start.13 = (bf16[64,1152]{1,0:T(8,128)(2,1)S(1)}, bf16[64,1152]{1,0:T(8,128)(2,1)S(1)}, u32[]{:S(2)}, u32[]{:S(2)}) collective-permute-start(bf16[64,1152]{1,0:T(8,128)(2,1)S(1)} %fusion.21), channel_id=1, source_target_pairs={{0,8},{4,12},{8,16},{12,20},{1,9},{5,13},{9,17},{13,21},{2,10},{6,... | collective-permute-start | bytes 442376 | tf_op jit(solution)/shard_map/ppermute | solution.py:89
  195.4 4.4 %collective-permute-start.7 = (bf16[64,1024]{1,0:T(8,128)(2,1)S(1)}, bf16[64,1024]{1,0:T(8,128)(2,1)S(1)}, u32[]{:S(2)}, u32[]{:S(2)}) collective-permute-start(bf16[64,1024]{1,0:T(8,128)(2,1)S(1)} %get-tuple-element.21), channel_id=1, source_target_pairs={{16,8},{20,12},{24,16},{28,20},{17,9},{21,13},{25,17},{29,21},{18,... | collective-permute-start | bytes 393224 | tf_op jit(solution)/shard_map/ppermute | solution.py:95
  196.1 13.2 %collective-permute-start.5 = (bf16[64,1024]{1,0:T(8,128)(2,1)S(1)}, bf16[64,1024]{1,0:T(8,128)(2,1)S(1)}, u32[]{:S(2)}, u32[]{:S(2)}) collective-permute-start(bf16[64,1024]{1,0:T(8,128)(2,1)S(1)} %get-tuple-element.20), channel_id=1, source_target_pairs={{0,8},{4,12},{8,16},{12,20},{16,24},{20,28},{1,9},{5,13},{9,17},{1... | collective-permute-start | bytes 393224 | tf_op jit(solution)/shard_map/ppermute | solution.py:89
  199.1 8.8 %collective-permute-start.16 = (bf16[64,1152]{1,0:T(8,128)(2,1)S(1)}, bf16[64,1152]{1,0:T(8,128)(2,1)S(1)}, u32[]{:S(2)}, u32[]{:S(2)}) collective-permute-start(bf16[64,1152]{1,0:T(8,128)(2,1)S(1)} %get-tuple-element.17), channel_id=1, source_target_pairs={{16,8},{20,12},{24,16},{28,20},{17,9},{21,13},{25,17},{29,21},{18,... | collective-permute-start | bytes 442376 | tf_op jit(solution)/shard_map/ppermute | solution.py:95
  199.9 10.0 %collective-permute-start.8 = (bf16[64,1024]{1,0:T(8,128)(2,1)S(1)}, bf16[64,1024]{1,0:T(8,128)(2,1)S(1)}, u32[]{:S(2)}, u32[]{:S(2)}) collective-permute-start(bf16[64,1024]{1,0:T(8,128)(2,1)S(1)} %fusion.25), channel_id=1, source_target_pairs={{8,0},{12,4},{16,8},{20,12},{24,16},{28,20},{9,1},{13,5},{17,9},{2... | collective-permute-start | bytes 393224 | tf_op jit(solution)/shard_map/ppermute | solution.py:95
  201.2 9.4 %collective-permute-start.14 = (bf16[64,1152]{1,0:T(8,128)(2,1)S(1)}, bf16[64,1152]{1,0:T(8,128)(2,1)S(1)}, u32[]{:S(2)}, u32[]{:S(2)}) collective-permute-start(bf16[64,1152]{1,0:T(8,128)(2,1)S(1)} %get-tuple-element.16), channel_id=1, source_target_pairs={{0,8},{4,12},{8,16},{12,20},{16,24},{20,28},{1,9},{5,13},{9,17},{1... | collective-permute-start | bytes 442376 | tf_op jit(solution)/shard_map/ppermute | solution.py:89
  208.0 7.0 %collective-permute-start.17 = (bf16[64,1152]{1,0:T(8,128)(2,1)S(1)}, bf16[64,1152]{1,0:T(8,128)(2,1)S(1)}, u32[]{:S(2)}, u32[]{:S(2)}) collective-permute-start(bf16[64,1152]{1,0:T(8,128)(2,1)S(1)} %fusion.20), channel_id=1, source_target_pairs={{8,0},{12,4},{16,8},{20,12},{24,16},{28,20},{9,1},{13,5},{17,9},{2... | collective-permute-start | bytes 442376 | tf_op jit(solution)/shard_map/ppermute | solution.py:95

commit v2 on v1

v2 whole, which is shorter than its diff:
```python
import math
import jax
import jax.numpy as jnp
from jax import lax
from jax.experimental import pallas as pl
from jax.experimental.pallas import tpu as pltpu
from jax.sharding import PartitionSpec as P

sharpness_divisor = 0.2
loss_scale = 4096.0
bn_eps = 1e-05
norm_eps = 1e-06
AXES = ("dp", "crop")
QUARTER = 0.25


def neg_kernel(q_ref, bank_ref, sum_ref, u_ref):
    @pl.when(pl.program_id(0) == 0)
    def _():
        sum_ref[...] = jnp.zeros_like(sum_ref)
        u_ref[...] = jnp.zeros_like(u_ref)

    q = q_ref[...]
    step = 256
    total = sum_ref[...]
    u = u_ref[...]
    for j in range(bank_ref.shape[0] // step):
        bank = bank_ref[j * step:(j + 1) * step, :]
        s = lax.dot_general(q, bank, (((1,), (1,)), ((), ())), preferred_element_type=jnp.float32)
        e = jnp.exp2(s * (1.0 / (sharpness_divisor * math.log(2.0))) - 2.0)
        for i in range(step // 128):
            total = total + e[:, i * 128:(i + 1) * 128]
        u = u + jnp.dot(e.astype(jnp.bfloat16), bank, preferred_element_type=jnp.float32)
    sum_ref[...] = total
    u_ref[...] = u


def negatives(q, bank):
    rows, emb = q.shape
    tile = 2048
    return pl.pallas_call(
        neg_kernel,
        grid=(bank.shape[0] // tile,),
        in_specs=[
            pl.BlockSpec((rows, emb), lambda i: (0, 0)),
            pl.BlockSpec((tile, emb), lambda i: (i, 0)),
        ],
        out_specs=[
            pl.BlockSpec((rows, 128), lambda i: (0, 0)),
            pl.BlockSpec((rows, emb), lambda i: (0, 0)),
        ],
        out_shape=[
            jax.ShapeDtypeStruct((rows, 128), jnp.float32),
            jax.ShapeDtypeStruct((rows, emb), jnp.float32),
        ],
        cost_estimate=pl.CostEstimate(
            flops=4 * rows * bank.shape[0] * emb,
            bytes_accessed=bank.shape[0] * emb * 2,
            transcendentals=rows * bank.shape[0],
        ),
        compiler_params=pltpu.CompilerParams(vmem_limit_bytes=32 * 1024 * 1024),
        name="negatives",
    )(q, bank)


TILE = 256
VMEM_LIMIT = 48 * 1024 * 1024


PAIRS = (4, 4)


def params():
    return pltpu.CompilerParams(
        dimension_semantics=("arbitrary",), vmem_limit_bytes=VMEM_LIMIT
    )


def dot(a, b):
    return jnp.dot(a, b, preferred_element_type=jnp.float32)


def dot_t(a, b):
    return lax.dot_general(a, b, (((1,), (1,)), ((), ())), preferred_element_type=jnp.float32)


def whole(shape):
    return pl.BlockSpec(shape, lambda *_: (0,) * len(shape))


def group_rows(groups, per_peer):
    rows = groups * per_peer
    row = lax.broadcasted_iota(jnp.int32, (groups, rows), 1)
    group = lax.broadcasted_iota(jnp.int32, (groups, rows), 0)
    inside = (row >= group * per_peer) & (row < (group + 1) * per_peer)
    return jnp.where(inside, 1.0, 0.0).astype(jnp.float32)


def group_sum(h, groups):
    rows, cols = h.shape
    per_peer = rows // groups
    if per_peer % 8 == 0:
        return jnp.sum(h.reshape(groups, per_peer, cols), axis=1)
    return jnp.dot(
        group_rows(groups, per_peer),
        h,
        precision=lax.Precision.HIGHEST,
        preferred_element_type=jnp.float32,
    )


def group_spread(v, rows):
    groups, cols = v.shape
    per_peer = rows // groups
    if per_peer % 8 == 0:
        return jnp.broadcast_to(v[:, None, :], (groups, per_peer, cols)).reshape(rows, cols)
    return lax.dot_general(
        group_rows(groups, per_peer),
        v,
        (((0,), (0,)), ((), ())),
        precision=lax.Precision.HIGHEST,
        preferred_element_type=jnp.float32,
    )


def key_hidden_kernel(groups, flat_ref, k_ref, w_ref, h_ref, sums_ref, sorted_ref):
    rows = k_ref.shape[0]

    @pl.when(pl.program_id(0) == 0)
    def _():
        cols = lax.broadcasted_iota(jnp.int32, (rows, rows), 1)
        pick = jnp.where(flat_ref[...] == cols, 1.0, 0.0).astype(jnp.bfloat16)
        for i in range(0, k_ref.shape[1], 512):
            sorted_ref[:, i:i + 512] = dot(pick, k_ref[:, i:i + 512]).astype(jnp.bfloat16)

    h = dot(sorted_ref[...], w_ref[...])
    h_ref[...] = h
    sums_ref[:, 0, :TILE] = group_sum(h, groups)
    sums_ref[:, 0, TILE:] = group_sum(h * h, groups)


def key_hidden(flat_col, k, w, groups):
    rows, d = k.shape
    hid = w.shape[1]
    return pl.pallas_call(
        lambda *refs: key_hidden_kernel(groups, *refs),
        grid=(hid // TILE,),
        in_specs=[
            whole((rows, 1)),
            whole((rows, d)),
            pl.BlockSpec((d, TILE), lambda i: (0, i)),
        ],
        out_specs=[
            pl.BlockSpec((rows, TILE), lambda i: (0, i)),
            pl.BlockSpec((groups, 1, 2 * TILE), lambda i: (0, 0, i)),
        ],
        out_shape=[
            jax.ShapeDtypeStruct((rows, hid), jnp.float32),
            jax.ShapeDtypeStruct((groups, 1, 2 * hid), jnp.float32),
        ],
        scratch_shapes=[pltpu.VMEM((rows, d), jnp.bfloat16)],
        cost_estimate=pl.CostEstimate(
            flops=2 * rows * d * (hid + rows), bytes_accessed=2 * d * hid, transcendentals=0
        ),
        compiler_params=params(),
        name="key_hidden",
    )(flat_col, k, w)


def batch_kernel(rows, part_ref, told_ref):
    groups = part_ref.shape[0]
    total = jnp.sum(part_ref[:, 0, :], axis=0, keepdims=True) / rows
    mu = total[:, :TILE]
    inv = lax.rsqrt(total[:, TILE:] - mu * mu + bn_eps)
    told = jnp.concatenate([mu, inv], axis=1)
    told_ref[:, 0, :] = jnp.broadcast_to(told, (groups, 2 * TILE))


def batch(part, rows):
    groups, _, size = part.shape
    block = pl.BlockSpec((groups, 1, 2 * TILE), lambda i: (0, 0, i))
    return pl.pallas_call(
        lambda *refs: batch_kernel(rows, *refs),
        grid=(size // (2 * TILE),),
        in_specs=[block],
        out_specs=block,
        out_shape=jax.ShapeDtypeStruct(part.shape, jnp.float32),
        compiler_params=params(),
        name="batch",
    )(part)


def query_kernel(x_ref, w_ref, w2_ref, n_ref, inv_ref, a_ref, z_ref, len_ref, q_ref, sum_ref):
    i = pl.program_id(0)
    rows = x_ref.shape[0]
    h = dot(x_ref[...], w_ref[...])
    mu = jnp.sum(h, axis=0, keepdims=True) / rows
    inv = lax.rsqrt(jnp.sum(h * h, axis=0, keepdims=True) / rows - mu * mu + bn_eps)
    normed = (h - mu) * inv
    active = jnp.maximum(normed, 0.0).astype(jnp.bfloat16)
    n_ref[...] = normed
    inv_ref[...] = inv
    a_ref[...] = active
    z = dot(active, w2_ref[...])

    @pl.when(i == 0)
    def _():
        sum_ref[...] = z

    @pl.when(i > 0)
    def _():
        sum_ref[...] += z

    @pl.when(i == pl.num_programs(0) - 1)
    def _():
        z = sum_ref[...]
        inv_len = lax.rsqrt(jnp.sum(z * z, axis=-1, keepdims=True) + norm_eps)
        q = z * inv_len
        z_ref[...] = q
        len_ref[...] = inv_len
        q_ref[...] = q.astype(jnp.bfloat16)


def query_forward(x, w, w2):
    rows, d = x.shape
    hid, emb = w2.shape
    return pl.pallas_call(
        query_kernel,
        grid=(hid // TILE,),
        in_specs=[
            whole((rows, d)),
            pl.BlockSpec((d, TILE), lambda i: (0, i)),
            pl.BlockSpec((TILE, emb), lambda i: (i, 0)),
        ],
        out_specs=[
            pl.BlockSpec((rows, TILE), lambda i: (0, i)),
            pl.BlockSpec((1, TILE), lambda i: (0, i)),
            pl.BlockSpec((rows, TILE), lambda i: (0, i)),
            whole((rows, emb)),
            whole((rows, 1)),
            whole((rows, emb)),
        ],
        out_shape=[
            jax.ShapeDtypeStruct((rows, hid), jnp.float32),
            jax.ShapeDtypeStruct((1, hid), jnp.float32),
            jax.ShapeDtypeStruct((rows, hid), jnp.bfloat16),
            jax.ShapeDtypeStruct((rows, emb), jnp.float32),
            jax.ShapeDtypeStruct((rows, 1), jnp.float32),
            jax.ShapeDtypeStruct((rows, emb), jnp.bfloat16),
        ],
        scratch_shapes=[pltpu.VMEM((rows, emb), jnp.float32)],
        cost_estimate=pl.CostEstimate(
            flops=2 * rows * hid * (d + emb), bytes_accessed=2 * d * hid, transcendentals=0
        ),
        compiler_params=params(),
        name="query_forward",
    )(x, w, w2)


def order_kernel(order_ref, x_ref, y_ref):
    rows = y_ref.shape[2]
    core = order_ref[pl.num_programs(0)]
    t = x_ref[...].T
    y_ref[core, 0] = t[:rows]
    y_ref[1 - core, 0] = t[rows:]


def ordered(x, order, core, blocks):
    n, d = x.shape
    half = blocks // 2
    rows = d // blocks
    width = 2 * rows
    if width % 128:
        y = x.T.reshape(half, 2, rows, n)
        y = jnp.zeros_like(y).at[order].set(y)
        return jnp.moveaxis(jnp.where(core == 0, y, y[:, ::-1]), 1, 0).reshape(d, n)
    return pl.pallas_call(
        order_kernel,
        grid_spec=pltpu.PrefetchScalarGridSpec(
            num_scalar_prefetch=1,
            grid=(half,),
            in_specs=[pl.BlockSpec((n, width), lambda i, o: (0, i))],
            out_specs=pl.BlockSpec((2, 1, rows, n), lambda i, o: (0, o[i], 0, 0)),
        ),
        out_shape=jax.ShapeDtypeStruct((2, half, rows, n), x.dtype),
        cost_estimate=pl.CostEstimate(flops=0, bytes_accessed=8 * n * d, transcendentals=0),
        compiler_params=params(),
        name="ordered",
    )(jnp.append(order, core), x).reshape(d, n)


def embed_kernel(
    all_rows,
    flat_ref, h_ref, told_ref, w2_ref, q_ref, len_ref, sum_ref, weighted_ref, dz_ref, z_ref,
):
    i = pl.program_id(0)
    rows, emb = q_ref.shape
    mu = group_spread(told_ref[:, 0, :TILE], rows)
    inv = group_spread(told_ref[:, 0, TILE:], rows)
    active = jnp.maximum((h_ref[...] - mu) * inv, 0.0).astype(jnp.bfloat16)
    z = dot(active, w2_ref[...])

    @pl.when(i == 0)
    def _():
        z_ref[...] = z

    @pl.when(i > 0)
    def _():
        z_ref[...] += z

    @pl.when(i == pl.num_programs(0) - 1)
    def _():
        z = z_ref[...]
        z = z * lax.rsqrt(jnp.sum(z * z, axis=-1, keepdims=True) + norm_eps)
        back = jnp.where(
            flat_ref[...] == lax.broadcasted_iota(jnp.int32, (rows, rows), 0), 1.0, 0.0
        ).astype(jnp.bfloat16)
        high = z.astype(jnp.bfloat16)
        rest = z - high.astype(jnp.float32)
        mid = rest.astype(jnp.bfloat16)
        low = (rest - mid.astype(jnp.float32)).astype(jnp.bfloat16)
        positives = dot(back, high) + dot(back, mid) + dot(back, low)
        q = q_ref[...]
        scale_coef = loss_scale / all_rows
        pos = jnp.sum(q * positives, axis=-1, keepdims=True) / sharpness_divisor
        exp_pos = jnp.exp(pos) * QUARTER
        total = exp_pos + jnp.sum(sum_ref[...], axis=-1, keepdims=True)
        d_pos = scale_coef * (exp_pos / total - 1.0)
        d_q = (d_pos * positives + weighted_ref[...] * (scale_coef / total)) / sharpness_divisor
        d_z = (d_q - q * jnp.sum(d_q * q, axis=-1, keepdims=True)) * len_ref[...]
        dz_ref[...] = d_z.astype(jnp.bfloat16)


def embed(flat_row, h, told, w2, q, inv_len, neg_sum, weighted, all_rows):
    rows, hid = h.shape
    emb = w2.shape[1]
    groups = told.shape[0]
    return pl.pallas_call(
        lambda *refs: embed_kernel(all_rows, *refs),
        grid=(hid // TILE,),
        in_specs=[
            whole((1, rows)),
            pl.BlockSpec((rows, TILE), lambda i: (0, i)),
            pl.BlockSpec((groups, 1, 2 * TILE), lambda i: (0, 0, i)),
            pl.BlockSpec((TILE, emb), lambda i: (i, 0)),
            whole((rows, emb)),
            whole((rows, 1)),
            whole((rows, emb)),
            whole((rows, emb)),
        ],
        out_specs=whole((rows, emb)),
        out_shape=jax.ShapeDtypeStruct((rows, emb), jnp.bfloat16),
        scratch_shapes=[pltpu.VMEM((rows, emb), jnp.float32)],
        cost_estimate=pl.CostEstimate(
            flops=2 * rows * hid * emb, bytes_accessed=4 * rows * hid, transcendentals=0
        ),
        compiler_params=params(),
        name="embed",
    )(flat_row, h, told, w2, q, inv_len, neg_sum, weighted)


def store_rows(out_ref, at, value, crossed):
    size = value.shape[0] // 4
    for i, j in enumerate((0, 2, 1, 3)):
        j = j if crossed else i
        out_ref[i * size:(i + 1) * size, at] = value[j * size:(j + 1) * size].astype(out_ref.dtype)


def send_kernel(plain, dz_ref, w2_ref, n_ref, inv_ref, xt_ref, at_ref, dh_ref, g_ref):
    i = pl.program_id(0)
    rows = dz_ref.shape[0]
    dz = dz_ref[...]
    normed = n_ref[...]
    d_norm = jnp.where(normed > 0.0, dot_t(dz, w2_ref[...]), 0.0)
    mean = jnp.sum(d_norm, axis=0, keepdims=True) / rows
    slope = jnp.sum(d_norm * normed, axis=0, keepdims=True) / rows
    d_hidden = (inv_ref[...] * (d_norm - mean - normed * slope)).astype(jnp.bfloat16)
    dh_ref[...] = d_hidden
    g = dot(xt_ref[...], d_hidden)
    at = pl.ds(pl.multiple_of(i * TILE, TILE), TILE)

    @pl.when(i < plain)
    def _():
        store_rows(g_ref, at, g, False)

    @pl.when(i >= plain)
    def _():
        store_rows(g_ref, at, g, True)

    if at_ref is not None:
        @pl.when(i == pl.num_programs(0) - 1)
        def _():
            end = g_ref.shape[1]
            store_rows(g_ref, pl.ds(end - dz.shape[1], dz.shape[1]), dot(at_ref[...], dz), True)


def send_half(dz, w2, normed, inv, xt, at, first, tiles, plain):
    rows, emb = dz.shape
    half = xt.shape[0] // 2
    extra = 0 if at is None else emb
    operands = [dz, w2, normed, inv, xt]
    in_specs = [
        whole((rows, emb)),
        pl.BlockSpec((TILE, emb), lambda i: (first + i, 0)),
        pl.BlockSpec((rows, TILE), lambda i: (0, first + i)),
        pl.BlockSpec((1, TILE), lambda i: (0, first + i)),
        pl.BlockSpec((half, rows), lambda i: (1, 0)),
    ]
    if at is None:
        kernel = lambda a, b, c, d, e, f, g: send_kernel(plain, a, b, c, d, e, None, f, g)
    else:
        kernel = lambda *refs: send_kernel(plain, *refs)
        operands.append(at)
        in_specs.append(pl.BlockSpec((half, rows), lambda i: (1, 0)))
    return pl.pallas_call(
        kernel,
        grid=(tiles,),
        in_specs=in_specs,
        out_specs=[
            pl.BlockSpec((rows, TILE), lambda i: (0, i)),
            whole((half, tiles * TILE + extra)),
        ],
        out_shape=[
            jax.ShapeDtypeStruct((rows, tiles * TILE), jnp.bfloat16),
            jax.ShapeDtypeStruct((half, tiles * TILE + extra), jnp.bfloat16),
        ],
        cost_estimate=pl.CostEstimate(
            flops=2 * rows * half * tiles * TILE, bytes_accessed=8 * rows * half, transcendentals=0
        ),
        compiler_params=params(),
        name="send_half",
    )(*operands)


def keep_kernel(plain, dz_ref, dh_ref, xt_ref, at_ref, g_ref):
    i = pl.program_id(0)
    g = dot(xt_ref[...], dh_ref[...])
    at = pl.ds(pl.multiple_of(i * TILE, TILE), TILE)

    @pl.when(i < plain)
    def _():
        store_rows(g_ref, at, g, False)

    @pl.when(i >= plain)
    def _():
        store_rows(g_ref, at, g, True)

    if at_ref is not None:
        @pl.when(i == pl.num_programs(0) - 1)
        def _():
            dz = dz_ref[...]
            end = g_ref.shape[1]
            store_rows(g_ref, pl.ds(end - dz.shape[1], dz.shape[1]), dot(at_ref[...], dz), True)


def keep_half(dz, dh, xt, at, plain):
    rows, emb = dz.shape
    half = xt.shape[0] // 2
    tiles = dh.shape[1] // TILE
    extra = 0 if at is None else emb
    operands = [dz, dh, xt]
    in_specs = [
        whole((rows, emb)),
        pl.BlockSpec((rows, TILE), lambda i: (0, i)),
        whole((half, rows)),
    ]
    if at is None:
        kernel = lambda a, b, c, d: keep_kernel(plain, a, b, c, None, d)
    else:
        kernel = lambda *refs: keep_kernel(plain, *refs)
        operands.append(at)
        in_specs.append(whole((half, rows)))
    return pl.pallas_call(
        kernel,
        grid=(tiles,),
        in_specs=in_specs,
        out_specs=whole((half, tiles * TILE + extra)),
        out_shape=jax.ShapeDtypeStruct((half, tiles * TILE + extra), jnp.float32),
        cost_estimate=pl.CostEstimate(
            flops=2 * rows * half * tiles * TILE, bytes_accessed=8 * rows * half, transcendentals=0
        ),
        compiler_params=params(),
        name="keep_half",
    )(*operands)


def swap(x, axis, bit):
    size = lax.axis_size(axis)
    return lax.ppermute(x, axis, [(i, i ^ bit) for i in range(size)])


def total(parts, rows, cols):
    parts = [p[rows, cols].astype(jnp.float32) for p in parts]
    out = parts[0]
    for p in parts[1:]:
        out = out + p
    return out


def scatter_pair(keep, sent, split):
    n_dp = lax.axis_size("dp")
    length = n_dp // 2
    half = keep.shape[0]
    quarter, eighth = half // 2, half // 4
    rows = eighth // length
    every = slice(None)
    came = swap(sent, "crop", 1)
    sides = []
    for side, (first, second) in enumerate(
        ((("dp", 1), ("crop", 2)), (("crop", 2), ("dp", 1)))
    ):
        cols = slice(0, split) if side == 0 else slice(split, None)
        held = [keep[:, cols], came[:, cols]]
        out = total(held, slice(quarter, half), every).astype(jnp.bfloat16)
        held.append(swap(out, *first))
        out = total(held, slice(eighth, quarter), every).astype(jnp.bfloat16)
        held.append(swap(out, *second))
        sides.append(held)
    own = jnp.concatenate([total(held, slice(0, rows), every) for held in sides], axis=1)
    for k in range(1, length):
        out = jnp.concatenate(
            [
                total(held, slice(k * rows, (k + 1) * rows), every).astype(jnp.bfloat16)
                for held in sides
            ],
            axis=1,
        )
        perm = [
            (2 * p + b, 2 * ((p + k) % length) + b) for p in range(length) for b in range(2)
        ]
        own = own + lax.ppermute(out, "dp", perm).astype(jnp.float32)
    return own


def per_device(
    query_crops, key_crops, shuffle, distractor_bank, query_inner, query_outer, key_inner, key_outer
):
    n_dp, n_crop = lax.axis_size("dp"), lax.axis_size("crop")
    group_count = n_dp * n_crop
    row_count = query_crops.shape[0]
    hid = query_inner.shape[1]
    per_peer = row_count // group_count
    all_rows = float(row_count * group_count)

    wanted = (shuffle % row_count).reshape(group_count, per_peer)
    requested = lax.all_to_all(wanted, AXES, split_axis=0, concat_axis=0, tiled=True)
    flat_req = requested.reshape(-1)

    hidden_k, sums = key_hidden(flat_req[:, None], key_crops, key_inner, group_count)
    told = batch(lax.all_to_all(sums, AXES, split_axis=0, concat_axis=0, tiled=True), row_count)
    told = lax.all_to_all(told, AXES, split_axis=0, concat_axis=0, tiled=True)

    normed, inv_q, active, q, inv_len, q_low = query_forward(query_crops, query_inner, query_outer)
    neg_sum, weighted = negatives(q_low, distractor_bank)

    length = n_dp // 2
    dp, crop = lax.axis_index("dp"), lax.axis_index("crop")
    block = lax.iota(jnp.int32, group_count // 2)
    z, x, y = block // (n_crop), (block // (n_crop // 2)) % 2, block % (n_crop // 2)
    order = ((x ^ (dp % 2)) * (n_crop // 2) + (y ^ (crop // 2))) * length
    order = order + (z + length - dp // 2) % length
    core = crop % 2
    xt = ordered(query_crops, order, core, group_count)
    at = ordered(active, order, core, group_count)

    told, neg_sum, weighted, xt, at = lax.optimization_barrier((told, neg_sum, weighted, xt, at))
    d_z = embed(
        flat_req[None, :], hidden_k, told, key_outer, q, inv_len, neg_sum, weighted, all_rows
    )

    tiles = hid // TILE
    pairs = PAIRS
    scale = tiles // sum(pairs)
    made = []
    first = 0
    for i, count in enumerate(pairs):
        last = at if i == len(pairs) - 1 else None
        dh, sent = send_half(
            d_z, query_outer, normed, inv_q, xt, last, first, count * scale, count * scale // 2
        )
        made.append((dh, sent, last, count * scale // 2))
        first += count * scale
    outs = []
    for dh, sent, last, plain in made:
        keep = keep_half(d_z, dh, xt, last, plain)
        outs.append(scatter_pair(keep, sent, plain * TILE))
    grad = jnp.concatenate(outs, axis=1)
    return (grad[:, :hid], grad[:, hid:])


def solution(mesh):
    placed = (
        P(AXES, None),
        P(AXES, None),
        P(AXES),
        P(),
        P(),
        P(),
        P(),
        P(),
    )
    return jax.shard_map(
        per_device,
        mesh=mesh,
        in_specs=placed,
        out_specs=(P(AXES, None), P(AXES, None)),
        check_vma=False,
    )
```

time: 218 us -> 179 us (0.82)
  Pallas kernels: 11 us -> 71.8 us
  matrix products: 39.1 us -> 0 us
  local copies, waits for them, and re-layouts: 36 us -> 12 us
  other arithmetic: 28.6 us -> 7.09 us
  starting transfers between devices: 38.8 us -> 26.3 us
  waiting for transfers between devices: 47.6 us -> 45.1 us
    pallas_call x0 -> x10, Pallas kernels: none -> 60.8 us  [the longest x1 12.4 us: query_forward(): pl.pallas_call(query_kernel, grid=(hid // TILE,), in_specs=[whole((rows,...]
    dot_general x9 -> x0, matrix products: 39.1 us -> none  [the longest x1 12.4 us: per_device(): hidden_k = jnp.dot(by_group, key_inner, preferred_element_type=jnp.float32)]
    ppermute x12 -> x6, starting transfers between devices: 26.3 us -> 10.5 us  [scatter_pair(): own = own + lax.ppermute(out, 'dp', perm).astype(jnp.float32)]
    all_to_all x1, waiting for transfers between devices: 1.14 us -> 15.5 us  [per_device(): lax.all_to_all(sums, AXES, split_axis=0, concat_axis=0, tiled=True)]
    convert_element_type x14 -> x10, other arithmetic: 15.5 us -> 4.61 us  [the longest x3 3.56 us: scatter_pair(): out = total(held, slice(quarter, half), every).astype(jnp.bfloat16)]
    all_to_all x1, waiting for transfers between devices: 9.2 us -> 0.01 us  [per_device(): told = lax.all_to_all(told, AXES, split_axis=0, concat_axis=0, tiled=True)]
    ppermute x6 -> x10, waiting for transfers between devices: 31.2 us -> 22.9 us  [swap(): return lax.ppermute(x, axis, [(i, i ^ bit) for i in range(size)])]
    concatenate x1 -> x0, local copies, waits for them, and re-layouts: 6.73 us -> none  [per_device(): grads[1] = jnp.concatenate([grads[1], grad_out], axis=1)]
  transfers between devices with their start and end apart: 20 -> 18, of which waited for: 10 -> 9; matrix products, arithmetic and copies ran while one was open for 25% -> 3% of each run, Pallas kernels for 0% -> 26%
where the time goes in v2:
time: 179 us; the launch traced here: 177 us
  Pallas kernels  71.8 us (40%)
  waiting for transfers between devices  45.1 us (25%)
  starting transfers between devices  26.3 us (15%)
  blocking collectives  14.2 us (8%)
  local copies, waits for them, and re-layouts  12 us (7%)
  other arithmetic  7.09 us (4%)
    ppermute x10, waiting for transfers between devices, swap(): return lax.ppermute(x, axis, [(i, i ^ bit) for i in range(size)])  22.9 us
    all_to_all x1, waiting for transfers between devices, per_device(): lax.all_to_all(sums, AXES, split_axis=0, concat_axis=0, tiled=True)  15.5 us
    all_to_all x1, blocking collectives, per_device(): lax.all_to_all(wanted, AXES, split_axis=0, concat_axis=0, tiled=True)  14.2 us
    pallas_call x1, Pallas kernels, query_forward(): pl.pallas_call(query_kernel, grid=(hid // TILE,), in_specs=[whole((rows,...  12.4 us
    pallas_call x2, Pallas kernels, send_half(): pl.pallas_call(kernel, grid=(tiles,), in_specs=in_specs, out_specs=[pl.Bl...  12.2 us
    pallas_call x1, Pallas kernels, key_hidden(): pl.pallas_call(lambda *refs: key_hidden_kernel(groups, *refs), grid=(hid...  11.9 us
    pallas_call x1, Pallas kernels, negatives(): pl.pallas_call(neg_kernel, grid=(bank.shape[0] // tile,), in_specs=[pl.Bl...  11.1 us
    ppermute x6, starting transfers between devices, scatter_pair(): own = own + lax.ppermute(out, 'dp', perm).astype(jnp.float32)  10.5 us
  transfers between devices with their start and end apart: 18, of which 9 were waited for; matrix products, arithmetic and copies ran while one was open for 3% of the time, Pallas kernels for 26%

profile of v2, /device:TPU:0, one launch (start us, length us, event | category | flops | bytes accessed | tf_op | source)
XLA Modules:
  0.0 177.5 jit_solution(13906410073826210187)
XLA Ops:
  0.6 0.7 add_select_fusion
  1.4 14.2 %all_to_all.19 = s32[32,1,16]{2,1,0:T(1,128)S(1)} all-to-all(s32[32,1,16]{2,1,0:T(1,128)S(1)} %bitcast.12), channel_id=1, replica_groups=mesh['dp'=8,'crop'=4] {'dp','crop'}, dimensions={0} | all-to-all | bytes 4096 | tf_op jit(solution)/shard_map/all_to_all | solution.py:546
  15.8 1.6 copy-done.12
  17.4 11.9 %key_hidden.1 = (f32[512,2048]{1,0:T(8,128)}, f32[32,1,4096]{2,1,0:T(1,128)}) custom-call(s32[512,1]{1,0:T(8,128)S(1)} %broadcast_in_dim_reshape.8.refs_0_, bf16[512,2048]{1,0:T(8,128)(2,1)S(1)} %copy-done.12, bf16[2048,2048]{1,0:T(8,128)(2,1)} %refs_2_.1), custom_call_target="tpu_custom_call" | custom-call | flops 5368709120 | bytes 8388608 | tf_op jit(solution)/shard_map/key_hidden/pallas_call | solution.py:145
  29.3 2.6 %all-to-all-start.1 = ((f32[32,1,4096]{2,1,0:T(1,128)}), f32[32,1,4096]{2,1,0:T(1,128)S(1)}, u32[]{:S(2)}, u32[]{:S(2)}) async-start(f32[32,1,4096]{2,1,0:T(1,128)} %get-tuple-element.22), calls=%async_computation.1 | async-start | bytes 1048576 | tf_op jit(solution)/shard_map/all_to_all | solution.py:550
  31.9 15.5 %all-to-all-done.1.refs_0_ = f32[32,1,4096]{2,1,0:T(1,128)S(1)} async-done(((f32[32,1,4096]{2,1,0:T(1,128)}), f32[32,1,4096]{2,1,0:T(1,128)S(1)}, u32[]{:S(2)}, u32[]{:S(2)}) %all-to-all-start.1) | async-done | bytes 524320 | tf_op jit(solution)/shard_map/all_to_all | solution.py:550
  47.4 2.8 %batch.1 = f32[32,1,4096]{2,1,0:T(1,128)} custom-call(f32[32,1,4096]{2,1,0:T(1,128)S(1)} %all-to-all-done.1.refs_0_), custom_call_target="tpu_custom_call" | custom-call | tf_op jit(solution)/shard_map/batch/pallas_call | solution.py:182
  50.3 3.0 %all-to-all-start.2 = ((f32[32,1,4096]{2,1,0:T(1,128)}), f32[32,1,4096]{2,1,0:T(1,128)S(1)}, u32[]{:S(2)}, u32[]{:S(2)}) async-start(f32[32,1,4096]{2,1,0:T(1,128)} %batch.1), calls=%async_computation.2 | async-start | bytes 1048576 | tf_op jit(solution)/shard_map/all_to_all | solution.py:551
  53.4 1.6 copy-done.2
  54.9 2.9 %ordered.2 = bf16[2,16,64,512]{3,2,1,0:T(8,128)(2,1)S(1)} custom-call(s32[17]{0:T(128)S(1)} %pad_add_fusion.order_ref, bf16[512,2048]{1,0:T(8,128)(2,1)S(1)} %copy-done.2), custom_call_target="tpu_custom_call" | custom-call | bytes 8388608 | tf_op jit(solution)/shard_map/ordered/pallas_call | solution.py:277
  57.9 12.4 %query_forward.1 = (f32[512,2048]{1,0:T(8,128)}, f32[1,2048]{1,0:T(1,128)S(1)}, bf16[512,2048]{1,0:T(8,128)(2,1)S(1)}, f32[512,128]{1,0:T(8,128)S(1)}, f32[512,1...) custom-call(bf16[512,2048]{1,0:T(8,128)(2,1)S(1)} %copy-done.2, bf16[2048,2048]{1,0:T(8,128)(2,1)} %w_ref.1, ...), custom_call_target="tpu_custom_call" | custom-call | flops 4563402752 | bytes 8388608 | tf_op jit(solution)/shard_map/query_forward/pallas_call | solution.py:227
  70.3 0.7 copy-done.5
  71.0 2.9 %ordered.3 = bf16[2,16,64,512]{3,2,1,0:T(8,128)(2,1)S(1)} custom-call(s32[17]{0:T(128)S(1)} %pad_add_fusion.order_ref, bf16[512,2048]{1,0:T(8,128)(2,1)S(1)} %get-tuple-element.26.x_ref), custom_call_target="tpu_custom_call" | custom-call | bytes 8388608 | tf_op jit(solution)/shard_map/ordered/pallas_call | solution.py:277
  74.0 1.3 copy-done
  75.3 11.1 %negatives.1 = (f32[512,128]{1,0:T(8,128)S(1)}, f32[512,128]{1,0:T(8,128)S(1)}) custom-call(bf16[512,128]{1,0:T(8,128)(2,1)S(1)} %get-tuple-element.23.q_ref, bf16[16384,128]{1,0:T(8,128)(2,1)S(1)} %copy-done.11), custom_call_target="tpu_custom_call" | custom-call | flops 4294967296 | bytes 4194304 | tf_op jit(solution)/shard_map/negatives/pallas_call | solution.py:41
  86.4 0.7 copy-done.7
  87.1 0.7 copy-done.9
  88.3 0.7 reduce.5
  89.1 1.0 copy-done.4
  90.1 0.9 copy-done.6
  91.1 0.9 copy-done.8
  92.0 0.9 copy-done.10
  93.0 6.6 %embed.1.a.refs_0_ = bf16[512,128]{1,0:T(8,128)(2,1)S(1)} custom-call(s32[1,512]{1,0:T(1,128)S(1)} %broadcast_in_dim_reshape.6.refs_0_, f32[512,2048]{1,0:T(8,128)} %get-tuple-element.21.refs_1_, f32[32,1,4096]{2,1,0:T(1,128)S(1)} %all-to-all-done.2.refs_2_, bf16[2048,128]{1,0:T(8,128)(2,1)S(1)} %copy-done.4, f32[512,128]{1,0:T(8,128)S(1)} %get-tuple-element.28.refs_4_, ...), custom_call_target="tpu_custom_call" | custom-call | flops 268435456 | bytes 4194304 | tf_op jit(solution)/shard_map/embed/pallas_call | solution.py:338
  99.6 5.3 %send_half.2 = (bf16[512,1024]{1,0:T(8,128)(2,1)S(1)}, bf16[1024,1024]{1,0:T(8,128)(2,1)S(1)}) custom-call(bf16[512,128]{1,0:T(8,128)(2,1)S(1)} %embed.1.a.refs_0_, bf16[2048,128]{1,0:T(8,128)(2,1)S(1)} %copy-done.3, f32[512,2048]{1,0:T(8,128)} %get-tuple-element.32.c.refs_2_, f32[1,2048]{1,0:T(1,128)S(1)} %get-tuple-element.33.d.refs_3_, ...), custom_call_target="tpu_custom_call" | custom-call | flops 1073741824 | bytes 4194304 | tf_op jit(solution)/shard_map/send_half/pallas_call | solution.py:415
  105.3 6.9 %send_half.3 = (bf16[512,1024]{1,0:T(8,128)(2,1)S(1)}, bf16[1024,1152]{1,0:T(8,128)(2,1)}) custom-call(bf16[512,128]{1,0:T(8,128)(2,1)S(1)} %embed.1.a.refs_0_, bf16[2048,128]{1,0:T(8,128)(2,1)S(1)} %copy-done.3, f32[512,2048]{1,0:T(8,128)} %get-tuple-element.32.c.refs_2_, f32[1,2048]{1,0:T(1,128)S(1)} %get-tuple-element.33.d.refs_3_, ...), custom_call_target="tpu_custom_call" | custom-call | flops 1073741824 | bytes 4194304 | tf_op jit(solution)/shard_map/send_half/pallas_call | solution.py:415
  112.4 4.2 %keep_half.2 = f32[1024,1024]{1,0:T(8,128)} custom-call(bf16[512,128]{1,0:T(8,128)(2,1)S(1)} %embed.1.a.refs_0_, bf16[512,1024]{1,0:T(8,128)(2,1)S(1)} %get-tuple-element.35.b, bf16[2048,512]{1,0:T(8,128)(2,1)S(1)} %bitcast.7), custom_call_target="tpu_custom_call" | custom-call | flops 1073741824 | bytes 4194304 | tf_op jit(solution)/shard_map/keep_half/pallas_call | solution.py:473
  116.6 1.9 %fusion.3 = (bf16[512,512]{1,0:T(8,128)(2,1)S(1)}, bf16[512,512]{1,0:T(8,128)(2,1)S(1)}) fusion(f32[1024,1024]{1,0:T(8,128)} %keep_half.2, bf16[1024,1024]{1,0:T(8,128)(2,1)S(1)} %collective-permute-done), kind=kLoop, calls=%fused_computation.7 | loop fusion | flops 1572864 | bytes 4194304 | tf_op jit(solution)/shard_map/convert_element_type | solution.py:514
  118.5 1.8 %collective-permute-start.1 = (bf16[512,512]{1,0:T(8,128)(2,1)S(1)}, bf16[512,512]{1,0:T(8,128)(2,1)S(1)}, u32[]{:S(2)}, u32[]{:S(2)}) collective-permute-start(bf16[512,512]{1,0:T(8,128)(2,1)S(1)} %get-tuple-element.58), channel_id=1, source_target_pairs={{0,4},{4,0},{8,12},{12,8},{16,20},{20,16},{24,28},{28,24},{1,5},{5... | collective-permute-start | bytes 1572872 | tf_op jit(solution)/shard_map/ppermute | solution.py:489
  120.3 1.5 collective-permute-start.3
  121.8 4.8 %keep_half.3 = f32[1024,1152]{1,0:T(8,128)} custom-call(bf16[512,128]{1,0:T(8,128)(2,1)S(1)} %embed.1.a.refs_0_, bf16[512,1024]{1,0:T(8,128)(2,1)S(1)} %get-tuple-element.38.refs_1_, bf16[2048,512]{1,0:T(8,128)(2,1)S(1)} %bitcast.8, bf16[2048,512]{1,0:T(8,128)(2,1)S(1)} %bitcast.10), custom_call_target="tpu_custom_call" | custom-call | flops 1073741824 | bytes 4194304 | tf_op jit(solution)/shard_map/keep_half/pallas_call | solution.py:473
  126.5 1.5 fusion.1
  128.7 4.6 %collective-permute-done.1 = bf16[512,512]{1,0:T(8,128)(2,1)S(1)} collective-permute-done((bf16[512,512]{1,0:T(8,128)(2,1)S(1)}, bf16[512,512]{1,0:T(8,128)(2,1)S(1)}, u32[]{:S(2)}, u32[]{:S(2)}) %collective-permute-start.1) | collective-permute-done | bytes 524320 | tf_op jit(solution)/shard_map/ppermute | solution.py:489
  133.3 0.8 collective-permute-done.3
  134.3 1.5 collective-permute-start.2
  135.8 1.0 collective-permute-start.4
  137.6 6.0 %collective-permute-done.2 = bf16[256,512]{1,0:T(8,128)(2,1)S(1)} collective-permute-done((bf16[256,512]{1,0:T(8,128)(2,1)S(1)}, bf16[256,512]{1,0:T(8,128)(2,1)S(1)}, u32[]{:S(2)}, u32[]{:S(2)}) %collective-permute-start.2) | collective-permute-done | bytes 262176 | tf_op jit(solution)/shard_map/ppermute | solution.py:489
  143.8 5.8 %collective-permute-done.4 = bf16[256,512]{1,0:T(8,128)(2,1)S(1)} collective-permute-done((bf16[256,512]{1,0:T(8,128)(2,1)S(1)}, bf16[256,512]{1,0:T(8,128)(2,1)S(1)}, u32[]{:S(2)}, u32[]{:S(2)}) %collective-permute-start.4) | collective-permute-done | bytes 262176 | tf_op jit(solution)/shard_map/ppermute | solution.py:489
  149.7 2.6 %collective-permute-start.6 = (bf16[64,1024]{1,0:T(8,128)(2,1)S(1)}, bf16[64,1024]{1,0:T(8,128)(2,1)S(1)}, u32[]{:S(2)}, u32[]{:S(2)}) collective-permute-start(bf16[64,1024]{1,0:T(8,128)(2,1)S(1)} %pad_maximum_fusion.5), channel_id=1, source_target_pairs={{0,16},{4,20},{8,24},{12,28},{16,0},{20,4},{24,8},{28,12},{1,17},{... | collective-permute-start | bytes 393224 | tf_op jit(solution)/shard_map/ppermute | solution.py:531
  152.4 1.5 collective-permute-start.7
  154.0 1.5 collective-permute-start.10
  156.1 1.1 collective-permute-start.12
  157.2 1.2 collective-permute-start.5
  158.4 2.9 %collective-permute-done.10 = bf16[256,512]{1,0:T(8,128)(2,1)S(1)} collective-permute-done((bf16[256,512]{1,0:T(8,128)(2,1)S(1)}, bf16[256,512]{1,0:T(8,128)(2,1)S(1)}, u32[]{:S(2)}, u32[]{:S(2)}) %collective-permute-start.10) | collective-permute-done | bytes 262176 | tf_op jit(solution)/shard_map/ppermute | solution.py:489
  161.5 2.4 %collective-permute-done.12 = bf16[256,640]{1,0:T(8,128)(2,1)S(1)} collective-permute-done((bf16[256,640]{1,0:T(8,128)(2,1)S(1)}, bf16[256,640]{1,0:T(8,128)(2,1)S(1)}, u32[]{:S(2)}, u32[]{:S(2)}) %collective-permute-start.12) | collective-permute-done | bytes 327712 | tf_op jit(solution)/shard_map/ppermute | solution.py:489
  164.0 2.6 %collective-permute-start.14 = (bf16[64,1152]{1,0:T(8,128)(2,1)S(1)}, bf16[64,1152]{1,0:T(8,128)(2,1)S(1)}, u32[]{:S(2)}, u32[]{:S(2)}) collective-permute-start(bf16[64,1152]{1,0:T(8,128)(2,1)S(1)} %pad_maximum_fusion.2), channel_id=1, source_target_pairs={{0,16},{4,20},{8,24},{12,28},{16,0},{20,4},{24,8},{28,12},{1,17},{... | collective-permute-start | bytes 442376 | tf_op jit(solution)/shard_map/ppermute | solution.py:531
  166.6 2.0 %collective-permute-start.15 = (bf16[64,1152]{1,0:T(8,128)(2,1)S(1)}, bf16[64,1152]{1,0:T(8,128)(2,1)S(1)}, u32[]{:S(2)}, u32[]{:S(2)}) collective-permute-start(bf16[64,1152]{1,0:T(8,128)(2,1)S(1)} %pad_maximum_fusion.3), channel_id=1, source_target_pairs={{0,24},{4,28},{8,0},{12,4},{16,8},{20,12},{24,16},{28,20},{1,25},{... | collective-permute-start | bytes 442376 | tf_op jit(solution)/shard_map/ppermute | solution.py:531
  169.3 6.6 %collective-permute-done.14 = bf16[64,1152]{1,0:T(8,128)(2,1)S(1)} collective-permute-done((bf16[64,1152]{1,0:T(8,128)(2,1)S(1)}, bf16[64,1152]{1,0:T(8,128)(2,1)S(1)}, u32[]{:S(2)}, u32[]{:S(2)}) %collective-permute-start.14) | collective-permute-done | bytes 147488 | tf_op jit(solution)/shard_map/ppermute | solution.py:531
  176.6 0.8 pad_maximum_fusion
  (58 shorter events, 5.9 us)
Async XLA Ops:
  15.8 1.6 copy-start.12
  29.3 18.2 %all-to-all-start.1 = ((f32[32,1,4096]{2,1,0:T(1,128)}), f32[32,1,4096]{2,1,0:T(1,128)S(1)}, u32[]{:S(2)}, u32[]{:S(2)}) async-start(f32[32,1,4096]{2,1,0:T(1,128)} %get-tuple-element.22), calls=%async_computation.1 | async-start | bytes 1048576 | tf_op jit(solution)/shard_map/all_to_all | solution.py:550
  50.3 7.6 %copy-start.3 = (bf16[2048,128]{1,0:T(8,128)(2,1)S(1)}, bf16[2048,128]{1,0:T(8,128)(2,1)}, u32[]{:S(2)}) copy-start(bf16[2048,128]{1,0:T(8,128)(2,1)} %refs_1_.3) | copy-start | bytes 1572868
  50.3 38.8 %all-to-all-start.2 = ((f32[32,1,4096]{2,1,0:T(1,128)}), f32[32,1,4096]{2,1,0:T(1,128)S(1)}, u32[]{:S(2)}, u32[]{:S(2)}) async-start(f32[32,1,4096]{2,1,0:T(1,128)} %batch.1), calls=%async_computation.2 | async-start | bytes 1048576 | tf_op jit(solution)/shard_map/all_to_all | solution.py:551
  53.4 1.6 copy-start.2
  70.3 0.7 copy-start.5
  71.0 4.3 %copy-start.11 = (bf16[16384,128]{1,0:T(8,128)(2,1)S(1)}, bf16[16384,128]{1,0:T(8,128)(2,1)}, u32[]{:S(2)}) copy-start(bf16[16384,128]{1,0:T(8,128)(2,1)} %bank_ref.1) | copy-start | bytes 12582916
  74.0 1.4 copy-start
  86.4 0.7 copy-start.7
  87.1 0.7 copy-start.9
  89.1 1.0 copy-start.4
  90.1 0.9 copy-start.6
  91.1 0.9 copy-start.8
  92.0 0.9 copy-start.10
  99.6 5.7 %copy-start.1 = (bf16[2,16,64,512]{3,2,1,0:T(8,128)(2,1)S(1)}, bf16[2,16,64,512]{3,2,1,0:T(8,128)(2,1)}, u32[]{:S(2)}) copy-start(bf16[2,16,64,512]{3,2,1,0:T(8,128)(2,1)} %copy-done) | copy-start | bytes 6291460
  104.9 11.7 %collective-permute-start = (bf16[1024,1024]{1,0:T(8,128)(2,1)S(1)}, bf16[1024,1024]{1,0:T(8,128)(2,1)S(1)}, u32[]{:S(2)}, u32[]{:S(2)}) collective-permute-start(bf16[1024,1024]{1,0:T(8,128)(2,1)S(1)} %get-tuple-element.36), channel_id=1, source_target_pairs={{0,1},{1,0},{2,3},{3,2},{4,5},{5,4},{6,7},{7,6},{8,9},{9,8},{10,11... | collective-permute-start | bytes 6291464 | tf_op jit(solution)/shard_map/ppermute | solution.py:489
  112.1 14.4 %collective-permute-start.8 = (bf16[1024,1152]{1,0:T(8,128)(2,1)}, bf16[1024,1152]{1,0:T(8,128)(2,1)S(1)}, u32[]{:S(2)}, u32[]{:S(2)}) collective-permute-start(bf16[1024,1152]{1,0:T(8,128)(2,1)} %get-tuple-element.39), channel_id=1, source_target_pairs={{0,1},{1,0},{2,3},{3,2},{4,5},{5,4},{6,7},{7,6},{8,9},{9,8},{10,11... | collective-permute-start | bytes 7077896 | tf_op jit(solution)/shard_map/ppermute | solution.py:489
  118.5 14.8 %collective-permute-start.1 = (bf16[512,512]{1,0:T(8,128)(2,1)S(1)}, bf16[512,512]{1,0:T(8,128)(2,1)S(1)}, u32[]{:S(2)}, u32[]{:S(2)}) collective-permute-start(bf16[512,512]{1,0:T(8,128)(2,1)S(1)} %get-tuple-element.58), channel_id=1, source_target_pairs={{0,4},{4,0},{8,12},{12,8},{16,20},{20,16},{24,28},{28,24},{1,5},{5... | collective-permute-start | bytes 1572872 | tf_op jit(solution)/shard_map/ppermute | solution.py:489
  120.3 13.8 %collective-permute-start.3 = (bf16[512,512]{1,0:T(8,128)(2,1)S(1)}, bf16[512,512]{1,0:T(8,128)(2,1)S(1)}, u32[]{:S(2)}, u32[]{:S(2)}) collective-permute-start(bf16[512,512]{1,0:T(8,128)(2,1)S(1)} %get-tuple-element.59), channel_id=1, source_target_pairs={{0,2},{1,3},{2,0},{3,1},{4,6},{5,7},{6,4},{7,5},{8,10},{9,11},{10,... | collective-permute-start | bytes 1572872 | tf_op jit(solution)/shard_map/ppermute | solution.py:489
  121.8 12.3 %copy-start.14 = (f32[1024,1024]{1,0:T(8,128)S(1)}, f32[1024,1024]{1,0:T(8,128)}, u32[]{:S(2)}) copy-start(f32[1024,1024]{1,0:T(8,128)} %keep_half.2) | copy-start | bytes 12582916
  126.5 10.3 %copy-start.13 = (f32[1024,1152]{1,0:T(8,128)S(1)}, f32[1024,1152]{1,0:T(8,128)}, u32[]{:S(2)}) copy-start(f32[1024,1152]{1,0:T(8,128)} %keep_half.3) | copy-start | bytes 14155780
  128.1 25.8 %collective-permute-start.9 = (bf16[512,512]{1,0:T(8,128)(2,1)S(1)}, bf16[512,512]{1,0:T(8,128)(2,1)S(1)}, u32[]{:S(2)}, u32[]{:S(2)}) collective-permute-start(bf16[512,512]{1,0:T(8,128)(2,1)S(1)} %fusion.1), channel_id=1, source_target_pairs={{0,4},{4,0},{8,12},{12,8},{16,20},{20,16},{24,28},{28,24},{1,5},{5... | collective-permute-start | bytes 1572872 | tf_op jit(solution)/shard_map/ppermute | solution.py:489
  134.3 9.3 %collective-permute-start.2 = (bf16[256,512]{1,0:T(8,128)(2,1)S(1)}, bf16[256,512]{1,0:T(8,128)(2,1)S(1)}, u32[]{:S(2)}, u32[]{:S(2)}) collective-permute-start(bf16[256,512]{1,0:T(8,128)(2,1)S(1)} %get-tuple-element.56), channel_id=1, source_target_pairs={{0,2},{1,3},{2,0},{3,1},{4,6},{5,7},{6,4},{7,5},{8,10},{9,11},{10,... | collective-permute-start | bytes 786440 | tf_op jit(solution)/shard_map/ppermute | solution.py:489
  135.8 13.7 %collective-permute-start.4 = (bf16[256,512]{1,0:T(8,128)(2,1)S(1)}, bf16[256,512]{1,0:T(8,128)(2,1)S(1)}, u32[]{:S(2)}, u32[]{:S(2)}) collective-permute-start(bf16[256,512]{1,0:T(8,128)(2,1)S(1)} %get-tuple-element.57), channel_id=1, source_target_pairs={{0,4},{4,0},{8,12},{12,8},{16,20},{20,16},{24,28},{28,24},{1,5},{5... | collective-permute-start | bytes 786440 | tf_op jit(solution)/shard_map/ppermute | solution.py:489
  137.0 19.0 %collective-permute-start.11 = (bf16[512,640]{1,0:T(8,128)(2,1)S(1)}, bf16[512,640]{1,0:T(8,128)(2,1)S(1)}, u32[]{:S(2)}, u32[]{:S(2)}) collective-permute-start(bf16[512,640]{1,0:T(8,128)(2,1)S(1)} %fusion), channel_id=1, source_target_pairs={{0,2},{1,3},{2,0},{3,1},{4,6},{5,7},{6,4},{7,5},{8,10},{9,11},{10,... | collective-permute-start | bytes 1966088 | tf_op jit(solution)/shard_map/ppermute | solution.py:489
  149.7 18.9 %collective-permute-start.6 = (bf16[64,1024]{1,0:T(8,128)(2,1)S(1)}, bf16[64,1024]{1,0:T(8,128)(2,1)S(1)}, u32[]{:S(2)}, u32[]{:S(2)}) collective-permute-start(bf16[64,1024]{1,0:T(8,128)(2,1)S(1)} %pad_maximum_fusion.5), channel_id=1, source_target_pairs={{0,16},{4,20},{8,24},{12,28},{16,0},{20,4},{24,8},{28,12},{1,17},{... | collective-permute-start | bytes 393224 | tf_op jit(solution)/shard_map/ppermute | solution.py:531
  152.4 16.9 %collective-permute-start.7 = (bf16[64,1024]{1,0:T(8,128)(2,1)S(1)}, bf16[64,1024]{1,0:T(8,128)(2,1)S(1)}, u32[]{:S(2)}, u32[]{:S(2)}) collective-permute-start(bf16[64,1024]{1,0:T(8,128)(2,1)S(1)} %pad_maximum_fusion.6), channel_id=1, source_target_pairs={{0,24},{4,28},{8,0},{12,4},{16,8},{20,12},{24,16},{28,20},{1,25},{... | collective-permute-start | bytes 393224 | tf_op jit(solution)/shard_map/ppermute | solution.py:531
  154.0 7.4 %collective-permute-start.10 = (bf16[256,512]{1,0:T(8,128)(2,1)S(1)}, bf16[256,512]{1,0:T(8,128)(2,1)S(1)}, u32[]{:S(2)}, u32[]{:S(2)}) collective-permute-start(bf16[256,512]{1,0:T(8,128)(2,1)S(1)} %fusion.7), channel_id=1, source_target_pairs={{0,2},{1,3},{2,0},{3,1},{4,6},{5,7},{6,4},{7,5},{8,10},{9,11},{10,... | collective-permute-start | bytes 786440 | tf_op jit(solution)/shard_map/ppermute | solution.py:489
  156.1 7.8 %collective-permute-start.12 = (bf16[256,640]{1,0:T(8,128)(2,1)S(1)}, bf16[256,640]{1,0:T(8,128)(2,1)S(1)}, u32[]{:S(2)}, u32[]{:S(2)}) collective-permute-start(bf16[256,640]{1,0:T(8,128)(2,1)S(1)} %fusion.5), channel_id=1, source_target_pairs={{0,4},{4,0},{8,12},{12,8},{16,20},{20,16},{24,28},{28,24},{1,5},{5... | collective-permute-start | bytes 983048 | tf_op jit(solution)/shard_map/ppermute | solution.py:489
  157.2 12.1 %collective-permute-start.5 = (bf16[64,1024]{1,0:T(8,128)(2,1)S(1)}, bf16[64,1024]{1,0:T(8,128)(2,1)S(1)}, u32[]{:S(2)}, u32[]{:S(2)}) collective-permute-start(bf16[64,1024]{1,0:T(8,128)(2,1)S(1)} %pad_maximum_fusion.4), channel_id=1, source_target_pairs={{0,8},{4,12},{8,16},{12,20},{16,24},{20,28},{24,0},{28,4},{1,9},{5... | collective-permute-start | bytes 393224 | tf_op jit(solution)/shard_map/ppermute | solution.py:531
  164.0 11.9 %collective-permute-start.14 = (bf16[64,1152]{1,0:T(8,128)(2,1)S(1)}, bf16[64,1152]{1,0:T(8,128)(2,1)S(1)}, u32[]{:S(2)}, u32[]{:S(2)}) collective-permute-start(bf16[64,1152]{1,0:T(8,128)(2,1)S(1)} %pad_maximum_fusion.2), channel_id=1, source_target_pairs={{0,16},{4,20},{8,24},{12,28},{16,0},{20,4},{24,8},{28,12},{1,17},{... | collective-permute-start | bytes 442376 | tf_op jit(solution)/shard_map/ppermute | solution.py:531
  166.6 9.3 %collective-permute-start.15 = (bf16[64,1152]{1,0:T(8,128)(2,1)S(1)}, bf16[64,1152]{1,0:T(8,128)(2,1)S(1)}, u32[]{:S(2)}, u32[]{:S(2)}) collective-permute-start(bf16[64,1152]{1,0:T(8,128)(2,1)S(1)} %pad_maximum_fusion.3), channel_id=1, source_target_pairs={{0,24},{4,28},{8,0},{12,4},{16,8},{20,12},{24,16},{28,20},{1,25},{... | collective-permute-start | bytes 442376 | tf_op jit(solution)/shard_map/ppermute | solution.py:531
  168.6 7.3 %collective-permute-start.13 = (bf16[64,1152]{1,0:T(8,128)(2,1)S(1)}, bf16[64,1152]{1,0:T(8,128)(2,1)S(1)}, u32[]{:S(2)}, u32[]{:S(2)}) collective-permute-start(bf16[64,1152]{1,0:T(8,128)(2,1)S(1)} %pad_maximum_fusion.1), channel_id=1, source_target_pairs={{0,8},{4,12},{8,16},{12,20},{16,24},{20,28},{24,0},{28,4},{1,9},{5... | collective-permute-start | bytes 442376 | tf_op jit(solution)/shard_map/ppermute | solution.py:531

commit v3 on v2

v3 whole, which is shorter than its diff:
```python
import math
import jax
import jax.numpy as jnp
from jax import lax
from jax.experimental import pallas as pl
from jax.experimental.pallas import tpu as pltpu
from jax.sharding import PartitionSpec as P

sharpness_divisor = 0.2
loss_scale = 4096.0
bn_eps = 1e-05
norm_eps = 1e-06
AXES = ("dp", "crop")
QUARTER = 0.25


def neg_kernel(q_ref, bank_ref, out_ref):
    rows, emb = q_ref.shape

    @pl.when(pl.program_id(0) == 0)
    def _():
        out_ref[...] = jnp.zeros_like(out_ref)

    q = q_ref[...]
    step = 512
    for j in range(bank_ref.shape[0] // step):
        bank = bank_ref[j * step:(j + 1) * step, :]
        s = lax.dot_general(q, bank, (((1,), (1,)), ((), ())), preferred_element_type=jnp.float32)
        e = jnp.exp2(s * (1.0 / (sharpness_divisor * math.log(2.0))) - 2.0)
        total = e[:, :128]
        for i in range(1, step // 128):
            total = total + e[:, i * 128:(i + 1) * 128]
        out_ref[:, emb:] += total
        out_ref[:, :emb] += jnp.dot(
            e.astype(jnp.bfloat16), bank, preferred_element_type=jnp.float32
        )


def negatives(q, bank):
    rows, emb = q.shape
    tile = 2048
    return pl.pallas_call(
        neg_kernel,
        grid=(bank.shape[0] // tile,),
        in_specs=[
            pl.BlockSpec((rows, emb), lambda i: (0, 0)),
            pl.BlockSpec((tile, emb), lambda i: (i, 0)),
        ],
        out_specs=pl.BlockSpec((rows, emb + 128), lambda i: (0, 0)),
        out_shape=jax.ShapeDtypeStruct((rows, emb + 128), jnp.float32),
        cost_estimate=pl.CostEstimate(
            flops=4 * rows * bank.shape[0] * emb,
            bytes_accessed=bank.shape[0] * emb * 2,
            transcendentals=rows * bank.shape[0],
        ),
        compiler_params=pltpu.CompilerParams(vmem_limit_bytes=32 * 1024 * 1024),
        name="negatives",
    )(q, bank)


TILE = 256
STEP = 512
VMEM_LIMIT = 48 * 1024 * 1024


def params():
    return pltpu.CompilerParams(
        dimension_semantics=("arbitrary",), vmem_limit_bytes=VMEM_LIMIT
    )


def dot(a, b):
    return jnp.dot(a, b, preferred_element_type=jnp.float32)


def dot_t(a, b):
    return lax.dot_general(a, b, (((1,), (1,)), ((), ())), preferred_element_type=jnp.float32)


def whole(shape):
    return pl.BlockSpec(shape, lambda *_: (0,) * len(shape))


def group_rows(groups, per_peer):
    rows = groups * per_peer
    row = lax.broadcasted_iota(jnp.int32, (groups, rows), 1)
    group = lax.broadcasted_iota(jnp.int32, (groups, rows), 0)
    inside = (row >= group * per_peer) & (row < (group + 1) * per_peer)
    return jnp.where(inside, 1.0, 0.0).astype(jnp.float32)


def group_sum(h, groups):
    rows, cols = h.shape
    per_peer = rows // groups
    if per_peer % 8 == 0:
        return jnp.sum(h.reshape(groups, per_peer, cols), axis=1)
    return jnp.dot(
        group_rows(groups, per_peer),
        h,
        precision=lax.Precision.HIGHEST,
        preferred_element_type=jnp.float32,
    )


def group_spread(v, rows):
    groups, cols = v.shape
    per_peer = rows // groups
    if per_peer % 8 == 0:
        return jnp.broadcast_to(v[:, None, :], (groups, per_peer, cols)).reshape(rows, cols)
    return lax.dot_general(
        group_rows(groups, per_peer),
        v,
        (((0,), (0,)), ((), ())),
        precision=lax.Precision.HIGHEST,
        preferred_element_type=jnp.float32,
    )


def key_hidden_kernel(groups, flat_ref, k_ref, w_ref, h_ref, sums_ref, sorted_ref):
    rows = k_ref.shape[0]

    @pl.when(pl.program_id(0) == 0)
    def _():
        cols = lax.broadcasted_iota(jnp.int32, (rows, rows), 1)
        pick = jnp.where(flat_ref[...] == cols, 1.0, 0.0).astype(jnp.bfloat16)
        for i in range(0, k_ref.shape[1], 512):
            sorted_ref[:, i:i + 512] = dot(pick, k_ref[:, i:i + 512]).astype(jnp.bfloat16)

    x = sorted_ref[...]
    for t in range(0, STEP, TILE):
        h = dot(x, w_ref[:, t:t + TILE])
        h_ref[:, t:t + TILE] = h
        sums_ref[:, 0, 2 * t:2 * t + TILE] = group_sum(h, groups)
        sums_ref[:, 0, 2 * t + TILE:2 * t + 2 * TILE] = group_sum(h * h, groups)


def key_hidden(flat_col, k, w, groups):
    rows, d = k.shape
    hid = w.shape[1]
    return pl.pallas_call(
        lambda *refs: key_hidden_kernel(groups, *refs),
        grid=(hid // STEP,),
        in_specs=[
            whole((rows, 1)),
            whole((rows, d)),
            pl.BlockSpec((d, STEP), lambda i: (0, i)),
        ],
        out_specs=[
            pl.BlockSpec((rows, STEP), lambda i: (0, i)),
            pl.BlockSpec((groups, 1, 2 * STEP), lambda i: (0, 0, i)),
        ],
        out_shape=[
            jax.ShapeDtypeStruct((rows, hid), jnp.float32),
            jax.ShapeDtypeStruct((groups, 1, 2 * hid), jnp.float32),
        ],
        scratch_shapes=[pltpu.VMEM((rows, d), jnp.bfloat16)],
        cost_estimate=pl.CostEstimate(
            flops=2 * rows * d * (hid + rows), bytes_accessed=2 * d * hid, transcendentals=0
        ),
        compiler_params=params(),
        name="key_hidden",
    )(flat_col, k, w)


def batch_kernel(rows, part_ref, told_ref):
    groups, _, size = part_ref.shape
    for t in range(0, size, 2 * TILE):
        total = jnp.sum(part_ref[:, 0, t:t + 2 * TILE], axis=0, keepdims=True) / rows
        mu = total[:, :TILE]
        inv = lax.rsqrt(total[:, TILE:] - mu * mu + bn_eps)
        told = jnp.concatenate([mu, inv], axis=1)
        told_ref[:, 0, t:t + 2 * TILE] = jnp.broadcast_to(told, (groups, 2 * TILE))


def batch(part, rows):
    return pl.pallas_call(
        lambda *refs: batch_kernel(rows, *refs),
        grid=(1,),
        in_specs=[whole(part.shape)],
        out_specs=whole(part.shape),
        out_shape=jax.ShapeDtypeStruct(part.shape, jnp.float32),
        compiler_params=params(),
        name="batch",
    )(part)


def query_kernel(x_ref, w_ref, w2_ref, n_ref, inv_ref, z_ref, q_ref, sum_ref):
    i = pl.program_id(0)
    rows = x_ref.shape[0]

    @pl.when(i == 0)
    def _():
        sum_ref[...] = jnp.zeros_like(sum_ref)

    x = x_ref[...]
    z = None
    for t in range(0, STEP, TILE):
        h = dot(x, w_ref[:, t:t + TILE])
        mu = jnp.sum(h, axis=0, keepdims=True) / rows
        inv = lax.rsqrt(jnp.sum(h * h, axis=0, keepdims=True) / rows - mu * mu + bn_eps)
        normed = ((h - mu) * inv).astype(jnp.bfloat16)
        n_ref[:, t:t + TILE] = normed
        inv_ref[:, t:t + TILE] = inv
        term = dot(jnp.maximum(normed, 0), w2_ref[t:t + TILE, :])
        z = term if z is None else z + term
    sum_ref[...] += z

    @pl.when(i == pl.num_programs(0) - 1)
    def _():
        z = sum_ref[...]
        z_ref[...] = z
        q = z * lax.rsqrt(jnp.sum(z * z, axis=-1, keepdims=True) + norm_eps)
        q_ref[...] = q.astype(jnp.bfloat16)


def query_forward(x, w, w2):
    rows, d = x.shape
    hid, emb = w2.shape
    return pl.pallas_call(
        query_kernel,
        grid=(hid // STEP,),
        in_specs=[
            whole((rows, d)),
            pl.BlockSpec((d, STEP), lambda i: (0, i)),
            pl.BlockSpec((STEP, emb), lambda i: (i, 0)),
        ],
        out_specs=[
            pl.BlockSpec((rows, STEP), lambda i: (0, i)),
            pl.BlockSpec((1, STEP), lambda i: (0, i)),
            whole((rows, emb)),
            whole((rows, emb)),
        ],
        out_shape=[
            jax.ShapeDtypeStruct((rows, hid), jnp.bfloat16),
            jax.ShapeDtypeStruct((1, hid), jnp.float32),
            jax.ShapeDtypeStruct((rows, emb), jnp.float32),
            jax.ShapeDtypeStruct((rows, emb), jnp.bfloat16),
        ],
        scratch_shapes=[pltpu.VMEM((rows, emb), jnp.float32)],
        cost_estimate=pl.CostEstimate(
            flops=2 * rows * hid * (d + emb), bytes_accessed=2 * d * hid, transcendentals=0
        ),
        compiler_params=params(),
        name="query_forward",
    )(x, w, w2)


def order_kernel(positive, order_ref, x_ref, y_ref):
    rows = y_ref.shape[2]
    core = order_ref[pl.num_programs(0)]
    t = x_ref[...]
    if positive:
        t = jnp.maximum(t, 0)
    t = t.T
    y_ref[core, 0] = t[:rows]
    y_ref[1 - core, 0] = t[rows:]


def ordered(x, order, core, blocks, positive):
    n, d = x.shape
    half = blocks // 2
    rows = d // blocks
    width = 2 * rows
    if width % 128:
        y = (jnp.maximum(x, 0) if positive else x).T.reshape(half, 2, rows, n)
        y = jnp.zeros_like(y).at[order].set(y)
        return jnp.moveaxis(jnp.where(core == 0, y, y[:, ::-1]), 1, 0).reshape(d, n)
    return pl.pallas_call(
        lambda *refs: order_kernel(positive, *refs),
        grid_spec=pltpu.PrefetchScalarGridSpec(
            num_scalar_prefetch=1,
            grid=(half,),
            in_specs=[pl.BlockSpec((n, width), lambda i, o: (0, i))],
            out_specs=pl.BlockSpec((2, 1, rows, n), lambda i, o: (0, o[i], 0, 0)),
        ),
        out_shape=jax.ShapeDtypeStruct((2, half, rows, n), x.dtype),
        cost_estimate=pl.CostEstimate(flops=0, bytes_accessed=8 * n * d, transcendentals=0),
        compiler_params=params(),
        name="ordered",
    )(jnp.append(order, core), x).reshape(d, n)


def embed_kernel(all_rows, flat_ref, h_ref, told_ref, w2_ref, zq_ref, neg_ref, dz_ref, z_ref):
    i = pl.program_id(0)
    rows, emb = zq_ref.shape

    @pl.when(i == 0)
    def _():
        z_ref[...] = jnp.zeros_like(z_ref)

    z = None
    for t in range(0, STEP, TILE):
        mu = group_spread(told_ref[:, 0, 2 * t:2 * t + TILE], rows)
        inv = group_spread(told_ref[:, 0, 2 * t + TILE:2 * t + 2 * TILE], rows)
        active = jnp.maximum((h_ref[:, t:t + TILE] - mu) * inv, 0.0).astype(jnp.bfloat16)
        term = dot(active, w2_ref[t:t + TILE, :])
        z = term if z is None else z + term
    z_ref[...] += z

    @pl.when(i == pl.num_programs(0) - 1)
    def _():
        z = z_ref[...]
        z = z * lax.rsqrt(jnp.sum(z * z, axis=-1, keepdims=True) + norm_eps)
        back = jnp.where(
            flat_ref[...] == lax.broadcasted_iota(jnp.int32, (rows, rows), 0), 1.0, 0.0
        ).astype(jnp.bfloat16)
        high = z.astype(jnp.bfloat16)
        rest = z - high.astype(jnp.float32)
        mid = rest.astype(jnp.bfloat16)
        low = (rest - mid.astype(jnp.float32)).astype(jnp.bfloat16)
        positives = dot(back, high) + dot(back, mid) + dot(back, low)
        zq = zq_ref[...]
        inv_len = lax.rsqrt(jnp.sum(zq * zq, axis=-1, keepdims=True) + norm_eps)
        q = zq * inv_len
        scale_coef = loss_scale / all_rows
        pos = jnp.sum(q * positives, axis=-1, keepdims=True) / sharpness_divisor
        exp_pos = jnp.exp(pos) * QUARTER
        total = exp_pos + jnp.sum(neg_ref[:, emb:], axis=-1, keepdims=True)
        d_pos = scale_coef * (exp_pos / total - 1.0)
        weighted = neg_ref[:, :emb] * (scale_coef / total)
        d_q = (d_pos * positives + weighted) / sharpness_divisor
        d_z = (d_q - q * jnp.sum(d_q * q, axis=-1, keepdims=True)) * inv_len
        dz_ref[...] = d_z.astype(jnp.bfloat16)


def embed(flat_row, h, told, w2, zq, negs, all_rows):
    rows, hid = h.shape
    emb = w2.shape[1]
    groups = told.shape[0]
    return pl.pallas_call(
        lambda *refs: embed_kernel(all_rows, *refs),
        grid=(hid // STEP,),
        in_specs=[
            whole((1, rows)),
            pl.BlockSpec((rows, STEP), lambda i: (0, i)),
            pl.BlockSpec((groups, 1, 2 * STEP), lambda i: (0, 0, i)),
            pl.BlockSpec((STEP, emb), lambda i: (i, 0)),
            whole((rows, emb)),
            whole(negs.shape),
        ],
        out_specs=whole((rows, emb)),
        out_shape=jax.ShapeDtypeStruct((rows, emb), jnp.bfloat16),
        scratch_shapes=[pltpu.VMEM((rows, emb), jnp.float32)],
        cost_estimate=pl.CostEstimate(
            flops=2 * rows * hid * emb, bytes_accessed=4 * rows * hid, transcendentals=0
        ),
        compiler_params=params(),
        name="embed",
    )(flat_row, h, told, w2, zq, negs)


def store_rows(out_ref, at, value, crossed):
    size = value.shape[0] // 4
    for i, j in enumerate((0, 2, 1, 3)):
        j = j if crossed else i
        out_ref[i * size:(i + 1) * size, at] = value[j * size:(j + 1) * size].astype(out_ref.dtype)


def send_kernel(plain, dz_ref, w2_ref, n_ref, inv_ref, xt_ref, at_ref, dh_ref, g_ref):
    rows = dz_ref.shape[0]
    dz = dz_ref[...]
    xt = xt_ref[...]
    cols = dh_ref.shape[1]
    for t in range(0, cols, TILE):
        normed = n_ref[:, t:t + TILE].astype(jnp.float32)
        d_norm = jnp.where(normed > 0.0, dot_t(dz, w2_ref[t:t + TILE, :]), 0.0)
        mean = jnp.sum(d_norm, axis=0, keepdims=True) / rows
        slope = jnp.sum(d_norm * normed, axis=0, keepdims=True) / rows
        d_hidden = inv_ref[:, t:t + TILE] * (d_norm - mean - normed * slope)
        d_hidden = d_hidden.astype(jnp.bfloat16)
        dh_ref[:, t:t + TILE] = d_hidden
        store_rows(g_ref, slice(t, t + TILE), dot(xt, d_hidden), t >= plain)
    if at_ref is not None:
        store_rows(g_ref, slice(cols, None), dot(at_ref[...], dz), True)


def send_half(dz, w2, normed, inv, xt, at, place, cols, plain):
    rows, emb = dz.shape
    half = xt.shape[0] // 2
    extra = 0 if at is None else emb
    operands = [dz, w2, normed, inv, xt]
    in_specs = [
        whole((rows, emb)),
        pl.BlockSpec((cols, emb), lambda i: (place, 0)),
        pl.BlockSpec((rows, cols), lambda i: (0, place)),
        pl.BlockSpec((1, cols), lambda i: (0, place)),
        pl.BlockSpec((half, rows), lambda i: (1, 0)),
    ]
    if at is None:
        kernel = lambda a, b, c, d, e, f, g: send_kernel(plain, a, b, c, d, e, None, f, g)
    else:
        kernel = lambda *refs: send_kernel(plain, *refs)
        operands.append(at)
        in_specs.append(pl.BlockSpec((half, rows), lambda i: (1, 0)))
    return pl.pallas_call(
        kernel,
        grid=(1,),
        in_specs=in_specs,
        out_specs=[whole((rows, cols)), whole((half, cols + extra))],
        out_shape=[
            jax.ShapeDtypeStruct((rows, cols), jnp.bfloat16),
            jax.ShapeDtypeStruct((half, cols + extra), jnp.bfloat16),
        ],
        cost_estimate=pl.CostEstimate(
            flops=2 * rows * half * cols, bytes_accessed=8 * rows * half, transcendentals=0
        ),
        compiler_params=params(),
        name="send_half",
    )(*operands)


def keep_kernel(plain, dz_ref, dh_ref, xt_ref, at_ref, g_ref):
    xt = xt_ref[...]
    cols = dh_ref.shape[1]
    for t in range(0, cols, TILE):
        g = dot(xt, dh_ref[:, t:t + TILE])
        store_rows(g_ref, slice(t, t + TILE), g, t >= plain)
    if at_ref is not None:
        store_rows(g_ref, slice(cols, None), dot(at_ref[...], dz_ref[...]), True)


def keep_half(dz, dh, xt, at, plain):
    rows, emb = dz.shape
    half = xt.shape[0] // 2
    cols = dh.shape[1]
    extra = 0 if at is None else emb
    operands = [dz, dh, xt]
    in_specs = [whole((rows, emb)), whole((rows, cols)), whole((half, rows))]
    if at is None:
        kernel = lambda a, b, c, d: keep_kernel(plain, a, b, c, None, d)
    else:
        kernel = lambda *refs: keep_kernel(plain, *refs)
        operands.append(at)
        in_specs.append(whole((half, rows)))
    return pl.pallas_call(
        kernel,
        grid=(1,),
        in_specs=in_specs,
        out_specs=whole((half, cols + extra)),
        out_shape=jax.ShapeDtypeStruct((half, cols + extra), jnp.float32),
        cost_estimate=pl.CostEstimate(
            flops=2 * rows * half * cols, bytes_accessed=8 * rows * half, transcendentals=0
        ),
        compiler_params=params(),
        name="keep_half",
    )(*operands)


def swap(x, axis, bit):
    size = lax.axis_size(axis)
    return lax.ppermute(x, axis, [(i, i ^ bit) for i in range(size)])


def total(parts, rows, cols):
    parts = [p[rows, cols].astype(jnp.float32) for p in parts]
    out = parts[0]
    for p in parts[1:]:
        out = out + p
    return out


def scatter_pair(keep, sent, split):
    n_dp = lax.axis_size("dp")
    length = n_dp // 2
    half = keep.shape[0]
    quarter, eighth = half // 2, half // 4
    rows = eighth // length
    every = slice(None)
    came = swap(sent, "crop", 1)
    sides = []
    for side, (first, second) in enumerate(
        ((("dp", 1), ("crop", 2)), (("crop", 2), ("dp", 1)))
    ):
        cols = slice(0, split) if side == 0 else slice(split, None)
        held = [keep[:, cols], came[:, cols]]
        out = total(held, slice(quarter, half), every).astype(jnp.bfloat16)
        held.append(swap(out, *first))
        out = total(held, slice(eighth, quarter), every).astype(jnp.bfloat16)
        held.append(swap(out, *second))
        sides.append(held)
    own = jnp.concatenate([total(held, slice(0, rows), every) for held in sides], axis=1)
    for k in range(1, length):
        out = jnp.concatenate(
            [
                total(held, slice(k * rows, (k + 1) * rows), every).astype(jnp.bfloat16)
                for held in sides
            ],
            axis=1,
        )
        own = own + swap(out, "dp", 2 * k).astype(jnp.float32)
    return own


def per_device(
    query_crops, key_crops, shuffle, distractor_bank, query_inner, query_outer, key_inner, key_outer
):
    n_dp, n_crop = lax.axis_size("dp"), lax.axis_size("crop")
    group_count = n_dp * n_crop
    row_count = query_crops.shape[0]
    hid = query_inner.shape[1]
    per_peer = row_count // group_count
    all_rows = float(row_count * group_count)

    wanted = (shuffle % row_count).reshape(group_count, per_peer)
    requested = lax.all_to_all(wanted, AXES, split_axis=0, concat_axis=0, tiled=True)
    flat_req = requested.reshape(-1)

    flat_col, flat_row = flat_req[:, None], flat_req[None, :]
    hidden_k, sums = key_hidden(flat_col, key_crops, key_inner, group_count)
    came = lax.all_to_all(sums, AXES, split_axis=0, concat_axis=0, tiled=True)

    normed, inv_q, z_q, q_low = query_forward(query_crops, query_inner, query_outer)
    came, q_low, flat_row = lax.optimization_barrier((came, q_low, flat_row))
    told = batch(came, row_count)
    told = lax.all_to_all(told, AXES, split_axis=0, concat_axis=0, tiled=True)

    negs = negatives(q_low, distractor_bank)

    length = n_dp // 2
    dp, crop = lax.axis_index("dp"), lax.axis_index("crop")
    block = lax.iota(jnp.int32, group_count // 2)
    z, x, y = block // n_crop, (block // (n_crop // 2)) % 2, block % (n_crop // 2)
    order = ((x ^ (dp % 2)) * (n_crop // 2) + (y ^ (crop // 2))) * length + (z ^ (dp // 2))
    core = crop % 2
    xt = ordered(query_crops, order, core, group_count, False)
    at = ordered(normed, order, core, group_count, True)

    told, negs, xt, at = lax.optimization_barrier((told, negs, xt, at))
    d_z = embed(flat_row, hidden_k, told, key_outer, z_q, negs, all_rows)

    outs, made = [], []
    parts = 2
    cols = hid // parts
    plain = cols // (2 * TILE) * TILE
    for i in range(parts):
        last = at if i == parts - 1 else None
        dh, sent = send_half(d_z, query_outer, normed, inv_q, xt, last, i, cols, plain)
        made.append((dh, sent, last))
    for dh, sent, last in made:
        keep = keep_half(d_z, dh, xt, last, plain)
        outs.append(scatter_pair(keep, sent, plain))
    grad = jnp.concatenate(outs, axis=1)
    return (grad[:, :hid], grad[:, hid:])


def solution(mesh):
    placed = (
        P(AXES, None),
        P(AXES, None),
        P(AXES),
        P(),
        P(),
        P(),
        P(),
        P(),
    )
    return jax.shard_map(
        per_device,
        mesh=mesh,
        in_specs=placed,
        out_specs=(P(AXES, None), P(AXES, None)),
        check_vma=False,
    )
```

time: 179 us -> 162 us (0.905)
  Pallas kernels: 71.8 us -> 56.3 us
  waiting for transfers between devices: 45.1 us -> 41.7 us
  local copies, waits for them, and re-layouts: 12 us -> 14.8 us
    ppermute x10 -> x16, waiting for transfers between devices: 22.9 us -> 37.6 us  [swap(): return lax.ppermute(x, axis, [(i, i ^ bit) for i in range(size)])]
    all_to_all x1, waiting for transfers between devices: 15.5 us -> 4.07 us  [per_device(): came = lax.all_to_all(sums, AXES, split_axis=0, concat_axis=0, tiled=True)]
    ppermute x6 -> x0, starting transfers between devices: 10.5 us -> none  [scatter_pair(): own = own + lax.ppermute(out, 'dp', perm).astype(jnp.float32)]
    pallas_call x8, Pallas kernels: 42.4 us -> 32.1 us  [the longest x2 9.12 us: send_half(): pl.pallas_call(kernel, grid=(1,), in_specs=in_specs, out_specs=[whole((ro...]
    ppermute x10 -> x16, starting transfers between devices: 10.2 us -> 19.8 us  [swap(): return lax.ppermute(x, axis, [(i, i ^ bit) for i in range(size)])]
    ppermute x6 -> x0, waiting for transfers between devices: 6.65 us -> none  [scatter_pair(): own = own + lax.ppermute(out, 'dp', perm).astype(jnp.float32)]
    pallas_call x1, Pallas kernels: 6.56 us -> 2.78 us  [embed(): pl.pallas_call(lambda *refs: embed_kernel(all_rows, *refs), grid=(hid //...]
    unnamed x30 -> x36, local copies, waits for them, and re-layouts: 10.5 us -> 12.6 us
  transfers between devices with their start and end apart: 18 -> 18, of which waited for: 9 -> 9; matrix products, arithmetic and copies ran while one was open for 3% -> 4% of each run, Pallas kernels for 26% -> 24%
where the time goes in v3:
time: 162 us; the launch traced here: 161 us
  Pallas kernels  56.3 us (35%)
  waiting for transfers between devices  41.7 us (26%)
  starting transfers between devices  25.3 us (16%)
  local copies, waits for them, and re-layouts  14.8 us (9%)
  blocking collectives  14.2 us (9%)
  other arithmetic  7.89 us (5%)
    ppermute x16, waiting for transfers between devices, swap(): return lax.ppermute(x, axis, [(i, i ^ bit) for i in range(size)])  37.6 us
    ppermute x16, starting transfers between devices, swap(): return lax.ppermute(x, axis, [(i, i ^ bit) for i in range(size)])  19.8 us
    all_to_all x1, blocking collectives, per_device(): lax.all_to_all(wanted, AXES, split_axis=0, concat_axis=0, tiled=True)  14.2 us
    unnamed x36, local copies, waits for them, and re-layouts  12.6 us
    pallas_call x1, Pallas kernels, negatives(): pl.pallas_call(neg_kernel, grid=(bank.shape[0] // tile,), in_specs=[pl.Bl...  11 us
    pallas_call x1, Pallas kernels, key_hidden(): pl.pallas_call(lambda *refs: key_hidden_kernel(groups, *refs), grid=(hid...  10.4 us
    pallas_call x2, Pallas kernels, send_half(): pl.pallas_call(kernel, grid=(1,), in_specs=in_specs, out_specs=[whole((ro...  9.12 us
    pallas_call x1, Pallas kernels, query_forward(): pl.pallas_call(query_kernel, grid=(hid // STEP,), in_specs=[whole((rows,...  9.06 us
  transfers between devices with their start and end apart: 18, of which 9 were waited for; matrix products, arithmetic and copies ran while one was open for 4% of the time, Pallas kernels for 24%

profile of v3, /device:TPU:0, one launch (start us, length us, event | category | flops | bytes accessed | tf_op | source)
XLA Modules:
  0.0 161.2 jit_solution(10315157929511024040)
XLA Ops:
  0.6 0.7 add_select_fusion
  1.4 14.2 %all_to_all.19 = s32[32,1,16]{2,1,0:T(1,128)S(1)} all-to-all(s32[32,1,16]{2,1,0:T(1,128)S(1)} %bitcast.12), channel_id=1, replica_groups=mesh['dp'=8,'crop'=4] {'dp','crop'}, dimensions={0} | all-to-all | bytes 4096 | tf_op jit(solution)/shard_map/all_to_all | solution.py:505
  17.0 1.6 copy-done.12
  18.6 10.4 %key_hidden.1 = (f32[512,2048]{1,0:T(8,128)}, f32[32,1,4096]{2,1,0:T(1,128)}) custom-call(s32[512,1]{1,0:T(8,128)S(1)} %broadcast_in_dim_reshape.8.refs_0_, bf16[512,2048]{1,0:T(8,128)(2,1)S(1)} %copy-done.12, bf16[2048,2048]{1,0:T(8,128)(2,1)} %refs_2_.1), custom_call_target="tpu_custom_call" | custom-call | flops 5368709120 | bytes 8388608 | tf_op jit(solution)/shard_map/key_hidden/pallas_call | solution.py:140
  29.0 2.6 %all-to-all-start.1 = ((f32[32,1,4096]{2,1,0:T(1,128)}), f32[32,1,4096]{2,1,0:T(1,128)S(1)}, u32[]{:S(2)}, u32[]{:S(2)}) async-start(f32[32,1,4096]{2,1,0:T(1,128)} %get-tuple-element.19), calls=%async_computation.1 | async-start | bytes 1048576 | tf_op jit(solution)/shard_map/all_to_all | solution.py:510
  31.7 1.6 copy-done.5
  33.2 9.1 %query_forward.1 = (bf16[512,2048]{1,0:T(8,128)(2,1)S(1)}, f32[1,2048]{1,0:T(1,128)S(1)}, f32[512,128]{1,0:T(8,128)S(1)}, bf16[512,128]{1,0:T(8,128)(2,1)S(1)}) custom-call(bf16[512,2048]{1,0:T(8,128)(2,1)S(1)} %copy-done.5, bf16[2048,2048]{1,0:T(8,128)(2,1)} %w_ref.1, bf16[2048,128]{1,0:T(8,128)(2,1)S(1)} %copy-done.7), custom_call_target="tpu_custom_call" | custom-call | flops 4563402752 | bytes 8388608 | tf_op jit(solution)/shard_map/query_forward/pallas_call | solution.py:219
  42.3 0.8 broadcast_in_dim_reshape.7.refs_0_
  43.1 4.1 %all-to-all-done.1.refs_0_ = f32[32,1,4096]{2,1,0:T(1,128)S(1)} async-done(((f32[32,1,4096]{2,1,0:T(1,128)}), f32[32,1,4096]{2,1,0:T(1,128)S(1)}, u32[]{:S(2)}, u32[]{:S(2)}) %all-to-all-start.1) | async-done | bytes 524320 | tf_op jit(solution)/shard_map/all_to_all | solution.py:510
  47.2 1.1 batch.1
  48.2 3.0 %all-to-all-start.2 = ((f32[32,1,4096]{2,1,0:T(1,128)}), f32[32,1,4096]{2,1,0:T(1,128)S(1)}, u32[]{:S(2)}, u32[]{:S(2)}) async-start(f32[32,1,4096]{2,1,0:T(1,128)} %batch.1), calls=%async_computation.2 | async-start | bytes 1048576 | tf_op jit(solution)/shard_map/all_to_all | solution.py:515
  51.3 1.6 copy-done.6
  52.9 2.9 %ordered.2 = bf16[2,16,64,512]{3,2,1,0:T(8,128)(2,1)S(1)} custom-call(s32[17]{0:T(128)S(1)} %pad_add_fusion.refs_0_, bf16[512,2048]{1,0:T(8,128)(2,1)S(1)} %copy-done.6), custom_call_target="tpu_custom_call" | custom-call | bytes 8388608 | tf_op jit(solution)/shard_map/ordered/pallas_call | solution.py:268
  55.9 1.4 copy-done
  57.3 3.0 %ordered.3 = bf16[2,16,64,512]{3,2,1,0:T(8,128)(2,1)S(1)} custom-call(s32[17]{0:T(128)S(1)} %pad_add_fusion.refs_0_, bf16[512,2048]{1,0:T(8,128)(2,1)S(1)} %get-tuple-element.25.refs_1_.c.refs_2_), custom_call_target="tpu_custom_call" | custom-call | bytes 8388608 | tf_op jit(solution)/shard_map/ordered/pallas_call | solution.py:268
  60.2 1.4 copy-done.2
  61.7 11.0 %negatives.1.refs_5_ = f32[512,256]{1,0:T(8,128)S(1)} custom-call(bf16[512,128]{1,0:T(8,128)(2,1)S(1)} %get-tuple-element.24.q_ref, bf16[16384,128]{1,0:T(8,128)(2,1)S(1)} %copy-done.11), custom_call_target="tpu_custom_call" | custom-call | flops 4294967296 | bytes 4194304 | tf_op jit(solution)/shard_map/negatives/pallas_call | solution.py:42
  72.7 0.8 copy-done.9
  73.5 2.2 %copy-done.4 = f32[512,2048]{1,0:T(8,128)S(1)} copy-done((f32[512,2048]{1,0:T(8,128)S(1)}, f32[512,2048]{1,0:T(8,128)}, u32[]{:S(2)}) %copy-start.4) | copy-done | bytes 4194328
  75.7 1.0 copy-done.8
  76.7 1.0 copy-done.10
  77.8 2.8 %embed.1.a.refs_0_ = bf16[512,128]{1,0:T(8,128)(2,1)S(1)} custom-call(s32[1,512]{1,0:T(1,128)S(1)} %broadcast_in_dim_reshape.7.refs_0_, f32[512,2048]{1,0:T(8,128)S(1)} %copy-done.4, f32[32,1,4096]{2,1,0:T(1,128)S(1)} %all-to-all-done.2.refs_2_, bf16[2048,128]{1,0:T(8,128)(2,1)S(1)} %copy-done.8, f32[512,128]{1,0:T(8,128)S(1)} %get-tuple-element.27.refs_4_, ...), custom_call_target="tpu_custom_call" | custom-call | flops 268435456 | bytes 4194304 | tf_op jit(solution)/shard_map/embed/pallas_call | solution.py:330
  80.6 3.8 %send_half.2 = (bf16[512,1024]{1,0:T(8,128)(2,1)S(1)}, bf16[1024,1024]{1,0:T(8,128)(2,1)S(1)}) custom-call(bf16[512,128]{1,0:T(8,128)(2,1)S(1)} %embed.1.a.refs_0_, bf16[2048,128]{1,0:T(8,128)(2,1)S(1)} %copy-done.7, bf16[512,2048]{1,0:T(8,128)(2,1)S(1)} %get-tuple-element.25.refs_1_.c.refs_2_, f32[1,2048]{1,0:T(1,128)S(1)} %get-tuple-element.29.d.refs_3_, ...), custom_call_target="tpu_custom_call" | custom-call | flops 1073741824 | bytes 4194304 | tf_op jit(solution)/shard_map/send_half/pallas_call | solution.py:395
  84.8 5.3 %send_half.3 = (bf16[512,1024]{1,0:T(8,128)(2,1)S(1)}, bf16[1024,1152]{1,0:T(8,128)(2,1)}) custom-call(bf16[512,128]{1,0:T(8,128)(2,1)S(1)} %embed.1.a.refs_0_, bf16[2048,128]{1,0:T(8,128)(2,1)S(1)} %copy-done.7, bf16[512,2048]{1,0:T(8,128)(2,1)S(1)} %get-tuple-element.25.refs_1_.c.refs_2_, f32[1,2048]{1,0:T(1,128)S(1)} %get-tuple-element.29.d.refs_3_, ...), custom_call_target="tpu_custom_call" | custom-call | flops 1073741824 | bytes 4194304 | tf_op jit(solution)/shard_map/send_half/pallas_call | solution.py:395
  90.3 3.3 %keep_half.2 = f32[1024,1024]{1,0:T(8,128)} custom-call(bf16[512,128]{1,0:T(8,128)(2,1)S(1)} %embed.1.a.refs_0_, bf16[512,1024]{1,0:T(8,128)(2,1)S(1)} %get-tuple-element.31.b, bf16[2048,512]{1,0:T(8,128)(2,1)S(1)} %bitcast.7), custom_call_target="tpu_custom_call" | custom-call | flops 1073741824 | bytes 4194304 | tf_op jit(solution)/shard_map/keep_half/pallas_call | solution.py:435
  93.6 2.7 %fusion.3 = (bf16[512,512]{1,0:T(8,128)(2,1)S(1)}, bf16[512,512]{1,0:T(8,128)(2,1)S(1)}) fusion(f32[1024,1024]{1,0:T(8,128)} %keep_half.2, bf16[1024,1024]{1,0:T(8,128)(2,1)S(1)} %collective-permute-done), kind=kLoop, calls=%fused_computation.7 | loop fusion | flops 1572864 | bytes 4194304 | tf_op jit(solution)/shard_map/convert_element_type | solution.py:476
  96.3 1.9 %collective-permute-start.1 = (bf16[512,512]{1,0:T(8,128)(2,1)S(1)}, bf16[512,512]{1,0:T(8,128)(2,1)S(1)}, u32[]{:S(2)}, u32[]{:S(2)}) collective-permute-start(bf16[512,512]{1,0:T(8,128)(2,1)S(1)} %get-tuple-element.54), channel_id=1, source_target_pairs={{0,4},{4,0},{8,12},{12,8},{16,20},{20,16},{24,28},{28,24},{1,5},{5... | collective-permute-start | bytes 1572872 | tf_op jit(solution)/shard_map/ppermute | solution.py:451
  98.1 1.4 collective-permute-start.3
  99.6 3.7 %keep_half.3 = f32[1024,1152]{1,0:T(8,128)} custom-call(bf16[512,128]{1,0:T(8,128)(2,1)S(1)} %embed.1.a.refs_0_, bf16[512,1024]{1,0:T(8,128)(2,1)S(1)} %get-tuple-element.34.refs_1_, bf16[2048,512]{1,0:T(8,128)(2,1)S(1)} %bitcast.8, bf16[2048,512]{1,0:T(8,128)(2,1)S(1)} %bitcast.10), custom_call_target="tpu_custom_call" | custom-call | flops 1073741824 | bytes 4194304 | tf_op jit(solution)/shard_map/keep_half/pallas_call | solution.py:435
  103.3 1.5 fusion.1
  105.4 5.7 %collective-permute-done.1 = bf16[512,512]{1,0:T(8,128)(2,1)S(1)} collective-permute-done((bf16[512,512]{1,0:T(8,128)(2,1)S(1)}, bf16[512,512]{1,0:T(8,128)(2,1)S(1)}, u32[]{:S(2)}, u32[]{:S(2)}) %collective-permute-start.1) | collective-permute-done | bytes 524320 | tf_op jit(solution)/shard_map/ppermute | solution.py:451
  111.1 0.8 collective-permute-done.3
  112.1 1.1 collective-permute-start.4
  113.4 1.5 collective-permute-start.11
  115.5 6.9 %collective-permute-done.9 = bf16[512,512]{1,0:T(8,128)(2,1)S(1)} collective-permute-done((bf16[512,512]{1,0:T(8,128)(2,1)S(1)}, bf16[512,512]{1,0:T(8,128)(2,1)S(1)}, u32[]{:S(2)}, u32[]{:S(2)}) %collective-permute-start.9) | collective-permute-done | bytes 524320 | tf_op jit(solution)/shard_map/ppermute | solution.py:451
  122.4 1.9 %collective-permute-start.10 = (bf16[256,512]{1,0:T(8,128)(2,1)S(1)}, bf16[256,512]{1,0:T(8,128)(2,1)S(1)}, u32[]{:S(2)}, u32[]{:S(2)}) collective-permute-start(bf16[256,512]{1,0:T(8,128)(2,1)S(1)} %fusion.7), channel_id=1, source_target_pairs={{0,2},{1,3},{2,0},{3,1},{4,6},{5,7},{6,4},{7,5},{8,10},{9,11},{10,... | collective-permute-start | bytes 786440 | tf_op jit(solution)/shard_map/ppermute | solution.py:451
  124.3 3.1 %collective-permute-done.4 = bf16[256,512]{1,0:T(8,128)(2,1)S(1)} collective-permute-done((bf16[256,512]{1,0:T(8,128)(2,1)S(1)}, bf16[256,512]{1,0:T(8,128)(2,1)S(1)}, u32[]{:S(2)}, u32[]{:S(2)}) %collective-permute-start.4) | collective-permute-done | bytes 262176 | tf_op jit(solution)/shard_map/ppermute | solution.py:451
  127.5 9.2 %collective-permute-done.2 = bf16[256,512]{1,0:T(8,128)(2,1)S(1)} collective-permute-done((bf16[256,512]{1,0:T(8,128)(2,1)S(1)}, bf16[256,512]{1,0:T(8,128)(2,1)S(1)}, u32[]{:S(2)}, u32[]{:S(2)}) %collective-permute-start.2) | collective-permute-done | bytes 262176 | tf_op jit(solution)/shard_map/ppermute | solution.py:451
  136.9 3.4 %collective-permute-start.7 = (bf16[64,1024]{1,0:T(8,128)(2,1)S(1)}, bf16[64,1024]{1,0:T(8,128)(2,1)S(1)}, u32[]{:S(2)}, u32[]{:S(2)}) collective-permute-start(bf16[64,1024]{1,0:T(8,128)(2,1)S(1)} %pad_maximum_fusion.6), channel_id=1, source_target_pairs={{0,24},{4,28},{8,16},{12,20},{16,8},{20,12},{24,0},{28,4},{1,25},{... | collective-permute-start | bytes 393224 | tf_op jit(solution)/shard_map/ppermute | solution.py:451
  140.5 1.1 collective-permute-start.12
  141.6 1.1 collective-permute-start.5
  142.8 4.8 %collective-permute-done.12 = bf16[256,640]{1,0:T(8,128)(2,1)S(1)} collective-permute-done((bf16[256,640]{1,0:T(8,128)(2,1)S(1)}, bf16[256,640]{1,0:T(8,128)(2,1)S(1)}, u32[]{:S(2)}, u32[]{:S(2)}) %collective-permute-start.12) | collective-permute-done | bytes 327712 | tf_op jit(solution)/shard_map/ppermute | solution.py:451
  147.8 2.0 %collective-permute-start.15 = (bf16[64,1152]{1,0:T(8,128)(2,1)S(1)}, bf16[64,1152]{1,0:T(8,128)(2,1)S(1)}, u32[]{:S(2)}, u32[]{:S(2)}) collective-permute-start(bf16[64,1152]{1,0:T(8,128)(2,1)S(1)} %pad_maximum_fusion.3), channel_id=1, source_target_pairs={{0,24},{4,28},{8,16},{12,20},{16,8},{20,12},{24,0},{28,4},{1,25},{... | collective-permute-start | bytes 442376 | tf_op jit(solution)/shard_map/ppermute | solution.py:451
  149.8 1.0 collective-permute-start.14
  150.9 1.5 collective-permute-start.13
  152.5 2.4 %collective-permute-done.15 = bf16[64,1152]{1,0:T(8,128)(2,1)S(1)} collective-permute-done((bf16[64,1152]{1,0:T(8,128)(2,1)S(1)}, bf16[64,1152]{1,0:T(8,128)(2,1)S(1)}, u32[]{:S(2)}, u32[]{:S(2)}) %collective-permute-start.15) | collective-permute-done | bytes 147488 | tf_op jit(solution)/shard_map/ppermute | solution.py:451
  155.0 4.7 %collective-permute-done.14 = bf16[64,1152]{1,0:T(8,128)(2,1)S(1)} collective-permute-done((bf16[64,1152]{1,0:T(8,128)(2,1)S(1)}, bf16[64,1152]{1,0:T(8,128)(2,1)S(1)}, u32[]{:S(2)}, u32[]{:S(2)}) %collective-permute-start.14) | collective-permute-done | bytes 147488 | tf_op jit(solution)/shard_map/ppermute | solution.py:451
  160.4 0.8 pad_maximum_fusion
  (64 shorter events, 5.5 us)
Async XLA Ops:
  15.6 1.2 copy-start.17
  17.0 1.6 copy-start.12
  18.6 13.0 %copy-start.7 = (bf16[2048,128]{1,0:T(8,128)(2,1)S(1)}, bf16[2048,128]{1,0:T(8,128)(2,1)}, u32[]{:S(2)}) copy-start(bf16[2048,128]{1,0:T(8,128)(2,1)} %refs_1_.5) | copy-start | bytes 1572868
  29.0 18.2 %all-to-all-start.1 = ((f32[32,1,4096]{2,1,0:T(1,128)}), f32[32,1,4096]{2,1,0:T(1,128)S(1)}, u32[]{:S(2)}, u32[]{:S(2)}) async-start(f32[32,1,4096]{2,1,0:T(1,128)} %get-tuple-element.19), calls=%async_computation.1 | async-start | bytes 1048576 | tf_op jit(solution)/shard_map/all_to_all | solution.py:510
  31.6 1.6 copy-start.5
  48.2 25.3 %all-to-all-start.2 = ((f32[32,1,4096]{2,1,0:T(1,128)}), f32[32,1,4096]{2,1,0:T(1,128)S(1)}, u32[]{:S(2)}, u32[]{:S(2)}) async-start(f32[32,1,4096]{2,1,0:T(1,128)} %batch.1), calls=%async_computation.2 | async-start | bytes 1048576 | tf_op jit(solution)/shard_map/all_to_all | solution.py:515
  51.3 1.6 copy-start.6
  55.9 1.4 copy-start
  57.3 4.4 %copy-start.11 = (bf16[16384,128]{1,0:T(8,128)(2,1)S(1)}, bf16[16384,128]{1,0:T(8,128)(2,1)}, u32[]{:S(2)}) copy-start(bf16[16384,128]{1,0:T(8,128)(2,1)} %bank_ref.1) | copy-start | bytes 12582916
  60.2 1.4 copy-start.2
  72.7 0.8 copy-start.9
  73.5 2.2 %copy-start.4 = (f32[512,2048]{1,0:T(8,128)S(1)}, f32[512,2048]{1,0:T(8,128)}, u32[]{:S(2)}) copy-start(f32[512,2048]{1,0:T(8,128)} %get-tuple-element.22.refs_1_) | copy-start | bytes 12582916
  75.7 1.0 copy-start.8
  76.7 1.0 copy-start.10
  80.6 4.2 %copy-start.1 = (bf16[2,16,64,512]{3,2,1,0:T(8,128)(2,1)S(1)}, bf16[2,16,64,512]{3,2,1,0:T(8,128)(2,1)}, u32[]{:S(2)}) copy-start(bf16[2,16,64,512]{3,2,1,0:T(8,128)(2,1)} %copy-done) | copy-start | bytes 6291460
  84.4 9.2 %collective-permute-start = (bf16[1024,1024]{1,0:T(8,128)(2,1)S(1)}, bf16[1024,1024]{1,0:T(8,128)(2,1)S(1)}, u32[]{:S(2)}, u32[]{:S(2)}) collective-permute-start(bf16[1024,1024]{1,0:T(8,128)(2,1)S(1)} %get-tuple-element.32), channel_id=1, source_target_pairs={{0,1},{1,0},{2,3},{3,2},{4,5},{5,4},{6,7},{7,6},{8,9},{9,8},{10,11... | collective-permute-start | bytes 6291464 | tf_op jit(solution)/shard_map/ppermute | solution.py:451
  90.1 13.2 %collective-permute-start.8 = (bf16[1024,1152]{1,0:T(8,128)(2,1)}, bf16[1024,1152]{1,0:T(8,128)(2,1)S(1)}, u32[]{:S(2)}, u32[]{:S(2)}) collective-permute-start(bf16[1024,1152]{1,0:T(8,128)(2,1)} %get-tuple-element.35), channel_id=1, source_target_pairs={{0,1},{1,0},{2,3},{3,2},{4,5},{5,4},{6,7},{7,6},{8,9},{9,8},{10,11... | collective-permute-start | bytes 7077896 | tf_op jit(solution)/shard_map/ppermute | solution.py:451
  93.6 6.0 %copy-start.3 = (bf16[2,16,64,512]{3,2,1,0:T(8,128)(2,1)S(1)}, bf16[2,16,64,512]{3,2,1,0:T(8,128)(2,1)}, u32[]{:S(2)}) copy-start(bf16[2,16,64,512]{3,2,1,0:T(8,128)(2,1)} %copy-done.2) | copy-start | bytes 6291460
  93.6 6.0 %copy-start.15 = (bf16[1024,1024]{1,0:T(8,128)(2,1)}, bf16[1024,1024]{1,0:T(8,128)(2,1)S(1)}, u32[]{:S(2)}) copy-start(bf16[1024,1024]{1,0:T(8,128)(2,1)S(1)} %collective-permute-done) | copy-start | bytes 6291460
  96.3 14.8 %collective-permute-start.1 = (bf16[512,512]{1,0:T(8,128)(2,1)S(1)}, bf16[512,512]{1,0:T(8,128)(2,1)S(1)}, u32[]{:S(2)}, u32[]{:S(2)}) collective-permute-start(bf16[512,512]{1,0:T(8,128)(2,1)S(1)} %get-tuple-element.54), channel_id=1, source_target_pairs={{0,4},{4,0},{8,12},{12,8},{16,20},{20,16},{24,28},{28,24},{1,5},{5... | collective-permute-start | bytes 1572872 | tf_op jit(solution)/shard_map/ppermute | solution.py:451
  98.1 13.8 %collective-permute-start.3 = (bf16[512,512]{1,0:T(8,128)(2,1)S(1)}, bf16[512,512]{1,0:T(8,128)(2,1)S(1)}, u32[]{:S(2)}, u32[]{:S(2)}) collective-permute-start(bf16[512,512]{1,0:T(8,128)(2,1)S(1)} %get-tuple-element.55), channel_id=1, source_target_pairs={{0,2},{1,3},{2,0},{3,1},{4,6},{5,7},{6,4},{7,5},{8,10},{9,11},{10,... | collective-permute-start | bytes 1572872 | tf_op jit(solution)/shard_map/ppermute | solution.py:451
  99.6 12.3 %copy-start.14 = (f32[1024,1024]{1,0:T(8,128)S(1)}, f32[1024,1024]{1,0:T(8,128)}, u32[]{:S(2)}) copy-start(f32[1024,1024]{1,0:T(8,128)} %keep_half.2) | copy-start | bytes 12582916
  99.6 12.3 %copy-start.16 = (bf16[1024,1024]{1,0:T(8,128)(2,1)S(1)}, bf16[1024,1024]{1,0:T(8,128)(2,1)}, u32[]{:S(2)}) copy-start(bf16[1024,1024]{1,0:T(8,128)(2,1)} %copy-done.15) | copy-start | bytes 6291460
  103.3 9.9 %copy-start.13 = (f32[1024,1152]{1,0:T(8,128)S(1)}, f32[1024,1152]{1,0:T(8,128)}, u32[]{:S(2)}) copy-start(f32[1024,1152]{1,0:T(8,128)} %keep_half.3) | copy-start | bytes 14155780
  104.8 17.5 %collective-permute-start.9 = (bf16[512,512]{1,0:T(8,128)(2,1)S(1)}, bf16[512,512]{1,0:T(8,128)(2,1)S(1)}, u32[]{:S(2)}, u32[]{:S(2)}) collective-permute-start(bf16[512,512]{1,0:T(8,128)(2,1)S(1)} %fusion.1), channel_id=1, source_target_pairs={{0,4},{4,0},{8,12},{12,8},{16,20},{20,16},{24,28},{28,24},{1,5},{5... | collective-permute-start | bytes 1572872 | tf_op jit(solution)/shard_map/ppermute | solution.py:451
  112.1 15.2 %collective-permute-start.4 = (bf16[256,512]{1,0:T(8,128)(2,1)S(1)}, bf16[256,512]{1,0:T(8,128)(2,1)S(1)}, u32[]{:S(2)}, u32[]{:S(2)}) collective-permute-start(bf16[256,512]{1,0:T(8,128)(2,1)S(1)} %get-tuple-element.53), channel_id=1, source_target_pairs={{0,4},{4,0},{8,12},{12,8},{16,20},{20,16},{24,28},{28,24},{1,5},{5... | collective-permute-start | bytes 786440 | tf_op jit(solution)/shard_map/ppermute | solution.py:451
  113.4 27.0 %collective-permute-start.11 = (bf16[512,640]{1,0:T(8,128)(2,1)S(1)}, bf16[512,640]{1,0:T(8,128)(2,1)S(1)}, u32[]{:S(2)}, u32[]{:S(2)}) collective-permute-start(bf16[512,640]{1,0:T(8,128)(2,1)S(1)} %fusion), channel_id=1, source_target_pairs={{0,2},{1,3},{2,0},{3,1},{4,6},{5,7},{6,4},{7,5},{8,10},{9,11},{10,... | collective-permute-start | bytes 1966088 | tf_op jit(solution)/shard_map/ppermute | solution.py:451
  114.9 21.8 %collective-permute-start.2 = (bf16[256,512]{1,0:T(8,128)(2,1)S(1)}, bf16[256,512]{1,0:T(8,128)(2,1)S(1)}, u32[]{:S(2)}, u32[]{:S(2)}) collective-permute-start(bf16[256,512]{1,0:T(8,128)(2,1)S(1)} %get-tuple-element.52), channel_id=1, source_target_pairs={{0,2},{1,3},{2,0},{3,1},{4,6},{5,7},{6,4},{7,5},{8,10},{9,11},{10,... | collective-permute-start | bytes 786440 | tf_op jit(solution)/shard_map/ppermute | solution.py:451
  122.4 20.3 %collective-permute-start.10 = (bf16[256,512]{1,0:T(8,128)(2,1)S(1)}, bf16[256,512]{1,0:T(8,128)(2,1)S(1)}, u32[]{:S(2)}, u32[]{:S(2)}) collective-permute-start(bf16[256,512]{1,0:T(8,128)(2,1)S(1)} %fusion.7), channel_id=1, source_target_pairs={{0,2},{1,3},{2,0},{3,1},{4,6},{5,7},{6,4},{7,5},{8,10},{9,11},{10,... | collective-permute-start | bytes 786440 | tf_op jit(solution)/shard_map/ppermute | solution.py:451
  136.9 14.0 %collective-permute-start.7 = (bf16[64,1024]{1,0:T(8,128)(2,1)S(1)}, bf16[64,1024]{1,0:T(8,128)(2,1)S(1)}, u32[]{:S(2)}, u32[]{:S(2)}) collective-permute-start(bf16[64,1024]{1,0:T(8,128)(2,1)S(1)} %pad_maximum_fusion.6), channel_id=1, source_target_pairs={{0,24},{4,28},{8,16},{12,20},{16,8},{20,12},{24,0},{28,4},{1,25},{... | collective-permute-start | bytes 393224 | tf_op jit(solution)/shard_map/ppermute | solution.py:451
  140.3 12.2 %collective-permute-start.6 = (bf16[64,1024]{1,0:T(8,128)(2,1)S(1)}, bf16[64,1024]{1,0:T(8,128)(2,1)S(1)}, u32[]{:S(2)}, u32[]{:S(2)}) collective-permute-start(bf16[64,1024]{1,0:T(8,128)(2,1)S(1)} %pad_maximum_fusion.5), channel_id=1, source_target_pairs={{0,16},{4,20},{8,24},{12,28},{16,0},{20,4},{24,8},{28,12},{1,17},{... | collective-permute-start | bytes 393224 | tf_op jit(solution)/shard_map/ppermute | solution.py:451
  140.5 7.1 %collective-permute-start.12 = (bf16[256,640]{1,0:T(8,128)(2,1)S(1)}, bf16[256,640]{1,0:T(8,128)(2,1)S(1)}, u32[]{:S(2)}, u32[]{:S(2)}) collective-permute-start(bf16[256,640]{1,0:T(8,128)(2,1)S(1)} %fusion.5), channel_id=1, source_target_pairs={{0,4},{4,0},{8,12},{12,8},{16,20},{20,16},{24,28},{28,24},{1,5},{5... | collective-permute-start | bytes 983048 | tf_op jit(solution)/shard_map/ppermute | solution.py:451
  141.6 10.9 %collective-permute-start.5 = (bf16[64,1024]{1,0:T(8,128)(2,1)S(1)}, bf16[64,1024]{1,0:T(8,128)(2,1)S(1)}, u32[]{:S(2)}, u32[]{:S(2)}) collective-permute-start(bf16[64,1024]{1,0:T(8,128)(2,1)S(1)} %pad_maximum_fusion.4), channel_id=1, source_target_pairs={{0,8},{4,12},{8,0},{12,4},{16,24},{20,28},{24,16},{28,20},{1,9},{5... | collective-permute-start | bytes 393224 | tf_op jit(solution)/shard_map/ppermute | solution.py:451
  147.8 7.1 %collective-permute-start.15 = (bf16[64,1152]{1,0:T(8,128)(2,1)S(1)}, bf16[64,1152]{1,0:T(8,128)(2,1)S(1)}, u32[]{:S(2)}, u32[]{:S(2)}) collective-permute-start(bf16[64,1152]{1,0:T(8,128)(2,1)S(1)} %pad_maximum_fusion.3), channel_id=1, source_target_pairs={{0,24},{4,28},{8,16},{12,20},{16,8},{20,12},{24,0},{28,4},{1,25},{... | collective-permute-start | bytes 442376 | tf_op jit(solution)/shard_map/ppermute | solution.py:451
  149.8 9.9 %collective-permute-start.14 = (bf16[64,1152]{1,0:T(8,128)(2,1)S(1)}, bf16[64,1152]{1,0:T(8,128)(2,1)S(1)}, u32[]{:S(2)}, u32[]{:S(2)}) collective-permute-start(bf16[64,1152]{1,0:T(8,128)(2,1)S(1)} %pad_maximum_fusion.2), channel_id=1, source_target_pairs={{0,16},{4,20},{8,24},{12,28},{16,0},{20,4},{24,8},{28,12},{1,17},{... | collective-permute-start | bytes 442376 | tf_op jit(solution)/shard_map/ppermute | solution.py:451
  150.9 8.8 %collective-permute-start.13 = (bf16[64,1152]{1,0:T(8,128)(2,1)S(1)}, bf16[64,1152]{1,0:T(8,128)(2,1)S(1)}, u32[]{:S(2)}, u32[]{:S(2)}) collective-permute-start(bf16[64,1152]{1,0:T(8,128)(2,1)S(1)} %pad_maximum_fusion.1), channel_id=1, source_target_pairs={{0,8},{4,12},{8,0},{12,4},{16,24},{20,28},{24,16},{28,20},{1,9},{5... | collective-permute-start | bytes 442376 | tf_op jit(solution)/shard_map/ppermute | solution.py:451

commit v4 on v3

--- a/solution.py
+++ b/solution.py
@@ -53,19 +53,20 @@
             bytes_accessed=bank.shape[0] * emb * 2,
             transcendentals=rows * bank.shape[0],
         ),
-        compiler_params=pltpu.CompilerParams(vmem_limit_bytes=32 * 1024 * 1024),
+        compiler_params=params(),
         name="negatives",
     )(q, bank)
 
 
 TILE = 256
 STEP = 512
-VMEM_LIMIT = 48 * 1024 * 1024
-
-
-def params():
+MIB = 1024 * 1024
+SOON = pl.CostEstimate(flops=1, bytes_accessed=1, transcendentals=0)
+
+
+def params(limit=56):
     return pltpu.CompilerParams(
-        dimension_semantics=("arbitrary",), vmem_limit_bytes=VMEM_LIMIT
+        dimension_semantics=("arbitrary",), vmem_limit_bytes=limit * MIB
     )
 
 
@@ -356,92 +357,112 @@
         out_ref[i * size:(i + 1) * size, at] = value[j * size:(j + 1) * size].astype(out_ref.dtype)
 
 
-def send_kernel(plain, dz_ref, w2_ref, n_ref, inv_ref, xt_ref, at_ref, dh_ref, g_ref):
-    rows = dz_ref.shape[0]
+def column_tiles(cols):
+    plain = cols // 2
+    for start, end in ((0, plain), (plain, cols)):
+        for t in range(start, end, TILE):
+            yield slice(t, min(t + TILE, end)), start > 0
+
+
+def keep_rows(keep_ref, xt_ref, dh_ref, at_ref, dz_ref):
+    cols = dh_ref.shape[1]
+    for at, crossed in column_tiles(cols):
+        store_rows(keep_ref, at, dot(xt_ref[...], dh_ref[:, at]), crossed)
+    if at_ref is not None:
+        store_rows(keep_ref, slice(cols, None), dot(at_ref[...], dz_ref[...]), True)
+
+
+def send_kernel(has_old, has_at, count, *refs):
+    refs = list(refs)
+    dz_ref, xt_ref = refs[:2]
+    refs = refs[2:]
+    at_ref = refs.pop(0) if has_at else None
     dz = dz_ref[...]
-    xt = xt_ref[...]
-    cols = dh_ref.shape[1]
-    for t in range(0, cols, TILE):
-        normed = n_ref[:, t:t + TILE].astype(jnp.float32)
-        d_norm = jnp.where(normed > 0.0, dot_t(dz, w2_ref[t:t + TILE, :]), 0.0)
-        mean = jnp.sum(d_norm, axis=0, keepdims=True) / rows
-        slope = jnp.sum(d_norm * normed, axis=0, keepdims=True) / rows
-        d_hidden = inv_ref[:, t:t + TILE] * (d_norm - mean - normed * slope)
-        d_hidden = d_hidden.astype(jnp.bfloat16)
-        dh_ref[:, t:t + TILE] = d_hidden
-        store_rows(g_ref, slice(t, t + TILE), dot(xt, d_hidden), t >= plain)
-    if at_ref is not None:
-        store_rows(g_ref, slice(cols, None), dot(at_ref[...], dz), True)
-
-
-def send_half(dz, w2, normed, inv, xt, at, place, cols, plain):
+    rows = dz.shape[0]
+    if has_old:
+        old_xt_ref, old_ref = refs[:2]
+        refs = refs[2:]
+    ins, outs = refs[:3 * count], refs[3 * count:]
+    if has_old:
+        keep_rows(outs.pop(0), old_xt_ref, old_ref, None, None)
+    for p in range(count):
+        w2_ref, n_ref, inv_ref = ins[3 * p:3 * p + 3]
+        dh_ref, sent_ref = outs[2 * p:2 * p + 2]
+        cols = n_ref.shape[1]
+        for at, crossed in column_tiles(cols):
+            normed = n_ref[:, at].astype(jnp.float32)
+            d_norm = jnp.where(normed > 0.0, dot_t(dz, w2_ref[at, :]), 0.0)
+            mean = jnp.sum(d_norm, axis=0, keepdims=True) / rows
+            slope = jnp.sum(d_norm * normed, axis=0, keepdims=True) / rows
+            d_hidden = inv_ref[:, at] * (d_norm - mean - normed * slope)
+            d_hidden = d_hidden.astype(jnp.bfloat16)
+            dh_ref[:, at] = d_hidden
+            store_rows(sent_ref, at, dot(xt_ref[...], d_hidden), crossed)
+        if has_at and p == count - 1:
+            store_rows(sent_ref, slice(cols, None), dot(at_ref[...], dz), True)
+
+
+def send_half(dz, xt, at, old, w2, normed, inv, pairs):
     rows, emb = dz.shape
     half = xt.shape[0] // 2
-    extra = 0 if at is None else emb
-    operands = [dz, w2, normed, inv, xt]
-    in_specs = [
-        whole((rows, emb)),
-        pl.BlockSpec((cols, emb), lambda i: (place, 0)),
-        pl.BlockSpec((rows, cols), lambda i: (0, place)),
-        pl.BlockSpec((1, cols), lambda i: (0, place)),
-        pl.BlockSpec((half, rows), lambda i: (1, 0)),
-    ]
-    if at is None:
-        kernel = lambda a, b, c, d, e, f, g: send_kernel(plain, a, b, c, d, e, None, f, g)
-    else:
-        kernel = lambda *refs: send_kernel(plain, *refs)
+    operands, in_specs = [dz, xt], [whole(dz.shape), pl.BlockSpec((half, rows), lambda i: (1, 0))]
+    shapes = []
+    if at is not None:
         operands.append(at)
         in_specs.append(pl.BlockSpec((half, rows), lambda i: (1, 0)))
+    if old is not None:
+        operands += [xt, old]
+        in_specs += [whole((half, rows)), whole(old.shape)]
+        shapes.append(jax.ShapeDtypeStruct((half, old.shape[1]), jnp.float32))
+    for p, (place, cols) in enumerate(pairs):
+        operands += [w2, normed, inv]
+        in_specs += [
+            pl.BlockSpec((cols, emb), lambda i, place=place: (place, 0)),
+            pl.BlockSpec((rows, cols), lambda i, place=place: (0, place)),
+            pl.BlockSpec((1, cols), lambda i, place=place: (0, place)),
+        ]
+        extra = emb if at is not None and p == len(pairs) - 1 else 0
+        shapes.append(jax.ShapeDtypeStruct((rows, cols), jnp.bfloat16))
+        shapes.append(jax.ShapeDtypeStruct((half, cols + extra), jnp.bfloat16))
+    return pl.pallas_call(
+        lambda *refs: send_kernel(old is not None, at is not None, len(pairs), *refs),
+        grid=(1,),
+        in_specs=in_specs,
+        out_specs=[whole(shape.shape) for shape in shapes],
+        out_shape=shapes,
+        cost_estimate=pl.CostEstimate(
+            flops=2 * rows * half * sum(cols for _, cols in pairs),
+            bytes_accessed=8 * rows * half,
+            transcendentals=0,
+        ),
+        compiler_params=params(36),
+        name="send_half",
+    )(*operands)
+
+
+def keep_half(dz, dh, xt, at):
+    rows, emb = dz.shape
+    half = xt.shape[0] // 2
+    cols = dh.shape[1]
+    operands = [xt, dh]
+    in_specs = [whole((half, rows)), whole((rows, cols))]
+    if at is None:
+        kernel = lambda x, d, g: keep_rows(g, x, d, None, None)
+    else:
+        kernel = lambda x, d, a, z, g: keep_rows(g, x, d, a, z)
+        operands += [at, dz]
+        in_specs += [whole((half, rows)), whole((rows, emb))]
+        cols += emb
     return pl.pallas_call(
         kernel,
         grid=(1,),
         in_specs=in_specs,
-        out_specs=[whole((rows, cols)), whole((half, cols + extra))],
-        out_shape=[
-            jax.ShapeDtypeStruct((rows, cols), jnp.bfloat16),
-            jax.ShapeDtypeStruct((half, cols + extra), jnp.bfloat16),
-        ],
+        out_specs=whole((half, cols)),
+        out_shape=jax.ShapeDtypeStruct((half, cols), jnp.float32),
         cost_estimate=pl.CostEstimate(
             flops=2 * rows * half * cols, bytes_accessed=8 * rows * half, transcendentals=0
         ),
-        compiler_params=params(),
-        name="send_half",
-    )(*operands)
-
-
-def keep_kernel(plain, dz_ref, dh_ref, xt_ref, at_ref, g_ref):
-    xt = xt_ref[...]
-    cols = dh_ref.shape[1]
-    for t in range(0, cols, TILE):
-        g = dot(xt, dh_ref[:, t:t + TILE])
-        store_rows(g_ref, slice(t, t + TILE), g, t >= plain)
-    if at_ref is not None:
-        store_rows(g_ref, slice(cols, None), dot(at_ref[...], dz_ref[...]), True)
-
-
-def keep_half(dz, dh, xt, at, plain):
-    rows, emb = dz.shape
-    half = xt.shape[0] // 2
-    cols = dh.shape[1]
-    extra = 0 if at is None else emb
-    operands = [dz, dh, xt]
-    in_specs = [whole((rows, emb)), whole((rows, cols)), whole((half, rows))]
-    if at is None:
-        kernel = lambda a, b, c, d: keep_kernel(plain, a, b, c, None, d)
-    else:
-        kernel = lambda *refs: keep_kernel(plain, *refs)
-        operands.append(at)
-        in_specs.append(whole((half, rows)))
-    return pl.pallas_call(
-        kernel,
-        grid=(1,),
-        in_specs=in_specs,
-        out_specs=whole((half, cols + extra)),
-        out_shape=jax.ShapeDtypeStruct((half, cols + extra), jnp.float32),
-        cost_estimate=pl.CostEstimate(
-            flops=2 * rows * half * cols, bytes_accessed=8 * rows * half, transcendentals=0
-        ),
-        compiler_params=params(),
+        compiler_params=params(28),
         name="keep_half",
     )(*operands)
 
@@ -451,44 +472,93 @@
     return lax.ppermute(x, axis, [(i, i ^ bit) for i in range(size)])
 
 
-def total(parts, rows, cols):
-    parts = [p[rows, cols].astype(jnp.float32) for p in parts]
-    out = parts[0]
-    for p in parts[1:]:
-        out = out + p
-    return out
-
-
-def scatter_pair(keep, sent, split):
-    n_dp = lax.axis_size("dp")
-    length = n_dp // 2
-    half = keep.shape[0]
-    quarter, eighth = half // 2, half // 4
-    rows = eighth // length
-    every = slice(None)
-    came = swap(sent, "crop", 1)
-    sides = []
-    for side, (first, second) in enumerate(
-        ((("dp", 1), ("crop", 2)), (("crop", 2), ("dp", 1)))
-    ):
-        cols = slice(0, split) if side == 0 else slice(split, None)
-        held = [keep[:, cols], came[:, cols]]
-        out = total(held, slice(quarter, half), every).astype(jnp.bfloat16)
-        held.append(swap(out, *first))
-        out = total(held, slice(eighth, quarter), every).astype(jnp.bfloat16)
-        held.append(swap(out, *second))
-        sides.append(held)
-    own = jnp.concatenate([total(held, slice(0, rows), every) for held in sides], axis=1)
-    for k in range(1, length):
-        out = jnp.concatenate(
-            [
-                total(held, slice(k * rows, (k + 1) * rows), every).astype(jnp.bfloat16)
-                for held in sides
-            ],
-            axis=1,
-        )
-        own = own + swap(out, "dp", 2 * k).astype(jnp.float32)
-    return own
+def after(x, *others):
+    return lax.optimization_barrier((x,) + others)[0]
+
+
+def fold_kernel(split, joined, *refs):
+    keep_ref, came_ref = refs[:2]
+    count = len(refs) - 4
+    sides = (refs[2:2 + count // 2], refs[2 + count // 2:2 + count])
+    outs = refs[-2:]
+    for side, cols in enumerate((slice(0, split), slice(split, keep_ref.shape[1]))):
+        v = keep_ref[:, cols] + came_ref[:, cols].astype(jnp.float32)
+        for ref in sides[side]:
+            v = v + ref[...].astype(jnp.float32)
+        if joined:
+            half = v.shape[0] // 2
+            outs[0][:, cols] = v[:half]
+            outs[1][:, cols] = v[half:].astype(jnp.bfloat16)
+        else:
+            outs[side][...] = v.astype(jnp.bfloat16)
+
+
+def fold(keep, came, left, right, split, rows, place, joined):
+    cols = keep.shape[1]
+
+    def spec(width):
+        return pl.BlockSpec((rows, width), lambda i: (place, 0))
+
+    if joined:
+        shapes = [
+            jax.ShapeDtypeStruct((rows // 2, cols), jnp.float32),
+            jax.ShapeDtypeStruct((rows // 2, cols), jnp.bfloat16),
+        ]
+    else:
+        shapes = [
+            jax.ShapeDtypeStruct((rows, split), jnp.bfloat16),
+            jax.ShapeDtypeStruct((rows, cols - split), jnp.bfloat16),
+        ]
+    return pl.pallas_call(
+        lambda *refs: fold_kernel(split, joined, *refs),
+        grid=(1,),
+        in_specs=[spec(cols)] * 2 + [spec(split)] * len(left) + [spec(cols - split)] * len(right),
+        out_specs=[whole(shape.shape) for shape in shapes],
+        out_shape=shapes,
+        cost_estimate=SOON,
+        compiler_params=params(16),
+        name="fold",
+    )(keep, came, *left, *right)
+
+
+class Pair:
+    def __init__(self, keep, came, split):
+        self.keep, self.came, self.split = keep, came, split
+        self.left, self.right = [], []
+        self.half = keep.shape[0]
+
+    def first(self):
+        rows = self.half // 2
+        out = fold(self.keep, self.came, [], [], self.split, rows, 1, False)
+        return out
+
+    def cross_first(self, out):
+        self.left.append(swap(out[0], "dp", 1))
+        self.right.append(swap(out[1], "crop", 2))
+
+    def second(self):
+        rows = self.half // 4
+        return fold(self.keep, self.came, self.left, self.right, self.split, rows, 1, False)
+
+    def cross_second(self, out):
+        self.left.append(swap(out[0], "crop", 2))
+        self.right.append(swap(out[1], "dp", 1))
+
+    def third(self):
+        rows = self.half // 4
+        return fold(self.keep, self.came, self.left, self.right, self.split, rows, 0, True)
+
+    def cross_third(self, out):
+        own, send = out
+        length = lax.axis_size("dp") // 2
+        bit = 1
+        own = own + swap(send, "dp", 2 * bit).astype(jnp.float32)
+        while 2 * bit < length:
+            bit *= 2
+            half = own.shape[0] // 2
+            own, send = own[:half], own[half:].astype(jnp.bfloat16)
+            own = own + swap(send, "dp", 2 * bit).astype(jnp.float32)
+        return own
 
 
 def per_device(
@@ -509,38 +579,70 @@
     hidden_k, sums = key_hidden(flat_col, key_crops, key_inner, group_count)
     came = lax.all_to_all(sums, AXES, split_axis=0, concat_axis=0, tiled=True)
 
-    normed, inv_q, z_q, q_low = query_forward(query_crops, query_inner, query_outer)
-    came, q_low, flat_row = lax.optimization_barrier((came, q_low, flat_row))
-    told = batch(came, row_count)
-    told = lax.all_to_all(told, AXES, split_axis=0, concat_axis=0, tiled=True)
-
-    negs = negatives(q_low, distractor_bank)
-
     length = n_dp // 2
+    bits = length.bit_length() - 1
     dp, crop = lax.axis_index("dp"), lax.axis_index("crop")
     block = lax.iota(jnp.int32, group_count // 2)
     z, x, y = block // n_crop, (block // (n_crop // 2)) % 2, block % (n_crop // 2)
-    order = ((x ^ (dp % 2)) * (n_crop // 2) + (y ^ (crop // 2))) * length + (z ^ (dp // 2))
+    order = (x ^ (dp % 2)) * (n_crop // 2) + (y ^ (crop // 2))
+    for bit in range(bits):
+        order = order * 2 + (((z ^ (dp // 2)) >> bit) & 1)
     core = crop % 2
+
+    normed, inv_q, z_q, q_low = query_forward(
+        after(query_crops, sums), query_inner, query_outer
+    )
     xt = ordered(query_crops, order, core, group_count, False)
+    came, q_low, flat_row, xt = lax.optimization_barrier((came, q_low, flat_row, xt))
+    told = batch(came, row_count)
+    told = lax.all_to_all(told, AXES, split_axis=0, concat_axis=0, tiled=True)
+
+    negs = negatives(q_low, distractor_bank)
     at = ordered(normed, order, core, group_count, True)
 
-    told, negs, xt, at = lax.optimization_barrier((told, negs, xt, at))
+    told, negs, at = lax.optimization_barrier((told, negs, at))
     d_z = embed(flat_row, hidden_k, told, key_outer, z_q, negs, all_rows)
 
-    outs, made = [], []
-    parts = 2
-    cols = hid // parts
-    plain = cols // (2 * TILE) * TILE
-    for i in range(parts):
-        last = at if i == parts - 1 else None
-        dh, sent = send_half(d_z, query_outer, normed, inv_q, xt, last, i, cols, plain)
-        made.append((dh, sent, last))
-    for dh, sent, last in made:
-        keep = keep_half(d_z, dh, xt, last, plain)
-        outs.append(scatter_pair(keep, sent, plain))
-    grad = jnp.concatenate(outs, axis=1)
-    return (grad[:, :hid], grad[:, hid:])
+    def send(last, old, pairs):
+        return send_half(d_z, xt, last, old, query_outer, normed, inv_q, pairs)
+
+    large = hid // 8 * 3
+    small = hid - 2 * large
+    dh_1, sent_1 = send(None, None, [(0, large)])
+    came_1 = swap(sent_1, "crop", 1)
+    keep_1, dh_2, sent_2, dh_3, sent_3 = send(
+        at, dh_1, [(1, large), (2 * large // small, small)]
+    )
+    came_2 = swap(sent_2, "crop", 1)
+    came_3 = swap(sent_3, "crop", 1)
+    one = Pair(keep_1, came_1, large // 2)
+    a_1 = lax.optimization_barrier(one.first())
+    one.cross_first(a_1)
+    keep_2 = keep_half(d_z, after(dh_2, *a_1), xt, None)
+    two = Pair(keep_2, came_2, large // 2)
+    a_2 = lax.optimization_barrier(two.first())
+    two.cross_first(a_2)
+    keep_3 = keep_half(d_z, after(dh_3, *a_2), xt, at)
+    one.left[0] = after(one.left[0], keep_3)
+    b_1 = lax.optimization_barrier(one.second())
+    one.cross_second(b_1)
+    three = Pair(keep_3, after(came_3, *b_1), small // 2)
+    a_3 = lax.optimization_barrier(three.first())
+    three.cross_first(a_3)
+    two.left[0] = after(two.left[0], *a_3)
+    b_2 = lax.optimization_barrier(two.second())
+    two.cross_second(b_2)
+    one.left[1] = after(one.left[1], *b_2)
+    c_1 = lax.optimization_barrier(one.third())
+    three.left[0] = after(three.left[0], *c_1)
+    b_3 = lax.optimization_barrier(three.second())
+    three.cross_second(b_3)
+    own_1 = one.cross_third(c_1)
+    two.left[1] = after(two.left[1], *b_3)
+    own_2 = two.cross_third(two.third())
+    own_3 = three.cross_third(three.third())
+    grad_inner = jnp.concatenate([own_1, own_2, own_3[:, :small]], axis=1)
+    return (grad_inner, own_3[:, small:])
 
 
 def solution(mesh):

time: 162 us -> 163 us (level)
  Pallas kernels: 56.3 us -> 74.4 us
  waiting for transfers between devices: 41.7 us -> 32 us
  local copies, waits for them, and re-layouts: 14.8 us -> 5.25 us
  starting transfers between devices: 25.3 us -> 32.6 us
  other arithmetic: 7.89 us -> 2.97 us
    pallas_call x2, Pallas kernels: 5.91 us -> 21.2 us  [ordered(): pl.pallas_call(lambda *refs: order_kernel(positive, *refs), grid_spec=plt...]
    unnamed x36 -> x16, local copies, waits for them, and re-layouts: 12.6 us -> 2.5 us
    ppermute x16 -> x21, waiting for transfers between devices: 37.6 us -> 32 us  [swap(): return lax.ppermute(x, axis, [(i, i ^ bit) for i in range(size)])]
    convert_element_type x10 -> x0, other arithmetic: 5.41 us -> none  [the longest x3 4.37 us: scatter_pair(): out = total(held, slice(quarter, half), every).astype(jnp.bfloat16)]
    pallas_call x2, Pallas kernels: 6.96 us -> 2.23 us  [keep_half(): pl.pallas_call(kernel, grid=(1,), in_specs=in_specs, out_specs=whole((hal...]
    ppermute x16 -> x21, starting transfers between devices: 19.8 us -> 24.1 us  [swap(): return lax.ppermute(x, axis, [(i, i ^ bit) for i in range(size)])]
    all_to_all x1, waiting for transfers between devices: 4.07 us -> 0.01 us  [per_device(): came = lax.all_to_all(sums, AXES, split_axis=0, concat_axis=0, tiled=True)]
    pallas_call x1, Pallas kernels: 2.78 us -> 6.03 us  [embed(): pl.pallas_call(lambda *refs: embed_kernel(all_rows, *refs), grid=(hid //...]
  transfers between devices with their start and end apart: 18 -> 23, of which waited for: 9 -> 14; matrix products, arithmetic and copies ran while one was open for 4% -> 1% of each run, Pallas kernels for 24% -> 33%
where the time goes in v4:
time: 163 us; the launch traced here: 162 us
  Pallas kernels  74.4 us (46%)
  starting transfers between devices  32.6 us (20%)
  waiting for transfers between devices  32 us (20%)
  blocking collectives  14.2 us (9%)
  local copies, waits for them, and re-layouts  5.25 us (3%)
  other arithmetic  2.97 us (2%)
    ppermute x21, waiting for transfers between devices, swap(): return lax.ppermute(x, axis, [(i, i ^ bit) for i in range(size)])  32 us
    ppermute x21, starting transfers between devices, swap(): return lax.ppermute(x, axis, [(i, i ^ bit) for i in range(size)])  24.1 us
    pallas_call x2, Pallas kernels, ordered(): pl.pallas_call(lambda *refs: order_kernel(positive, *refs), grid_spec=plt...  21.2 us
    all_to_all x1, blocking collectives, per_device(): lax.all_to_all(wanted, AXES, split_axis=0, concat_axis=0, tiled=True)  14.2 us
    pallas_call x1, Pallas kernels, negatives(): pl.pallas_call(neg_kernel, grid=(bank.shape[0] // tile,), in_specs=[pl.Bl...  12.9 us
    pallas_call x1, Pallas kernels, query_forward(): pl.pallas_call(query_kernel, grid=(hid // STEP,), in_specs=[whole((rows,...  11.2 us
    pallas_call x1, Pallas kernels, key_hidden(): pl.pallas_call(lambda *refs: key_hidden_kernel(groups, *refs), grid=(hid...  10.9 us
    pallas_call x2, Pallas kernels, send_half(): pl.pallas_call(lambda *refs: send_kernel(old is not None, at is not None,...  6.64 us
  transfers between devices with their start and end apart: 23, of which 14 were waited for; matrix products, arithmetic and copies ran while one was open for 1% of the time, Pallas kernels for 33%

profile of v4, /device:TPU:0, one launch (start us, length us, event | category | flops | bytes accessed | tf_op | source)
XLA Modules:
  0.0 162.3 jit_solution(12754331938656261764)
XLA Ops:
  0.6 0.7 add_select_fusion
  1.4 14.2 %all_to_all.19 = s32[32,1,16]{2,1,0:T(1,128)S(1)} all-to-all(s32[32,1,16]{2,1,0:T(1,128)S(1)} %bitcast.13), channel_id=1, replica_groups=mesh['dp'=8,'crop'=4] {'dp','crop'}, dimensions={0} | all-to-all | bytes 4096 | tf_op jit(solution)/shard_map/all_to_all | solution.py:575
  16.2 0.7 reduce.5
  16.9 0.9 broadcast_in_dim_reshape.8.refs_0_
  17.7 10.9 %key_hidden.1 = (f32[512,2048]{1,0:T(8,128)}, f32[32,1,4096]{2,1,0:T(1,128)}) custom-call(s32[512,1]{1,0:T(8,128)} %broadcast_in_dim_reshape.8.refs_0_, bf16[512,2048]{1,0:T(8,128)(2,1)} %refs_1_.2, bf16[2048,2048]{1,0:T(8,128)(2,1)} %refs_2_.2), custom_call_target="tpu_custom_call" | custom-call | flops 5368709120 | bytes 8388608 | tf_op jit(solution)/shard_map/key_hidden/pallas_call | solution.py:141
  28.6 2.6 %all-to-all-start.1 = ((f32[32,1,4096]{2,1,0:T(1,128)}), f32[32,1,4096]{2,1,0:T(1,128)S(1)}, u32[]{:S(2)}, u32[]{:S(2)}) async-start(f32[32,1,4096]{2,1,0:T(1,128)} %get-tuple-element.49), calls=%async_computation.1 | async-start | bytes 1048576 | tf_op jit(solution)/shard_map/all_to_all | solution.py:580
  31.9 10.6 %ordered.2 = bf16[2,16,64,512]{3,2,1,0:T(8,128)(2,1)} custom-call(s32[17]{0:T(128)} %pad_add_fusion.refs_0_, bf16[512,2048]{1,0:T(8,128)(2,1)} %refs_1_.3), custom_call_target="tpu_custom_call" | custom-call | bytes 8388608 | tf_op jit(solution)/shard_map/ordered/pallas_call | solution.py:269
  42.5 0.6 broadcast_in_dim_reshape.7.refs_0_
  43.1 11.2 %query_forward.1 = (bf16[512,2048]{1,0:T(8,128)(2,1)}, f32[1,2048]{1,0:T(1,128)}, f32[512,128]{1,0:T(8,128)}, bf16[512,128]{1,0:T(8,128)(2,1)}) custom-call(bf16[512,2048]{1,0:T(8,128)(2,1)} %refs_1_.3, bf16[2048,2048]{1,0:T(8,128)(2,1)} %w_ref.1, bf16[2048,128]{1,0:T(8,128)(2,1)} %refs_8_.1), custom_call_target="tpu_custom_call" | custom-call | flops 4563402752 | bytes 8388608 | tf_op jit(solution)/shard_map/query_forward/pallas_call | solution.py:220
  54.3 0.8 copy-done.6
  55.1 2.1 %batch.1 = f32[32,1,4096]{2,1,0:T(1,128)} custom-call(f32[32,1,4096]{2,1,0:T(1,128)} %copy-done.6), custom_call_target="tpu_custom_call" | custom-call | tf_op jit(solution)/shard_map/batch/pallas_call | solution.py:177
  57.2 5.8 %all-to-all-start.2 = ((f32[32,1,4096]{2,1,0:T(1,128)}), f32[32,1,4096]{2,1,0:T(1,128)S(1)}, u32[]{:S(2)}, u32[]{:S(2)}) async-start(f32[32,1,4096]{2,1,0:T(1,128)} %batch.1), calls=%async_computation.2 | async-start | bytes 1048576 | tf_op jit(solution)/shard_map/all_to_all | solution.py:598
  63.0 10.6 %ordered.3 = bf16[2,16,64,512]{3,2,1,0:T(8,128)(2,1)} custom-call(s32[17]{0:T(128)} %pad_add_fusion.refs_0_, bf16[512,2048]{1,0:T(8,128)(2,1)} %get-tuple-element.56.refs_1_.refs_3_.refs_6_.refs_9_), custom_call_target="tpu_custom_call" | custom-call | bytes 8388608 | tf_op jit(solution)/shard_map/ordered/pallas_call | solution.py:269
  73.6 12.9 %negatives.1.refs_5_ = f32[512,256]{1,0:T(8,128)} custom-call(bf16[512,128]{1,0:T(8,128)(2,1)} %get-tuple-element.55.q_ref, bf16[16384,128]{1,0:T(8,128)(2,1)} %bank_ref.1), custom_call_target="tpu_custom_call" | custom-call | flops 4294967296 | bytes 4194304 | tf_op jit(solution)/shard_map/negatives/pallas_call | solution.py:42
  86.5 0.8 copy-done.7
  87.3 6.0 %embed.1.refs_0_.z = bf16[512,128]{1,0:T(8,128)(2,1)} custom-call(s32[1,512]{1,0:T(1,128)} %broadcast_in_dim_reshape.7.refs_0_, f32[512,2048]{1,0:T(8,128)} %get-tuple-element.53.refs_1_, f32[32,1,4096]{2,1,0:T(1,128)} %copy-done.7, bf16[2048,128]{1,0:T(8,128)(2,1)} %refs_3_.1, f32[512,128]{1,0:T(8,128)} %get-tuple-element.58.refs_4_, ...), custom_call_target="tpu_custom_call" | custom-call | flops 268435456 | bytes 4194304 | tf_op jit(solution)/shard_map/embed/pallas_call | solution.py:331
  93.4 0.9 copy-done.4
  94.3 2.1 %send_half.2 = (bf16[512,768]{1,0:T(8,128)(2,1)S(1)}, bf16[1024,768]{1,0:T(8,128)(2,1)S(1)}) custom-call(bf16[512,128]{1,0:T(8,128)(2,1)S(1)} %copy-done.4, bf16[2048,512]{1,0:T(8,128)(2,1)S(1)} %bitcast.5, bf16[2048,128]{1,0:T(8,128)(2,1)S(1)} %copy-done.3, bf16[512,2048]{1,0:T(8,128)(2,1)S(1)} %copy-done.1, f32[1,2048]{1,0:T(1,128)S(1)} %copy-done.5), custom_call_target="tpu_custom_call" | custom-call | flops 805306368 | bytes 4194304 | tf_op jit(solution)/shard_map/send_half/pallas_call | solution.py:427
  96.8 4.5 %send_half.3 = (f32[1024,768]{1,0:T(8,128)S(1)}, bf16[512,768]{1,0:T(8,128)(2,1)S(1)}, bf16[1024,768]{1,0:T(8,128)(2,1)S(1)}, bf16[512,512]{1,0:T(8,128)(2,1)S(1)}, bf16[1024,640]{1,0:T(8,128)(2,1)S(1)}) custom-call(bf16[512,128]{1,0:T(8,128)(2,1)S(1)} %copy-done.4, bf16[2048,512]{1,0:T(8,128)(2,1)S(1)} %bitcast.6, bf16[2048,512]{1,0:T(8,128)(2,1)S(1)} %bitcast.10, ...), custom_call_target="tpu_custom_call" | custom-call | flops 1342177280 | bytes 4194304 | tf_op jit(solution)/shard_map/send_half/pallas_call | solution.py:427
  102.0 1.7 %collective-permute-start.1 = (bf16[512,384]{1,0:T(8,128)(2,1)S(1)}, bf16[512,384]{1,0:T(8,128)(2,1)S(1)}, u32[]{:S(2)}, u32[]{:S(2)}) collective-permute-start(bf16[512,384]{1,0:T(8,128)(2,1)S(1)} %get-tuple-element.66), channel_id=1, source_target_pairs={{0,4},{4,0},{8,12},{12,8},{16,20},{20,16},{24,28},{28,24},{1,5},{5... | collective-permute-start | bytes 1179656 | tf_op jit(solution)/shard_map/ppermute | solution.py:472
  103.7 1.5 collective-permute-start.3
  105.2 1.2 keep_half.2.refs_0_
  106.6 0.6 collective-permute-start.5
  107.3 0.9 collective-permute-start.7
  108.1 1.0 keep_half.3.refs_0_
  109.1 4.9 %collective-permute-done.1.refs_2_ = bf16[512,384]{1,0:T(8,128)(2,1)S(1)} collective-permute-done((bf16[512,384]{1,0:T(8,128)(2,1)S(1)}, bf16[512,384]{1,0:T(8,128)(2,1)S(1)}, u32[]{:S(2)}, u32[]{:S(2)}) %collective-permute-start.1) | collective-permute-done | bytes 393248 | tf_op jit(solution)/shard_map/ppermute | solution.py:472
  114.0 1.7 %collective-permute-done.3.refs_3_.refs_4_ = bf16[512,384]{1,0:T(8,128)(2,1)S(1)} collective-permute-done((bf16[512,384]{1,0:T(8,128)(2,1)S(1)}, bf16[512,384]{1,0:T(8,128)(2,1)S(1)}, u32[]{:S(2)}, u32[]{:S(2)}) %collective-permute-start.3) | collective-permute-done | bytes 393248 | tf_op jit(solution)/shard_map/ppermute | solution.py:472
  115.8 1.5 collective-permute-start.4
  118.1 4.4 %collective-permute-done.5.refs_2_ = bf16[512,384]{1,0:T(8,128)(2,1)S(1)} collective-permute-done((bf16[512,384]{1,0:T(8,128)(2,1)S(1)}, bf16[512,384]{1,0:T(8,128)(2,1)S(1)}, u32[]{:S(2)}, u32[]{:S(2)}) %collective-permute-start.5) | collective-permute-done | bytes 393248 | tf_op jit(solution)/shard_map/ppermute | solution.py:472
  122.4 1.7 %collective-permute-done.7.refs_3_.refs_4_ = bf16[512,384]{1,0:T(8,128)(2,1)S(1)} collective-permute-done((bf16[512,384]{1,0:T(8,128)(2,1)S(1)}, bf16[512,384]{1,0:T(8,128)(2,1)S(1)}, u32[]{:S(2)}, u32[]{:S(2)}) %collective-permute-start.7) | collective-permute-done | bytes 393248 | tf_op jit(solution)/shard_map/ppermute | solution.py:472
  124.3 3.2 %collective-permute-done.4.refs_3_ = bf16[256,384]{1,0:T(8,128)(2,1)S(1)} collective-permute-done((bf16[256,384]{1,0:T(8,128)(2,1)S(1)}, bf16[256,384]{1,0:T(8,128)(2,1)S(1)}, u32[]{:S(2)}, u32[]{:S(2)}) %collective-permute-start.4) | collective-permute-done | bytes 196640 | tf_op jit(solution)/shard_map/ppermute | solution.py:472
  127.6 1.5 collective-permute-start.9
  129.2 1.5 collective-permute-start.13
  131.8 1.5 collective-permute-start.14
  133.8 2.4 %collective-permute-start.10 = (bf16[64,768]{1,0:T(8,128)(2,1)S(1)}, bf16[64,768]{1,0:T(8,128)(2,1)S(1)}, u32[]{:S(2)}, u32[]{:S(2)}) collective-permute-start(bf16[64,768]{1,0:T(8,128)(2,1)S(1)} %slice.50), channel_id=1, source_target_pairs={{0,16},{4,20},{8,24},{12,28},{16,0},{20,4},{24,8},{28,12},{1,17},{... | collective-permute-start | bytes 294920 | tf_op jit(solution)/shard_map/ppermute | solution.py:472
  136.3 3.4 %collective-permute-done.12.refs_2_ = bf16[512,256]{1,0:T(8,128)(2,1)S(1)} collective-permute-done((bf16[512,256]{1,0:T(8,128)(2,1)S(1)}, bf16[512,256]{1,0:T(8,128)(2,1)S(1)}, u32[]{:S(2)}, u32[]{:S(2)}) %collective-permute-start.12) | collective-permute-done | bytes 262176 | tf_op jit(solution)/shard_map/ppermute | solution.py:472
  139.6 1.6 collective-permute-done.13.refs_3_.refs_4_
  141.3 1.5 collective-permute-start.17
  143.4 1.3 collective-permute-done.11.refs_3_
  145.6 0.8 collective-permute-done.17.refs_3_
  146.4 2.2 %collective-permute-done.18.refs_5_ = bf16[256,384]{1,0:T(8,128)(2,1)S(1)} collective-permute-done((bf16[256,384]{1,0:T(8,128)(2,1)S(1)}, bf16[256,384]{1,0:T(8,128)(2,1)S(1)}, u32[]{:S(2)}, u32[]{:S(2)}) %collective-permute-start.18) | collective-permute-done | bytes 196640 | tf_op jit(solution)/shard_map/ppermute | solution.py:472
  148.7 0.6 collective-permute-start.19
  149.3 2.6 %collective-permute-done.15 = bf16[128,768]{1,0:T(8,128)(2,1)S(1)} collective-permute-done((bf16[128,768]{1,0:T(8,128)(2,1)S(1)}, bf16[128,768]{1,0:T(8,128)(2,1)S(1)}, u32[]{:S(2)}, u32[]{:S(2)}) %collective-permute-start.15) | collective-permute-done | bytes 196640 | tf_op jit(solution)/shard_map/ppermute | solution.py:472
  152.0 3.4 %collective-permute-start.16 = (bf16[64,768]{1,0:T(8,128)(2,1)S(1)}, bf16[64,768]{1,0:T(8,128)(2,1)S(1)}, u32[]{:S(2)}, u32[]{:S(2)}) collective-permute-start(bf16[64,768]{1,0:T(8,128)(2,1)S(1)} %slice.49), channel_id=1, source_target_pairs={{0,16},{4,20},{8,24},{12,28},{16,0},{20,4},{24,8},{28,12},{1,17},{... | collective-permute-start | bytes 294920 | tf_op jit(solution)/shard_map/ppermute | solution.py:472
  155.4 1.7 %collective-permute-start.20 = (bf16[64,640]{1,0:T(8,128)(2,1)S(1)}, bf16[64,640]{1,0:T(8,128)(2,1)S(1)}, u32[]{:S(2)}, u32[]{:S(2)}) collective-permute-start(bf16[64,640]{1,0:T(8,128)(2,1)S(1)} %slice.51), channel_id=1, source_target_pairs={{0,16},{4,20},{8,24},{12,28},{16,0},{20,4},{24,8},{28,12},{1,17},{... | collective-permute-start | bytes 245768 | tf_op jit(solution)/shard_map/ppermute | solution.py:472
  157.1 1.4 collective-permute-done.16
  158.6 2.3 %collective-permute-done.20 = bf16[64,640]{1,0:T(8,128)(2,1)S(1)} collective-permute-done((bf16[64,640]{1,0:T(8,128)(2,1)S(1)}, bf16[64,640]{1,0:T(8,128)(2,1)S(1)}, u32[]{:S(2)}, u32[]{:S(2)}) %collective-permute-start.20) | collective-permute-done | bytes 81952 | tf_op jit(solution)/shard_map/ppermute | solution.py:472
  161.5 0.8 pad_maximum_fusion
  (55 shorter events, 7.6 us)
Async XLA Ops:
  28.6 25.7 %all-to-all-start.1 = ((f32[32,1,4096]{2,1,0:T(1,128)}), f32[32,1,4096]{2,1,0:T(1,128)S(1)}, u32[]{:S(2)}, u32[]{:S(2)}) async-start(f32[32,1,4096]{2,1,0:T(1,128)} %get-tuple-element.49), calls=%async_computation.1 | async-start | bytes 1048576 | tf_op jit(solution)/shard_map/all_to_all | solution.py:580
  54.3 0.8 copy-start.6
  57.2 29.3 %all-to-all-start.2 = ((f32[32,1,4096]{2,1,0:T(1,128)}), f32[32,1,4096]{2,1,0:T(1,128)S(1)}, u32[]{:S(2)}, u32[]{:S(2)}) async-start(f32[32,1,4096]{2,1,0:T(1,128)} %batch.1), calls=%async_computation.2 | async-start | bytes 1048576 | tf_op jit(solution)/shard_map/all_to_all | solution.py:598
  86.5 0.8 copy-start.7
  87.3 6.0 %copy-start = (bf16[2,16,64,512]{3,2,1,0:T(8,128)(2,1)S(1)}, bf16[2,16,64,512]{3,2,1,0:T(8,128)(2,1)}, u32[]{:S(2)}) copy-start(bf16[2,16,64,512]{3,2,1,0:T(8,128)(2,1)} %ordered.2) | copy-start | bytes 6291460
  87.3 6.0 %copy-start.1 = (bf16[512,2048]{1,0:T(8,128)(2,1)S(1)}, bf16[512,2048]{1,0:T(8,128)(2,1)}, u32[]{:S(2)}) copy-start(bf16[512,2048]{1,0:T(8,128)(2,1)} %get-tuple-element.56.refs_1_.refs_3_.refs_6_.refs_9_) | copy-start | bytes 6291460
  87.3 6.0 %copy-start.3 = (bf16[2048,128]{1,0:T(8,128)(2,1)S(1)}, bf16[2048,128]{1,0:T(8,128)(2,1)}, u32[]{:S(2)}) copy-start(bf16[2048,128]{1,0:T(8,128)(2,1)} %refs_8_.1) | copy-start | bytes 1572868
  87.3 6.1 %copy-start.5 = (f32[1,2048]{1,0:T(1,128)S(1)}, f32[1,2048]{1,0:T(1,128)}, u32[]{:S(2)}) copy-start(f32[1,2048]{1,0:T(1,128)} %get-tuple-element.62.refs_4_.refs_7_.refs_10_) | copy-start | bytes 24580
  93.4 0.9 copy-start.4
  94.3 2.5 %copy-start.2 = (bf16[2,16,64,512]{3,2,1,0:T(8,128)(2,1)S(1)}, bf16[2,16,64,512]{3,2,1,0:T(8,128)(2,1)}, u32[]{:S(2)}) copy-start(bf16[2,16,64,512]{3,2,1,0:T(8,128)(2,1)} %ordered.3) | copy-start | bytes 6291460
  96.4 5.4 %collective-permute-start = (bf16[1024,768]{1,0:T(8,128)(2,1)S(1)}, bf16[1024,768]{1,0:T(8,128)(2,1)S(1)}, u32[]{:S(2)}, u32[]{:S(2)}) collective-permute-start(bf16[1024,768]{1,0:T(8,128)(2,1)S(1)} %get-tuple-element.65), channel_id=1, source_target_pairs={{0,1},{1,0},{2,3},{3,2},{4,5},{5,4},{6,7},{7,6},{8,9},{9,8},{10,11... | collective-permute-start | bytes 4718600 | tf_op jit(solution)/shard_map/ppermute | solution.py:472
  101.3 5.2 %collective-permute-start.2 = (bf16[1024,768]{1,0:T(8,128)(2,1)S(1)}, bf16[1024,768]{1,0:T(8,128)(2,1)S(1)}, u32[]{:S(2)}, u32[]{:S(2)}) collective-permute-start(bf16[1024,768]{1,0:T(8,128)(2,1)S(1)} %get-tuple-element.71), channel_id=1, source_target_pairs={{0,1},{1,0},{2,3},{3,2},{4,5},{5,4},{6,7},{7,6},{8,9},{9,8},{10,11... | collective-permute-start | bytes 4718600 | tf_op jit(solution)/shard_map/ppermute | solution.py:472
  101.6 16.3 %collective-permute-start.6 = (bf16[1024,640]{1,0:T(8,128)(2,1)S(1)}, bf16[1024,640]{1,0:T(8,128)(2,1)S(1)}, u32[]{:S(2)}, u32[]{:S(2)}) collective-permute-start(bf16[1024,640]{1,0:T(8,128)(2,1)S(1)} %get-tuple-element.77), channel_id=1, source_target_pairs={{0,1},{1,0},{2,3},{3,2},{4,5},{5,4},{6,7},{7,6},{8,9},{9,8},{10,11... | collective-permute-start | bytes 3932168 | tf_op jit(solution)/shard_map/ppermute | solution.py:472
  102.0 12.0 %collective-permute-start.1 = (bf16[512,384]{1,0:T(8,128)(2,1)S(1)}, bf16[512,384]{1,0:T(8,128)(2,1)S(1)}, u32[]{:S(2)}, u32[]{:S(2)}) collective-permute-start(bf16[512,384]{1,0:T(8,128)(2,1)S(1)} %get-tuple-element.66), channel_id=1, source_target_pairs={{0,4},{4,0},{8,12},{12,8},{16,20},{20,16},{24,28},{28,24},{1,5},{5... | collective-permute-start | bytes 1179656 | tf_op jit(solution)/shard_map/ppermute | solution.py:472
  103.7 12.0 %collective-permute-start.3 = (bf16[512,384]{1,0:T(8,128)(2,1)S(1)}, bf16[512,384]{1,0:T(8,128)(2,1)S(1)}, u32[]{:S(2)}, u32[]{:S(2)}) collective-permute-start(bf16[512,384]{1,0:T(8,128)(2,1)S(1)} %get-tuple-element.69), channel_id=1, source_target_pairs={{0,2},{1,3},{2,0},{3,1},{4,6},{5,7},{6,4},{7,5},{8,10},{9,11},{10,... | collective-permute-start | bytes 1179656 | tf_op jit(solution)/shard_map/ppermute | solution.py:472
  106.6 15.8 %collective-permute-start.5 = (bf16[512,384]{1,0:T(8,128)(2,1)S(1)}, bf16[512,384]{1,0:T(8,128)(2,1)S(1)}, u32[]{:S(2)}, u32[]{:S(2)}) collective-permute-start(bf16[512,384]{1,0:T(8,128)(2,1)S(1)} %get-tuple-element.72), channel_id=1, source_target_pairs={{0,4},{4,0},{8,12},{12,8},{16,20},{20,16},{24,28},{28,24},{1,5},{5... | collective-permute-start | bytes 1179656 | tf_op jit(solution)/shard_map/ppermute | solution.py:472
  107.3 16.9 %collective-permute-start.7 = (bf16[512,384]{1,0:T(8,128)(2,1)S(1)}, bf16[512,384]{1,0:T(8,128)(2,1)S(1)}, u32[]{:S(2)}, u32[]{:S(2)}) collective-permute-start(bf16[512,384]{1,0:T(8,128)(2,1)S(1)} %get-tuple-element.73), channel_id=1, source_target_pairs={{0,2},{1,3},{2,0},{3,1},{4,6},{5,7},{6,4},{7,5},{8,10},{9,11},{10,... | collective-permute-start | bytes 1179656 | tf_op jit(solution)/shard_map/ppermute | solution.py:472
  115.8 11.6 %collective-permute-start.4 = (bf16[256,384]{1,0:T(8,128)(2,1)S(1)}, bf16[256,384]{1,0:T(8,128)(2,1)S(1)}, u32[]{:S(2)}, u32[]{:S(2)}) collective-permute-start(bf16[256,384]{1,0:T(8,128)(2,1)S(1)} %get-tuple-element.76), channel_id=1, source_target_pairs={{0,2},{1,3},{2,0},{3,1},{4,6},{5,7},{6,4},{7,5},{8,10},{9,11},{10,... | collective-permute-start | bytes 589832 | tf_op jit(solution)/shard_map/ppermute | solution.py:472
  117.4 10.1 %collective-permute-start.8 = (bf16[256,384]{1,0:T(8,128)(2,1)S(1)}, bf16[256,384]{1,0:T(8,128)(2,1)S(1)}, u32[]{:S(2)}, u32[]{:S(2)}) collective-permute-start(bf16[256,384]{1,0:T(8,128)(2,1)S(1)} %get-tuple-element.78), channel_id=1, source_target_pairs={{0,4},{4,0},{8,12},{12,8},{16,20},{20,16},{24,28},{28,24},{1,5},{5... | collective-permute-start | bytes 589832 | tf_op jit(solution)/shard_map/ppermute | solution.py:472
  127.6 6.1 %collective-permute-start.9 = (bf16[128,768]{1,0:T(8,128)(2,1)S(1)}, bf16[128,768]{1,0:T(8,128)(2,1)S(1)}, u32[]{:S(2)}, u32[]{:S(2)}) collective-permute-start(bf16[128,768]{1,0:T(8,128)(2,1)S(1)} %get-tuple-element.87), channel_id=1, source_target_pairs={{0,8},{4,12},{8,0},{12,4},{16,24},{20,28},{24,16},{28,20},{1,9},{5... | collective-permute-start | bytes 589832 | tf_op jit(solution)/shard_map/ppermute | solution.py:472
  129.2 12.1 %collective-permute-start.13 = (bf16[512,384]{1,0:T(8,128)(2,1)S(1)}, bf16[512,384]{1,0:T(8,128)(2,1)S(1)}, u32[]{:S(2)}, u32[]{:S(2)}) collective-permute-start(bf16[512,384]{1,0:T(8,128)(2,1)S(1)} %get-tuple-element.81), channel_id=1, source_target_pairs={{0,2},{1,3},{2,0},{3,1},{4,6},{5,7},{6,4},{7,5},{8,10},{9,11},{10,... | collective-permute-start | bytes 1179656 | tf_op jit(solution)/shard_map/ppermute | solution.py:472
  130.6 9.0 %collective-permute-start.12 = (bf16[512,256]{1,0:T(8,128)(2,1)S(1)}, bf16[512,256]{1,0:T(8,128)(2,1)S(1)}, u32[]{:S(2)}, u32[]{:S(2)}) collective-permute-start(bf16[512,256]{1,0:T(8,128)(2,1)S(1)} %get-tuple-element.80), channel_id=1, source_target_pairs={{0,4},{4,0},{8,12},{12,8},{16,20},{20,16},{24,28},{28,24},{1,5},{5... | collective-permute-start | bytes 786440 | tf_op jit(solution)/shard_map/ppermute | solution.py:472
  131.2 13.6 %collective-permute-start.11 = (bf16[256,384]{1,0:T(8,128)(2,1)S(1)}, bf16[256,384]{1,0:T(8,128)(2,1)S(1)}, u32[]{:S(2)}, u32[]{:S(2)}) collective-permute-start(bf16[256,384]{1,0:T(8,128)(2,1)S(1)} %get-tuple-element.83), channel_id=1, source_target_pairs={{0,2},{1,3},{2,0},{3,1},{4,6},{5,7},{6,4},{7,5},{8,10},{9,11},{10,... | collective-permute-start | bytes 589832 | tf_op jit(solution)/shard_map/ppermute | solution.py:472
  131.8 13.0 %collective-permute-start.14 = (bf16[256,384]{1,0:T(8,128)(2,1)S(1)}, bf16[256,384]{1,0:T(8,128)(2,1)S(1)}, u32[]{:S(2)}, u32[]{:S(2)}) collective-permute-start(bf16[256,384]{1,0:T(8,128)(2,1)S(1)} %get-tuple-element.84), channel_id=1, source_target_pairs={{0,4},{4,0},{8,12},{12,8},{16,20},{20,16},{24,28},{28,24},{1,5},{5... | collective-permute-start | bytes 589832 | tf_op jit(solution)/shard_map/ppermute | solution.py:472
  133.8 11.8 %collective-permute-start.10 = (bf16[64,768]{1,0:T(8,128)(2,1)S(1)}, bf16[64,768]{1,0:T(8,128)(2,1)S(1)}, u32[]{:S(2)}, u32[]{:S(2)}) collective-permute-start(bf16[64,768]{1,0:T(8,128)(2,1)S(1)} %slice.50), channel_id=1, source_target_pairs={{0,16},{4,20},{8,24},{12,28},{16,0},{20,4},{24,8},{28,12},{1,17},{... | collective-permute-start | bytes 294920 | tf_op jit(solution)/shard_map/ppermute | solution.py:472
  141.3 5.0 %collective-permute-start.17 = (bf16[256,256]{1,0:T(8,128)(2,1)S(1)}, bf16[256,256]{1,0:T(8,128)(2,1)S(1)}, u32[]{:S(2)}, u32[]{:S(2)}) collective-permute-start(bf16[256,256]{1,0:T(8,128)(2,1)S(1)} %get-tuple-element.89), channel_id=1, source_target_pairs={{0,2},{1,3},{2,0},{3,1},{4,6},{5,7},{6,4},{7,5},{8,10},{9,11},{10,... | collective-permute-start | bytes 393224 | tf_op jit(solution)/shard_map/ppermute | solution.py:472
  142.9 5.7 %collective-permute-start.18 = (bf16[256,384]{1,0:T(8,128)(2,1)S(1)}, bf16[256,384]{1,0:T(8,128)(2,1)S(1)}, u32[]{:S(2)}, u32[]{:S(2)}) collective-permute-start(bf16[256,384]{1,0:T(8,128)(2,1)S(1)} %get-tuple-element.90), channel_id=1, source_target_pairs={{0,4},{4,0},{8,12},{12,8},{16,20},{20,16},{24,28},{28,24},{1,5},{5... | collective-permute-start | bytes 589832 | tf_op jit(solution)/shard_map/ppermute | solution.py:472
  144.9 7.0 %collective-permute-start.15 = (bf16[128,768]{1,0:T(8,128)(2,1)S(1)}, bf16[128,768]{1,0:T(8,128)(2,1)S(1)}, u32[]{:S(2)}, u32[]{:S(2)}) collective-permute-start(bf16[128,768]{1,0:T(8,128)(2,1)S(1)} %get-tuple-element.93), channel_id=1, source_target_pairs={{0,8},{4,12},{8,0},{12,4},{16,24},{20,28},{24,16},{28,20},{1,9},{5... | collective-permute-start | bytes 589832 | tf_op jit(solution)/shard_map/ppermute | solution.py:472
  148.7 6.7 %collective-permute-start.19 = (bf16[128,640]{1,0:T(8,128)(2,1)S(1)}, bf16[128,640]{1,0:T(8,128)(2,1)S(1)}, u32[]{:S(2)}, u32[]{:S(2)}) collective-permute-start(bf16[128,640]{1,0:T(8,128)(2,1)S(1)} %get-tuple-element.95), channel_id=1, source_target_pairs={{0,8},{4,12},{8,0},{12,4},{16,24},{20,28},{24,16},{28,20},{1,9},{5... | collective-permute-start | bytes 491528 | tf_op jit(solution)/shard_map/ppermute | solution.py:472
  152.0 6.5 %collective-permute-start.16 = (bf16[64,768]{1,0:T(8,128)(2,1)S(1)}, bf16[64,768]{1,0:T(8,128)(2,1)S(1)}, u32[]{:S(2)}, u32[]{:S(2)}) collective-permute-start(bf16[64,768]{1,0:T(8,128)(2,1)S(1)} %slice.49), channel_id=1, source_target_pairs={{0,16},{4,20},{8,24},{12,28},{16,0},{20,4},{24,8},{28,12},{1,17},{... | collective-permute-start | bytes 294920 | tf_op jit(solution)/shard_map/ppermute | solution.py:472
  155.4 5.4 %collective-permute-start.20 = (bf16[64,640]{1,0:T(8,128)(2,1)S(1)}, bf16[64,640]{1,0:T(8,128)(2,1)S(1)}, u32[]{:S(2)}, u32[]{:S(2)}) collective-permute-start(bf16[64,640]{1,0:T(8,128)(2,1)S(1)} %slice.51), channel_id=1, source_target_pairs={{0,16},{4,20},{8,24},{12,28},{16,0},{20,4},{24,8},{28,12},{1,17},{... | collective-permute-start | bytes 245768 | tf_op jit(solution)/shard_map/ppermute | solution.py:472

commit v5 on v4

--- a/solution.py
+++ b/solution.py
@@ -64,7 +64,7 @@
 SOON = pl.CostEstimate(flops=1, bytes_accessed=1, transcendentals=0)
 
 
-def params(limit=56):
+def params(limit=24):
     return pltpu.CompilerParams(
         dimension_semantics=("arbitrary",), vmem_limit_bytes=limit * MIB
     )
@@ -370,6 +370,20 @@
         store_rows(keep_ref, at, dot(xt_ref[...], dh_ref[:, at]), crossed)
     if at_ref is not None:
         store_rows(keep_ref, slice(cols, None), dot(at_ref[...], dz_ref[...]), True)
+
+
+def keep_some(quarters, keep_ref, xt_ref, dh_ref, at_ref, dz_ref):
+    cols = dh_ref.shape[1]
+    size = xt_ref.shape[0] // 4
+
+    def make(at, ref, other, crossed):
+        for i, quarter in enumerate(quarters):
+            j = (0, 2, 1, 3)[quarter] if crossed else quarter
+            keep_ref[i * size:(i + 1) * size, at] = dot(ref[j * size:(j + 1) * size, :], other)
+
+    for at, crossed in column_tiles(cols):
+        make(at, xt_ref, dh_ref[:, at], crossed)
+    make(slice(cols, None), at_ref, dz_ref[...], True)
 
 
 def send_kernel(has_old, has_at, count, *refs):
@@ -440,27 +454,29 @@
     )(*operands)
 
 
-def keep_half(dz, dh, xt, at):
+def keep_half(dz, dh, xt, at, quarters):
     rows, emb = dz.shape
     half = xt.shape[0] // 2
     cols = dh.shape[1]
     operands = [xt, dh]
     in_specs = [whole((half, rows)), whole((rows, cols))]
+    made = half
     if at is None:
         kernel = lambda x, d, g: keep_rows(g, x, d, None, None)
     else:
-        kernel = lambda x, d, a, z, g: keep_rows(g, x, d, a, z)
+        kernel = lambda x, d, a, z, g: keep_some(quarters, g, x, d, a, z)
         operands += [at, dz]
         in_specs += [whole((half, rows)), whole((rows, emb))]
         cols += emb
+        made = half // 4 * len(quarters)
     return pl.pallas_call(
         kernel,
         grid=(1,),
         in_specs=in_specs,
-        out_specs=whole((half, cols)),
-        out_shape=jax.ShapeDtypeStruct((half, cols), jnp.float32),
+        out_specs=whole((made, cols)),
+        out_shape=jax.ShapeDtypeStruct((made, cols), jnp.float32),
         cost_estimate=pl.CostEstimate(
-            flops=2 * rows * half * cols, bytes_accessed=8 * rows * half, transcendentals=0
+            flops=2 * rows * made * cols, bytes_accessed=8 * rows * half, transcendentals=0
         ),
         compiler_params=params(28),
         name="keep_half",
@@ -493,10 +509,10 @@
             outs[side][...] = v.astype(jnp.bfloat16)
 
 
-def fold(keep, came, left, right, split, rows, place, joined):
+def fold(keep, came, left, right, split, rows, place, joined, keep_place):
     cols = keep.shape[1]
 
-    def spec(width):
+    def spec(width, place=place):
         return pl.BlockSpec((rows, width), lambda i: (place, 0))
 
     if joined:
@@ -512,7 +528,7 @@
     return pl.pallas_call(
         lambda *refs: fold_kernel(split, joined, *refs),
         grid=(1,),
-        in_specs=[spec(cols)] * 2 + [spec(split)] * len(left) + [spec(cols - split)] * len(right),
+        in_specs=[spec(cols, keep_place), spec(cols)] + [spec(split)] * len(left) + [spec(cols - split)] * len(right),
         out_specs=[whole(shape.shape) for shape in shapes],
         out_shape=shapes,
         cost_estimate=SOON,
@@ -525,34 +541,45 @@
     def __init__(self, keep, came, split):
         self.keep, self.came, self.split = keep, came, split
         self.left, self.right = [], []
-        self.half = keep.shape[0]
+        self.half = came.shape[0]
+
+    def add(self, rows, place, joined):
+        keep, keep_place = self.keep, place
+        if isinstance(keep, list):
+            keep, keep_place = keep[len(self.left)], 0
+        return fold(
+            keep, self.came, self.left, self.right, self.split, rows, place, joined, keep_place
+        )
+
+    def hold(self, *others):
+        self.left[-1], self.right[-1] = lax.optimization_barrier(
+            (self.left[-1], self.right[-1]) + others
+        )[:2]
 
     def first(self):
-        rows = self.half // 2
-        out = fold(self.keep, self.came, [], [], self.split, rows, 1, False)
-        return out
+        return self.add(self.half // 2, 1, False)
 
     def cross_first(self, out):
         self.left.append(swap(out[0], "dp", 1))
         self.right.append(swap(out[1], "crop", 2))
 
     def second(self):
-        rows = self.half // 4
-        return fold(self.keep, self.came, self.left, self.right, self.split, rows, 1, False)
+        return self.add(self.half // 4, 1, False)
 
     def cross_second(self, out):
         self.left.append(swap(out[0], "crop", 2))
         self.right.append(swap(out[1], "dp", 1))
 
     def third(self):
-        rows = self.half // 4
-        return fold(self.keep, self.came, self.left, self.right, self.split, rows, 0, True)
+        return self.add(self.half // 4, 0, True)
 
     def cross_third(self, out):
         own, send = out
+        return own + swap(send, "dp", 2).astype(jnp.float32)
+
+    def cross_rest(self, own):
         length = lax.axis_size("dp") // 2
         bit = 1
-        own = own + swap(send, "dp", 2 * bit).astype(jnp.float32)
         while 2 * bit < length:
             bit *= 2
             half = own.shape[0] // 2
@@ -618,29 +645,34 @@
     one = Pair(keep_1, came_1, large // 2)
     a_1 = lax.optimization_barrier(one.first())
     one.cross_first(a_1)
-    keep_2 = keep_half(d_z, after(dh_2, *a_1), xt, None)
+    keep_2 = keep_half(d_z, after(dh_2, *a_1), xt, None, None)
     two = Pair(keep_2, came_2, large // 2)
     a_2 = lax.optimization_barrier(two.first())
     two.cross_first(a_2)
-    keep_3 = keep_half(d_z, after(dh_3, *a_2), xt, at)
-    one.left[0] = after(one.left[0], keep_3)
+    three = Pair([keep_half(d_z, after(dh_3, *a_2), xt, at, (2, 3))], came_3, small // 2)
+    a_3 = lax.optimization_barrier(three.first())
+    three.cross_first(a_3)
+    three.keep.append(keep_half(d_z, after(dh_3, *a_3), xt, at, (1,)))
+    one.hold(three.keep[1])
     b_1 = lax.optimization_barrier(one.second())
     one.cross_second(b_1)
-    three = Pair(keep_3, after(came_3, *b_1), small // 2)
-    a_3 = lax.optimization_barrier(three.first())
-    three.cross_first(a_3)
-    two.left[0] = after(two.left[0], *a_3)
+    three.keep.append(keep_half(d_z, after(dh_3, *b_1), xt, at, (0,)))
+    two.hold(three.keep[2])
     b_2 = lax.optimization_barrier(two.second())
     two.cross_second(b_2)
-    one.left[1] = after(one.left[1], *b_2)
-    c_1 = lax.optimization_barrier(one.third())
-    three.left[0] = after(three.left[0], *c_1)
+    three.hold(*b_2)
     b_3 = lax.optimization_barrier(three.second())
     three.cross_second(b_3)
-    own_1 = one.cross_third(c_1)
-    two.left[1] = after(two.left[1], *b_3)
-    own_2 = two.cross_third(two.third())
-    own_3 = three.cross_third(three.third())
+    one.hold(*b_3)
+    c_1 = lax.optimization_barrier(one.third())
+    two.hold(*c_1)
+    c_2 = lax.optimization_barrier(two.third())
+    own_1 = lax.optimization_barrier(one.cross_third(c_1))
+    three.hold(own_1, *c_2)
+    c_3 = lax.optimization_barrier(three.third())
+    own_1 = one.cross_rest(own_1)
+    own_2 = two.cross_rest(two.cross_third(c_2))
+    own_3 = three.cross_rest(three.cross_third(c_3))
     grad_inner = jnp.concatenate([own_1, own_2, own_3[:, :small]], axis=1)
     return (grad_inner, own_3[:, small:])
 

time: 163 us -> 155 us (0.951)
  Pallas kernels: 74.4 us -> 48.7 us
  local copies, waits for them, and re-layouts: 5.25 us -> 23.3 us
  waiting for transfers between devices: 32 us -> 29.4 us
  starting transfers between devices: 32.6 us -> 35 us
    unnamed x16 -> x32, local copies, waits for them, and re-layouts: 2.5 us -> 21.8 us
    pallas_call x2, Pallas kernels: 21.2 us -> 5.91 us  [ordered(): pl.pallas_call(lambda *refs: order_kernel(positive, *refs), grid_spec=plt...]
    pallas_call x1, Pallas kernels: 11.2 us -> 8.13 us  [query_forward(): pl.pallas_call(query_kernel, grid=(hid // STEP,), in_specs=[whole((rows,...]
    ppermute x21, waiting for transfers between devices: 32 us -> 29.4 us  [swap(): return lax.ppermute(x, axis, [(i, i ^ bit) for i in range(size)])]
    ppermute x21, starting transfers between devices: 24.1 us -> 26.5 us  [swap(): return lax.ppermute(x, axis, [(i, i ^ bit) for i in range(size)])]
    pallas_call x1, Pallas kernels: 10.9 us -> 8.7 us  [key_hidden(): pl.pallas_call(lambda *refs: key_hidden_kernel(groups, *refs), grid=(hid...]
    pallas_call x1, Pallas kernels: 12.9 us -> 11 us  [negatives(): pl.pallas_call(neg_kernel, grid=(bank.shape[0] // tile,), in_specs=[pl.Bl...]
    pallas_call x1, Pallas kernels: 2.09 us -> 0.24 us  [batch(): pl.pallas_call(lambda *refs: batch_kernel(rows, *refs), grid=(1,), in_spe...]
  transfers between devices with their start and end apart: 23 -> 23, of which waited for: 14 -> 11; matrix products, arithmetic and copies ran while one was open for 1% -> 0% of each run, Pallas kernels for 33% -> 22%
where the time goes in v5:
time: 155 us; the launch traced here: 154 us
  Pallas kernels  48.7 us (31%)
  starting transfers between devices  35 us (23%)
  waiting for transfers between devices  29.4 us (19%)
  local copies, waits for them, and re-layouts  23.3 us (15%)
  blocking collectives  14.2 us (9%)
  other arithmetic  2.45 us (2%)
    ppermute x21, waiting for transfers between devices, swap(): return lax.ppermute(x, axis, [(i, i ^ bit) for i in range(size)])  29.4 us
    ppermute x21, starting transfers between devices, swap(): return lax.ppermute(x, axis, [(i, i ^ bit) for i in range(size)])  26.5 us
    unnamed x32, local copies, waits for them, and re-layouts  21.8 us
    all_to_all x1, blocking collectives, per_device(): lax.all_to_all(wanted, AXES, split_axis=0, concat_axis=0, tiled=True)  14.2 us
    pallas_call x1, Pallas kernels, negatives(): pl.pallas_call(neg_kernel, grid=(bank.shape[0] // tile,), in_specs=[pl.Bl...  11 us
    pallas_call x1, Pallas kernels, key_hidden(): pl.pallas_call(lambda *refs: key_hidden_kernel(groups, *refs), grid=(hid...  8.7 us
    pallas_call x1, Pallas kernels, query_forward(): pl.pallas_call(query_kernel, grid=(hid // STEP,), in_specs=[whole((rows,...  8.13 us
    pallas_call x2, Pallas kernels, send_half(): pl.pallas_call(lambda *refs: send_kernel(old is not None, at is not None,...  6.65 us
  transfers between devices with their start and end apart: 23, of which 11 were waited for; matrix products, arithmetic and copies ran while one was open for 0% of the time, Pallas kernels for 22%

profile of v5, /device:TPU:0, one launch (start us, length us, event | category | flops | bytes accessed | tf_op | source)
XLA Modules:
  0.0 154.2 jit_solution(11868256767083235030)
XLA Ops:
  1.4 14.2 %all_to_all.19 = s32[32,1,16]{2,1,0:T(1,128)S(1)} all-to-all(s32[32,1,16]{2,1,0:T(1,128)S(1)} %bitcast.17), channel_id=1, replica_groups=mesh['dp'=8,'crop'=4] {'dp','crop'}, dimensions={0} | all-to-all | bytes 4096 | tf_op jit(solution)/shard_map/all_to_all | solution.py:602
  17.0 3.4 %copy-done.12 = bf16[2048,2048]{1,0:T(8,128)(2,1)S(1)} copy-done((bf16[2048,2048]{1,0:T(8,128)(2,1)S(1)}, bf16[2048,2048]{1,0:T(8,128)(2,1)}, u32[]{:S(2)}) %copy-start.12) | copy-done | bytes 8388632
  20.4 1.6 %copy-done.15 = bf16[512,2048]{1,0:T(8,128)(2,1)S(1)} copy-done((bf16[512,2048]{1,0:T(8,128)(2,1)S(1)}, bf16[512,2048]{1,0:T(8,128)(2,1)}, u32[]{:S(2)}) %copy-start.15) | copy-done | bytes 2097176
  22.0 8.7 %key_hidden.1 = (f32[512,2048]{1,0:T(8,128)S(1)}, f32[32,1,4096]{2,1,0:T(1,128)}) custom-call(s32[512,1]{1,0:T(8,128)S(1)} %broadcast_in_dim_reshape.8.refs_0_, bf16[512,2048]{1,0:T(8,128)(2,1)S(1)} %copy-done.15, bf16[2048,2048]{1,0:T(8,128)(2,1)S(1)} %copy-done.12), custom_call_target="tpu_custom_call" | custom-call | flops 5368709120 | bytes 8388608 | tf_op jit(solution)/shard_map/key_hidden/pallas_call | solution.py:141
  30.7 2.0 %copy-done.6 = f32[512,2048]{1,0:T(8,128)} copy-done((f32[512,2048]{1,0:T(8,128)}, f32[512,2048]{1,0:T(8,128)S(1)}, u32[]{:S(2)}) %copy-start.6) | copy-done | bytes 4194328
  32.7 2.6 %all-to-all-start.1 = ((f32[32,1,4096]{2,1,0:T(1,128)}), f32[32,1,4096]{2,1,0:T(1,128)S(1)}, u32[]{:S(2)}, u32[]{:S(2)}) async-start(f32[32,1,4096]{2,1,0:T(1,128)} %get-tuple-element.57), calls=%async_computation.1 | async-start | bytes 1048576 | tf_op jit(solution)/shard_map/all_to_all | solution.py:607
  35.4 1.6 %copy-done.8 = bf16[512,2048]{1,0:T(8,128)(2,1)S(1)} copy-done((bf16[512,2048]{1,0:T(8,128)(2,1)S(1)}, bf16[512,2048]{1,0:T(8,128)(2,1)}, u32[]{:S(2)}) %copy-start.8) | copy-done | bytes 2097176
  37.0 2.9 %ordered.2 = bf16[2,16,64,512]{3,2,1,0:T(8,128)(2,1)S(1)} custom-call(s32[17]{0:T(128)S(1)} %pad_add_fusion.refs_0_, bf16[512,2048]{1,0:T(8,128)(2,1)S(1)} %copy-done.8), custom_call_target="tpu_custom_call" | custom-call | bytes 8388608 | tf_op jit(solution)/shard_map/ordered/pallas_call | solution.py:269
  40.0 1.6 %copy-done.9 = bf16[512,2048]{1,0:T(8,128)(2,1)S(1)} copy-done((bf16[512,2048]{1,0:T(8,128)(2,1)S(1)}, bf16[512,2048]{1,0:T(8,128)(2,1)}, u32[]{:S(2)}) %copy-start.9) | copy-done | bytes 2097176
  41.6 3.4 %copy-done.13 = bf16[2048,2048]{1,0:T(8,128)(2,1)S(1)} copy-done((bf16[2048,2048]{1,0:T(8,128)(2,1)S(1)}, bf16[2048,2048]{1,0:T(8,128)(2,1)}, u32[]{:S(2)}) %copy-start.13) | copy-done | bytes 8388632
  45.0 8.1 %query_forward.1 = (bf16[512,2048]{1,0:T(8,128)(2,1)S(1)}, f32[1,2048]{1,0:T(1,128)S(1)}, f32[512,128]{1,0:T(8,128)S(1)}, bf16[512,128]{1,0:T(8,128)(2,1)S(1)}) custom-call(bf16[512,2048]{1,0:T(8,128)(2,1)S(1)} %copy-done.9, bf16[2048,2048]{1,0:T(8,128)(2,1)S(1)} %copy-done.13, bf16[2048,128]{1,0:T(8,128)(2,1)S(1)} %copy-done.5), custom_call_target="tpu_custom_call" | custom-call | flops 4563402752 | bytes 8388608 | tf_op jit(solution)/shard_map/query_forward/pallas_call | solution.py:220
  53.2 1.4 copy-done.2
  55.6 6.0 %all-to-all-start.2 = ((f32[32,1,4096]{2,1,0:T(1,128)}), f32[32,1,4096]{2,1,0:T(1,128)}, u32[]{:S(2)}, u32[]{:S(2)}) async-start(f32[32,1,4096]{2,1,0:T(1,128)} %copy-done.10), calls=%async_computation.2 | async-start | bytes 1048576 | tf_op jit(solution)/shard_map/all_to_all | solution.py:625
  61.5 1.6 %copy-done.3 = bf16[512,2048]{1,0:T(8,128)(2,1)S(1)} copy-done((bf16[512,2048]{1,0:T(8,128)(2,1)S(1)}, bf16[512,2048]{1,0:T(8,128)(2,1)}, u32[]{:S(2)}) %copy-start.3) | copy-done | bytes 2097176
  63.1 3.0 %ordered.3 = bf16[2,16,64,512]{3,2,1,0:T(8,128)(2,1)S(1)} custom-call(s32[17]{0:T(128)S(1)} %pad_add_fusion.refs_0_, bf16[512,2048]{1,0:T(8,128)(2,1)S(1)} %copy-done.3), custom_call_target="tpu_custom_call" | custom-call | bytes 8388608 | tf_op jit(solution)/shard_map/ordered/pallas_call | solution.py:269
  66.1 1.4 copy-done
  67.5 11.0 %negatives.1.refs_5_ = f32[512,256]{1,0:T(8,128)S(1)} custom-call(bf16[512,128]{1,0:T(8,128)(2,1)S(1)} %get-tuple-element.63.q_ref, bf16[16384,128]{1,0:T(8,128)(2,1)S(1)} %copy-done.14), custom_call_target="tpu_custom_call" | custom-call | flops 4294967296 | bytes 4194304 | tf_op jit(solution)/shard_map/negatives/pallas_call | solution.py:42
  78.5 2.2 %copy-done.7 = f32[512,2048]{1,0:T(8,128)S(1)} copy-done((f32[512,2048]{1,0:T(8,128)S(1)}, f32[512,2048]{1,0:T(8,128)}, u32[]{:S(2)}) %copy-start.7) | copy-done | bytes 4194328
  80.7 1.0 copy-done.11
  81.7 4.3 %embed.1.refs_0_.z = bf16[512,128]{1,0:T(8,128)(2,1)S(1)} custom-call(s32[1,512]{1,0:T(1,128)S(1)} %broadcast_in_dim_reshape.7.refs_0_, f32[512,2048]{1,0:T(8,128)S(1)} %copy-done.7, f32[32,1,4096]{2,1,0:T(1,128)} %all-to-all-done.2.refs_2_, bf16[2048,128]{1,0:T(8,128)(2,1)S(1)} %copy-done.11, f32[512,128]{1,0:T(8,128)S(1)} %get-tuple-element.66.refs_4_, ...), custom_call_target="tpu_custom_call" | custom-call | flops 268435456 | bytes 4194304 | tf_op jit(solution)/shard_map/embed/pallas_call | solution.py:331
  86.0 2.1 %send_half.2 = (bf16[512,768]{1,0:T(8,128)(2,1)S(1)}, bf16[1024,768]{1,0:T(8,128)(2,1)S(1)}) custom-call(bf16[512,128]{1,0:T(8,128)(2,1)S(1)} %embed.1.refs_0_.z, bf16[2048,512]{1,0:T(8,128)(2,1)S(1)} %bitcast.5, bf16[2048,128]{1,0:T(8,128)(2,1)S(1)} %copy-done.5, bf16[512,2048]{1,0:T(8,128)(2,1)S(1)} %copy-done.4, ...), custom_call_target="tpu_custom_call" | custom-call | flops 805306368 | bytes 4194304 | tf_op jit(solution)/shard_map/send_half/pallas_call | solution.py:441
  88.4 4.5 %send_half.3 = (f32[1024,768]{1,0:T(8,128)S(1)}, bf16[512,768]{1,0:T(8,128)(2,1)S(1)}, bf16[1024,768]{1,0:T(8,128)(2,1)S(1)}, bf16[512,512]{1,0:T(8,128)(2,1)S(1)}, bf16[1024,640]{1,0:T(8,128)(2,1)S(1)}) custom-call(bf16[512,128]{1,0:T(8,128)(2,1)S(1)} %embed.1.refs_0_.z, bf16[2048,512]{1,0:T(8,128)(2,1)S(1)} %bitcast.6, bf16[2048,512]{1,0:T(8,128)(2,1)S(1)} %bitcast.12, ...), custom_call_target="tpu_custom_call" | custom-call | flops 1342177280 | bytes 4194304 | tf_op jit(solution)/shard_map/send_half/pallas_call | solution.py:441
  93.7 1.7 %collective-permute-start.1 = (bf16[512,384]{1,0:T(8,128)(2,1)S(1)}, bf16[512,384]{1,0:T(8,128)(2,1)S(1)}, u32[]{:S(2)}, u32[]{:S(2)}) collective-permute-start(bf16[512,384]{1,0:T(8,128)(2,1)S(1)} %get-tuple-element.74), channel_id=1, source_target_pairs={{0,4},{4,0},{8,12},{12,8},{16,20},{20,16},{24,28},{28,24},{1,5},{5... | collective-permute-start | bytes 1179656 | tf_op jit(solution)/shard_map/ppermute | solution.py:488
  95.4 1.5 collective-permute-start.2
  96.9 1.2 keep_half.4.refs_0_
  98.9 0.9 collective-permute-start.10
  100.5 1.2 collective-permute-start.8
  101.7 4.0 %collective-permute-done.1.refs_2_ = bf16[512,384]{1,0:T(8,128)(2,1)S(1)} collective-permute-done((bf16[512,384]{1,0:T(8,128)(2,1)S(1)}, bf16[512,384]{1,0:T(8,128)(2,1)S(1)}, u32[]{:S(2)}, u32[]{:S(2)}) %collective-permute-start.1) | collective-permute-done | bytes 393248 | tf_op jit(solution)/shard_map/ppermute | solution.py:488
  105.7 1.7 %collective-permute-start.7 = (bf16[512,256]{1,0:T(8,128)(2,1)S(1)}, bf16[512,256]{1,0:T(8,128)(2,1)S(1)}, u32[]{:S(2)}, u32[]{:S(2)}) collective-permute-start(bf16[512,256]{1,0:T(8,128)(2,1)S(1)} %get-tuple-element.84), channel_id=1, source_target_pairs={{0,4},{4,0},{8,12},{12,8},{16,20},{20,16},{24,28},{28,24},{1,5},{5... | collective-permute-start | bytes 786440 | tf_op jit(solution)/shard_map/ppermute | solution.py:488
  107.9 1.5 collective-permute-start.5
  109.4 4.7 %collective-permute-done.9.refs_2_ = bf16[512,384]{1,0:T(8,128)(2,1)S(1)} collective-permute-done((bf16[512,384]{1,0:T(8,128)(2,1)S(1)}, bf16[512,384]{1,0:T(8,128)(2,1)S(1)}, u32[]{:S(2)}, u32[]{:S(2)}) %collective-permute-start.9) | collective-permute-done | bytes 393248 | tf_op jit(solution)/shard_map/ppermute | solution.py:488
  114.1 1.7 %collective-permute-start.6 = (bf16[256,384]{1,0:T(8,128)(2,1)S(1)}, bf16[256,384]{1,0:T(8,128)(2,1)S(1)}, u32[]{:S(2)}, u32[]{:S(2)}) collective-permute-start(bf16[256,384]{1,0:T(8,128)(2,1)S(1)} %get-tuple-element.90), channel_id=1, source_target_pairs={{0,4},{4,0},{8,12},{12,8},{16,20},{20,16},{24,28},{28,24},{1,5},{5... | collective-permute-start | bytes 589832 | tf_op jit(solution)/shard_map/ppermute | solution.py:488
  116.3 1.5 collective-permute-start.13
  117.8 1.9 %collective-permute-done.7.refs_2_ = bf16[512,256]{1,0:T(8,128)(2,1)S(1)} collective-permute-done((bf16[512,256]{1,0:T(8,128)(2,1)S(1)}, bf16[512,256]{1,0:T(8,128)(2,1)S(1)}, u32[]{:S(2)}, u32[]{:S(2)}) %collective-permute-start.7) | collective-permute-done | bytes 262176 | tf_op jit(solution)/shard_map/ppermute | solution.py:488
  119.7 1.7 %collective-permute-start.14 = (bf16[256,384]{1,0:T(8,128)(2,1)S(1)}, bf16[256,384]{1,0:T(8,128)(2,1)S(1)}, u32[]{:S(2)}, u32[]{:S(2)}) collective-permute-start(bf16[256,384]{1,0:T(8,128)(2,1)S(1)} %get-tuple-element.95), channel_id=1, source_target_pairs={{0,4},{4,0},{8,12},{12,8},{16,20},{20,16},{24,28},{28,24},{1,5},{5... | collective-permute-start | bytes 589832 | tf_op jit(solution)/shard_map/ppermute | solution.py:488
  121.4 2.9 %collective-permute-done.8.refs_3_.refs_4_ = bf16[512,384]{1,0:T(8,128)(2,1)S(1)} collective-permute-done((bf16[512,384]{1,0:T(8,128)(2,1)S(1)}, bf16[512,384]{1,0:T(8,128)(2,1)S(1)}, u32[]{:S(2)}, u32[]{:S(2)}) %collective-permute-start.8) | collective-permute-done | bytes 393248 | tf_op jit(solution)/shard_map/ppermute | solution.py:488
  124.3 4.1 %collective-permute-done.5.refs_3_ = bf16[256,384]{1,0:T(8,128)(2,1)S(1)} collective-permute-done((bf16[256,384]{1,0:T(8,128)(2,1)S(1)}, bf16[256,384]{1,0:T(8,128)(2,1)S(1)}, u32[]{:S(2)}, u32[]{:S(2)}) %collective-permute-start.5) | collective-permute-done | bytes 196640 | tf_op jit(solution)/shard_map/ppermute | solution.py:488
  128.6 1.5 collective-permute-start.11
  130.2 1.5 collective-permute-start.17
  132.8 1.5 collective-permute-start.15
  134.9 2.4 %collective-permute-start.12 = (bf16[64,768]{1,0:T(8,128)(2,1)S(1)}, bf16[64,768]{1,0:T(8,128)(2,1)S(1)}, u32[]{:S(2)}, u32[]{:S(2)}) collective-permute-start(bf16[64,768]{1,0:T(8,128)(2,1)S(1)} %slice.50), channel_id=1, source_target_pairs={{0,16},{4,20},{8,24},{12,28},{16,0},{20,4},{24,8},{28,12},{1,17},{... | collective-permute-start | bytes 294920 | tf_op jit(solution)/shard_map/ppermute | solution.py:488
  137.5 1.6 %collective-permute-start.19 = (bf16[128,640]{1,0:T(8,128)(2,1)S(1)}, bf16[128,640]{1,0:T(8,128)(2,1)S(1)}, u32[]{:S(2)}, u32[]{:S(2)}) collective-permute-start(bf16[128,640]{1,0:T(8,128)(2,1)S(1)} %get-tuple-element.111), channel_id=1, source_target_pairs={{0,8},{4,12},{8,0},{12,4},{16,24},{20,28},{24,16},{28,20},{1,9},{5... | collective-permute-start | bytes 491528 | tf_op jit(solution)/shard_map/ppermute | solution.py:488
  139.1 4.4 %collective-permute-done.15 = bf16[128,768]{1,0:T(8,128)(2,1)S(1)} collective-permute-done((bf16[128,768]{1,0:T(8,128)(2,1)S(1)}, bf16[128,768]{1,0:T(8,128)(2,1)S(1)}, u32[]{:S(2)}, u32[]{:S(2)}) %collective-permute-start.15) | collective-permute-done | bytes 196640 | tf_op jit(solution)/shard_map/ppermute | solution.py:488
  143.7 1.6 %collective-permute-done.19 = bf16[128,640]{1,0:T(8,128)(2,1)S(1)} collective-permute-done((bf16[128,640]{1,0:T(8,128)(2,1)S(1)}, bf16[128,640]{1,0:T(8,128)(2,1)S(1)}, u32[]{:S(2)}, u32[]{:S(2)}) %collective-permute-start.19) | collective-permute-done | bytes 163872 | tf_op jit(solution)/shard_map/ppermute | solution.py:488
  145.3 2.4 %collective-permute-start.20 = (bf16[64,640]{1,0:T(8,128)(2,1)S(1)}, bf16[64,640]{1,0:T(8,128)(2,1)S(1)}, u32[]{:S(2)}, u32[]{:S(2)}) collective-permute-start(bf16[64,640]{1,0:T(8,128)(2,1)S(1)} %slice.51), channel_id=1, source_target_pairs={{0,16},{4,20},{8,24},{12,28},{16,0},{20,4},{24,8},{28,12},{1,17},{... | collective-permute-start | bytes 245768 | tf_op jit(solution)/shard_map/ppermute | solution.py:488
  147.7 4.1 %collective-permute-done.16 = bf16[64,768]{1,0:T(8,128)(2,1)S(1)} collective-permute-done((bf16[64,768]{1,0:T(8,128)(2,1)S(1)}, bf16[64,768]{1,0:T(8,128)(2,1)S(1)}, u32[]{:S(2)}, u32[]{:S(2)}) %collective-permute-start.16) | collective-permute-done | bytes 98336 | tf_op jit(solution)/shard_map/ppermute | solution.py:488
  151.8 0.9 collective-permute-done.20
  153.3 0.8 pad_maximum_fusion
  (73 shorter events, 9.8 us)
Async XLA Ops:
  17.0 3.4 %copy-start.12 = (bf16[2048,2048]{1,0:T(8,128)(2,1)S(1)}, bf16[2048,2048]{1,0:T(8,128)(2,1)}, u32[]{:S(2)}) copy-start(bf16[2048,2048]{1,0:T(8,128)(2,1)} %refs_2_.2) | copy-start | bytes 25165828
  20.4 1.6 %copy-start.15 = (bf16[512,2048]{1,0:T(8,128)(2,1)S(1)}, bf16[512,2048]{1,0:T(8,128)(2,1)}, u32[]{:S(2)}) copy-start(bf16[512,2048]{1,0:T(8,128)(2,1)} %refs_1_.2) | copy-start | bytes 6291460
  30.7 2.0 %copy-start.6 = (f32[512,2048]{1,0:T(8,128)}, f32[512,2048]{1,0:T(8,128)S(1)}, u32[]{:S(2)}) copy-start(f32[512,2048]{1,0:T(8,128)S(1)} %get-tuple-element.61.refs_1_) | copy-start | bytes 12582916
  32.7 21.9 %all-to-all-start.1 = ((f32[32,1,4096]{2,1,0:T(1,128)}), f32[32,1,4096]{2,1,0:T(1,128)S(1)}, u32[]{:S(2)}, u32[]{:S(2)}) async-start(f32[32,1,4096]{2,1,0:T(1,128)} %get-tuple-element.57), calls=%async_computation.1 | async-start | bytes 1048576 | tf_op jit(solution)/shard_map/all_to_all | solution.py:607
  35.4 1.6 %copy-start.8 = (bf16[512,2048]{1,0:T(8,128)(2,1)S(1)}, bf16[512,2048]{1,0:T(8,128)(2,1)}, u32[]{:S(2)}) copy-start(bf16[512,2048]{1,0:T(8,128)(2,1)} %refs_1_.3) | copy-start | bytes 6291460
  37.0 3.0 %copy-start.5 = (bf16[2048,128]{1,0:T(8,128)(2,1)S(1)}, bf16[2048,128]{1,0:T(8,128)(2,1)}, u32[]{:S(2)}) copy-start(bf16[2048,128]{1,0:T(8,128)(2,1)} %refs_8_.1) | copy-start | bytes 1572868
  40.0 1.6 %copy-start.9 = (bf16[512,2048]{1,0:T(8,128)(2,1)S(1)}, bf16[512,2048]{1,0:T(8,128)(2,1)}, u32[]{:S(2)}) copy-start(bf16[512,2048]{1,0:T(8,128)(2,1)} %refs_1_.3) | copy-start | bytes 6291460
  41.6 3.4 %copy-start.13 = (bf16[2048,2048]{1,0:T(8,128)(2,1)S(1)}, bf16[2048,2048]{1,0:T(8,128)(2,1)}, u32[]{:S(2)}) copy-start(bf16[2048,2048]{1,0:T(8,128)(2,1)} %w_ref.1) | copy-start | bytes 25165828
  53.1 1.4 copy-start.2
  54.8 0.8 copy-start.10
  55.6 22.9 %all-to-all-start.2 = ((f32[32,1,4096]{2,1,0:T(1,128)}), f32[32,1,4096]{2,1,0:T(1,128)}, u32[]{:S(2)}, u32[]{:S(2)}) async-start(f32[32,1,4096]{2,1,0:T(1,128)} %copy-done.10), calls=%async_computation.2 | async-start | bytes 1048576 | tf_op jit(solution)/shard_map/all_to_all | solution.py:625
  61.5 1.6 %copy-start.3 = (bf16[512,2048]{1,0:T(8,128)(2,1)S(1)}, bf16[512,2048]{1,0:T(8,128)(2,1)}, u32[]{:S(2)}) copy-start(bf16[512,2048]{1,0:T(8,128)(2,1)} %copy-done.2) | copy-start | bytes 6291460
  63.1 4.4 %copy-start.14 = (bf16[16384,128]{1,0:T(8,128)(2,1)S(1)}, bf16[16384,128]{1,0:T(8,128)(2,1)}, u32[]{:S(2)}) copy-start(bf16[16384,128]{1,0:T(8,128)(2,1)} %bank_ref.1) | copy-start | bytes 12582916
  66.1 1.4 copy-start
  78.5 2.2 %copy-start.7 = (f32[512,2048]{1,0:T(8,128)S(1)}, f32[512,2048]{1,0:T(8,128)}, u32[]{:S(2)}) copy-start(f32[512,2048]{1,0:T(8,128)} %copy-done.6) | copy-start | bytes 12582916
  80.7 1.0 copy-start.11
  81.7 4.3 %copy-start.4 = (bf16[512,2048]{1,0:T(8,128)(2,1)S(1)}, bf16[512,2048]{1,0:T(8,128)(2,1)}, u32[]{:S(2)}) copy-start(bf16[512,2048]{1,0:T(8,128)(2,1)} %copy-done.2) | copy-start | bytes 6291460
  86.0 2.4 %copy-start.1 = (bf16[2,16,64,512]{3,2,1,0:T(8,128)(2,1)S(1)}, bf16[2,16,64,512]{3,2,1,0:T(8,128)(2,1)}, u32[]{:S(2)}) copy-start(bf16[2,16,64,512]{3,2,1,0:T(8,128)(2,1)} %copy-done) | copy-start | bytes 6291460
  88.2 5.4 %collective-permute-start = (bf16[1024,768]{1,0:T(8,128)(2,1)S(1)}, bf16[1024,768]{1,0:T(8,128)(2,1)S(1)}, u32[]{:S(2)}, u32[]{:S(2)}) collective-permute-start(bf16[1024,768]{1,0:T(8,128)(2,1)S(1)} %get-tuple-element.73), channel_id=1, source_target_pairs={{0,1},{1,0},{2,3},{3,2},{4,5},{5,4},{6,7},{7,6},{8,9},{9,8},{10,11... | collective-permute-start | bytes 4718600 | tf_op jit(solution)/shard_map/ppermute | solution.py:488
  93.0 5.2 %collective-permute-start.3 = (bf16[1024,768]{1,0:T(8,128)(2,1)S(1)}, bf16[1024,768]{1,0:T(8,128)(2,1)S(1)}, u32[]{:S(2)}, u32[]{:S(2)}) collective-permute-start(bf16[1024,768]{1,0:T(8,128)(2,1)S(1)} %get-tuple-element.79), channel_id=1, source_target_pairs={{0,1},{1,0},{2,3},{3,2},{4,5},{5,4},{6,7},{7,6},{8,9},{9,8},{10,11... | collective-permute-start | bytes 4718600 | tf_op jit(solution)/shard_map/ppermute | solution.py:488
  93.3 7.0 %collective-permute-start.4 = (bf16[1024,640]{1,0:T(8,128)(2,1)S(1)}, bf16[1024,640]{1,0:T(8,128)(2,1)S(1)}, u32[]{:S(2)}, u32[]{:S(2)}) collective-permute-start(bf16[1024,640]{1,0:T(8,128)(2,1)S(1)} %get-tuple-element.83), channel_id=1, source_target_pairs={{0,1},{1,0},{2,3},{3,2},{4,5},{5,4},{6,7},{7,6},{8,9},{9,8},{10,11... | collective-permute-start | bytes 3932168 | tf_op jit(solution)/shard_map/ppermute | solution.py:488
  93.7 12.0 %collective-permute-start.1 = (bf16[512,384]{1,0:T(8,128)(2,1)S(1)}, bf16[512,384]{1,0:T(8,128)(2,1)S(1)}, u32[]{:S(2)}, u32[]{:S(2)}) collective-permute-start(bf16[512,384]{1,0:T(8,128)(2,1)S(1)} %get-tuple-element.74), channel_id=1, source_target_pairs={{0,4},{4,0},{8,12},{12,8},{16,20},{20,16},{24,28},{28,24},{1,5},{5... | collective-permute-start | bytes 1179656 | tf_op jit(solution)/shard_map/ppermute | solution.py:488
  95.4 12.3 %collective-permute-start.2 = (bf16[512,384]{1,0:T(8,128)(2,1)S(1)}, bf16[512,384]{1,0:T(8,128)(2,1)S(1)}, u32[]{:S(2)}, u32[]{:S(2)}) collective-permute-start(bf16[512,384]{1,0:T(8,128)(2,1)S(1)} %get-tuple-element.75), channel_id=1, source_target_pairs={{0,2},{1,3},{2,0},{3,1},{4,6},{5,7},{6,4},{7,5},{8,10},{9,11},{10,... | collective-permute-start | bytes 1179656 | tf_op jit(solution)/shard_map/ppermute | solution.py:488
  98.3 15.8 %collective-permute-start.9 = (bf16[512,384]{1,0:T(8,128)(2,1)S(1)}, bf16[512,384]{1,0:T(8,128)(2,1)S(1)}, u32[]{:S(2)}, u32[]{:S(2)}) collective-permute-start(bf16[512,384]{1,0:T(8,128)(2,1)S(1)} %get-tuple-element.80), channel_id=1, source_target_pairs={{0,4},{4,0},{8,12},{12,8},{16,20},{20,16},{24,28},{28,24},{1,5},{5... | collective-permute-start | bytes 1179656 | tf_op jit(solution)/shard_map/ppermute | solution.py:488
  98.9 17.2 %collective-permute-start.10 = (bf16[512,384]{1,0:T(8,128)(2,1)S(1)}, bf16[512,384]{1,0:T(8,128)(2,1)S(1)}, u32[]{:S(2)}, u32[]{:S(2)}) collective-permute-start(bf16[512,384]{1,0:T(8,128)(2,1)S(1)} %get-tuple-element.81), channel_id=1, source_target_pairs={{0,2},{1,3},{2,0},{3,1},{4,6},{5,7},{6,4},{7,5},{8,10},{9,11},{10,... | collective-permute-start | bytes 1179656 | tf_op jit(solution)/shard_map/ppermute | solution.py:488
  100.5 23.8 %collective-permute-start.8 = (bf16[512,384]{1,0:T(8,128)(2,1)S(1)}, bf16[512,384]{1,0:T(8,128)(2,1)S(1)}, u32[]{:S(2)}, u32[]{:S(2)}) collective-permute-start(bf16[512,384]{1,0:T(8,128)(2,1)S(1)} %get-tuple-element.85), channel_id=1, source_target_pairs={{0,2},{1,3},{2,0},{3,1},{4,6},{5,7},{6,4},{7,5},{8,10},{9,11},{10,... | collective-permute-start | bytes 1179656 | tf_op jit(solution)/shard_map/ppermute | solution.py:488
  105.7 14.0 %collective-permute-start.7 = (bf16[512,256]{1,0:T(8,128)(2,1)S(1)}, bf16[512,256]{1,0:T(8,128)(2,1)S(1)}, u32[]{:S(2)}, u32[]{:S(2)}) collective-permute-start(bf16[512,256]{1,0:T(8,128)(2,1)S(1)} %get-tuple-element.84), channel_id=1, source_target_pairs={{0,4},{4,0},{8,12},{12,8},{16,20},{20,16},{24,28},{28,24},{1,5},{5... | collective-permute-start | bytes 786440 | tf_op jit(solution)/shard_map/ppermute | solution.py:488
  107.9 20.6 %collective-permute-start.5 = (bf16[256,384]{1,0:T(8,128)(2,1)S(1)}, bf16[256,384]{1,0:T(8,128)(2,1)S(1)}, u32[]{:S(2)}, u32[]{:S(2)}) collective-permute-start(bf16[256,384]{1,0:T(8,128)(2,1)S(1)} %get-tuple-element.89), channel_id=1, source_target_pairs={{0,2},{1,3},{2,0},{3,1},{4,6},{5,7},{6,4},{7,5},{8,10},{9,11},{10,... | collective-permute-start | bytes 589832 | tf_op jit(solution)/shard_map/ppermute | solution.py:488
  114.1 14.3 %collective-permute-start.6 = (bf16[256,384]{1,0:T(8,128)(2,1)S(1)}, bf16[256,384]{1,0:T(8,128)(2,1)S(1)}, u32[]{:S(2)}, u32[]{:S(2)}) collective-permute-start(bf16[256,384]{1,0:T(8,128)(2,1)S(1)} %get-tuple-element.90), channel_id=1, source_target_pairs={{0,4},{4,0},{8,12},{12,8},{16,20},{20,16},{24,28},{28,24},{1,5},{5... | collective-permute-start | bytes 589832 | tf_op jit(solution)/shard_map/ppermute | solution.py:488
  116.3 16.4 %collective-permute-start.13 = (bf16[256,384]{1,0:T(8,128)(2,1)S(1)}, bf16[256,384]{1,0:T(8,128)(2,1)S(1)}, u32[]{:S(2)}, u32[]{:S(2)}) collective-permute-start(bf16[256,384]{1,0:T(8,128)(2,1)S(1)} %get-tuple-element.94), channel_id=1, source_target_pairs={{0,2},{1,3},{2,0},{3,1},{4,6},{5,7},{6,4},{7,5},{8,10},{9,11},{10,... | collective-permute-start | bytes 589832 | tf_op jit(solution)/shard_map/ppermute | solution.py:488
  119.7 12.9 %collective-permute-start.14 = (bf16[256,384]{1,0:T(8,128)(2,1)S(1)}, bf16[256,384]{1,0:T(8,128)(2,1)S(1)}, u32[]{:S(2)}, u32[]{:S(2)}) collective-permute-start(bf16[256,384]{1,0:T(8,128)(2,1)S(1)} %get-tuple-element.95), channel_id=1, source_target_pairs={{0,4},{4,0},{8,12},{12,8},{16,20},{20,16},{24,28},{28,24},{1,5},{5... | collective-permute-start | bytes 589832 | tf_op jit(solution)/shard_map/ppermute | solution.py:488
  128.6 6.2 %collective-permute-start.11 = (bf16[128,768]{1,0:T(8,128)(2,1)S(1)}, bf16[128,768]{1,0:T(8,128)(2,1)S(1)}, u32[]{:S(2)}, u32[]{:S(2)}) collective-permute-start(bf16[128,768]{1,0:T(8,128)(2,1)S(1)} %get-tuple-element.103), channel_id=1, source_target_pairs={{0,8},{4,12},{8,0},{12,4},{16,24},{20,28},{24,16},{28,20},{1,9},{5... | collective-permute-start | bytes 589832 | tf_op jit(solution)/shard_map/ppermute | solution.py:488
  130.2 7.2 %collective-permute-start.17 = (bf16[256,256]{1,0:T(8,128)(2,1)S(1)}, bf16[256,256]{1,0:T(8,128)(2,1)S(1)}, u32[]{:S(2)}, u32[]{:S(2)}) collective-permute-start(bf16[256,256]{1,0:T(8,128)(2,1)S(1)} %get-tuple-element.98), channel_id=1, source_target_pairs={{0,2},{1,3},{2,0},{3,1},{4,6},{5,7},{6,4},{7,5},{8,10},{9,11},{10,... | collective-permute-start | bytes 393224 | tf_op jit(solution)/shard_map/ppermute | solution.py:488
  131.6 5.7 %collective-permute-start.18 = (bf16[256,384]{1,0:T(8,128)(2,1)S(1)}, bf16[256,384]{1,0:T(8,128)(2,1)S(1)}, u32[]{:S(2)}, u32[]{:S(2)}) collective-permute-start(bf16[256,384]{1,0:T(8,128)(2,1)S(1)} %get-tuple-element.99), channel_id=1, source_target_pairs={{0,4},{4,0},{8,12},{12,8},{16,20},{20,16},{24,28},{28,24},{1,5},{5... | collective-permute-start | bytes 589832 | tf_op jit(solution)/shard_map/ppermute | solution.py:488
  132.8 10.7 %collective-permute-start.15 = (bf16[128,768]{1,0:T(8,128)(2,1)S(1)}, bf16[128,768]{1,0:T(8,128)(2,1)S(1)}, u32[]{:S(2)}, u32[]{:S(2)}) collective-permute-start(bf16[128,768]{1,0:T(8,128)(2,1)S(1)} %get-tuple-element.107), channel_id=1, source_target_pairs={{0,8},{4,12},{8,0},{12,4},{16,24},{20,28},{24,16},{28,20},{1,9},{5... | collective-permute-start | bytes 589832 | tf_op jit(solution)/shard_map/ppermute | solution.py:488
  134.9 8.7 %collective-permute-start.12 = (bf16[64,768]{1,0:T(8,128)(2,1)S(1)}, bf16[64,768]{1,0:T(8,128)(2,1)S(1)}, u32[]{:S(2)}, u32[]{:S(2)}) collective-permute-start(bf16[64,768]{1,0:T(8,128)(2,1)S(1)} %slice.50), channel_id=1, source_target_pairs={{0,16},{4,20},{8,24},{12,28},{16,0},{20,4},{24,8},{28,12},{1,17},{... | collective-permute-start | bytes 294920 | tf_op jit(solution)/shard_map/ppermute | solution.py:488
  137.5 7.7 %collective-permute-start.19 = (bf16[128,640]{1,0:T(8,128)(2,1)S(1)}, bf16[128,640]{1,0:T(8,128)(2,1)S(1)}, u32[]{:S(2)}, u32[]{:S(2)}) collective-permute-start(bf16[128,640]{1,0:T(8,128)(2,1)S(1)} %get-tuple-element.111), channel_id=1, source_target_pairs={{0,8},{4,12},{8,0},{12,4},{16,24},{20,28},{24,16},{28,20},{1,9},{5... | collective-permute-start | bytes 491528 | tf_op jit(solution)/shard_map/ppermute | solution.py:488
  143.5 8.3 %collective-permute-start.16 = (bf16[64,768]{1,0:T(8,128)(2,1)S(1)}, bf16[64,768]{1,0:T(8,128)(2,1)S(1)}, u32[]{:S(2)}, u32[]{:S(2)}) collective-permute-start(bf16[64,768]{1,0:T(8,128)(2,1)S(1)} %slice.49), channel_id=1, source_target_pairs={{0,16},{4,20},{8,24},{12,28},{16,0},{20,4},{24,8},{28,12},{1,17},{... | collective-permute-start | bytes 294920 | tf_op jit(solution)/shard_map/ppermute | solution.py:488
  145.3 7.4 %collective-permute-start.20 = (bf16[64,640]{1,0:T(8,128)(2,1)S(1)}, bf16[64,640]{1,0:T(8,128)(2,1)S(1)}, u32[]{:S(2)}, u32[]{:S(2)}) collective-permute-start(bf16[64,640]{1,0:T(8,128)(2,1)S(1)} %slice.51), channel_id=1, source_target_pairs={{0,16},{4,20},{8,24},{12,28},{16,0},{20,4},{24,8},{28,12},{1,17},{... | collective-permute-start | bytes 245768 | tf_op jit(solution)/shard_map/ppermute | solution.py:488

commit v6 on v4

--- a/solution.py
+++ b/solution.py
@@ -53,7 +53,7 @@
             bytes_accessed=bank.shape[0] * emb * 2,
             transcendentals=rows * bank.shape[0],
         ),
-        compiler_params=params(),
+        compiler_params=params(44),
         name="negatives",
     )(q, bank)
 
@@ -64,7 +64,7 @@
 SOON = pl.CostEstimate(flops=1, bytes_accessed=1, transcendentals=0)
 
 
-def params(limit=56):
+def params(limit=24):
     return pltpu.CompilerParams(
         dimension_semantics=("arbitrary",), vmem_limit_bytes=limit * MIB
     )
@@ -158,7 +158,7 @@
         cost_estimate=pl.CostEstimate(
             flops=2 * rows * d * (hid + rows), bytes_accessed=2 * d * hid, transcendentals=0
         ),
-        compiler_params=params(),
+        compiler_params=params(50),
         name="key_hidden",
     )(flat_col, k, w)
 
@@ -185,7 +185,18 @@
     )(part)
 
 
-def query_kernel(x_ref, w_ref, w2_ref, n_ref, inv_ref, z_ref, q_ref, sum_ref):
+def place_rows(order_ref, which, first, rows, t, out_ref):
+    for i in range(t.shape[0] // (2 * rows)):
+        at = order_ref[which, first + i]
+        core = order_ref[2, 0]
+        out_ref[core, at] = t[2 * i * rows:(2 * i + 1) * rows]
+        out_ref[1 - core, at] = t[(2 * i + 1) * rows:(2 * i + 2) * rows]
+
+
+def query_kernel(
+    rows_of_block, order_ref, x_ref, w_ref, w2_ref,
+    n_ref, inv_ref, z_ref, q_ref, xt_ref, xt3_ref, at3_ref, sum_ref,
+):
     i = pl.program_id(0)
     rows = x_ref.shape[0]
 
@@ -202,8 +213,14 @@
         normed = ((h - mu) * inv).astype(jnp.bfloat16)
         n_ref[:, t:t + TILE] = normed
         inv_ref[:, t:t + TILE] = inv
-        term = dot(jnp.maximum(normed, 0), w2_ref[t:t + TILE, :])
+        active = jnp.maximum(normed, 0)
+        term = dot(active, w2_ref[t:t + TILE, :])
         z = term if z is None else z + term
+        block = (i * STEP + t) // (2 * rows_of_block)
+        own = x_ref[:, pl.ds(pl.multiple_of(i * STEP + t, TILE), TILE)].T
+        place_rows(order_ref, 0, block, rows_of_block, own, xt_ref)
+        place_rows(order_ref, 1, block, rows_of_block, own, xt3_ref)
+        place_rows(order_ref, 1, block, rows_of_block, active.T, at3_ref)
     sum_ref[...] += z
 
     @pl.when(i == pl.num_programs(0) - 1)
@@ -214,71 +231,48 @@
         q_ref[...] = q.astype(jnp.bfloat16)
 
 
-def query_forward(x, w, w2):
+def query_forward(order, blocks, x, w, w2):
     rows, d = x.shape
     hid, emb = w2.shape
-    return pl.pallas_call(
-        query_kernel,
-        grid=(hid // STEP,),
-        in_specs=[
-            whole((rows, d)),
-            pl.BlockSpec((d, STEP), lambda i: (0, i)),
-            pl.BlockSpec((STEP, emb), lambda i: (i, 0)),
-        ],
-        out_specs=[
-            pl.BlockSpec((rows, STEP), lambda i: (0, i)),
-            pl.BlockSpec((1, STEP), lambda i: (0, i)),
-            whole((rows, emb)),
-            whole((rows, emb)),
-        ],
+    half, size = blocks // 2, d // blocks
+    turned = jax.ShapeDtypeStruct((2, half, size, rows), jnp.bfloat16)
+    out = pl.pallas_call(
+        lambda *refs: query_kernel(size, *refs),
+        grid_spec=pltpu.PrefetchScalarGridSpec(
+            num_scalar_prefetch=1,
+            grid=(hid // STEP,),
+            in_specs=[
+                whole((rows, d)),
+                pl.BlockSpec((d, STEP), lambda i, o: (0, i)),
+                pl.BlockSpec((STEP, emb), lambda i, o: (i, 0)),
+            ],
+            out_specs=[
+                pl.BlockSpec((rows, STEP), lambda i, o: (0, i)),
+                pl.BlockSpec((1, STEP), lambda i, o: (0, i)),
+                whole((rows, emb)),
+                whole((rows, emb)),
+                whole(turned.shape),
+                whole(turned.shape),
+                whole(turned.shape),
+            ],
+            scratch_shapes=[pltpu.VMEM((rows, emb), jnp.float32)],
+        ),
         out_shape=[
             jax.ShapeDtypeStruct((rows, hid), jnp.bfloat16),
             jax.ShapeDtypeStruct((1, hid), jnp.float32),
             jax.ShapeDtypeStruct((rows, emb), jnp.float32),
             jax.ShapeDtypeStruct((rows, emb), jnp.bfloat16),
+            turned,
+            turned,
+            turned,
         ],
-        scratch_shapes=[pltpu.VMEM((rows, emb), jnp.float32)],
         cost_estimate=pl.CostEstimate(
             flops=2 * rows * hid * (d + emb), bytes_accessed=2 * d * hid, transcendentals=0
         ),
-        compiler_params=params(),
+        compiler_params=params(44),
         name="query_forward",
-    )(x, w, w2)
-
-
-def order_kernel(positive, order_ref, x_ref, y_ref):
-    rows = y_ref.shape[2]
-    core = order_ref[pl.num_programs(0)]
-    t = x_ref[...]
-    if positive:
-        t = jnp.maximum(t, 0)
-    t = t.T
-    y_ref[core, 0] = t[:rows]
-    y_ref[1 - core, 0] = t[rows:]
-
-
-def ordered(x, order, core, blocks, positive):
-    n, d = x.shape
-    half = blocks // 2
-    rows = d // blocks
-    width = 2 * rows
-    if width % 128:
-        y = (jnp.maximum(x, 0) if positive else x).T.reshape(half, 2, rows, n)
-        y = jnp.zeros_like(y).at[order].set(y)
-        return jnp.moveaxis(jnp.where(core == 0, y, y[:, ::-1]), 1, 0).reshape(d, n)
-    return pl.pallas_call(
-        lambda *refs: order_kernel(positive, *refs),
-        grid_spec=pltpu.PrefetchScalarGridSpec(
-            num_scalar_prefetch=1,
-            grid=(half,),
-            in_specs=[pl.BlockSpec((n, width), lambda i, o: (0, i))],
-            out_specs=pl.BlockSpec((2, 1, rows, n), lambda i, o: (0, o[i], 0, 0)),
-        ),
-        out_shape=jax.ShapeDtypeStruct((2, half, rows, n), x.dtype),
-        cost_estimate=pl.CostEstimate(flops=0, bytes_accessed=8 * n * d, transcendentals=0),
-        compiler_params=params(),
-        name="ordered",
-    )(jnp.append(order, core), x).reshape(d, n)
+    )(order, x, w, w2)
+    return (*out[:4], *(t.reshape(d, rows) for t in out[4:]))
 
 
 def embed_kernel(all_rows, flat_ref, h_ref, told_ref, w2_ref, zq_ref, neg_ref, dz_ref, z_ref):
@@ -345,16 +339,19 @@
         cost_estimate=pl.CostEstimate(
             flops=2 * rows * hid * emb, bytes_accessed=4 * rows * hid, transcendentals=0
         ),
-        compiler_params=params(),
+        compiler_params=params(30),
         name="embed",
     )(flat_row, h, told, w2, zq, negs)
 
 
-def store_rows(out_ref, at, value, crossed):
-    size = value.shape[0] // 4
-    for i, j in enumerate((0, 2, 1, 3)):
-        j = j if crossed else i
-        out_ref[i * size:(i + 1) * size, at] = value[j * size:(j + 1) * size].astype(out_ref.dtype)
+def store_rows(out_ref, at, value, crossed, size):
+    if not crossed:
+        out_ref[:, at] = value.astype(out_ref.dtype)
+        return
+    for four in range(0, value.shape[0], 4 * size):
+        for i, j in enumerate((0, 2, 1, 3)):
+            i, j = four + i * size, four + j * size
+            out_ref[i:i + size, at] = value[j:j + size].astype(out_ref.dtype)
 
 
 def column_tiles(cols):
@@ -364,29 +361,29 @@
             yield slice(t, min(t + TILE, end)), start > 0
 
 
-def keep_rows(keep_ref, xt_ref, dh_ref, at_ref, dz_ref):
+def keep_rows(keep_ref, xt_ref, dh_ref, size, at_ref=None, dz_ref=None):
     cols = dh_ref.shape[1]
     for at, crossed in column_tiles(cols):
-        store_rows(keep_ref, at, dot(xt_ref[...], dh_ref[:, at]), crossed)
+        store_rows(keep_ref, at, dot(xt_ref[...], dh_ref[:, at]), crossed, size)
     if at_ref is not None:
-        store_rows(keep_ref, slice(cols, None), dot(at_ref[...], dz_ref[...]), True)
-
-
-def send_kernel(has_old, has_at, count, *refs):
+        store_rows(keep_ref, slice(cols, None), dot(at_ref[...], dz_ref[...]), True, size)
+
+
+def send_kernel(sizes, has_old, has_at, *refs):
     refs = list(refs)
-    dz_ref, xt_ref = refs[:2]
-    refs = refs[2:]
+    count = len(sizes)
+    dz_ref = refs.pop(0)
     at_ref = refs.pop(0) if has_at else None
     dz = dz_ref[...]
     rows = dz.shape[0]
     if has_old:
         old_xt_ref, old_ref = refs[:2]
         refs = refs[2:]
-    ins, outs = refs[:3 * count], refs[3 * count:]
+    ins, outs = refs[:4 * count], refs[4 * count:]
     if has_old:
-        keep_rows(outs.pop(0), old_xt_ref, old_ref, None, None)
+        keep_rows(outs.pop(0), old_xt_ref, old_ref, sizes[0])
     for p in range(count):
-        w2_ref, n_ref, inv_ref = ins[3 * p:3 * p + 3]
+        xt_ref, w2_ref, n_ref, inv_ref = ins[4 * p:4 * p + 4]
         dh_ref, sent_ref = outs[2 * p:2 * p + 2]
         cols = n_ref.shape[1]
         for at, crossed in column_tiles(cols):
@@ -397,26 +394,28 @@
             d_hidden = inv_ref[:, at] * (d_norm - mean - normed * slope)
             d_hidden = d_hidden.astype(jnp.bfloat16)
             dh_ref[:, at] = d_hidden
-            store_rows(sent_ref, at, dot(xt_ref[...], d_hidden), crossed)
+            store_rows(sent_ref, at, dot(xt_ref[...], d_hidden), crossed, sizes[p])
         if has_at and p == count - 1:
-            store_rows(sent_ref, slice(cols, None), dot(at_ref[...], dz), True)
-
-
-def send_half(dz, xt, at, old, w2, normed, inv, pairs):
+            store_rows(sent_ref, slice(cols, None), dot(at_ref[...], dz), True, sizes[p])
+
+
+def send_half(dz, at, old, w2, normed, inv, pairs):
     rows, emb = dz.shape
-    half = xt.shape[0] // 2
-    operands, in_specs = [dz, xt], [whole(dz.shape), pl.BlockSpec((half, rows), lambda i: (1, 0))]
-    shapes = []
+    operands, in_specs, shapes = [dz], [whole(dz.shape)], []
     if at is not None:
+        half = at.shape[0] // 2
         operands.append(at)
         in_specs.append(pl.BlockSpec((half, rows), lambda i: (1, 0)))
     if old is not None:
-        operands += [xt, old]
-        in_specs += [whole((half, rows)), whole(old.shape)]
-        shapes.append(jax.ShapeDtypeStruct((half, old.shape[1]), jnp.float32))
-    for p, (place, cols) in enumerate(pairs):
-        operands += [w2, normed, inv]
+        half = old[0].shape[0] // 2
+        operands += list(old)
+        in_specs += [whole((half, rows)), whole(old[1].shape)]
+        shapes.append(jax.ShapeDtypeStruct((half, old[1].shape[1]), jnp.float32))
+    for p, (xt, place, cols, _) in enumerate(pairs):
+        half = xt.shape[0] // 2
+        operands += [xt, w2, normed, inv]
         in_specs += [
+            pl.BlockSpec((half, rows), lambda i: (1, 0)),
             pl.BlockSpec((cols, emb), lambda i, place=place: (place, 0)),
             pl.BlockSpec((rows, cols), lambda i, place=place: (0, place)),
             pl.BlockSpec((1, cols), lambda i, place=place: (0, place)),
@@ -424,14 +423,15 @@
         extra = emb if at is not None and p == len(pairs) - 1 else 0
         shapes.append(jax.ShapeDtypeStruct((rows, cols), jnp.bfloat16))
         shapes.append(jax.ShapeDtypeStruct((half, cols + extra), jnp.bfloat16))
+    sizes = [size for *_, size in pairs]
     return pl.pallas_call(
-        lambda *refs: send_kernel(old is not None, at is not None, len(pairs), *refs),
+        lambda *refs: send_kernel(sizes, old is not None, at is not None, *refs),
         grid=(1,),
         in_specs=in_specs,
         out_specs=[whole(shape.shape) for shape in shapes],
         out_shape=shapes,
         cost_estimate=pl.CostEstimate(
-            flops=2 * rows * half * sum(cols for _, cols in pairs),
+            flops=2 * rows * half * sum(cols for _, _, cols, _ in pairs),
             bytes_accessed=8 * rows * half,
             transcendentals=0,
         ),
@@ -440,27 +440,27 @@
     )(*operands)
 
 
-def keep_half(dz, dh, xt, at):
+def keep_half(dz, dh, xt, at, size, made, place):
     rows, emb = dz.shape
-    half = xt.shape[0] // 2
     cols = dh.shape[1]
+    block = pl.BlockSpec((made, rows), lambda i: (place, 0))
     operands = [xt, dh]
-    in_specs = [whole((half, rows)), whole((rows, cols))]
+    in_specs = [block, whole((rows, cols))]
     if at is None:
-        kernel = lambda x, d, g: keep_rows(g, x, d, None, None)
+        kernel = lambda x, d, g: keep_rows(g, x, d, size)
     else:
-        kernel = lambda x, d, a, z, g: keep_rows(g, x, d, a, z)
+        kernel = lambda x, d, a, z, g: keep_rows(g, x, d, size, a, z)
         operands += [at, dz]
-        in_specs += [whole((half, rows)), whole((rows, emb))]
+        in_specs += [block, whole((rows, emb))]
         cols += emb
     return pl.pallas_call(
         kernel,
         grid=(1,),
         in_specs=in_specs,
-        out_specs=whole((half, cols)),
-        out_shape=jax.ShapeDtypeStruct((half, cols), jnp.float32),
+        out_specs=whole((made, cols)),
+        out_shape=jax.ShapeDtypeStruct((made, cols), jnp.float32),
         cost_estimate=pl.CostEstimate(
-            flops=2 * rows * half * cols, bytes_accessed=8 * rows * half, transcendentals=0
+            flops=2 * rows * made * cols, bytes_accessed=8 * rows * made, transcendentals=0
         ),
         compiler_params=params(28),
         name="keep_half",
@@ -476,83 +476,96 @@
     return lax.optimization_barrier((x,) + others)[0]
 
 
-def fold_kernel(split, joined, *refs):
-    keep_ref, came_ref = refs[:2]
-    count = len(refs) - 4
-    sides = (refs[2:2 + count // 2], refs[2 + count // 2:2 + count])
-    outs = refs[-2:]
-    for side, cols in enumerate((slice(0, split), slice(split, keep_ref.shape[1]))):
-        v = keep_ref[:, cols] + came_ref[:, cols].astype(jnp.float32)
+def fold_kernel(split, form, counts, *refs):
+    both, left, right = counts
+    joined = refs[:both]
+    sides = (refs[both:both + left], refs[both + left:both + left + right])
+    outs = refs[both + left + right:]
+    for side, cols in enumerate((slice(0, split), slice(split, refs[0].shape[1]))):
+        v = joined[0][:, cols].astype(jnp.float32)
+        for ref in joined[1:]:
+            v = v + ref[:, cols].astype(jnp.float32)
         for ref in sides[side]:
             v = v + ref[...].astype(jnp.float32)
-        if joined:
+        if form == "halves":
             half = v.shape[0] // 2
             outs[0][:, cols] = v[:half]
             outs[1][:, cols] = v[half:].astype(jnp.bfloat16)
+        elif form == "sides":
+            outs[side][...] = v.astype(jnp.bfloat16)
         else:
-            outs[side][...] = v.astype(jnp.bfloat16)
-
-
-def fold(keep, came, left, right, split, rows, place, joined):
+            outs[0][:, cols] = v.astype(outs[0].dtype)
+
+
+def fold(keep, keep_place, both, left, right, split, rows, place, form):
     cols = keep.shape[1]
 
-    def spec(width):
+    def spec(width, place=place):
         return pl.BlockSpec((rows, width), lambda i: (place, 0))
 
-    if joined:
-        shapes = [
-            jax.ShapeDtypeStruct((rows // 2, cols), jnp.float32),
-            jax.ShapeDtypeStruct((rows // 2, cols), jnp.bfloat16),
-        ]
-    else:
-        shapes = [
-            jax.ShapeDtypeStruct((rows, split), jnp.bfloat16),
-            jax.ShapeDtypeStruct((rows, cols - split), jnp.bfloat16),
-        ]
+    low, full = jnp.bfloat16, jnp.float32
+    shapes = {
+        "halves": [((rows // 2, cols), full), ((rows // 2, cols), low)],
+        "sides": [((rows, split), low), ((rows, cols - split), low)],
+        "send": [((rows, cols), low)],
+        "own": [((rows, cols), full)],
+    }[form]
+    in_specs = [spec(cols, keep_place)] + [spec(cols)] * len(both)
+    in_specs += [spec(split)] * len(left) + [spec(cols - split)] * len(right)
     return pl.pallas_call(
-        lambda *refs: fold_kernel(split, joined, *refs),
+        lambda *refs: fold_kernel(split, form, (1 + len(both), len(left), len(right)), *refs),
         grid=(1,),
-        in_specs=[spec(cols)] * 2 + [spec(split)] * len(left) + [spec(cols - split)] * len(right),
-        out_specs=[whole(shape.shape) for shape in shapes],
-        out_shape=shapes,
+        in_specs=in_specs,
+        out_specs=[whole(shape) for shape, _ in shapes],
+        out_shape=[jax.ShapeDtypeStruct(*shape) for shape in shapes],
         cost_estimate=SOON,
         compiler_params=params(16),
         name="fold",
-    )(keep, came, *left, *right)
+    )(keep, *both, *left, *right)
 
 
 class Pair:
     def __init__(self, keep, came, split):
-        self.keep, self.came, self.split = keep, came, split
+        self.keep, self.both, self.split = keep, [came], split
         self.left, self.right = [], []
-        self.half = keep.shape[0]
-
-    def first(self):
-        rows = self.half // 2
-        out = fold(self.keep, self.came, [], [], self.split, rows, 1, False)
-        return out
+
+    def hold(self, *others):
+        for came in (self.both, self.left, self.right):
+            if came:
+                came[-1] = after(came[-1], *others)
+
+    def add(self, rows, place, form):
+        keep, keep_place = self.keep, place
+        if isinstance(keep, list):
+            keep, start = keep[-1]
+            keep_place = (place * rows - start) // rows
+        out = fold(
+            keep, keep_place, self.both, self.left, self.right, self.split, rows, place, form
+        )
+        return lax.optimization_barrier(out)
 
     def cross_first(self, out):
         self.left.append(swap(out[0], "dp", 1))
         self.right.append(swap(out[1], "crop", 2))
 
-    def second(self):
-        rows = self.half // 4
-        return fold(self.keep, self.came, self.left, self.right, self.split, rows, 1, False)
-
     def cross_second(self, out):
         self.left.append(swap(out[0], "crop", 2))
         self.right.append(swap(out[1], "dp", 1))
 
-    def third(self):
-        rows = self.half // 4
-        return fold(self.keep, self.came, self.left, self.right, self.split, rows, 0, True)
+    def cross_line_apart(self, out):
+        self.left.append(swap(out[0], "dp", 2))
+        self.right.append(swap(out[1], "dp", 2))
+
+    def cross_line(self, out, bit):
+        self.both.append(swap(out[0], "dp", 2 * bit))
 
     def cross_third(self, out):
         own, send = out
+        return own + swap(send, "dp", 2).astype(jnp.float32)
+
+    def cross_rest(self, own):
         length = lax.axis_size("dp") // 2
         bit = 1
-        own = own + swap(send, "dp", 2 * bit).astype(jnp.float32)
         while 2 * bit < length:
             bit *= 2
             half = own.shape[0] // 2
@@ -584,63 +597,83 @@
     dp, crop = lax.axis_index("dp"), lax.axis_index("crop")
     block = lax.iota(jnp.int32, group_count // 2)
     z, x, y = block // n_crop, (block // (n_crop // 2)) % 2, block % (n_crop // 2)
-    order = (x ^ (dp % 2)) * (n_crop // 2) + (y ^ (crop // 2))
+    plane = (x ^ (dp % 2)) * (n_crop // 2) + (y ^ (crop // 2))
+    line = jnp.zeros_like(block)
     for bit in range(bits):
-        order = order * 2 + (((z ^ (dp // 2)) >> bit) & 1)
-    core = crop % 2
-
-    normed, inv_q, z_q, q_low = query_forward(
-        after(query_crops, sums), query_inner, query_outer
-    )
-    xt = ordered(query_crops, order, core, group_count, False)
-    came, q_low, flat_row, xt = lax.optimization_barrier((came, q_low, flat_row, xt))
+        line = line * 2 + (((z ^ (dp // 2)) >> bit) & 1)
+    order = jnp.stack(
+        [plane * length + line, line * n_crop + plane, jnp.full_like(block, crop % 2)]
+    )
+
+    normed, inv_q, z_q, q_low, xt, xt3, at3 = query_forward(
+        order, group_count, after(query_crops, sums), query_inner, query_outer
+    )
+    came, q_low, flat_row = lax.optimization_barrier((came, q_low, flat_row))
     told = batch(came, row_count)
     told = lax.all_to_all(told, AXES, split_axis=0, concat_axis=0, tiled=True)
 
     negs = negatives(q_low, distractor_bank)
-    at = ordered(normed, order, core, group_count, True)
-
-    told, negs, at = lax.optimization_barrier((told, negs, at))
+    told, negs = lax.optimization_barrier((told, negs))
     d_z = embed(flat_row, hidden_k, told, key_outer, z_q, negs, all_rows)
 
     def send(last, old, pairs):
-        return send_half(d_z, xt, last, old, query_outer, normed, inv_q, pairs)
+        return send_half(d_z, last, old, query_outer, normed, inv_q, pairs)
 
     large = hid // 8 * 3
     small = hid - 2 * large
-    dh_1, sent_1 = send(None, None, [(0, large)])
+    half = xt.shape[0] // 2
+    size, size_3 = half // 4, half // (4 * length)
+    dh_1, sent_1 = send(None, None, [(xt, 0, large, size)])
     came_1 = swap(sent_1, "crop", 1)
     keep_1, dh_2, sent_2, dh_3, sent_3 = send(
-        at, dh_1, [(1, large), (2 * large // small, small)]
+        at3, (xt, dh_1), [(xt, 1, large, size), (xt3, 2 * large // small, small, size_3)]
     )
     came_2 = swap(sent_2, "crop", 1)
     came_3 = swap(sent_3, "crop", 1)
     one = Pair(keep_1, came_1, large // 2)
-    a_1 = lax.optimization_barrier(one.first())
+    a_1 = one.add(half // 2, 1, "sides")
     one.cross_first(a_1)
-    keep_2 = keep_half(d_z, after(dh_2, *a_1), xt, None)
+    keep_2 = keep_half(d_z, after(dh_2, *a_1), xt, None, size, half, 0)
     two = Pair(keep_2, came_2, large // 2)
-    a_2 = lax.optimization_barrier(two.first())
+    a_2 = two.add(half // 2, 1, "sides")
     two.cross_first(a_2)
-    keep_3 = keep_half(d_z, after(dh_3, *a_2), xt, at)
-    one.left[0] = after(one.left[0], keep_3)
-    b_1 = lax.optimization_barrier(one.second())
+    upper = keep_half(d_z, after(dh_3, *a_2), xt3, at3, size_3, half // 2, 1)
+    three = Pair([(upper, half // 2)], came_3, small // 2)
+    rows = half // 2
+    l_3 = three.add(rows, 1, "sides")
+    three.cross_line_apart(l_3)
+    lower = keep_half(d_z, after(dh_3, *l_3), xt3, at3, size_3, half // 4, 1)
+    one.hold(lower)
+    b_1 = one.add(half // 4, 1, "sides")
     one.cross_second(b_1)
-    three = Pair(keep_3, after(came_3, *b_1), small // 2)
-    a_3 = lax.optimization_barrier(three.first())
-    three.cross_first(a_3)
-    two.left[0] = after(two.left[0], *a_3)
-    b_2 = lax.optimization_barrier(two.second())
+    lowest = keep_half(d_z, after(dh_3, *b_1), xt3, at3, size_3, half // 4, 0)
+    two.hold(lowest)
+    b_2 = two.add(half // 4, 1, "sides")
     two.cross_second(b_2)
-    one.left[1] = after(one.left[1], *b_2)
-    c_1 = lax.optimization_barrier(one.third())
-    three.left[0] = after(three.left[0], *c_1)
-    b_3 = lax.optimization_barrier(three.second())
-    three.cross_second(b_3)
-    own_1 = one.cross_third(c_1)
-    two.left[1] = after(two.left[1], *b_3)
-    own_2 = two.cross_third(two.third())
-    own_3 = three.cross_third(three.third())
+    held = b_2
+    for bit in range(1, bits):
+        rows //= 2
+        three.hold(*held)
+        three.keep = [(lower, half // 4) if bit == 1 else (lowest, 0)]
+        held = three.add(rows, 1, "send")
+        three.cross_line(held, 2 ** bit)
+    one.hold(*held)
+    c_1 = one.add(half // 4, 0, "halves")
+    two.hold(*c_1)
+    c_2 = two.add(half // 4, 0, "halves")
+    own_1 = lax.optimization_barrier(one.cross_third(c_1))
+    own_2 = lax.optimization_barrier(two.cross_third(c_2))
+    three.keep = [(lowest, 0)]
+    three.hold(own_1, own_2)
+    rows //= 2
+    e_3 = three.add(rows, 1, "sides")
+    three.cross_first(e_3)
+    rows //= 2
+    f_3 = three.add(rows, 1, "sides")
+    three.cross_second(f_3)
+    own_1 = one.cross_rest(own_1)
+    own_2 = two.cross_rest(own_2)
+    own_3 = three.add(rows, 0, "own")[0]
     grad_inner = jnp.concatenate([own_1, own_2, own_3[:, :small]], axis=1)
     return (grad_inner, own_3[:, small:])
 

time: 163 us -> 142 us (0.87)
  Pallas kernels: 74.4 us -> 45.1 us
  local copies, waits for them, and re-layouts: 5.25 us -> 15.2 us
  starting transfers between devices: 32.6 us -> 28.7 us
  waiting for transfers between devices: 32 us -> 34.4 us
    pallas_call x16 -> x18, Pallas kernels: 42.5 us -> 20.8 us  [the longest x1 10.3 us: query_forward(): pl.pallas_call(lambda *refs: query_kernel(size, *refs), grid_spec=pltpu.P...]
    unnamed x16 -> x28, local copies, waits for them, and re-layouts: 2.5 us -> 13.7 us
    pallas_call x1, Pallas kernels: 6.03 us -> 2.78 us  [embed(): pl.pallas_call(lambda *refs: embed_kernel(all_rows, *refs), grid=(hid //...]
    ppermute x21 -> x22, starting transfers between devices: 24.1 us -> 21.1 us  [swap(): return lax.ppermute(x, axis, [(i, i ^ bit) for i in range(size)])]
    pallas_call x1, Pallas kernels: 12.9 us -> 11 us  [negatives(): pl.pallas_call(neg_kernel, grid=(bank.shape[0] // tile,), in_specs=[pl.Bl...]
    pallas_call x1, Pallas kernels: 2.09 us -> 0.24 us  [batch(): pl.pallas_call(lambda *refs: batch_kernel(rows, *refs), grid=(1,), in_spe...]
    ppermute x21 -> x22, waiting for transfers between devices: 32 us -> 32 us  [swap(): return lax.ppermute(x, axis, [(i, i ^ bit) for i in range(size)])]
  transfers between devices with their start and end apart: 23 -> 24, of which waited for: 14 -> 10; matrix products, arithmetic and copies ran while one was open for 1% -> 0% of each run, Pallas kernels for 33% -> 21%
where the time goes in v6:
time: 142 us; the launch traced here: 141 us
  Pallas kernels  45.1 us (32%)
  waiting for transfers between devices  34.4 us (24%)
  starting transfers between devices  28.7 us (20%)
  local copies, waits for them, and re-layouts  15.2 us (11%)
  blocking collectives  14.2 us (10%)
  other arithmetic  2.4 us (2%)
    ppermute x22, waiting for transfers between devices, swap(): return lax.ppermute(x, axis, [(i, i ^ bit) for i in range(size)])  32 us
    ppermute x22, starting transfers between devices, swap(): return lax.ppermute(x, axis, [(i, i ^ bit) for i in range(size)])  21.1 us
    all_to_all x1, blocking collectives, per_device(): lax.all_to_all(wanted, AXES, split_axis=0, concat_axis=0, tiled=True)  14.2 us
    unnamed x28, local copies, waits for them, and re-layouts  13.7 us
    pallas_call x1, Pallas kernels, negatives(): pl.pallas_call(neg_kernel, grid=(bank.shape[0] // tile,), in_specs=[pl.Bl...  11 us
    pallas_call x1, Pallas kernels, key_hidden(): pl.pallas_call(lambda *refs: key_hidden_kernel(groups, *refs), grid=(hid...  10.3 us
    pallas_call x1, Pallas kernels, query_forward(): pl.pallas_call(lambda *refs: query_kernel(size, *refs), grid_spec=pltpu.P...  10.3 us
    pallas_call x2, Pallas kernels, send_half(): pl.pallas_call(lambda *refs: send_kernel(sizes, old is not None, at is no...  6.65 us
  transfers between devices with their start and end apart: 24, of which 10 were waited for; matrix products, arithmetic and copies ran while one was open for 0% of the time, Pallas kernels for 21%

profile of v6, /device:TPU:0, one launch (start us, length us, event | category | flops | bytes accessed | tf_op | source)
XLA Modules:
  0.0 141.1 jit_solution(8314135703504951828)
XLA Ops:
  0.6 0.7 add_select_fusion
  1.4 14.2 %all_to_all.19 = s32[32,1,16]{2,1,0:T(1,128)S(1)} all-to-all(s32[32,1,16]{2,1,0:T(1,128)S(1)} %bitcast.19), channel_id=1, replica_groups=mesh['dp'=8,'crop'=4] {'dp','crop'}, dimensions={0} | all-to-all | bytes 4096 | tf_op jit(solution)/shard_map/all_to_all | solution.py:588
  16.2 0.7 reduce.5
  17.0 1.6 %copy-done.13 = bf16[512,2048]{1,0:T(8,128)(2,1)S(1)} copy-done((bf16[512,2048]{1,0:T(8,128)(2,1)S(1)}, bf16[512,2048]{1,0:T(8,128)(2,1)}, u32[]{:S(2)}) %copy-start.13) | copy-done | bytes 2097176
  18.6 10.3 %key_hidden.1 = (f32[512,2048]{1,0:T(8,128)}, f32[32,1,4096]{2,1,0:T(1,128)}) custom-call(s32[512,1]{1,0:T(8,128)S(1)} %broadcast_in_dim_reshape.8.refs_0_, bf16[512,2048]{1,0:T(8,128)(2,1)S(1)} %copy-done.13, bf16[2048,2048]{1,0:T(8,128)(2,1)} %refs_2_.3), custom_call_target="tpu_custom_call" | custom-call | flops 5368709120 | bytes 8388608 | tf_op jit(solution)/shard_map/key_hidden/pallas_call | solution.py:141
  28.9 2.6 %all-to-all-start.1 = ((f32[32,1,4096]{2,1,0:T(1,128)}), f32[32,1,4096]{2,1,0:T(1,128)S(1)}, u32[]{:S(2)}, u32[]{:S(2)}) async-start(f32[32,1,4096]{2,1,0:T(1,128)} %get-tuple-element.64), calls=%async_computation.1 | async-start | bytes 1048576 | tf_op jit(solution)/shard_map/all_to_all | solution.py:593
  31.8 10.3 %query_forward.1 = (bf16[512,2048]{1,0:T(8,128)(2,1)S(1)}, f32[1,2048]{1,0:T(1,128)S(1)}, f32[512,128]{1,0:T(8,128)S(1)}, bf16[512,128]{1,0:T(8,128)(2,1)S(1)}, ...) custom-call(s32[3,16]{1,0:T(4,128)S(1)} %add_add_fusion.refs_0_, ...), custom_call_target="tpu_custom_call" | custom-call | flops 4563402752 | bytes 8388608 | tf_op jit(solution)/shard_map/query_forward/pallas_call | solution.py:239
  42.2 1.4 copy-done
  43.5 1.4 copy-done.2
  44.9 1.3 copy-done.4
  46.2 0.9 all-to-all-done.1.refs_0_
  47.4 0.8 copy-done.8
  48.1 5.0 %all-to-all-start.2 = ((f32[32,1,4096]{2,1,0:T(1,128)}), f32[32,1,4096]{2,1,0:T(1,128)S(1)}, u32[]{:S(2)}, u32[]{:S(2)}) async-start(f32[32,1,4096]{2,1,0:T(1,128)} %copy-done.8), calls=%async_computation.2 | async-start | bytes 1048576 | tf_op jit(solution)/shard_map/all_to_all | solution.py:613
  53.1 2.2 %copy-done.12 = bf16[16384,128]{1,0:T(8,128)(2,1)S(1)} copy-done((bf16[16384,128]{1,0:T(8,128)(2,1)S(1)}, bf16[16384,128]{1,0:T(8,128)(2,1)}, u32[]{:S(2)}) %copy-start.12) | copy-done | bytes 4194328
  55.3 11.0 %negatives.1.refs_5_ = f32[512,256]{1,0:T(8,128)S(1)} custom-call(bf16[512,128]{1,0:T(8,128)(2,1)S(1)} %get-tuple-element.70.q_ref, bf16[16384,128]{1,0:T(8,128)(2,1)S(1)} %copy-done.12), custom_call_target="tpu_custom_call" | custom-call | flops 4294967296 | bytes 4194304 | tf_op jit(solution)/shard_map/negatives/pallas_call | solution.py:42
  66.3 0.8 copy-done.10
  67.1 1.6 %all-to-all-done.2.refs_2_ = f32[32,1,4096]{2,1,0:T(1,128)S(1)} async-done(((f32[32,1,4096]{2,1,0:T(1,128)}), f32[32,1,4096]{2,1,0:T(1,128)S(1)}, u32[]{:S(2)}, u32[]{:S(2)}) %all-to-all-start.2) | async-done | bytes 524320 | tf_op jit(solution)/shard_map/all_to_all | solution.py:613
  68.7 2.2 %copy-done.7 = f32[512,2048]{1,0:T(8,128)S(1)} copy-done((f32[512,2048]{1,0:T(8,128)S(1)}, f32[512,2048]{1,0:T(8,128)}, u32[]{:S(2)}) %copy-start.7) | copy-done | bytes 4194328
  70.9 1.0 copy-done.9
  71.9 1.0 copy-done.11
  72.9 2.8 %embed.1.refs_0_.z = bf16[512,128]{1,0:T(8,128)(2,1)S(1)} custom-call(s32[1,512]{1,0:T(1,128)S(1)} %broadcast_in_dim_reshape.7.refs_0_, f32[512,2048]{1,0:T(8,128)S(1)} %copy-done.7, f32[32,1,4096]{2,1,0:T(1,128)S(1)} %all-to-all-done.2.refs_2_, bf16[2048,128]{1,0:T(8,128)(2,1)S(1)} %copy-done.9, f32[512,128]{1,0:T(8,128)S(1)} %get-tuple-element.72.refs_4_, ...), custom_call_target="tpu_custom_call" | custom-call | flops 268435456 | bytes 4194304 | tf_op jit(solution)/shard_map/embed/pallas_call | solution.py:325
  75.8 2.1 %send_half.2 = (bf16[512,768]{1,0:T(8,128)(2,1)S(1)}, bf16[1024,768]{1,0:T(8,128)(2,1)S(1)}) custom-call(bf16[512,128]{1,0:T(8,128)(2,1)S(1)} %embed.1.refs_0_.z, bf16[2048,512]{1,0:T(8,128)(2,1)S(1)} %bitcast.14, bf16[2048,128]{1,0:T(8,128)(2,1)S(1)} %copy-done.6, bf16[512,2048]{1,0:T(8,128)(2,1)S(1)} %copy-done.5, ...), custom_call_target="tpu_custom_call" | custom-call | flops 805306368 | bytes 4194304 | tf_op jit(solution)/shard_map/send_half/pallas_call | solution.py:427
  78.0 4.5 %send_half.3 = (f32[1024,768]{1,0:T(8,128)S(1)}, bf16[512,768]{1,0:T(8,128)(2,1)S(1)}, bf16[1024,768]{1,0:T(8,128)(2,1)S(1)}, bf16[512,512]{1,0:T(8,128)(2,1)S(1)}, bf16[1024,640]{1,0:T(8,128)(2,1)S(1)}) custom-call(bf16[512,128]{1,0:T(8,128)(2,1)S(1)} %embed.1.refs_0_.z, bf16[2048,512]{1,0:T(8,128)(2,1)S(1)} %bitcast.10, bf16[2048,512]{1,0:T(8,128)(2,1)S(1)} %bitcast.15, ...), custom_call_target="tpu_custom_call" | custom-call | flops 1342177280 | bytes 4194304 | tf_op jit(solution)/shard_map/send_half/pallas_call | solution.py:427
  83.3 1.3 collective-permute-start.3
  84.6 1.1 collective-permute-start.4
  85.8 1.2 keep_half.4.refs_0_
  87.2 0.9 collective-permute-start.6
  88.1 0.8 collective-permute-start.5
  89.6 1.3 collective-permute-start.8
  90.9 5.7 %collective-permute-done.4.refs_3_.refs_4_ = bf16[512,384]{1,0:T(8,128)(2,1)S(1)} collective-permute-done((bf16[512,384]{1,0:T(8,128)(2,1)S(1)}, bf16[512,384]{1,0:T(8,128)(2,1)S(1)}, u32[]{:S(2)}, u32[]{:S(2)}) %collective-permute-start.4) | collective-permute-done | bytes 393248 | tf_op jit(solution)/shard_map/ppermute | solution.py:472
  96.6 0.8 collective-permute-start.7
  97.9 1.3 collective-permute-start.10
  99.2 5.0 %collective-permute-done.6.refs_3_.refs_4_ = bf16[512,384]{1,0:T(8,128)(2,1)S(1)} collective-permute-done((bf16[512,384]{1,0:T(8,128)(2,1)S(1)}, bf16[512,384]{1,0:T(8,128)(2,1)S(1)}, u32[]{:S(2)}, u32[]{:S(2)}) %collective-permute-start.6) | collective-permute-done | bytes 393248 | tf_op jit(solution)/shard_map/ppermute | solution.py:472
  104.2 1.1 collective-permute-start.9
  105.9 0.9 collective-permute-start.13
  106.8 0.8 collective-permute-start.14
  107.7 4.4 %collective-permute-done.9.refs_3_ = bf16[256,384]{1,0:T(8,128)(2,1)S(1)} collective-permute-done((bf16[256,384]{1,0:T(8,128)(2,1)S(1)}, bf16[256,384]{1,0:T(8,128)(2,1)S(1)}, u32[]{:S(2)}, u32[]{:S(2)}) %collective-permute-start.9) | collective-permute-done | bytes 196640 | tf_op jit(solution)/shard_map/ppermute | solution.py:472
  112.2 0.9 collective-permute-start.11
  113.1 2.0 %collective-permute-start.17 = (bf16[256,640]{1,0:T(8,128)(2,1)S(1)}, bf16[256,640]{1,0:T(8,128)(2,1)S(1)}, u32[]{:S(2)}, u32[]{:S(2)}) collective-permute-start(bf16[256,640]{1,0:T(8,128)(2,1)S(1)} %fold.16), channel_id=1, source_target_pairs={{0,16},{4,20},{8,24},{12,28},{16,0},{20,4},{24,8},{28,12},{1,17},{... | collective-permute-start | bytes 983048 | tf_op jit(solution)/shard_map/ppermute | solution.py:472
  115.9 8.4 %collective-permute-done.11 = bf16[128,768]{1,0:T(8,128)(2,1)S(1)} collective-permute-done((bf16[128,768]{1,0:T(8,128)(2,1)S(1)}, bf16[128,768]{1,0:T(8,128)(2,1)S(1)}, u32[]{:S(2)}, u32[]{:S(2)}) %collective-permute-start.11) | collective-permute-done | bytes 196640 | tf_op jit(solution)/shard_map/ppermute | solution.py:472
  124.3 3.6 %collective-permute-done.15 = bf16[128,768]{1,0:T(8,128)(2,1)S(1)} collective-permute-done((bf16[128,768]{1,0:T(8,128)(2,1)S(1)}, bf16[128,768]{1,0:T(8,128)(2,1)S(1)}, u32[]{:S(2)}, u32[]{:S(2)}) %collective-permute-start.15) | collective-permute-done | bytes 196640 | tf_op jit(solution)/shard_map/ppermute | solution.py:472
  128.6 1.5 %collective-permute-start.12 = (bf16[64,768]{1,0:T(8,128)(2,1)S(1)}, bf16[64,768]{1,0:T(8,128)(2,1)S(1)}, u32[]{:S(2)}, u32[]{:S(2)}) collective-permute-start(bf16[64,768]{1,0:T(8,128)(2,1)S(1)} %slice.37), channel_id=1, source_target_pairs={{0,16},{4,20},{8,24},{12,28},{16,0},{20,4},{24,8},{28,12},{1,17},{... | collective-permute-start | bytes 294920 | tf_op jit(solution)/shard_map/ppermute | solution.py:472
  130.6 2.2 %collective-permute-start.16 = (bf16[64,768]{1,0:T(8,128)(2,1)S(1)}, bf16[64,768]{1,0:T(8,128)(2,1)S(1)}, u32[]{:S(2)}, u32[]{:S(2)}) collective-permute-start(bf16[64,768]{1,0:T(8,128)(2,1)S(1)} %slice.36), channel_id=1, source_target_pairs={{0,16},{4,20},{8,24},{12,28},{16,0},{20,4},{24,8},{28,12},{1,17},{... | collective-permute-start | bytes 294920 | tf_op jit(solution)/shard_map/ppermute | solution.py:472
  132.8 2.1 %collective-permute-done.18.refs_4_ = bf16[128,256]{1,0:T(8,128)(2,1)S(1)} collective-permute-done((bf16[128,256]{1,0:T(8,128)(2,1)S(1)}, bf16[128,256]{1,0:T(8,128)(2,1)S(1)}, u32[]{:S(2)}, u32[]{:S(2)}) %collective-permute-start.18) | collective-permute-done | bytes 65568 | tf_op jit(solution)/shard_map/ppermute | solution.py:472
  135.5 1.2 collective-permute-start.21
  136.7 2.1 %collective-permute-done.20.refs_5_ = bf16[64,256]{1,0:T(8,128)(2,1)S(1)} collective-permute-done((bf16[64,256]{1,0:T(8,128)(2,1)S(1)}, bf16[64,256]{1,0:T(8,128)(2,1)S(1)}, u32[]{:S(2)}, u32[]{:S(2)}) %collective-permute-start.20) | collective-permute-done | bytes 32800 | tf_op jit(solution)/shard_map/ppermute | solution.py:472
  138.9 0.7 collective-permute-done.21.refs_8_
  140.2 0.8 pad_maximum_fusion
  (69 shorter events, 7.5 us)
Async XLA Ops:
  17.0 1.6 %copy-start.13 = (bf16[512,2048]{1,0:T(8,128)(2,1)S(1)}, bf16[512,2048]{1,0:T(8,128)(2,1)}, u32[]{:S(2)}) copy-start(bf16[512,2048]{1,0:T(8,128)(2,1)} %refs_1_.1) | copy-start | bytes 6291460
  18.6 13.2 %copy-start.6 = (bf16[2048,128]{1,0:T(8,128)(2,1)S(1)}, bf16[2048,128]{1,0:T(8,128)(2,1)}, u32[]{:S(2)}) copy-start(bf16[2048,128]{1,0:T(8,128)(2,1)} %refs_9_.1) | copy-start | bytes 1572868
  28.9 18.2 %all-to-all-start.1 = ((f32[32,1,4096]{2,1,0:T(1,128)}), f32[32,1,4096]{2,1,0:T(1,128)S(1)}, u32[]{:S(2)}, u32[]{:S(2)}) async-start(f32[32,1,4096]{2,1,0:T(1,128)} %get-tuple-element.64), calls=%async_computation.1 | async-start | bytes 1048576 | tf_op jit(solution)/shard_map/all_to_all | solution.py:593
  42.2 1.4 copy-start
  43.5 1.4 copy-start.2
  44.9 1.3 copy-start.4
  47.3 0.8 copy-start.8
  48.1 20.5 %all-to-all-start.2 = ((f32[32,1,4096]{2,1,0:T(1,128)}), f32[32,1,4096]{2,1,0:T(1,128)S(1)}, u32[]{:S(2)}, u32[]{:S(2)}) async-start(f32[32,1,4096]{2,1,0:T(1,128)} %copy-done.8), calls=%async_computation.2 | async-start | bytes 1048576 | tf_op jit(solution)/shard_map/all_to_all | solution.py:613
  53.1 2.2 %copy-start.12 = (bf16[16384,128]{1,0:T(8,128)(2,1)S(1)}, bf16[16384,128]{1,0:T(8,128)(2,1)}, u32[]{:S(2)}) copy-start(bf16[16384,128]{1,0:T(8,128)(2,1)} %bank_ref.1) | copy-start | bytes 12582916
  66.3 0.8 copy-start.10
  68.7 2.2 %copy-start.7 = (f32[512,2048]{1,0:T(8,128)S(1)}, f32[512,2048]{1,0:T(8,128)}, u32[]{:S(2)}) copy-start(f32[512,2048]{1,0:T(8,128)} %get-tuple-element.68.refs_1_) | copy-start | bytes 12582916
  70.8 1.0 copy-start.9
  71.9 1.0 copy-start.11
  72.9 2.8 %copy-start.3 = (bf16[2,16,64,512]{3,2,1,0:T(8,128)(2,1)S(1)}, bf16[2,16,64,512]{3,2,1,0:T(8,128)(2,1)}, u32[]{:S(2)}) copy-start(bf16[2,16,64,512]{3,2,1,0:T(8,128)(2,1)} %copy-done.2) | copy-start | bytes 6291460
  72.9 2.8 %copy-start.5 = (bf16[512,2048]{1,0:T(8,128)(2,1)S(1)}, bf16[512,2048]{1,0:T(8,128)(2,1)}, u32[]{:S(2)}) copy-start(bf16[512,2048]{1,0:T(8,128)(2,1)} %copy-done.4) | copy-start | bytes 6291460
  75.7 2.2 %copy-start.1 = (bf16[2,16,64,512]{3,2,1,0:T(8,128)(2,1)S(1)}, bf16[2,16,64,512]{3,2,1,0:T(8,128)(2,1)}, u32[]{:S(2)}) copy-start(bf16[2,16,64,512]{3,2,1,0:T(8,128)(2,1)} %copy-done) | copy-start | bytes 6291460
  77.9 5.2 %collective-permute-start = (bf16[1024,768]{1,0:T(8,128)(2,1)S(1)}, bf16[1024,768]{1,0:T(8,128)(2,1)S(1)}, u32[]{:S(2)}, u32[]{:S(2)}) collective-permute-start(bf16[1024,768]{1,0:T(8,128)(2,1)S(1)} %get-tuple-element.81), channel_id=1, source_target_pairs={{0,1},{1,0},{2,3},{3,2},{4,5},{5,4},{6,7},{7,6},{8,9},{9,8},{10,11... | collective-permute-start | bytes 4718600 | tf_op jit(solution)/shard_map/ppermute | solution.py:472
  82.5 4.5 %collective-permute-start.1 = (bf16[1024,768]{1,0:T(8,128)(2,1)S(1)}, bf16[1024,768]{1,0:T(8,128)(2,1)S(1)}, u32[]{:S(2)}, u32[]{:S(2)}) collective-permute-start(bf16[1024,768]{1,0:T(8,128)(2,1)S(1)} %get-tuple-element.87), channel_id=1, source_target_pairs={{0,1},{1,0},{2,3},{3,2},{4,5},{5,4},{6,7},{7,6},{8,9},{9,8},{10,11... | collective-permute-start | bytes 4718600 | tf_op jit(solution)/shard_map/ppermute | solution.py:472
  83.0 6.4 %collective-permute-start.2 = (bf16[1024,640]{1,0:T(8,128)(2,1)S(1)}, bf16[1024,640]{1,0:T(8,128)(2,1)S(1)}, u32[]{:S(2)}, u32[]{:S(2)}) collective-permute-start(bf16[1024,640]{1,0:T(8,128)(2,1)S(1)} %get-tuple-element.91), channel_id=1, source_target_pairs={{0,1},{1,0},{2,3},{3,2},{4,5},{5,4},{6,7},{7,6},{8,9},{9,8},{10,11... | collective-permute-start | bytes 3932168 | tf_op jit(solution)/shard_map/ppermute | solution.py:472
  83.3 14.5 %collective-permute-start.3 = (bf16[512,384]{1,0:T(8,128)(2,1)S(1)}, bf16[512,384]{1,0:T(8,128)(2,1)S(1)}, u32[]{:S(2)}, u32[]{:S(2)}) collective-permute-start(bf16[512,384]{1,0:T(8,128)(2,1)S(1)} %get-tuple-element.84), channel_id=1, source_target_pairs={{0,4},{4,0},{8,12},{12,8},{16,20},{20,16},{24,28},{28,24},{1,5},{5... | collective-permute-start | bytes 1179656 | tf_op jit(solution)/shard_map/ppermute | solution.py:472
  84.6 12.0 %collective-permute-start.4 = (bf16[512,384]{1,0:T(8,128)(2,1)S(1)}, bf16[512,384]{1,0:T(8,128)(2,1)S(1)}, u32[]{:S(2)}, u32[]{:S(2)}) collective-permute-start(bf16[512,384]{1,0:T(8,128)(2,1)S(1)} %get-tuple-element.85), channel_id=1, source_target_pairs={{0,2},{1,3},{2,0},{3,1},{4,6},{5,7},{6,4},{7,5},{8,10},{9,11},{10,... | collective-permute-start | bytes 1179656 | tf_op jit(solution)/shard_map/ppermute | solution.py:472
  87.2 17.1 %collective-permute-start.6 = (bf16[512,384]{1,0:T(8,128)(2,1)S(1)}, bf16[512,384]{1,0:T(8,128)(2,1)S(1)}, u32[]{:S(2)}, u32[]{:S(2)}) collective-permute-start(bf16[512,384]{1,0:T(8,128)(2,1)S(1)} %get-tuple-element.89), channel_id=1, source_target_pairs={{0,2},{1,3},{2,0},{3,1},{4,6},{5,7},{6,4},{7,5},{8,10},{9,11},{10,... | collective-permute-start | bytes 1179656 | tf_op jit(solution)/shard_map/ppermute | solution.py:472
  88.1 17.6 %collective-permute-start.5 = (bf16[512,384]{1,0:T(8,128)(2,1)S(1)}, bf16[512,384]{1,0:T(8,128)(2,1)S(1)}, u32[]{:S(2)}, u32[]{:S(2)}) collective-permute-start(bf16[512,384]{1,0:T(8,128)(2,1)S(1)} %get-tuple-element.88), channel_id=1, source_target_pairs={{0,4},{4,0},{8,12},{12,8},{16,20},{20,16},{24,28},{28,24},{1,5},{5... | collective-permute-start | bytes 1179656 | tf_op jit(solution)/shard_map/ppermute | solution.py:472
  89.6 17.3 %collective-permute-start.8 = (bf16[512,384]{1,0:T(8,128)(2,1)S(1)}, bf16[512,384]{1,0:T(8,128)(2,1)S(1)}, u32[]{:S(2)}, u32[]{:S(2)}) collective-permute-start(bf16[512,384]{1,0:T(8,128)(2,1)S(1)} %get-tuple-element.93), channel_id=1, source_target_pairs={{0,8},{4,12},{8,0},{12,4},{16,24},{20,28},{24,16},{28,20},{1,9},{5... | collective-permute-start | bytes 1179656 | tf_op jit(solution)/shard_map/ppermute | solution.py:472
  96.6 11.0 %collective-permute-start.7 = (bf16[512,256]{1,0:T(8,128)(2,1)S(1)}, bf16[512,256]{1,0:T(8,128)(2,1)S(1)}, u32[]{:S(2)}, u32[]{:S(2)}) collective-permute-start(bf16[512,256]{1,0:T(8,128)(2,1)S(1)} %get-tuple-element.92), channel_id=1, source_target_pairs={{0,8},{4,12},{8,0},{12,4},{16,24},{20,28},{24,16},{28,20},{1,9},{5... | collective-permute-start | bytes 786440 | tf_op jit(solution)/shard_map/ppermute | solution.py:472
  97.9 9.8 %collective-permute-start.10 = (bf16[256,384]{1,0:T(8,128)(2,1)S(1)}, bf16[256,384]{1,0:T(8,128)(2,1)S(1)}, u32[]{:S(2)}, u32[]{:S(2)}) collective-permute-start(bf16[256,384]{1,0:T(8,128)(2,1)S(1)} %get-tuple-element.99), channel_id=1, source_target_pairs={{0,4},{4,0},{8,12},{12,8},{16,20},{20,16},{24,28},{28,24},{1,5},{5... | collective-permute-start | bytes 589832 | tf_op jit(solution)/shard_map/ppermute | solution.py:472
  104.2 7.8 %collective-permute-start.9 = (bf16[256,384]{1,0:T(8,128)(2,1)S(1)}, bf16[256,384]{1,0:T(8,128)(2,1)S(1)}, u32[]{:S(2)}, u32[]{:S(2)}) collective-permute-start(bf16[256,384]{1,0:T(8,128)(2,1)S(1)} %get-tuple-element.98), channel_id=1, source_target_pairs={{0,2},{1,3},{2,0},{3,1},{4,6},{5,7},{6,4},{7,5},{8,10},{9,11},{10,... | collective-permute-start | bytes 589832 | tf_op jit(solution)/shard_map/ppermute | solution.py:472
  105.9 9.3 %collective-permute-start.13 = (bf16[256,384]{1,0:T(8,128)(2,1)S(1)}, bf16[256,384]{1,0:T(8,128)(2,1)S(1)}, u32[]{:S(2)}, u32[]{:S(2)}) collective-permute-start(bf16[256,384]{1,0:T(8,128)(2,1)S(1)} %get-tuple-element.104), channel_id=1, source_target_pairs={{0,2},{1,3},{2,0},{3,1},{4,6},{5,7},{6,4},{7,5},{8,10},{9,11},{10,... | collective-permute-start | bytes 589832 | tf_op jit(solution)/shard_map/ppermute | solution.py:472
  106.8 8.3 %collective-permute-start.14 = (bf16[256,384]{1,0:T(8,128)(2,1)S(1)}, bf16[256,384]{1,0:T(8,128)(2,1)S(1)}, u32[]{:S(2)}, u32[]{:S(2)}) collective-permute-start(bf16[256,384]{1,0:T(8,128)(2,1)S(1)} %get-tuple-element.105), channel_id=1, source_target_pairs={{0,4},{4,0},{8,12},{12,8},{16,20},{20,16},{24,28},{28,24},{1,5},{5... | collective-permute-start | bytes 589832 | tf_op jit(solution)/shard_map/ppermute | solution.py:472
  112.2 12.0 %collective-permute-start.11 = (bf16[128,768]{1,0:T(8,128)(2,1)S(1)}, bf16[128,768]{1,0:T(8,128)(2,1)S(1)}, u32[]{:S(2)}, u32[]{:S(2)}) collective-permute-start(bf16[128,768]{1,0:T(8,128)(2,1)S(1)} %get-tuple-element.113), channel_id=1, source_target_pairs={{0,8},{4,12},{8,0},{12,4},{16,24},{20,28},{24,16},{28,20},{1,9},{5... | collective-permute-start | bytes 589832 | tf_op jit(solution)/shard_map/ppermute | solution.py:472
  113.1 14.8 %collective-permute-start.17 = (bf16[256,640]{1,0:T(8,128)(2,1)S(1)}, bf16[256,640]{1,0:T(8,128)(2,1)S(1)}, u32[]{:S(2)}, u32[]{:S(2)}) collective-permute-start(bf16[256,640]{1,0:T(8,128)(2,1)S(1)} %fold.16), channel_id=1, source_target_pairs={{0,16},{4,20},{8,24},{12,28},{16,0},{20,4},{24,8},{28,12},{1,17},{... | collective-permute-start | bytes 983048 | tf_op jit(solution)/shard_map/ppermute | solution.py:472
  115.3 12.6 %collective-permute-start.15 = (bf16[128,768]{1,0:T(8,128)(2,1)S(1)}, bf16[128,768]{1,0:T(8,128)(2,1)S(1)}, u32[]{:S(2)}, u32[]{:S(2)}) collective-permute-start(bf16[128,768]{1,0:T(8,128)(2,1)S(1)} %get-tuple-element.118), channel_id=1, source_target_pairs={{0,8},{4,12},{8,0},{12,4},{16,24},{20,28},{24,16},{28,20},{1,9},{5... | collective-permute-start | bytes 589832 | tf_op jit(solution)/shard_map/ppermute | solution.py:472
  128.0 6.8 %collective-permute-start.19 = (bf16[128,384]{1,0:T(8,128)(2,1)S(1)}, bf16[128,384]{1,0:T(8,128)(2,1)S(1)}, u32[]{:S(2)}, u32[]{:S(2)}) collective-permute-start(bf16[128,384]{1,0:T(8,128)(2,1)S(1)} %get-tuple-element.123), channel_id=1, source_target_pairs={{0,2},{1,3},{2,0},{3,1},{4,6},{5,7},{6,4},{7,5},{8,10},{9,11},{10,... | collective-permute-start | bytes 294920 | tf_op jit(solution)/shard_map/ppermute | solution.py:472
  128.6 8.1 %collective-permute-start.12 = (bf16[64,768]{1,0:T(8,128)(2,1)S(1)}, bf16[64,768]{1,0:T(8,128)(2,1)S(1)}, u32[]{:S(2)}, u32[]{:S(2)}) collective-permute-start(bf16[64,768]{1,0:T(8,128)(2,1)S(1)} %slice.37), channel_id=1, source_target_pairs={{0,16},{4,20},{8,24},{12,28},{16,0},{20,4},{24,8},{28,12},{1,17},{... | collective-permute-start | bytes 294920 | tf_op jit(solution)/shard_map/ppermute | solution.py:472
  130.1 4.8 %collective-permute-start.18 = (bf16[128,256]{1,0:T(8,128)(2,1)S(1)}, bf16[128,256]{1,0:T(8,128)(2,1)S(1)}, u32[]{:S(2)}, u32[]{:S(2)}) collective-permute-start(bf16[128,256]{1,0:T(8,128)(2,1)S(1)} %get-tuple-element.122), channel_id=1, source_target_pairs={{0,4},{4,0},{8,12},{12,8},{16,20},{20,16},{24,28},{28,24},{1,5},{5... | collective-permute-start | bytes 196616 | tf_op jit(solution)/shard_map/ppermute | solution.py:472
  130.6 6.1 %collective-permute-start.16 = (bf16[64,768]{1,0:T(8,128)(2,1)S(1)}, bf16[64,768]{1,0:T(8,128)(2,1)S(1)}, u32[]{:S(2)}, u32[]{:S(2)}) collective-permute-start(bf16[64,768]{1,0:T(8,128)(2,1)S(1)} %slice.36), channel_id=1, source_target_pairs={{0,16},{4,20},{8,24},{12,28},{16,0},{20,4},{24,8},{28,12},{1,17},{... | collective-permute-start | bytes 294920 | tf_op jit(solution)/shard_map/ppermute | solution.py:472
  134.9 4.0 %collective-permute-start.20 = (bf16[64,256]{1,0:T(8,128)(2,1)S(1)}, bf16[64,256]{1,0:T(8,128)(2,1)S(1)}, u32[]{:S(2)}, u32[]{:S(2)}) collective-permute-start(bf16[64,256]{1,0:T(8,128)(2,1)S(1)} %get-tuple-element.124), channel_id=1, source_target_pairs={{0,2},{1,3},{2,0},{3,1},{4,6},{5,7},{6,4},{7,5},{8,10},{9,11},{10,... | collective-permute-start | bytes 98312 | tf_op jit(solution)/shard_map/ppermute | solution.py:472
  135.5 4.1 %collective-permute-start.21 = (bf16[64,384]{1,0:T(8,128)(2,1)S(1)}, bf16[64,384]{1,0:T(8,128)(2,1)S(1)}, u32[]{:S(2)}, u32[]{:S(2)}) collective-permute-start(bf16[64,384]{1,0:T(8,128)(2,1)S(1)} %get-tuple-element.125), channel_id=1, source_target_pairs={{0,4},{4,0},{8,12},{12,8},{16,20},{20,16},{24,28},{28,24},{1,5},{5... | collective-permute-start | bytes 147464 | tf_op jit(solution)/shard_map/ppermute | solution.py:472

commit v7 on v6

--- a/solution.py
+++ b/solution.py
@@ -354,39 +354,48 @@
             out_ref[i:i + size, at] = value[j:j + size].astype(out_ref.dtype)
 
 
-def column_tiles(cols):
-    plain = cols // 2
+def column_tiles(cols, plain):
     for start, end in ((0, plain), (plain, cols)):
         for t in range(start, end, TILE):
             yield slice(t, min(t + TILE, end)), start > 0
 
 
-def keep_rows(keep_ref, xt_ref, dh_ref, size, at_ref=None, dz_ref=None):
+def keep_rows(keep_ref, xt_ref, dh_ref, plain, size, at_ref=None, dz_ref=None):
     cols = dh_ref.shape[1]
-    for at, crossed in column_tiles(cols):
+    for at, crossed in column_tiles(cols, plain):
         store_rows(keep_ref, at, dot(xt_ref[...], dh_ref[:, at]), crossed, size)
     if at_ref is not None:
         store_rows(keep_ref, slice(cols, None), dot(at_ref[...], dz_ref[...]), True, size)
 
 
-def send_kernel(sizes, has_old, has_at, *refs):
+def keep_blocks(keep_ref, xt_ref, dh_ref, plain, size, blocks):
+    for at, crossed in column_tiles(dh_ref.shape[1], plain):
+        for i, block in enumerate(blocks):
+            j = (0, 2, 1, 3)[block] if crossed else block
+            keep_ref[i * size:(i + 1) * size, at] = dot(
+                xt_ref[j * size:(j + 1) * size, :], dh_ref[:, at]
+            )
+
+
+def send_kernel(sizes, old_plain, has_at, *refs):
     refs = list(refs)
     count = len(sizes)
     dz_ref = refs.pop(0)
     at_ref = refs.pop(0) if has_at else None
     dz = dz_ref[...]
     rows = dz.shape[0]
-    if has_old:
+    if old_plain:
         old_xt_ref, old_ref = refs[:2]
         refs = refs[2:]
     ins, outs = refs[:4 * count], refs[4 * count:]
-    if has_old:
-        keep_rows(outs.pop(0), old_xt_ref, old_ref, sizes[0])
+    if old_plain:
+        keep_blocks(outs.pop(0), old_xt_ref, old_ref, old_plain, sizes[0][1], (2, 3))
     for p in range(count):
         xt_ref, w2_ref, n_ref, inv_ref = ins[4 * p:4 * p + 4]
         dh_ref, sent_ref = outs[2 * p:2 * p + 2]
         cols = n_ref.shape[1]
-        for at, crossed in column_tiles(cols):
+        plain, size = sizes[p]
+        for at, crossed in column_tiles(cols, plain):
             normed = n_ref[:, at].astype(jnp.float32)
             d_norm = jnp.where(normed > 0.0, dot_t(dz, w2_ref[at, :]), 0.0)
             mean = jnp.sum(d_norm, axis=0, keepdims=True) / rows
@@ -394,9 +403,9 @@
             d_hidden = inv_ref[:, at] * (d_norm - mean - normed * slope)
             d_hidden = d_hidden.astype(jnp.bfloat16)
             dh_ref[:, at] = d_hidden
-            store_rows(sent_ref, at, dot(xt_ref[...], d_hidden), crossed, sizes[p])
+            store_rows(sent_ref, at, dot(xt_ref[...], d_hidden), crossed, size)
         if has_at and p == count - 1:
-            store_rows(sent_ref, slice(cols, None), dot(at_ref[...], dz), True, sizes[p])
+            store_rows(sent_ref, slice(cols, None), dot(at_ref[...], dz), True, size)
 
 
 def send_half(dz, at, old, w2, normed, inv, pairs):
@@ -408,10 +417,10 @@
         in_specs.append(pl.BlockSpec((half, rows), lambda i: (1, 0)))
     if old is not None:
         half = old[0].shape[0] // 2
-        operands += list(old)
+        operands += old[:2]
         in_specs += [whole((half, rows)), whole(old[1].shape)]
-        shapes.append(jax.ShapeDtypeStruct((half, old[1].shape[1]), jnp.float32))
-    for p, (xt, place, cols, _) in enumerate(pairs):
+        shapes.append(jax.ShapeDtypeStruct((half // 2, old[1].shape[1]), jnp.float32))
+    for p, (xt, place, cols, *_) in enumerate(pairs):
         half = xt.shape[0] // 2
         operands += [xt, w2, normed, inv]
         in_specs += [
@@ -423,15 +432,16 @@
         extra = emb if at is not None and p == len(pairs) - 1 else 0
         shapes.append(jax.ShapeDtypeStruct((rows, cols), jnp.bfloat16))
         shapes.append(jax.ShapeDtypeStruct((half, cols + extra), jnp.bfloat16))
-    sizes = [size for *_, size in pairs]
+    sizes = [pair[3:] for pair in pairs]
+    old_plain = 0 if old is None else old[2]
     return pl.pallas_call(
-        lambda *refs: send_kernel(sizes, old is not None, at is not None, *refs),
+        lambda *refs: send_kernel(sizes, old_plain, at is not None, *refs),
         grid=(1,),
         in_specs=in_specs,
         out_specs=[whole(shape.shape) for shape in shapes],
         out_shape=shapes,
         cost_estimate=pl.CostEstimate(
-            flops=2 * rows * half * sum(cols for _, _, cols, _ in pairs),
+            flops=2 * rows * half * sum(pair[2] for pair in pairs),
             bytes_accessed=8 * rows * half,
             transcendentals=0,
         ),
@@ -440,16 +450,18 @@
     )(*operands)
 
 
-def keep_half(dz, dh, xt, at, size, made, place):
+def keep_half(dz, dh, xt, at, plain, size, made, place):
     rows, emb = dz.shape
     cols = dh.shape[1]
     block = pl.BlockSpec((made, rows), lambda i: (place, 0))
     operands = [xt, dh]
     in_specs = [block, whole((rows, cols))]
     if at is None:
-        kernel = lambda x, d, g: keep_rows(g, x, d, size)
+        blocks = tuple(range(made // size * place, made // size * (place + 1)))
+        kernel = lambda x, d, g: keep_blocks(g, x, d, plain, size, blocks)
+        in_specs[0] = whole((4 * size, rows))
     else:
-        kernel = lambda x, d, a, z, g: keep_rows(g, x, d, size, a, z)
+        kernel = lambda x, d, a, z, g: keep_rows(g, x, d, plain, size, a, z)
         operands += [at, dz]
         in_specs += [block, whole((rows, emb))]
         cols += emb
@@ -535,10 +547,8 @@
                 came[-1] = after(came[-1], *others)
 
     def add(self, rows, place, form):
-        keep, keep_place = self.keep, place
-        if isinstance(keep, list):
-            keep, start = keep[-1]
-            keep_place = (place * rows - start) // rows
+        keep, start = self.keep
+        keep_place = (place * rows - start) // rows
         out = fold(
             keep, keep_place, self.both, self.left, self.right, self.split, rows, place, form
         )
@@ -551,10 +561,6 @@
     def cross_second(self, out):
         self.left.append(swap(out[0], "crop", 2))
         self.right.append(swap(out[1], "dp", 1))
-
-    def cross_line_apart(self, out):
-        self.left.append(swap(out[0], "dp", 2))
-        self.right.append(swap(out[1], "dp", 2))
 
     def cross_line(self, out, bit):
         self.both.append(swap(out[0], "dp", 2 * bit))
@@ -585,8 +591,9 @@
     all_rows = float(row_count * group_count)
 
     wanted = (shuffle % row_count).reshape(group_count, per_peer)
+    wanted = jnp.pad(wanted.astype(jnp.float32), ((0, 0), (0, 128 - per_peer)))
     requested = lax.all_to_all(wanted, AXES, split_axis=0, concat_axis=0, tiled=True)
-    flat_req = requested.reshape(-1)
+    flat_req = requested[:, :per_peer].astype(jnp.int32).reshape(-1)
 
     flat_col, flat_row = flat_req[:, None], flat_req[None, :]
     hidden_k, sums = key_hidden(flat_col, key_crops, key_inner, group_count)
@@ -619,61 +626,78 @@
     def send(last, old, pairs):
         return send_half(d_z, last, old, query_outer, normed, inv_q, pairs)
 
-    large = hid // 8 * 3
+    large = hid // 16 * 7
     small = hid - 2 * large
+    wide = hid // 4
+    narrow = large - wide
     half = xt.shape[0] // 2
     size, size_3 = half // 4, half // (4 * length)
-    dh_1, sent_1 = send(None, None, [(xt, 0, large, size)])
+    dh_1, sent_1 = send(None, None, [(xt, 0, large, wide, size)])
     came_1 = swap(sent_1, "crop", 1)
     keep_1, dh_2, sent_2, dh_3, sent_3 = send(
-        at3, (xt, dh_1), [(xt, 1, large, size), (xt3, 2 * large // small, small, size_3)]
+        at3,
+        (xt, dh_1, wide),
+        [
+            (xt, 1, large, narrow, size),
+            (xt3, 2 * large // small, small, small // 2, size_3),
+        ],
     )
     came_2 = swap(sent_2, "crop", 1)
     came_3 = swap(sent_3, "crop", 1)
-    one = Pair(keep_1, came_1, large // 2)
-    a_1 = one.add(half // 2, 1, "sides")
-    one.cross_first(a_1)
-    keep_2 = keep_half(d_z, after(dh_2, *a_1), xt, None, size, half, 0)
-    two = Pair(keep_2, came_2, large // 2)
-    a_2 = two.add(half // 2, 1, "sides")
-    two.cross_first(a_2)
-    upper = keep_half(d_z, after(dh_3, *a_2), xt3, at3, size_3, half // 2, 1)
-    three = Pair([(upper, half // 2)], came_3, small // 2)
-    rows = half // 2
-    l_3 = three.add(rows, 1, "sides")
-    three.cross_line_apart(l_3)
-    lower = keep_half(d_z, after(dh_3, *l_3), xt3, at3, size_3, half // 4, 1)
-    one.hold(lower)
-    b_1 = one.add(half // 4, 1, "sides")
-    one.cross_second(b_1)
-    lowest = keep_half(d_z, after(dh_3, *b_1), xt3, at3, size_3, half // 4, 0)
-    two.hold(lowest)
-    b_2 = two.add(half // 4, 1, "sides")
-    two.cross_second(b_2)
-    held = b_2
+
+    def piece(part, rows, place, *others):
+        if part == 3:
+            dh = after(dh_3, *others)
+            keep = keep_half(d_z, dh, xt3, at3, small // 2, size_3, rows, place)
+        else:
+            dh = after(dh_1 if part == 1 else dh_2, *others)
+            plain = wide if part == 1 else narrow
+            keep = keep_half(d_z, dh, xt, None, plain, size, rows, place)
+        return keep, rows * place
+
+    half_rows, rows = half // 2, half // 4
+    one = Pair((keep_1, half_rows), came_1, wide)
+    out = one.add(half_rows, 1, "sides")
+    one.cross_first(out)
+    two = Pair(piece(2, half_rows, 1, *out), came_2, narrow)
+    out = two.add(half_rows, 1, "sides")
+    two.cross_first(out)
+    three = Pair(piece(3, half_rows, 1, *out), came_3, small // 2)
+    out = three.add(half_rows, 1, "send")
+    three.cross_line(out, 1)
+    one.keep = piece(1, rows, 1, *out)
+    one.hold(one.keep[0])
+    out = one.add(rows, 1, "sides")
+    one.cross_second(out)
+    two.keep = piece(2, half_rows, 0, *out)
+    three.keep = piece(3, half_rows, 0, two.keep[0])
+    two.hold(three.keep[0])
+    out = two.add(rows, 1, "sides")
+    two.cross_second(out)
+    line_rows = half_rows
     for bit in range(1, bits):
-        rows //= 2
-        three.hold(*held)
-        three.keep = [(lower, half // 4) if bit == 1 else (lowest, 0)]
-        held = three.add(rows, 1, "send")
-        three.cross_line(held, 2 ** bit)
-    one.hold(*held)
-    c_1 = one.add(half // 4, 0, "halves")
+        line_rows //= 2
+        three.hold(*out)
+        out = three.add(line_rows, 1, "send")
+        three.cross_line(out, 2 ** bit)
+    one.keep = piece(1, rows, 0, *out)
+    one.hold(one.keep[0])
+    c_1 = one.add(rows, 0, "halves")
     two.hold(*c_1)
-    c_2 = two.add(half // 4, 0, "halves")
+    c_2 = two.add(rows, 0, "halves")
     own_1 = lax.optimization_barrier(one.cross_third(c_1))
+    three.hold(*c_2)
+    line_rows //= 2
+    out = three.add(line_rows, 1, "sides")
+    three.cross_first(out)
     own_2 = lax.optimization_barrier(two.cross_third(c_2))
-    three.keep = [(lowest, 0)]
-    three.hold(own_1, own_2)
-    rows //= 2
-    e_3 = three.add(rows, 1, "sides")
-    three.cross_first(e_3)
-    rows //= 2
-    f_3 = three.add(rows, 1, "sides")
-    three.cross_second(f_3)
+    three.hold(own_1)
+    line_rows //= 2
+    out = three.add(line_rows, 1, "sides")
+    three.cross_second(out)
     own_1 = one.cross_rest(own_1)
     own_2 = two.cross_rest(own_2)
-    own_3 = three.add(rows, 0, "own")[0]
+    own_3 = three.add(line_rows, 0, "own")[0]
     grad_inner = jnp.concatenate([own_1, own_2, own_3[:, :small]], axis=1)
     return (grad_inner, own_3[:, small:])
 

time: 142 us -> 138 us (0.972)
  waiting for transfers between devices: 34.4 us -> 26.8 us
  starting transfers between devices: 28.7 us -> 33.1 us
    ppermute x22 -> x21, waiting for transfers between devices: 32 us -> 24.3 us  [swap(): return lax.ppermute(x, axis, [(i, i ^ bit) for i in range(size)])]
    ppermute x22 -> x21, starting transfers between devices: 21.1 us -> 25.5 us  [swap(): return lax.ppermute(x, axis, [(i, i ^ bit) for i in range(size)])]
    pallas_call x4 -> x6, Pallas kernels: 2.55 us -> 3.42 us  [keep_half(): pl.pallas_call(kernel, grid=(1,), in_specs=in_specs, out_specs=whole((mad...]
  transfers between devices with their start and end apart: 24 -> 23, of which waited for: 10 -> 13; matrix products, arithmetic and copies ran while one was open for 0% -> 1% of each run, Pallas kernels for 21% -> 22%
where the time goes in v7:
time: 138 us; the launch traced here: 137 us
  Pallas kernels  45.4 us (33%)
  starting transfers between devices  33.1 us (24%)
  waiting for transfers between devices  26.8 us (19%)
  local copies, waits for them, and re-layouts  14.7 us (11%)
  blocking collectives  14.2 us (10%)
  other arithmetic  1.74 us (1%)
    ppermute x21, starting transfers between devices, swap(): return lax.ppermute(x, axis, [(i, i ^ bit) for i in range(size)])  25.5 us
    ppermute x21, waiting for transfers between devices, swap(): return lax.ppermute(x, axis, [(i, i ^ bit) for i in range(size)])  24.3 us
    all_to_all x1, blocking collectives, per_device(): lax.all_to_all(wanted, AXES, split_axis=0, concat_axis=0, tiled=True)  14.2 us
    unnamed x28, local copies, waits for them, and re-layouts  13.7 us
    pallas_call x1, Pallas kernels, negatives(): pl.pallas_call(neg_kernel, grid=(bank.shape[0] // tile,), in_specs=[pl.Bl...  11 us
    pallas_call x1, Pallas kernels, key_hidden(): pl.pallas_call(lambda *refs: key_hidden_kernel(groups, *refs), grid=(hid...  10.3 us
    pallas_call x1, Pallas kernels, query_forward(): pl.pallas_call(lambda *refs: query_kernel(size, *refs), grid_spec=pltpu.P...  10.3 us
    pallas_call x2, Pallas kernels, send_half(): pl.pallas_call(lambda *refs: send_kernel(sizes, old_plain, at is not None...  6.14 us
  transfers between devices with their start and end apart: 23, of which 13 were waited for; matrix products, arithmetic and copies ran while one was open for 1% of the time, Pallas kernels for 22%

profile of v7, /device:TPU:0, one launch (start us, length us, event | category | flops | bytes accessed | tf_op | source)
XLA Modules:
  0.0 137.0 jit_solution(15562331147122079986)
XLA Ops:
  1.4 14.2 %all_to_all.22 = f32[32,1,128]{2,1,0:T(1,128)S(1)} all-to-all(f32[32,1,128]{2,1,0:T(1,128)S(1)} %bitcast.21), channel_id=1, replica_groups=mesh['dp'=8,'crop'=4] {'dp','crop'}, dimensions={0} | all-to-all | bytes 32768 | tf_op jit(solution)/shard_map/all_to_all | solution.py:595
  15.8 1.6 %copy-done.13 = bf16[512,2048]{1,0:T(8,128)(2,1)S(1)} copy-done((bf16[512,2048]{1,0:T(8,128)(2,1)S(1)}, bf16[512,2048]{1,0:T(8,128)(2,1)}, u32[]{:S(2)}) %copy-start.13) | copy-done | bytes 2097176
  17.4 10.3 %key_hidden.1 = (f32[512,2048]{1,0:T(8,128)}, f32[32,1,4096]{2,1,0:T(1,128)}) custom-call(s32[512,1]{1,0:T(8,128)S(1)} %broadcast_in_dim_reshape.8.refs_0_, bf16[512,2048]{1,0:T(8,128)(2,1)S(1)} %copy-done.13, bf16[2048,2048]{1,0:T(8,128)(2,1)} %refs_2_.3), custom_call_target="tpu_custom_call" | custom-call | flops 5368709120 | bytes 8388608 | tf_op jit(solution)/shard_map/key_hidden/pallas_call | solution.py:141
  27.7 2.6 %all-to-all-start.1 = ((f32[32,1,4096]{2,1,0:T(1,128)}), f32[32,1,4096]{2,1,0:T(1,128)S(1)}, u32[]{:S(2)}, u32[]{:S(2)}) async-start(f32[32,1,4096]{2,1,0:T(1,128)} %get-tuple-element.63), calls=%async_computation.1 | async-start | bytes 1048576 | tf_op jit(solution)/shard_map/all_to_all | solution.py:600
  30.6 10.3 %query_forward.1 = (bf16[512,2048]{1,0:T(8,128)(2,1)S(1)}, f32[1,2048]{1,0:T(1,128)S(1)}, f32[512,128]{1,0:T(8,128)S(1)}, bf16[512,128]{1,0:T(8,128)(2,1)S(1)}, ...) custom-call(s32[3,16]{1,0:T(4,128)S(1)} %add_add_fusion.refs_0_, ...), custom_call_target="tpu_custom_call" | custom-call | flops 4563402752 | bytes 8388608 | tf_op jit(solution)/shard_map/query_forward/pallas_call | solution.py:239
  41.0 1.3 copy-done
  42.3 1.4 copy-done.2
  43.7 1.4 %copy-done.4 = bf16[2,16,64,512]{3,2,1,0:T(8,128)(2,1)} copy-done((bf16[2,16,64,512]{3,2,1,0:T(8,128)(2,1)}, bf16[2,16,64,512]{3,2,1,0:T(8,128)(2,1)S(1)}, u32[]{:S(2)}) %copy-start.4) | copy-done | bytes 2097176
  45.0 0.9 all-to-all-done.1.refs_0_
  46.2 0.8 copy-done.8
  47.0 5.0 %all-to-all-start.2 = ((f32[32,1,4096]{2,1,0:T(1,128)}), f32[32,1,4096]{2,1,0:T(1,128)S(1)}, u32[]{:S(2)}, u32[]{:S(2)}) async-start(f32[32,1,4096]{2,1,0:T(1,128)} %copy-done.8), calls=%async_computation.2 | async-start | bytes 1048576 | tf_op jit(solution)/shard_map/all_to_all | solution.py:620
  51.9 2.2 %copy-done.12 = bf16[16384,128]{1,0:T(8,128)(2,1)S(1)} copy-done((bf16[16384,128]{1,0:T(8,128)(2,1)S(1)}, bf16[16384,128]{1,0:T(8,128)(2,1)}, u32[]{:S(2)}) %copy-start.12) | copy-done | bytes 4194328
  54.1 11.0 %negatives.1.refs_5_ = f32[512,256]{1,0:T(8,128)S(1)} custom-call(bf16[512,128]{1,0:T(8,128)(2,1)S(1)} %get-tuple-element.70.q_ref, bf16[16384,128]{1,0:T(8,128)(2,1)S(1)} %copy-done.12), custom_call_target="tpu_custom_call" | custom-call | flops 4294967296 | bytes 4194304 | tf_op jit(solution)/shard_map/negatives/pallas_call | solution.py:42
  65.1 0.8 copy-done.10
  65.9 1.6 %all-to-all-done.2.refs_2_ = f32[32,1,4096]{2,1,0:T(1,128)S(1)} async-done(((f32[32,1,4096]{2,1,0:T(1,128)}), f32[32,1,4096]{2,1,0:T(1,128)S(1)}, u32[]{:S(2)}, u32[]{:S(2)}) %all-to-all-start.2) | async-done | bytes 524320 | tf_op jit(solution)/shard_map/all_to_all | solution.py:620
  67.5 2.2 %copy-done.7 = f32[512,2048]{1,0:T(8,128)S(1)} copy-done((f32[512,2048]{1,0:T(8,128)S(1)}, f32[512,2048]{1,0:T(8,128)}, u32[]{:S(2)}) %copy-start.7) | copy-done | bytes 4194328
  69.7 1.0 copy-done.9
  70.7 1.0 copy-done.11
  71.7 2.8 %embed.1.refs_0_.z = bf16[512,128]{1,0:T(8,128)(2,1)S(1)} custom-call(s32[1,512]{1,0:T(1,128)S(1)} %broadcast_in_dim_reshape.7.refs_0_, f32[512,2048]{1,0:T(8,128)S(1)} %copy-done.7, f32[32,1,4096]{2,1,0:T(1,128)S(1)} %all-to-all-done.2.refs_2_, bf16[2048,128]{1,0:T(8,128)(2,1)S(1)} %copy-done.9, f32[512,128]{1,0:T(8,128)S(1)} %get-tuple-element.72.refs_4_, ...), custom_call_target="tpu_custom_call" | custom-call | flops 268435456 | bytes 4194304 | tf_op jit(solution)/shard_map/embed/pallas_call | solution.py:325
  74.6 2.2 %send_half.2 = (bf16[512,896]{1,0:T(8,128)(2,1)S(1)}, bf16[1024,896]{1,0:T(8,128)(2,1)S(1)}) custom-call(bf16[512,128]{1,0:T(8,128)(2,1)S(1)} %embed.1.refs_0_.z, bf16[2048,512]{1,0:T(8,128)(2,1)S(1)} %bitcast.8, bf16[2048,128]{1,0:T(8,128)(2,1)S(1)} %copy-done.6, bf16[512,2048]{1,0:T(8,128)(2,1)S(1)} %copy-done.1, ...), custom_call_target="tpu_custom_call" | custom-call | flops 939524096 | bytes 4194304 | tf_op jit(solution)/shard_map/send_half/pallas_call | solution.py:437
  76.9 4.0 %send_half.3 = (f32[512,896]{1,0:T(8,128)S(1)}, bf16[512,896]{1,0:T(8,128)(2,1)S(1)}, bf16[1024,896]{1,0:T(8,128)(2,1)S(1)}, bf16[512,256]{1,0:T(8,128)(2,1)S(1)}, bf16[1024,384]{1,0:T(8,128)(2,1)S(1)}) custom-call(bf16[512,128]{1,0:T(8,128)(2,1)S(1)} %embed.1.refs_0_.z, bf16[2048,512]{1,0:T(8,128)(2,1)S(1)} %bitcast.18, bf16[2048,512]{1,0:T(8,128)(2,1)S(1)} %bitcast.9, ...), custom_call_target="tpu_custom_call" | custom-call | flops 1207959552 | bytes 4194304 | tf_op jit(solution)/shard_map/send_half/pallas_call | solution.py:437
  81.6 1.3 collective-permute-start.3
  82.9 1.2 collective-permute-start.4
  84.1 0.7 keep_half.6.refs_0_
  85.0 1.2 collective-permute-start.7
  86.2 1.3 collective-permute-start.6
  88.1 0.8 collective-permute-start.5
  89.3 5.5 %collective-permute-done.4.refs_3_.refs_4_ = bf16[512,384]{1,0:T(8,128)(2,1)S(1)} collective-permute-done((bf16[512,384]{1,0:T(8,128)(2,1)S(1)}, bf16[512,384]{1,0:T(8,128)(2,1)S(1)}, u32[]{:S(2)}, u32[]{:S(2)}) %collective-permute-start.4) | collective-permute-done | bytes 393248 | tf_op jit(solution)/shard_map/ppermute | solution.py:484
  94.9 1.5 %collective-permute-done.3.refs_2_ = bf16[512,512]{1,0:T(8,128)(2,1)S(1)} collective-permute-done((bf16[512,512]{1,0:T(8,128)(2,1)S(1)}, bf16[512,512]{1,0:T(8,128)(2,1)S(1)}, u32[]{:S(2)}, u32[]{:S(2)}) %collective-permute-start.3) | collective-permute-done | bytes 524320 | tf_op jit(solution)/shard_map/ppermute | solution.py:484
  96.5 1.3 collective-permute-start.8
  97.9 1.1 collective-permute-start.9
  100.3 5.8 %collective-permute-done.7.refs_3_.refs_4_ = bf16[512,512]{1,0:T(8,128)(2,1)S(1)} collective-permute-done((bf16[512,512]{1,0:T(8,128)(2,1)S(1)}, bf16[512,512]{1,0:T(8,128)(2,1)S(1)}, u32[]{:S(2)}, u32[]{:S(2)}) %collective-permute-start.7) | collective-permute-done | bytes 524320 | tf_op jit(solution)/shard_map/ppermute | solution.py:484
  106.3 0.9 collective-permute-start.13
  107.6 1.4 %collective-permute-done.9.refs_5_ = bf16[256,384]{1,0:T(8,128)(2,1)S(1)} collective-permute-done((bf16[256,384]{1,0:T(8,128)(2,1)S(1)}, bf16[256,384]{1,0:T(8,128)(2,1)S(1)}, u32[]{:S(2)}, u32[]{:S(2)}) %collective-permute-start.9) | collective-permute-done | bytes 196640 | tf_op jit(solution)/shard_map/ppermute | solution.py:484
  109.0 1.9 %collective-permute-done.8.refs_3_ = bf16[256,512]{1,0:T(8,128)(2,1)S(1)} collective-permute-done((bf16[256,512]{1,0:T(8,128)(2,1)S(1)}, bf16[256,512]{1,0:T(8,128)(2,1)S(1)}, u32[]{:S(2)}, u32[]{:S(2)}) %collective-permute-start.8) | collective-permute-done | bytes 262176 | tf_op jit(solution)/shard_map/ppermute | solution.py:484
  111.1 0.9 collective-permute-start.10
  112.0 1.1 collective-permute-start.12
  113.1 2.5 %collective-permute-start.16 = (bf16[256,384]{1,0:T(8,128)(2,1)S(1)}, bf16[256,384]{1,0:T(8,128)(2,1)S(1)}, u32[]{:S(2)}, u32[]{:S(2)}) collective-permute-start(bf16[256,384]{1,0:T(8,128)(2,1)S(1)} %fold.16), channel_id=1, source_target_pairs={{0,16},{4,20},{8,24},{12,28},{16,0},{20,4},{24,8},{28,12},{1,17},{... | collective-permute-start | bytes 589832 | tf_op jit(solution)/shard_map/ppermute | solution.py:484
  115.5 2.3 %collective-permute-done.12.refs_3_ = bf16[256,384]{1,0:T(8,128)(2,1)S(1)} collective-permute-done((bf16[256,384]{1,0:T(8,128)(2,1)S(1)}, bf16[256,384]{1,0:T(8,128)(2,1)S(1)}, u32[]{:S(2)}, u32[]{:S(2)}) %collective-permute-start.12) | collective-permute-done | bytes 196640 | tf_op jit(solution)/shard_map/ppermute | solution.py:484
  118.1 1.3 collective-permute-start.14
  119.4 3.3 %collective-permute-done.16.refs_3_ = bf16[256,384]{1,0:T(8,128)(2,1)S(1)} collective-permute-done((bf16[256,384]{1,0:T(8,128)(2,1)S(1)}, bf16[256,384]{1,0:T(8,128)(2,1)S(1)}, u32[]{:S(2)}, u32[]{:S(2)}) %collective-permute-start.16) | collective-permute-done | bytes 196640 | tf_op jit(solution)/shard_map/ppermute | solution.py:484
  122.7 0.9 collective-permute-start.17
  123.7 1.8 %collective-permute-start.18 = (bf16[128,256]{1,0:T(8,128)(2,1)S(1)}, bf16[128,256]{1,0:T(8,128)(2,1)S(1)}, u32[]{:S(2)}, u32[]{:S(2)}) collective-permute-start(bf16[128,256]{1,0:T(8,128)(2,1)S(1)} %get-tuple-element.120), channel_id=1, source_target_pairs={{0,2},{1,3},{2,0},{3,1},{4,6},{5,7},{6,4},{7,5},{8,10},{9,11},{10,... | collective-permute-start | bytes 196616 | tf_op jit(solution)/shard_map/ppermute | solution.py:484
  125.5 2.1 %collective-permute-start.11 = (bf16[64,896]{1,0:T(8,128)(2,1)S(1)}, bf16[64,896]{1,0:T(8,128)(2,1)S(1)}, u32[]{:S(2)}, u32[]{:S(2)}) collective-permute-start(bf16[64,896]{1,0:T(8,128)(2,1)S(1)} %slice.43), channel_id=1, source_target_pairs={{0,16},{4,20},{8,24},{12,28},{16,0},{20,4},{24,8},{28,12},{1,17},{... | collective-permute-start | bytes 344072 | tf_op jit(solution)/shard_map/ppermute | solution.py:484
  128.0 1.8 %collective-permute-start.19 = (bf16[64,128]{1,0:T(8,128)(2,1)S(1)}, bf16[64,128]{1,0:T(8,128)(2,1)S(1)}, u32[]{:S(2)}, u32[]{:S(2)}) collective-permute-start(bf16[64,128]{1,0:T(8,128)(2,1)S(1)} %get-tuple-element.122), channel_id=1, source_target_pairs={{0,2},{1,3},{2,0},{3,1},{4,6},{5,7},{6,4},{7,5},{8,10},{9,11},{10,... | collective-permute-start | bytes 49160 | tf_op jit(solution)/shard_map/ppermute | solution.py:484
  130.1 3.2 %collective-permute-start.15 = (bf16[64,896]{1,0:T(8,128)(2,1)S(1)}, bf16[64,896]{1,0:T(8,128)(2,1)S(1)}, u32[]{:S(2)}, u32[]{:S(2)}) collective-permute-start(bf16[64,896]{1,0:T(8,128)(2,1)S(1)} %slice.42), channel_id=1, source_target_pairs={{0,16},{4,20},{8,24},{12,28},{16,0},{20,4},{24,8},{28,12},{1,17},{... | collective-permute-start | bytes 344072 | tf_op jit(solution)/shard_map/ppermute | solution.py:484
  134.6 1.6 %collective-permute-done.15 = bf16[64,896]{1,0:T(8,128)(2,1)S(1)} collective-permute-done((bf16[64,896]{1,0:T(8,128)(2,1)S(1)}, bf16[64,896]{1,0:T(8,128)(2,1)S(1)}, u32[]{:S(2)}, u32[]{:S(2)}) %collective-permute-start.15) | collective-permute-done | bytes 114720 | tf_op jit(solution)/shard_map/ppermute | solution.py:484
  136.2 0.8 pad_maximum_fusion
  (69 shorter events, 8.1 us)
Async XLA Ops:
  15.8 1.6 %copy-start.13 = (bf16[512,2048]{1,0:T(8,128)(2,1)S(1)}, bf16[512,2048]{1,0:T(8,128)(2,1)}, u32[]{:S(2)}) copy-start(bf16[512,2048]{1,0:T(8,128)(2,1)} %refs_1_.1) | copy-start | bytes 6291460
  17.4 13.2 %copy-start.6 = (bf16[2048,128]{1,0:T(8,128)(2,1)S(1)}, bf16[2048,128]{1,0:T(8,128)(2,1)}, u32[]{:S(2)}) copy-start(bf16[2048,128]{1,0:T(8,128)(2,1)} %refs_9_.1) | copy-start | bytes 1572868
  27.7 18.2 %all-to-all-start.1 = ((f32[32,1,4096]{2,1,0:T(1,128)}), f32[32,1,4096]{2,1,0:T(1,128)S(1)}, u32[]{:S(2)}, u32[]{:S(2)}) async-start(f32[32,1,4096]{2,1,0:T(1,128)} %get-tuple-element.63), calls=%async_computation.1 | async-start | bytes 1048576 | tf_op jit(solution)/shard_map/all_to_all | solution.py:600
  41.0 1.3 copy-start
  42.3 1.4 copy-start.2
  43.7 1.4 %copy-start.4 = (bf16[2,16,64,512]{3,2,1,0:T(8,128)(2,1)}, bf16[2,16,64,512]{3,2,1,0:T(8,128)(2,1)S(1)}, u32[]{:S(2)}) copy-start(bf16[2,16,64,512]{3,2,1,0:T(8,128)(2,1)S(1)} %get-tuple-element.78) | copy-start | bytes 6291460
  46.2 0.8 copy-start.8
  47.0 20.5 %all-to-all-start.2 = ((f32[32,1,4096]{2,1,0:T(1,128)}), f32[32,1,4096]{2,1,0:T(1,128)S(1)}, u32[]{:S(2)}, u32[]{:S(2)}) async-start(f32[32,1,4096]{2,1,0:T(1,128)} %copy-done.8), calls=%async_computation.2 | async-start | bytes 1048576 | tf_op jit(solution)/shard_map/all_to_all | solution.py:620
  51.9 2.2 %copy-start.12 = (bf16[16384,128]{1,0:T(8,128)(2,1)S(1)}, bf16[16384,128]{1,0:T(8,128)(2,1)}, u32[]{:S(2)}) copy-start(bf16[16384,128]{1,0:T(8,128)(2,1)} %bank_ref.1) | copy-start | bytes 12582916
  65.1 0.8 copy-start.10
  67.5 2.2 %copy-start.7 = (f32[512,2048]{1,0:T(8,128)S(1)}, f32[512,2048]{1,0:T(8,128)}, u32[]{:S(2)}) copy-start(f32[512,2048]{1,0:T(8,128)} %get-tuple-element.68.refs_1_) | copy-start | bytes 12582916
  69.7 1.0 copy-start.9
  70.7 1.0 copy-start.11
  71.7 2.8 %copy-start.1 = (bf16[512,2048]{1,0:T(8,128)(2,1)S(1)}, bf16[512,2048]{1,0:T(8,128)(2,1)}, u32[]{:S(2)}) copy-start(bf16[512,2048]{1,0:T(8,128)(2,1)} %copy-done) | copy-start | bytes 6291460
  74.6 2.3 %copy-start.3 = (bf16[2,16,64,512]{3,2,1,0:T(8,128)(2,1)S(1)}, bf16[2,16,64,512]{3,2,1,0:T(8,128)(2,1)}, u32[]{:S(2)}) copy-start(bf16[2,16,64,512]{3,2,1,0:T(8,128)(2,1)} %copy-done.2) | copy-start | bytes 6291460
  74.6 2.3 %copy-start.5 = (bf16[2,16,64,512]{3,2,1,0:T(8,128)(2,1)S(1)}, bf16[2,16,64,512]{3,2,1,0:T(8,128)(2,1)}, u32[]{:S(2)}) copy-start(bf16[2,16,64,512]{3,2,1,0:T(8,128)(2,1)} %copy-done.4) | copy-start | bytes 6291460
  76.8 4.7 %collective-permute-start = (bf16[1024,896]{1,0:T(8,128)(2,1)S(1)}, bf16[1024,896]{1,0:T(8,128)(2,1)S(1)}, u32[]{:S(2)}, u32[]{:S(2)}) collective-permute-start(bf16[1024,896]{1,0:T(8,128)(2,1)S(1)} %get-tuple-element.82), channel_id=1, source_target_pairs={{0,1},{1,0},{2,3},{3,2},{4,5},{5,4},{6,7},{7,6},{8,9},{9,8},{10,11... | collective-permute-start | bytes 5505032 | tf_op jit(solution)/shard_map/ppermute | solution.py:484
  80.8 4.0 %collective-permute-start.1 = (bf16[1024,896]{1,0:T(8,128)(2,1)S(1)}, bf16[1024,896]{1,0:T(8,128)(2,1)S(1)}, u32[]{:S(2)}, u32[]{:S(2)}) collective-permute-start(bf16[1024,896]{1,0:T(8,128)(2,1)S(1)} %get-tuple-element.86), channel_id=1, source_target_pairs={{0,1},{1,0},{2,3},{3,2},{4,5},{5,4},{6,7},{7,6},{8,9},{9,8},{10,11... | collective-permute-start | bytes 5505032 | tf_op jit(solution)/shard_map/ppermute | solution.py:484
  81.4 6.6 %collective-permute-start.2 = (bf16[1024,384]{1,0:T(8,128)(2,1)S(1)}, bf16[1024,384]{1,0:T(8,128)(2,1)S(1)}, u32[]{:S(2)}, u32[]{:S(2)}) collective-permute-start(bf16[1024,384]{1,0:T(8,128)(2,1)S(1)} %get-tuple-element.90), channel_id=1, source_target_pairs={{0,1},{1,0},{2,3},{3,2},{4,5},{5,4},{6,7},{7,6},{8,9},{9,8},{10,11... | collective-permute-start | bytes 2359304 | tf_op jit(solution)/shard_map/ppermute | solution.py:484
  81.6 14.8 %collective-permute-start.3 = (bf16[512,512]{1,0:T(8,128)(2,1)S(1)}, bf16[512,512]{1,0:T(8,128)(2,1)S(1)}, u32[]{:S(2)}, u32[]{:S(2)}) collective-permute-start(bf16[512,512]{1,0:T(8,128)(2,1)S(1)} %get-tuple-element.83), channel_id=1, source_target_pairs={{0,4},{4,0},{8,12},{12,8},{16,20},{20,16},{24,28},{28,24},{1,5},{5... | collective-permute-start | bytes 1572872 | tf_op jit(solution)/shard_map/ppermute | solution.py:484
  82.9 12.0 %collective-permute-start.4 = (bf16[512,384]{1,0:T(8,128)(2,1)S(1)}, bf16[512,384]{1,0:T(8,128)(2,1)S(1)}, u32[]{:S(2)}, u32[]{:S(2)}) collective-permute-start(bf16[512,384]{1,0:T(8,128)(2,1)S(1)} %get-tuple-element.84), channel_id=1, source_target_pairs={{0,2},{1,3},{2,0},{3,1},{4,6},{5,7},{6,4},{7,5},{8,10},{9,11},{10,... | collective-permute-start | bytes 1179656 | tf_op jit(solution)/shard_map/ppermute | solution.py:484
  85.0 21.1 %collective-permute-start.7 = (bf16[512,512]{1,0:T(8,128)(2,1)S(1)}, bf16[512,512]{1,0:T(8,128)(2,1)S(1)}, u32[]{:S(2)}, u32[]{:S(2)}) collective-permute-start(bf16[512,512]{1,0:T(8,128)(2,1)S(1)} %get-tuple-element.88), channel_id=1, source_target_pairs={{0,2},{1,3},{2,0},{3,1},{4,6},{5,7},{6,4},{7,5},{8,10},{9,11},{10,... | collective-permute-start | bytes 1572872 | tf_op jit(solution)/shard_map/ppermute | solution.py:484
  86.2 19.9 %collective-permute-start.6 = (bf16[512,384]{1,0:T(8,128)(2,1)S(1)}, bf16[512,384]{1,0:T(8,128)(2,1)S(1)}, u32[]{:S(2)}, u32[]{:S(2)}) collective-permute-start(bf16[512,384]{1,0:T(8,128)(2,1)S(1)} %get-tuple-element.87), channel_id=1, source_target_pairs={{0,4},{4,0},{8,12},{12,8},{16,20},{20,16},{24,28},{28,24},{1,5},{5... | collective-permute-start | bytes 1179656 | tf_op jit(solution)/shard_map/ppermute | solution.py:484
  88.1 19.0 %collective-permute-start.5 = (bf16[512,384]{1,0:T(8,128)(2,1)S(1)}, bf16[512,384]{1,0:T(8,128)(2,1)S(1)}, u32[]{:S(2)}, u32[]{:S(2)}) collective-permute-start(bf16[512,384]{1,0:T(8,128)(2,1)S(1)} %fold.13), channel_id=1, source_target_pairs={{0,8},{4,12},{8,0},{12,4},{16,24},{20,28},{24,16},{28,20},{1,9},{5... | collective-permute-start | bytes 1179656 | tf_op jit(solution)/shard_map/ppermute | solution.py:484
  96.5 14.4 %collective-permute-start.8 = (bf16[256,512]{1,0:T(8,128)(2,1)S(1)}, bf16[256,512]{1,0:T(8,128)(2,1)S(1)}, u32[]{:S(2)}, u32[]{:S(2)}) collective-permute-start(bf16[256,512]{1,0:T(8,128)(2,1)S(1)} %get-tuple-element.95), channel_id=1, source_target_pairs={{0,2},{1,3},{2,0},{3,1},{4,6},{5,7},{6,4},{7,5},{8,10},{9,11},{10,... | collective-permute-start | bytes 786440 | tf_op jit(solution)/shard_map/ppermute | solution.py:484
  97.9 11.2 %collective-permute-start.9 = (bf16[256,384]{1,0:T(8,128)(2,1)S(1)}, bf16[256,384]{1,0:T(8,128)(2,1)S(1)}, u32[]{:S(2)}, u32[]{:S(2)}) collective-permute-start(bf16[256,384]{1,0:T(8,128)(2,1)S(1)} %get-tuple-element.96), channel_id=1, source_target_pairs={{0,4},{4,0},{8,12},{12,8},{16,20},{20,16},{24,28},{28,24},{1,5},{5... | collective-permute-start | bytes 589832 | tf_op jit(solution)/shard_map/ppermute | solution.py:484
  106.3 11.6 %collective-permute-start.13 = (bf16[256,512]{1,0:T(8,128)(2,1)S(1)}, bf16[256,512]{1,0:T(8,128)(2,1)S(1)}, u32[]{:S(2)}, u32[]{:S(2)}) collective-permute-start(bf16[256,512]{1,0:T(8,128)(2,1)S(1)} %get-tuple-element.103), channel_id=1, source_target_pairs={{0,4},{4,0},{8,12},{12,8},{16,20},{20,16},{24,28},{28,24},{1,5},{5... | collective-permute-start | bytes 786440 | tf_op jit(solution)/shard_map/ppermute | solution.py:484
  111.1 14.3 %collective-permute-start.10 = (bf16[128,896]{1,0:T(8,128)(2,1)S(1)}, bf16[128,896]{1,0:T(8,128)(2,1)S(1)}, u32[]{:S(2)}, u32[]{:S(2)}) collective-permute-start(bf16[128,896]{1,0:T(8,128)(2,1)S(1)} %get-tuple-element.110), channel_id=1, source_target_pairs={{0,8},{4,12},{8,0},{12,4},{16,24},{20,28},{24,16},{28,20},{1,9},{5... | collective-permute-start | bytes 688136 | tf_op jit(solution)/shard_map/ppermute | solution.py:484
  112.0 5.9 %collective-permute-start.12 = (bf16[256,384]{1,0:T(8,128)(2,1)S(1)}, bf16[256,384]{1,0:T(8,128)(2,1)S(1)}, u32[]{:S(2)}, u32[]{:S(2)}) collective-permute-start(bf16[256,384]{1,0:T(8,128)(2,1)S(1)} %get-tuple-element.102), channel_id=1, source_target_pairs={{0,2},{1,3},{2,0},{3,1},{4,6},{5,7},{6,4},{7,5},{8,10},{9,11},{10,... | collective-permute-start | bytes 589832 | tf_op jit(solution)/shard_map/ppermute | solution.py:484
  113.1 9.6 %collective-permute-start.16 = (bf16[256,384]{1,0:T(8,128)(2,1)S(1)}, bf16[256,384]{1,0:T(8,128)(2,1)S(1)}, u32[]{:S(2)}, u32[]{:S(2)}) collective-permute-start(bf16[256,384]{1,0:T(8,128)(2,1)S(1)} %fold.16), channel_id=1, source_target_pairs={{0,16},{4,20},{8,24},{12,28},{16,0},{20,4},{24,8},{28,12},{1,17},{... | collective-permute-start | bytes 589832 | tf_op jit(solution)/shard_map/ppermute | solution.py:484
  118.1 12.0 %collective-permute-start.14 = (bf16[128,896]{1,0:T(8,128)(2,1)S(1)}, bf16[128,896]{1,0:T(8,128)(2,1)S(1)}, u32[]{:S(2)}, u32[]{:S(2)}) collective-permute-start(bf16[128,896]{1,0:T(8,128)(2,1)S(1)} %get-tuple-element.115), channel_id=1, source_target_pairs={{0,8},{4,12},{8,0},{12,4},{16,24},{20,28},{24,16},{28,20},{1,9},{5... | collective-permute-start | bytes 688136 | tf_op jit(solution)/shard_map/ppermute | solution.py:484
  122.7 4.8 %collective-permute-start.17 = (bf16[128,128]{1,0:T(8,128)(2,1)S(1)}, bf16[128,128]{1,0:T(8,128)(2,1)S(1)}, u32[]{:S(2)}, u32[]{:S(2)}) collective-permute-start(bf16[128,128]{1,0:T(8,128)(2,1)S(1)} %get-tuple-element.118), channel_id=1, source_target_pairs={{0,4},{4,0},{8,12},{12,8},{16,20},{20,16},{24,28},{28,24},{1,5},{5... | collective-permute-start | bytes 98312 | tf_op jit(solution)/shard_map/ppermute | solution.py:484
  123.7 4.3 %collective-permute-start.18 = (bf16[128,256]{1,0:T(8,128)(2,1)S(1)}, bf16[128,256]{1,0:T(8,128)(2,1)S(1)}, u32[]{:S(2)}, u32[]{:S(2)}) collective-permute-start(bf16[128,256]{1,0:T(8,128)(2,1)S(1)} %get-tuple-element.120), channel_id=1, source_target_pairs={{0,2},{1,3},{2,0},{3,1},{4,6},{5,7},{6,4},{7,5},{8,10},{9,11},{10,... | collective-permute-start | bytes 196616 | tf_op jit(solution)/shard_map/ppermute | solution.py:484
  125.5 9.1 %collective-permute-start.11 = (bf16[64,896]{1,0:T(8,128)(2,1)S(1)}, bf16[64,896]{1,0:T(8,128)(2,1)S(1)}, u32[]{:S(2)}, u32[]{:S(2)}) collective-permute-start(bf16[64,896]{1,0:T(8,128)(2,1)S(1)} %slice.43), channel_id=1, source_target_pairs={{0,16},{4,20},{8,24},{12,28},{16,0},{20,4},{24,8},{28,12},{1,17},{... | collective-permute-start | bytes 344072 | tf_op jit(solution)/shard_map/ppermute | solution.py:484
  128.0 5.4 %collective-permute-start.19 = (bf16[64,128]{1,0:T(8,128)(2,1)S(1)}, bf16[64,128]{1,0:T(8,128)(2,1)S(1)}, u32[]{:S(2)}, u32[]{:S(2)}) collective-permute-start(bf16[64,128]{1,0:T(8,128)(2,1)S(1)} %get-tuple-element.122), channel_id=1, source_target_pairs={{0,2},{1,3},{2,0},{3,1},{4,6},{5,7},{6,4},{7,5},{8,10},{9,11},{10,... | collective-permute-start | bytes 49160 | tf_op jit(solution)/shard_map/ppermute | solution.py:484
  129.8 3.9 %collective-permute-start.20 = (bf16[64,256]{1,0:T(8,128)(2,1)S(1)}, bf16[64,256]{1,0:T(8,128)(2,1)S(1)}, u32[]{:S(2)}, u32[]{:S(2)}) collective-permute-start(bf16[64,256]{1,0:T(8,128)(2,1)S(1)} %get-tuple-element.123), channel_id=1, source_target_pairs={{0,4},{4,0},{8,12},{12,8},{16,20},{20,16},{24,28},{28,24},{1,5},{5... | collective-permute-start | bytes 98312 | tf_op jit(solution)/shard_map/ppermute | solution.py:484
  130.1 6.0 %collective-permute-start.15 = (bf16[64,896]{1,0:T(8,128)(2,1)S(1)}, bf16[64,896]{1,0:T(8,128)(2,1)S(1)}, u32[]{:S(2)}, u32[]{:S(2)}) collective-permute-start(bf16[64,896]{1,0:T(8,128)(2,1)S(1)} %slice.42), channel_id=1, source_target_pairs={{0,16},{4,20},{8,24},{12,28},{16,0},{20,4},{24,8},{28,12},{1,17},{... | collective-permute-start | bytes 344072 | tf_op jit(solution)/shard_map/ppermute | solution.py:484

commit v8 on v7

--- a/solution.py
+++ b/solution.py
@@ -53,7 +53,7 @@
             bytes_accessed=bank.shape[0] * emb * 2,
             transcendentals=rows * bank.shape[0],
         ),
-        compiler_params=params(44),
+        compiler_params=params(20),
         name="negatives",
     )(q, bank)
 
@@ -158,7 +158,7 @@
         cost_estimate=pl.CostEstimate(
             flops=2 * rows * d * (hid + rows), bytes_accessed=2 * d * hid, transcendentals=0
         ),
-        compiler_params=params(50),
+        compiler_params=params(44),
         name="key_hidden",
     )(flat_col, k, w)
 
@@ -269,7 +269,7 @@
         cost_estimate=pl.CostEstimate(
             flops=2 * rows * hid * (d + emb), bytes_accessed=2 * d * hid, transcendentals=0
         ),
-        compiler_params=params(44),
+        compiler_params=params(40),
         name="query_forward",
     )(order, x, w, w2)
     return (*out[:4], *(t.reshape(d, rows) for t in out[4:]))
@@ -339,7 +339,7 @@
         cost_estimate=pl.CostEstimate(
             flops=2 * rows * hid * emb, bytes_accessed=4 * rows * hid, transcendentals=0
         ),
-        compiler_params=params(30),
+        compiler_params=params(20),
         name="embed",
     )(flat_row, h, told, w2, zq, negs)
 
@@ -666,32 +666,32 @@
     out = three.add(half_rows, 1, "send")
     three.cross_line(out, 1)
     one.keep = piece(1, rows, 1, *out)
-    one.hold(one.keep[0])
+    three.keep = piece(3, half_rows, 0, one.keep[0])
+    one.hold(three.keep[0])
     out = one.add(rows, 1, "sides")
     one.cross_second(out)
-    two.keep = piece(2, half_rows, 0, *out)
-    three.keep = piece(3, half_rows, 0, two.keep[0])
-    two.hold(three.keep[0])
-    out = two.add(rows, 1, "sides")
-    two.cross_second(out)
     line_rows = half_rows
     for bit in range(1, bits):
         line_rows //= 2
         three.hold(*out)
         out = three.add(line_rows, 1, "send")
         three.cross_line(out, 2 ** bit)
-    one.keep = piece(1, rows, 0, *out)
-    one.hold(one.keep[0])
+    two.keep = piece(2, half_rows, 0, *out)
+    one.keep = piece(1, rows, 0, two.keep[0])
+    two.hold(two.keep[0], one.keep[0])
+    out = two.add(rows, 1, "sides")
+    two.cross_second(out)
+    three.hold(*out)
+    line_rows //= 2
+    out = three.add(line_rows, 1, "sides")
+    three.cross_first(out)
+    one.hold(*out)
     c_1 = one.add(rows, 0, "halves")
     two.hold(*c_1)
     c_2 = two.add(rows, 0, "halves")
     own_1 = lax.optimization_barrier(one.cross_third(c_1))
-    three.hold(*c_2)
-    line_rows //= 2
-    out = three.add(line_rows, 1, "sides")
-    three.cross_first(out)
     own_2 = lax.optimization_barrier(two.cross_third(c_2))
-    three.hold(own_1)
+    three.hold(own_1, own_2)
     line_rows //= 2
     out = three.add(line_rows, 1, "sides")
     three.cross_second(out)

time: 138 us -> 138 us (level)
  starting transfers between devices: 33.1 us -> 29.4 us
  local copies, waits for them, and re-layouts: 14.7 us -> 18.3 us
  waiting for transfers between devices: 26.8 us -> 28.4 us
    ppermute x21, starting transfers between devices: 25.5 us -> 21 us  [swap(): return lax.ppermute(x, axis, [(i, i ^ bit) for i in range(size)])]
    unnamed x28 -> x32, local copies, waits for them, and re-layouts: 13.7 us -> 17.2 us
    ppermute x21, waiting for transfers between devices: 24.3 us -> 26.9 us  [swap(): return lax.ppermute(x, axis, [(i, i ^ bit) for i in range(size)])]
  transfers between devices with their start and end apart: 23 -> 23, of which waited for: 13 -> 11; matrix products, arithmetic and copies ran while one was open for 1% -> 1% of each run, Pallas kernels for 22% -> 21%
where the time goes in v8:
time: 138 us; the launch traced here: 137 us
  Pallas kernels  44.2 us (32%)
  starting transfers between devices  29.4 us (21%)
  waiting for transfers between devices  28.4 us (21%)
  local copies, waits for them, and re-layouts  18.3 us (13%)
  blocking collectives  14.2 us (10%)
  other arithmetic  1.74 us (1%)
    ppermute x21, waiting for transfers between devices, swap(): return lax.ppermute(x, axis, [(i, i ^ bit) for i in range(size)])  26.9 us
    ppermute x21, starting transfers between devices, swap(): return lax.ppermute(x, axis, [(i, i ^ bit) for i in range(size)])  21 us
    unnamed x32, local copies, waits for them, and re-layouts  17.2 us
    all_to_all x1, blocking collectives, per_device(): lax.all_to_all(wanted, AXES, split_axis=0, concat_axis=0, tiled=True)  14.2 us
    pallas_call x1, Pallas kernels, negatives(): pl.pallas_call(neg_kernel, grid=(bank.shape[0] // tile,), in_specs=[pl.Bl...  11 us
    pallas_call x1, Pallas kernels, key_hidden(): pl.pallas_call(lambda *refs: key_hidden_kernel(groups, *refs), grid=(hid...  9.81 us
    pallas_call x1, Pallas kernels, query_forward(): pl.pallas_call(lambda *refs: query_kernel(size, *refs), grid_spec=pltpu.P...  9.64 us
    pallas_call x2, Pallas kernels, send_half(): pl.pallas_call(lambda *refs: send_kernel(sizes, old_plain, at is not None...  6.14 us
  transfers between devices with their start and end apart: 23, of which 11 were waited for; matrix products, arithmetic and copies ran while one was open for 1% of the time, Pallas kernels for 21%

profile of v8, /device:TPU:0, one launch (start us, length us, event | category | flops | bytes accessed | tf_op | source)
XLA Modules:
  0.0 137.4 jit_solution(7212336304127788201)
XLA Ops:
  1.4 14.2 %all_to_all.22 = f32[32,1,128]{2,1,0:T(1,128)S(1)} all-to-all(f32[32,1,128]{2,1,0:T(1,128)S(1)} %bitcast.21), channel_id=1, replica_groups=mesh['dp'=8,'crop'=4] {'dp','crop'}, dimensions={0} | all-to-all | bytes 32768 | tf_op jit(solution)/shard_map/all_to_all | solution.py:595
  15.8 1.6 %copy-done.14 = bf16[512,2048]{1,0:T(8,128)(2,1)S(1)} copy-done((bf16[512,2048]{1,0:T(8,128)(2,1)S(1)}, bf16[512,2048]{1,0:T(8,128)(2,1)}, u32[]{:S(2)}) %copy-start.14) | copy-done | bytes 2097176
  17.4 9.8 %key_hidden.1 = (f32[512,2048]{1,0:T(8,128)S(1)}, f32[32,1,4096]{2,1,0:T(1,128)}) custom-call(s32[512,1]{1,0:T(8,128)S(1)} %broadcast_in_dim_reshape.8.refs_0_, bf16[512,2048]{1,0:T(8,128)(2,1)S(1)} %copy-done.14, bf16[2048,2048]{1,0:T(8,128)(2,1)} %refs_2_.3), custom_call_target="tpu_custom_call" | custom-call | flops 5368709120 | bytes 8388608 | tf_op jit(solution)/shard_map/key_hidden/pallas_call | solution.py:141
  27.2 2.0 %copy-done.7 = f32[512,2048]{1,0:T(8,128)} copy-done((f32[512,2048]{1,0:T(8,128)}, f32[512,2048]{1,0:T(8,128)S(1)}, u32[]{:S(2)}) %copy-start.7) | copy-done | bytes 4194328
  29.2 2.6 %all-to-all-start.1 = ((f32[32,1,4096]{2,1,0:T(1,128)}), f32[32,1,4096]{2,1,0:T(1,128)S(1)}, u32[]{:S(2)}, u32[]{:S(2)}) async-start(f32[32,1,4096]{2,1,0:T(1,128)} %get-tuple-element.63), calls=%async_computation.1 | async-start | bytes 1048576 | tf_op jit(solution)/shard_map/all_to_all | solution.py:600
  32.1 1.6 %copy-done.15 = bf16[512,2048]{1,0:T(8,128)(2,1)S(1)} copy-done((bf16[512,2048]{1,0:T(8,128)(2,1)S(1)}, bf16[512,2048]{1,0:T(8,128)(2,1)}, u32[]{:S(2)}) %copy-start.15) | copy-done | bytes 2097176
  33.7 9.6 %query_forward.1 = (bf16[512,2048]{1,0:T(8,128)(2,1)S(1)}, f32[1,2048]{1,0:T(1,128)S(1)}, f32[512,128]{1,0:T(8,128)S(1)}, bf16[512,128]{1,0:T(8,128)(2,1)S(1)}, ...) custom-call(s32[3,16]{1,0:T(4,128)S(1)} %add_add_fusion.refs_0_, ...), custom_call_target="tpu_custom_call" | custom-call | flops 4563402752 | bytes 8388608 | tf_op jit(solution)/shard_map/query_forward/pallas_call | solution.py:239
  43.4 1.3 copy-done
  44.7 1.4 copy-done.2
  46.0 1.4 %copy-done.4 = bf16[2,16,64,512]{3,2,1,0:T(8,128)(2,1)} copy-done((bf16[2,16,64,512]{3,2,1,0:T(8,128)(2,1)}, bf16[2,16,64,512]{3,2,1,0:T(8,128)(2,1)S(1)}, u32[]{:S(2)}) %copy-start.4) | copy-done | bytes 2097176
  47.7 0.8 copy-done.9
  48.5 5.8 %all-to-all-start.2 = ((f32[32,1,4096]{2,1,0:T(1,128)}), f32[32,1,4096]{2,1,0:T(1,128)S(1)}, u32[]{:S(2)}, u32[]{:S(2)}) async-start(f32[32,1,4096]{2,1,0:T(1,128)} %copy-done.9), calls=%async_computation.2 | async-start | bytes 1048576 | tf_op jit(solution)/shard_map/all_to_all | solution.py:620
  54.3 2.2 %copy-done.13 = bf16[16384,128]{1,0:T(8,128)(2,1)S(1)} copy-done((bf16[16384,128]{1,0:T(8,128)(2,1)S(1)}, bf16[16384,128]{1,0:T(8,128)(2,1)}, u32[]{:S(2)}) %copy-start.13) | copy-done | bytes 4194328
  56.5 11.0 %negatives.1.refs_5_ = f32[512,256]{1,0:T(8,128)S(1)} custom-call(bf16[512,128]{1,0:T(8,128)(2,1)S(1)} %get-tuple-element.70.q_ref, bf16[16384,128]{1,0:T(8,128)(2,1)S(1)} %copy-done.13), custom_call_target="tpu_custom_call" | custom-call | flops 4294967296 | bytes 4194304 | tf_op jit(solution)/shard_map/negatives/pallas_call | solution.py:42
  67.5 0.8 copy-done.11
  68.3 1.6 %all-to-all-done.2.refs_2_ = f32[32,1,4096]{2,1,0:T(1,128)S(1)} async-done(((f32[32,1,4096]{2,1,0:T(1,128)}), f32[32,1,4096]{2,1,0:T(1,128)S(1)}, u32[]{:S(2)}, u32[]{:S(2)}) %all-to-all-start.2) | async-done | bytes 524320 | tf_op jit(solution)/shard_map/all_to_all | solution.py:620
  69.9 2.2 %copy-done.8 = f32[512,2048]{1,0:T(8,128)S(1)} copy-done((f32[512,2048]{1,0:T(8,128)S(1)}, f32[512,2048]{1,0:T(8,128)}, u32[]{:S(2)}) %copy-start.8) | copy-done | bytes 4194328
  72.1 1.0 copy-done.10
  73.1 1.0 copy-done.12
  74.1 2.8 %embed.1.refs_0_.z = bf16[512,128]{1,0:T(8,128)(2,1)S(1)} custom-call(s32[1,512]{1,0:T(1,128)S(1)} %broadcast_in_dim_reshape.7.refs_0_, f32[512,2048]{1,0:T(8,128)S(1)} %copy-done.8, f32[32,1,4096]{2,1,0:T(1,128)S(1)} %all-to-all-done.2.refs_2_, bf16[2048,128]{1,0:T(8,128)(2,1)S(1)} %copy-done.10, f32[512,128]{1,0:T(8,128)S(1)} %get-tuple-element.72.refs_4_, ...), custom_call_target="tpu_custom_call" | custom-call | flops 268435456 | bytes 4194304 | tf_op jit(solution)/shard_map/embed/pallas_call | solution.py:325
  77.0 2.2 %send_half.2 = (bf16[512,896]{1,0:T(8,128)(2,1)S(1)}, bf16[1024,896]{1,0:T(8,128)(2,1)S(1)}) custom-call(bf16[512,128]{1,0:T(8,128)(2,1)S(1)} %embed.1.refs_0_.z, bf16[2048,512]{1,0:T(8,128)(2,1)S(1)} %bitcast.8, bf16[2048,128]{1,0:T(8,128)(2,1)S(1)} %copy-done.6, bf16[512,2048]{1,0:T(8,128)(2,1)S(1)} %copy-done.1, ...), custom_call_target="tpu_custom_call" | custom-call | flops 939524096 | bytes 4194304 | tf_op jit(solution)/shard_map/send_half/pallas_call | solution.py:437
  79.2 4.0 %send_half.3 = (f32[512,896]{1,0:T(8,128)S(1)}, bf16[512,896]{1,0:T(8,128)(2,1)S(1)}, bf16[1024,896]{1,0:T(8,128)(2,1)S(1)}, bf16[512,256]{1,0:T(8,128)(2,1)S(1)}, bf16[1024,384]{1,0:T(8,128)(2,1)S(1)}) custom-call(bf16[512,128]{1,0:T(8,128)(2,1)S(1)} %embed.1.refs_0_.z, bf16[2048,512]{1,0:T(8,128)(2,1)S(1)} %bitcast.18, bf16[2048,512]{1,0:T(8,128)(2,1)S(1)} %bitcast.9, ...), custom_call_target="tpu_custom_call" | custom-call | flops 1207959552 | bytes 4194304 | tf_op jit(solution)/shard_map/send_half/pallas_call | solution.py:437
  84.0 1.3 collective-permute-start.4
  85.3 1.2 collective-permute-start.5
  86.5 0.7 keep_half.6.refs_0_
  88.4 1.3 collective-permute-start.3
  90.3 1.2 collective-permute-start.7
  92.6 4.7 %collective-permute-done.5.refs_3_.refs_4_ = bf16[512,384]{1,0:T(8,128)(2,1)S(1)} collective-permute-done((bf16[512,384]{1,0:T(8,128)(2,1)S(1)}, bf16[512,384]{1,0:T(8,128)(2,1)S(1)}, u32[]{:S(2)}, u32[]{:S(2)}) %collective-permute-start.5) | collective-permute-done | bytes 393248 | tf_op jit(solution)/shard_map/ppermute | solution.py:484
  97.3 1.5 %collective-permute-done.4.refs_2_ = bf16[512,512]{1,0:T(8,128)(2,1)S(1)} collective-permute-done((bf16[512,512]{1,0:T(8,128)(2,1)S(1)}, bf16[512,512]{1,0:T(8,128)(2,1)S(1)}, u32[]{:S(2)}, u32[]{:S(2)}) %collective-permute-start.4) | collective-permute-done | bytes 524320 | tf_op jit(solution)/shard_map/ppermute | solution.py:484
  98.9 1.4 collective-permute-start.9
  100.3 1.5 %collective-permute-start.6 = (bf16[256,384]{1,0:T(8,128)(2,1)S(1)}, bf16[256,384]{1,0:T(8,128)(2,1)S(1)}, u32[]{:S(2)}, u32[]{:S(2)}) collective-permute-start(bf16[256,384]{1,0:T(8,128)(2,1)S(1)} %fold.15), channel_id=1, source_target_pairs={{0,16},{4,20},{8,24},{12,28},{16,0},{20,4},{24,8},{28,12},{1,17},{... | collective-permute-start | bytes 589832 | tf_op jit(solution)/shard_map/ppermute | solution.py:484
  101.8 1.5 %collective-permute-start.10 = (bf16[256,384]{1,0:T(8,128)(2,1)S(1)}, bf16[256,384]{1,0:T(8,128)(2,1)S(1)}, u32[]{:S(2)}, u32[]{:S(2)}) collective-permute-start(bf16[256,384]{1,0:T(8,128)(2,1)S(1)} %get-tuple-element.97), channel_id=1, source_target_pairs={{0,4},{4,0},{8,12},{12,8},{16,20},{20,16},{24,28},{28,24},{1,5},{5... | collective-permute-start | bytes 589832 | tf_op jit(solution)/shard_map/ppermute | solution.py:484
  104.4 4.1 %collective-permute-done.8.refs_3_.refs_4_ = bf16[512,512]{1,0:T(8,128)(2,1)S(1)} collective-permute-done((bf16[512,512]{1,0:T(8,128)(2,1)S(1)}, bf16[512,512]{1,0:T(8,128)(2,1)S(1)}, u32[]{:S(2)}, u32[]{:S(2)}) %collective-permute-start.8) | collective-permute-done | bytes 524320 | tf_op jit(solution)/shard_map/ppermute | solution.py:484
  108.6 0.8 collective-permute-start.14
  109.5 1.9 %collective-permute-done.6.refs_3_ = bf16[256,384]{1,0:T(8,128)(2,1)S(1)} collective-permute-done((bf16[256,384]{1,0:T(8,128)(2,1)S(1)}, bf16[256,384]{1,0:T(8,128)(2,1)S(1)}, u32[]{:S(2)}, u32[]{:S(2)}) %collective-permute-start.6) | collective-permute-done | bytes 196640 | tf_op jit(solution)/shard_map/ppermute | solution.py:484
  111.5 1.9 %collective-permute-done.9.refs_3_ = bf16[256,512]{1,0:T(8,128)(2,1)S(1)} collective-permute-done((bf16[256,512]{1,0:T(8,128)(2,1)S(1)}, bf16[256,512]{1,0:T(8,128)(2,1)S(1)}, u32[]{:S(2)}, u32[]{:S(2)}) %collective-permute-start.9) | collective-permute-done | bytes 262176 | tf_op jit(solution)/shard_map/ppermute | solution.py:484
  113.5 0.9 collective-permute-start.11
  114.4 1.1 collective-permute-start.13
  116.0 1.6 %collective-permute-start.18 = (bf16[128,256]{1,0:T(8,128)(2,1)S(1)}, bf16[128,256]{1,0:T(8,128)(2,1)S(1)}, u32[]{:S(2)}, u32[]{:S(2)}) collective-permute-start(bf16[128,256]{1,0:T(8,128)(2,1)S(1)} %get-tuple-element.108), channel_id=1, source_target_pairs={{0,2},{1,3},{2,0},{3,1},{4,6},{5,7},{6,4},{7,5},{8,10},{9,11},{10,... | collective-permute-start | bytes 196616 | tf_op jit(solution)/shard_map/ppermute | solution.py:484
  117.7 3.3 %collective-permute-done.13.refs_3_ = bf16[256,384]{1,0:T(8,128)(2,1)S(1)} collective-permute-done((bf16[256,384]{1,0:T(8,128)(2,1)S(1)}, bf16[256,384]{1,0:T(8,128)(2,1)S(1)}, u32[]{:S(2)}, u32[]{:S(2)}) %collective-permute-start.13) | collective-permute-done | bytes 196640 | tf_op jit(solution)/shard_map/ppermute | solution.py:484
  121.2 1.3 collective-permute-start.15
  122.5 1.3 collective-permute-start.12
  123.8 4.8 %collective-permute-done.15 = bf16[128,896]{1,0:T(8,128)(2,1)S(1)} collective-permute-done((bf16[128,896]{1,0:T(8,128)(2,1)S(1)}, bf16[128,896]{1,0:T(8,128)(2,1)S(1)}, u32[]{:S(2)}, u32[]{:S(2)}) %collective-permute-start.15) | collective-permute-done | bytes 229408 | tf_op jit(solution)/shard_map/ppermute | solution.py:484
  128.7 1.3 collective-permute-start.20
  130.2 1.3 collective-permute-start.16
  131.5 2.3 %collective-permute-done.19.refs_5_ = bf16[64,128]{1,0:T(8,128)(2,1)S(1)} collective-permute-done((bf16[64,128]{1,0:T(8,128)(2,1)S(1)}, bf16[64,128]{1,0:T(8,128)(2,1)S(1)}, u32[]{:S(2)}, u32[]{:S(2)}) %collective-permute-start.19) | collective-permute-done | bytes 16416 | tf_op jit(solution)/shard_map/ppermute | solution.py:484
  134.5 2.0 %collective-permute-done.16 = bf16[64,896]{1,0:T(8,128)(2,1)S(1)} collective-permute-done((bf16[64,896]{1,0:T(8,128)(2,1)S(1)}, bf16[64,896]{1,0:T(8,128)(2,1)S(1)}, u32[]{:S(2)}, u32[]{:S(2)}) %collective-permute-start.16) | collective-permute-done | bytes 114720 | tf_op jit(solution)/shard_map/ppermute | solution.py:484
  136.6 0.8 pad_maximum_fusion
  (73 shorter events, 8.6 us)
Async XLA Ops:
  15.8 1.6 %copy-start.14 = (bf16[512,2048]{1,0:T(8,128)(2,1)S(1)}, bf16[512,2048]{1,0:T(8,128)(2,1)}, u32[]{:S(2)}) copy-start(bf16[512,2048]{1,0:T(8,128)(2,1)} %refs_1_.1) | copy-start | bytes 6291460
  17.4 14.7 %copy-start.6 = (bf16[2048,128]{1,0:T(8,128)(2,1)S(1)}, bf16[2048,128]{1,0:T(8,128)(2,1)}, u32[]{:S(2)}) copy-start(bf16[2048,128]{1,0:T(8,128)(2,1)} %refs_9_.1) | copy-start | bytes 1572868
  27.2 2.0 %copy-start.7 = (f32[512,2048]{1,0:T(8,128)}, f32[512,2048]{1,0:T(8,128)S(1)}, u32[]{:S(2)}) copy-start(f32[512,2048]{1,0:T(8,128)S(1)} %get-tuple-element.68.refs_1_) | copy-start | bytes 12582916
  29.2 18.2 %all-to-all-start.1 = ((f32[32,1,4096]{2,1,0:T(1,128)}), f32[32,1,4096]{2,1,0:T(1,128)S(1)}, u32[]{:S(2)}, u32[]{:S(2)}) async-start(f32[32,1,4096]{2,1,0:T(1,128)} %get-tuple-element.63), calls=%async_computation.1 | async-start | bytes 1048576 | tf_op jit(solution)/shard_map/all_to_all | solution.py:600
  32.1 1.6 %copy-start.15 = (bf16[512,2048]{1,0:T(8,128)(2,1)S(1)}, bf16[512,2048]{1,0:T(8,128)(2,1)}, u32[]{:S(2)}) copy-start(bf16[512,2048]{1,0:T(8,128)(2,1)} %refs_1_.2) | copy-start | bytes 6291460
  43.4 1.3 copy-start
  44.7 1.4 copy-start.2
  46.0 1.4 %copy-start.4 = (bf16[2,16,64,512]{3,2,1,0:T(8,128)(2,1)}, bf16[2,16,64,512]{3,2,1,0:T(8,128)(2,1)S(1)}, u32[]{:S(2)}) copy-start(bf16[2,16,64,512]{3,2,1,0:T(8,128)(2,1)S(1)} %get-tuple-element.77) | copy-start | bytes 6291460
  47.7 0.8 copy-start.9
  48.5 21.4 %all-to-all-start.2 = ((f32[32,1,4096]{2,1,0:T(1,128)}), f32[32,1,4096]{2,1,0:T(1,128)S(1)}, u32[]{:S(2)}, u32[]{:S(2)}) async-start(f32[32,1,4096]{2,1,0:T(1,128)} %copy-done.9), calls=%async_computation.2 | async-start | bytes 1048576 | tf_op jit(solution)/shard_map/all_to_all | solution.py:620
  54.3 2.2 %copy-start.13 = (bf16[16384,128]{1,0:T(8,128)(2,1)S(1)}, bf16[16384,128]{1,0:T(8,128)(2,1)}, u32[]{:S(2)}) copy-start(bf16[16384,128]{1,0:T(8,128)(2,1)} %bank_ref.1) | copy-start | bytes 12582916
  67.5 0.8 copy-start.11
  69.9 2.2 %copy-start.8 = (f32[512,2048]{1,0:T(8,128)S(1)}, f32[512,2048]{1,0:T(8,128)}, u32[]{:S(2)}) copy-start(f32[512,2048]{1,0:T(8,128)} %copy-done.7) | copy-start | bytes 12582916
  72.0 1.0 copy-start.10
  73.1 1.0 copy-start.12
  74.1 2.8 %copy-start.1 = (bf16[512,2048]{1,0:T(8,128)(2,1)S(1)}, bf16[512,2048]{1,0:T(8,128)(2,1)}, u32[]{:S(2)}) copy-start(bf16[512,2048]{1,0:T(8,128)(2,1)} %copy-done) | copy-start | bytes 6291460
  76.9 2.3 %copy-start.3 = (bf16[2,16,64,512]{3,2,1,0:T(8,128)(2,1)S(1)}, bf16[2,16,64,512]{3,2,1,0:T(8,128)(2,1)}, u32[]{:S(2)}) copy-start(bf16[2,16,64,512]{3,2,1,0:T(8,128)(2,1)} %copy-done.2) | copy-start | bytes 6291460
  76.9 2.3 %copy-start.5 = (bf16[2,16,64,512]{3,2,1,0:T(8,128)(2,1)S(1)}, bf16[2,16,64,512]{3,2,1,0:T(8,128)(2,1)}, u32[]{:S(2)}) copy-start(bf16[2,16,64,512]{3,2,1,0:T(8,128)(2,1)} %copy-done.4) | copy-start | bytes 6291460
  79.1 4.7 %collective-permute-start = (bf16[1024,896]{1,0:T(8,128)(2,1)S(1)}, bf16[1024,896]{1,0:T(8,128)(2,1)S(1)}, u32[]{:S(2)}, u32[]{:S(2)}) collective-permute-start(bf16[1024,896]{1,0:T(8,128)(2,1)S(1)} %get-tuple-element.82), channel_id=1, source_target_pairs={{0,1},{1,0},{2,3},{3,2},{4,5},{5,4},{6,7},{7,6},{8,9},{9,8},{10,11... | collective-permute-start | bytes 5505032 | tf_op jit(solution)/shard_map/ppermute | solution.py:484
  83.2 4.0 %collective-permute-start.1 = (bf16[1024,896]{1,0:T(8,128)(2,1)S(1)}, bf16[1024,896]{1,0:T(8,128)(2,1)S(1)}, u32[]{:S(2)}, u32[]{:S(2)}) collective-permute-start(bf16[1024,896]{1,0:T(8,128)(2,1)S(1)} %get-tuple-element.86), channel_id=1, source_target_pairs={{0,1},{1,0},{2,3},{3,2},{4,5},{5,4},{6,7},{7,6},{8,9},{9,8},{10,11... | collective-permute-start | bytes 5505032 | tf_op jit(solution)/shard_map/ppermute | solution.py:484
  83.7 4.5 %collective-permute-start.2 = (bf16[1024,384]{1,0:T(8,128)(2,1)S(1)}, bf16[1024,384]{1,0:T(8,128)(2,1)S(1)}, u32[]{:S(2)}, u32[]{:S(2)}) collective-permute-start(bf16[1024,384]{1,0:T(8,128)(2,1)S(1)} %get-tuple-element.90), channel_id=1, source_target_pairs={{0,1},{1,0},{2,3},{3,2},{4,5},{5,4},{6,7},{7,6},{8,9},{9,8},{10,11... | collective-permute-start | bytes 2359304 | tf_op jit(solution)/shard_map/ppermute | solution.py:484
  84.0 14.8 %collective-permute-start.4 = (bf16[512,512]{1,0:T(8,128)(2,1)S(1)}, bf16[512,512]{1,0:T(8,128)(2,1)S(1)}, u32[]{:S(2)}, u32[]{:S(2)}) collective-permute-start(bf16[512,512]{1,0:T(8,128)(2,1)S(1)} %get-tuple-element.83), channel_id=1, source_target_pairs={{0,4},{4,0},{8,12},{12,8},{16,20},{20,16},{24,28},{28,24},{1,5},{5... | collective-permute-start | bytes 1572872 | tf_op jit(solution)/shard_map/ppermute | solution.py:484
  85.3 12.0 %collective-permute-start.5 = (bf16[512,384]{1,0:T(8,128)(2,1)S(1)}, bf16[512,384]{1,0:T(8,128)(2,1)S(1)}, u32[]{:S(2)}, u32[]{:S(2)}) collective-permute-start(bf16[512,384]{1,0:T(8,128)(2,1)S(1)} %get-tuple-element.84), channel_id=1, source_target_pairs={{0,2},{1,3},{2,0},{3,1},{4,6},{5,7},{6,4},{7,5},{8,10},{9,11},{10,... | collective-permute-start | bytes 1179656 | tf_op jit(solution)/shard_map/ppermute | solution.py:484
  88.4 11.9 %collective-permute-start.3 = (bf16[512,384]{1,0:T(8,128)(2,1)S(1)}, bf16[512,384]{1,0:T(8,128)(2,1)S(1)}, u32[]{:S(2)}, u32[]{:S(2)}) collective-permute-start(bf16[512,384]{1,0:T(8,128)(2,1)S(1)} %fold.13), channel_id=1, source_target_pairs={{0,8},{4,12},{8,0},{12,4},{16,24},{20,28},{24,16},{28,20},{1,9},{5... | collective-permute-start | bytes 1179656 | tf_op jit(solution)/shard_map/ppermute | solution.py:484
  89.7 18.8 %collective-permute-start.8 = (bf16[512,512]{1,0:T(8,128)(2,1)S(1)}, bf16[512,512]{1,0:T(8,128)(2,1)S(1)}, u32[]{:S(2)}, u32[]{:S(2)}) collective-permute-start(bf16[512,512]{1,0:T(8,128)(2,1)S(1)} %get-tuple-element.88), channel_id=1, source_target_pairs={{0,2},{1,3},{2,0},{3,1},{4,6},{5,7},{6,4},{7,5},{8,10},{9,11},{10,... | collective-permute-start | bytes 1572872 | tf_op jit(solution)/shard_map/ppermute | solution.py:484
  90.3 18.2 %collective-permute-start.7 = (bf16[512,384]{1,0:T(8,128)(2,1)S(1)}, bf16[512,384]{1,0:T(8,128)(2,1)S(1)}, u32[]{:S(2)}, u32[]{:S(2)}) collective-permute-start(bf16[512,384]{1,0:T(8,128)(2,1)S(1)} %get-tuple-element.87), channel_id=1, source_target_pairs={{0,4},{4,0},{8,12},{12,8},{16,20},{20,16},{24,28},{28,24},{1,5},{5... | collective-permute-start | bytes 1179656 | tf_op jit(solution)/shard_map/ppermute | solution.py:484
  98.9 14.4 %collective-permute-start.9 = (bf16[256,512]{1,0:T(8,128)(2,1)S(1)}, bf16[256,512]{1,0:T(8,128)(2,1)S(1)}, u32[]{:S(2)}, u32[]{:S(2)}) collective-permute-start(bf16[256,512]{1,0:T(8,128)(2,1)S(1)} %get-tuple-element.96), channel_id=1, source_target_pairs={{0,2},{1,3},{2,0},{3,1},{4,6},{5,7},{6,4},{7,5},{8,10},{9,11},{10,... | collective-permute-start | bytes 786440 | tf_op jit(solution)/shard_map/ppermute | solution.py:484
  100.3 11.1 %collective-permute-start.6 = (bf16[256,384]{1,0:T(8,128)(2,1)S(1)}, bf16[256,384]{1,0:T(8,128)(2,1)S(1)}, u32[]{:S(2)}, u32[]{:S(2)}) collective-permute-start(bf16[256,384]{1,0:T(8,128)(2,1)S(1)} %fold.15), channel_id=1, source_target_pairs={{0,16},{4,20},{8,24},{12,28},{16,0},{20,4},{24,8},{28,12},{1,17},{... | collective-permute-start | bytes 589832 | tf_op jit(solution)/shard_map/ppermute | solution.py:484
  101.8 9.7 %collective-permute-start.10 = (bf16[256,384]{1,0:T(8,128)(2,1)S(1)}, bf16[256,384]{1,0:T(8,128)(2,1)S(1)}, u32[]{:S(2)}, u32[]{:S(2)}) collective-permute-start(bf16[256,384]{1,0:T(8,128)(2,1)S(1)} %get-tuple-element.97), channel_id=1, source_target_pairs={{0,4},{4,0},{8,12},{12,8},{16,20},{20,16},{24,28},{28,24},{1,5},{5... | collective-permute-start | bytes 589832 | tf_op jit(solution)/shard_map/ppermute | solution.py:484
  108.6 12.3 %collective-permute-start.14 = (bf16[256,512]{1,0:T(8,128)(2,1)S(1)}, bf16[256,512]{1,0:T(8,128)(2,1)S(1)}, u32[]{:S(2)}, u32[]{:S(2)}) collective-permute-start(bf16[256,512]{1,0:T(8,128)(2,1)S(1)} %get-tuple-element.105), channel_id=1, source_target_pairs={{0,4},{4,0},{8,12},{12,8},{16,20},{20,16},{24,28},{28,24},{1,5},{5... | collective-permute-start | bytes 786440 | tf_op jit(solution)/shard_map/ppermute | solution.py:484
  113.5 8.9 %collective-permute-start.11 = (bf16[128,896]{1,0:T(8,128)(2,1)S(1)}, bf16[128,896]{1,0:T(8,128)(2,1)S(1)}, u32[]{:S(2)}, u32[]{:S(2)}) collective-permute-start(bf16[128,896]{1,0:T(8,128)(2,1)S(1)} %get-tuple-element.113), channel_id=1, source_target_pairs={{0,8},{4,12},{8,0},{12,4},{16,24},{20,28},{24,16},{28,20},{1,9},{5... | collective-permute-start | bytes 688136 | tf_op jit(solution)/shard_map/ppermute | solution.py:484
  114.4 6.6 %collective-permute-start.13 = (bf16[256,384]{1,0:T(8,128)(2,1)S(1)}, bf16[256,384]{1,0:T(8,128)(2,1)S(1)}, u32[]{:S(2)}, u32[]{:S(2)}) collective-permute-start(bf16[256,384]{1,0:T(8,128)(2,1)S(1)} %get-tuple-element.104), channel_id=1, source_target_pairs={{0,2},{1,3},{2,0},{3,1},{4,6},{5,7},{6,4},{7,5},{8,10},{9,11},{10,... | collective-permute-start | bytes 589832 | tf_op jit(solution)/shard_map/ppermute | solution.py:484
  115.5 13.2 %collective-permute-start.17 = (bf16[128,128]{1,0:T(8,128)(2,1)S(1)}, bf16[128,128]{1,0:T(8,128)(2,1)S(1)}, u32[]{:S(2)}, u32[]{:S(2)}) collective-permute-start(bf16[128,128]{1,0:T(8,128)(2,1)S(1)} %get-tuple-element.107), channel_id=1, source_target_pairs={{0,4},{4,0},{8,12},{12,8},{16,20},{20,16},{24,28},{28,24},{1,5},{5... | collective-permute-start | bytes 98312 | tf_op jit(solution)/shard_map/ppermute | solution.py:484
  116.0 12.6 %collective-permute-start.18 = (bf16[128,256]{1,0:T(8,128)(2,1)S(1)}, bf16[128,256]{1,0:T(8,128)(2,1)S(1)}, u32[]{:S(2)}, u32[]{:S(2)}) collective-permute-start(bf16[128,256]{1,0:T(8,128)(2,1)S(1)} %get-tuple-element.108), channel_id=1, source_target_pairs={{0,2},{1,3},{2,0},{3,1},{4,6},{5,7},{6,4},{7,5},{8,10},{9,11},{10,... | collective-permute-start | bytes 196616 | tf_op jit(solution)/shard_map/ppermute | solution.py:484
  121.2 7.5 %collective-permute-start.15 = (bf16[128,896]{1,0:T(8,128)(2,1)S(1)}, bf16[128,896]{1,0:T(8,128)(2,1)S(1)}, u32[]{:S(2)}, u32[]{:S(2)}) collective-permute-start(bf16[128,896]{1,0:T(8,128)(2,1)S(1)} %get-tuple-element.118), channel_id=1, source_target_pairs={{0,8},{4,12},{8,0},{12,4},{16,24},{20,28},{24,16},{28,20},{1,9},{5... | collective-permute-start | bytes 688136 | tf_op jit(solution)/shard_map/ppermute | solution.py:484
  122.5 11.9 %collective-permute-start.12 = (bf16[64,896]{1,0:T(8,128)(2,1)S(1)}, bf16[64,896]{1,0:T(8,128)(2,1)S(1)}, u32[]{:S(2)}, u32[]{:S(2)}) collective-permute-start(bf16[64,896]{1,0:T(8,128)(2,1)S(1)} %slice.43), channel_id=1, source_target_pairs={{0,16},{4,20},{8,24},{12,28},{16,0},{20,4},{24,8},{28,12},{1,17},{... | collective-permute-start | bytes 344072 | tf_op jit(solution)/shard_map/ppermute | solution.py:484
  128.7 5.1 %collective-permute-start.20 = (bf16[64,256]{1,0:T(8,128)(2,1)S(1)}, bf16[64,256]{1,0:T(8,128)(2,1)S(1)}, u32[]{:S(2)}, u32[]{:S(2)}) collective-permute-start(bf16[64,256]{1,0:T(8,128)(2,1)S(1)} %get-tuple-element.123), channel_id=1, source_target_pairs={{0,4},{4,0},{8,12},{12,8},{16,20},{20,16},{24,28},{28,24},{1,5},{5... | collective-permute-start | bytes 98312 | tf_op jit(solution)/shard_map/ppermute | solution.py:484
  130.0 3.7 %collective-permute-start.19 = (bf16[64,128]{1,0:T(8,128)(2,1)S(1)}, bf16[64,128]{1,0:T(8,128)(2,1)S(1)}, u32[]{:S(2)}, u32[]{:S(2)}) collective-permute-start(bf16[64,128]{1,0:T(8,128)(2,1)S(1)} %get-tuple-element.122), channel_id=1, source_target_pairs={{0,2},{1,3},{2,0},{3,1},{4,6},{5,7},{6,4},{7,5},{8,10},{9,11},{10,... | collective-permute-start | bytes 49160 | tf_op jit(solution)/shard_map/ppermute | solution.py:484
  130.2 6.3 %collective-permute-start.16 = (bf16[64,896]{1,0:T(8,128)(2,1)S(1)}, bf16[64,896]{1,0:T(8,128)(2,1)S(1)}, u32[]{:S(2)}, u32[]{:S(2)}) collective-permute-start(bf16[64,896]{1,0:T(8,128)(2,1)S(1)} %slice.42), channel_id=1, source_target_pairs={{0,16},{4,20},{8,24},{12,28},{16,0},{20,4},{24,8},{28,12},{1,17},{... | collective-permute-start | bytes 344072 | tf_op jit(solution)/shard_map/ppermute | solution.py:484

commit v9 on v8

--- a/solution.py
+++ b/solution.py
@@ -53,7 +53,7 @@
             bytes_accessed=bank.shape[0] * emb * 2,
             transcendentals=rows * bank.shape[0],
         ),
-        compiler_params=params(20),
+        compiler_params=params(44),
         name="negatives",
     )(q, bank)
 
@@ -158,7 +158,7 @@
         cost_estimate=pl.CostEstimate(
             flops=2 * rows * d * (hid + rows), bytes_accessed=2 * d * hid, transcendentals=0
         ),
-        compiler_params=params(44),
+        compiler_params=params(50),
         name="key_hidden",
     )(flat_col, k, w)
 
@@ -269,7 +269,7 @@
         cost_estimate=pl.CostEstimate(
             flops=2 * rows * hid * (d + emb), bytes_accessed=2 * d * hid, transcendentals=0
         ),
-        compiler_params=params(40),
+        compiler_params=params(44),
         name="query_forward",
     )(order, x, w, w2)
     return (*out[:4], *(t.reshape(d, rows) for t in out[4:]))
@@ -339,7 +339,7 @@
         cost_estimate=pl.CostEstimate(
             flops=2 * rows * hid * emb, bytes_accessed=4 * rows * hid, transcendentals=0
         ),
-        compiler_params=params(20),
+        compiler_params=params(30),
         name="embed",
     )(flat_row, h, told, w2, zq, negs)
 
@@ -504,21 +504,27 @@
             outs[0][:, cols] = v[:half]
             outs[1][:, cols] = v[half:].astype(jnp.bfloat16)
         elif form == "sides":
-            outs[side][...] = v.astype(jnp.bfloat16)
+            width = v.shape[1]
+            outs[side][:, :width] = v.astype(jnp.bfloat16)
+            if outs[side].shape[1] > width:
+                outs[side][:, width:] = jnp.zeros_like(outs[side][:, width:])
         else:
             outs[0][:, cols] = v.astype(outs[0].dtype)
 
 
-def fold(keep, keep_place, both, left, right, split, rows, place, form):
+def fold(keep, keep_place, both, left, right, split, rows, place, form, even):
     cols = keep.shape[1]
 
     def spec(width, place=place):
         return pl.BlockSpec((rows, width), lambda i: (place, 0))
 
     low, full = jnp.bfloat16, jnp.float32
+    widths = (split, cols - split)
+    if even:
+        widths = (max(widths),) * 2
     shapes = {
         "halves": [((rows // 2, cols), full), ((rows // 2, cols), low)],
-        "sides": [((rows, split), low), ((rows, cols - split), low)],
+        "sides": [((rows, width), low) for width in widths],
         "send": [((rows, cols), low)],
         "own": [((rows, cols), full)],
     }[form]
@@ -546,11 +552,11 @@
             if came:
                 came[-1] = after(came[-1], *others)
 
-    def add(self, rows, place, form):
+    def add(self, rows, place, form, even=False):
         keep, start = self.keep
         keep_place = (place * rows - start) // rows
         out = fold(
-            keep, keep_place, self.both, self.left, self.right, self.split, rows, place, form
+            keep, keep_place, self.both, self.left, self.right, self.split, rows, place, form, even
         )
         return lax.optimization_barrier(out)
 
@@ -679,7 +685,7 @@
     two.keep = piece(2, half_rows, 0, *out)
     one.keep = piece(1, rows, 0, two.keep[0])
     two.hold(two.keep[0], one.keep[0])
-    out = two.add(rows, 1, "sides")
+    out = two.add(rows, 1, "sides", even=True)
     two.cross_second(out)
     three.hold(*out)
     line_rows //= 2

time: 138 us -> 136 us (0.986)
  local copies, waits for them, and re-layouts: 18.3 us -> 14.7 us
  Pallas kernels: 44.2 us -> 45.6 us
    unnamed x32 -> x28, local copies, waits for them, and re-layouts: 17.2 us -> 13.7 us
  transfers between devices with their start and end apart: 23 -> 23, of which waited for: 11 -> 12; matrix products, arithmetic and copies ran while one was open for 1% -> 1% of each run, Pallas kernels for 21% -> 22%
where the time goes in v9:
time: 136 us
  Pallas kernels  45.6 us (34%)
  waiting for transfers between devices  29.7 us (22%)
  starting transfers between devices  28.6 us (21%)
  local copies, waits for them, and re-layouts  14.7 us (11%)
  blocking collectives  14.2 us (10%)
  other arithmetic  1.74 us (1%)
    ppermute x21, waiting for transfers between devices, swap(): return lax.ppermute(x, axis, [(i, i ^ bit) for i in range(size)])  27.2 us
    ppermute x21, starting transfers between devices, swap(): return lax.ppermute(x, axis, [(i, i ^ bit) for i in range(size)])  21.1 us
    all_to_all x1, blocking collectives, per_device(): lax.all_to_all(wanted, AXES, split_axis=0, concat_axis=0, tiled=True)  14.2 us
    unnamed x28, local copies, waits for them, and re-layouts  13.7 us
    pallas_call x1, Pallas kernels, negatives(): pl.pallas_call(neg_kernel, grid=(bank.shape[0] // tile,), in_specs=[pl.Bl...  11 us
    pallas_call x1, Pallas kernels, key_hidden(): pl.pallas_call(lambda *refs: key_hidden_kernel(groups, *refs), grid=(hid...  10.3 us
    pallas_call x1, Pallas kernels, query_forward(): pl.pallas_call(lambda *refs: query_kernel(size, *refs), grid_spec=pltpu.P...  10.3 us
    pallas_call x2, Pallas kernels, send_half(): pl.pallas_call(lambda *refs: send_kernel(sizes, old_plain, at is not None...  6.14 us
  transfers between devices with their start and end apart: 23, of which 12 were waited for; matrix products, arithmetic and copies ran while one was open for 1% of the time, Pallas kernels for 22%

profile of v9, /device:TPU:0, one launch (start us, length us, event | category | flops | bytes accessed | tf_op | source)
XLA Modules:
  0.0 135.6 jit_solution(16549191333803916230)
XLA Ops:
  1.4 14.2 %all_to_all.22 = f32[32,1,128]{2,1,0:T(1,128)S(1)} all-to-all(f32[32,1,128]{2,1,0:T(1,128)S(1)} %bitcast.21), channel_id=1, replica_groups=mesh['dp'=8,'crop'=4] {'dp','crop'}, dimensions={0} | all-to-all | bytes 32768 | tf_op jit(solution)/shard_map/all_to_all | solution.py:601
  15.8 1.6 %copy-done.13 = bf16[512,2048]{1,0:T(8,128)(2,1)S(1)} copy-done((bf16[512,2048]{1,0:T(8,128)(2,1)S(1)}, bf16[512,2048]{1,0:T(8,128)(2,1)}, u32[]{:S(2)}) %copy-start.13) | copy-done | bytes 2097176
  17.4 10.3 %key_hidden.1 = (f32[512,2048]{1,0:T(8,128)}, f32[32,1,4096]{2,1,0:T(1,128)}) custom-call(s32[512,1]{1,0:T(8,128)S(1)} %broadcast_in_dim_reshape.8.refs_0_, bf16[512,2048]{1,0:T(8,128)(2,1)S(1)} %copy-done.13, bf16[2048,2048]{1,0:T(8,128)(2,1)} %refs_2_.3), custom_call_target="tpu_custom_call" | custom-call | flops 5368709120 | bytes 8388608 | tf_op jit(solution)/shard_map/key_hidden/pallas_call | solution.py:141
  27.7 2.6 %all-to-all-start.1 = ((f32[32,1,4096]{2,1,0:T(1,128)}), f32[32,1,4096]{2,1,0:T(1,128)S(1)}, u32[]{:S(2)}, u32[]{:S(2)}) async-start(f32[32,1,4096]{2,1,0:T(1,128)} %get-tuple-element.63), calls=%async_computation.1 | async-start | bytes 1048576 | tf_op jit(solution)/shard_map/all_to_all | solution.py:606
  30.6 10.3 %query_forward.1 = (bf16[512,2048]{1,0:T(8,128)(2,1)S(1)}, f32[1,2048]{1,0:T(1,128)S(1)}, f32[512,128]{1,0:T(8,128)S(1)}, bf16[512,128]{1,0:T(8,128)(2,1)S(1)}, ...) custom-call(s32[3,16]{1,0:T(4,128)S(1)} %add_add_fusion.refs_0_, ...), custom_call_target="tpu_custom_call" | custom-call | flops 4563402752 | bytes 8388608 | tf_op jit(solution)/shard_map/query_forward/pallas_call | solution.py:239
  41.0 1.3 copy-done
  42.3 1.4 %copy-done.2 = bf16[2,16,64,512]{3,2,1,0:T(8,128)(2,1)} copy-done((bf16[2,16,64,512]{3,2,1,0:T(8,128)(2,1)}, bf16[2,16,64,512]{3,2,1,0:T(8,128)(2,1)S(1)}, u32[]{:S(2)}) %copy-start.2) | copy-done | bytes 2097176
  43.7 1.4 %copy-done.4 = bf16[2,16,64,512]{3,2,1,0:T(8,128)(2,1)} copy-done((bf16[2,16,64,512]{3,2,1,0:T(8,128)(2,1)}, bf16[2,16,64,512]{3,2,1,0:T(8,128)(2,1)S(1)}, u32[]{:S(2)}) %copy-start.4) | copy-done | bytes 2097176
  45.0 0.9 all-to-all-done.1.refs_0_
  46.2 0.8 copy-done.8
  47.0 5.0 %all-to-all-start.2 = ((f32[32,1,4096]{2,1,0:T(1,128)}), f32[32,1,4096]{2,1,0:T(1,128)S(1)}, u32[]{:S(2)}, u32[]{:S(2)}) async-start(f32[32,1,4096]{2,1,0:T(1,128)} %copy-done.8), calls=%async_computation.2 | async-start | bytes 1048576 | tf_op jit(solution)/shard_map/all_to_all | solution.py:626
  51.9 2.2 %copy-done.12 = bf16[16384,128]{1,0:T(8,128)(2,1)S(1)} copy-done((bf16[16384,128]{1,0:T(8,128)(2,1)S(1)}, bf16[16384,128]{1,0:T(8,128)(2,1)}, u32[]{:S(2)}) %copy-start.12) | copy-done | bytes 4194328
  54.1 11.0 %negatives.1.refs_5_ = f32[512,256]{1,0:T(8,128)S(1)} custom-call(bf16[512,128]{1,0:T(8,128)(2,1)S(1)} %get-tuple-element.70.q_ref, bf16[16384,128]{1,0:T(8,128)(2,1)S(1)} %copy-done.12), custom_call_target="tpu_custom_call" | custom-call | flops 4294967296 | bytes 4194304 | tf_op jit(solution)/shard_map/negatives/pallas_call | solution.py:42
  65.1 0.8 copy-done.10
  65.9 1.6 %all-to-all-done.2.refs_2_ = f32[32,1,4096]{2,1,0:T(1,128)S(1)} async-done(((f32[32,1,4096]{2,1,0:T(1,128)}), f32[32,1,4096]{2,1,0:T(1,128)S(1)}, u32[]{:S(2)}, u32[]{:S(2)}) %all-to-all-start.2) | async-done | bytes 524320 | tf_op jit(solution)/shard_map/all_to_all | solution.py:626
  67.5 2.2 %copy-done.7 = f32[512,2048]{1,0:T(8,128)S(1)} copy-done((f32[512,2048]{1,0:T(8,128)S(1)}, f32[512,2048]{1,0:T(8,128)}, u32[]{:S(2)}) %copy-start.7) | copy-done | bytes 4194328
  69.7 1.0 copy-done.9
  70.7 1.0 copy-done.11
  71.7 2.8 %embed.1.refs_0_.z = bf16[512,128]{1,0:T(8,128)(2,1)S(1)} custom-call(s32[1,512]{1,0:T(1,128)S(1)} %broadcast_in_dim_reshape.7.refs_0_, f32[512,2048]{1,0:T(8,128)S(1)} %copy-done.7, f32[32,1,4096]{2,1,0:T(1,128)S(1)} %all-to-all-done.2.refs_2_, bf16[2048,128]{1,0:T(8,128)(2,1)S(1)} %copy-done.9, f32[512,128]{1,0:T(8,128)S(1)} %get-tuple-element.72.refs_4_, ...), custom_call_target="tpu_custom_call" | custom-call | flops 268435456 | bytes 4194304 | tf_op jit(solution)/shard_map/embed/pallas_call | solution.py:325
  74.6 2.2 %send_half.2 = (bf16[512,896]{1,0:T(8,128)(2,1)S(1)}, bf16[1024,896]{1,0:T(8,128)(2,1)S(1)}) custom-call(bf16[512,128]{1,0:T(8,128)(2,1)S(1)} %embed.1.refs_0_.z, bf16[2048,512]{1,0:T(8,128)(2,1)S(1)} %bitcast.8, bf16[2048,128]{1,0:T(8,128)(2,1)S(1)} %copy-done.6, bf16[512,2048]{1,0:T(8,128)(2,1)S(1)} %copy-done.1, ...), custom_call_target="tpu_custom_call" | custom-call | flops 939524096 | bytes 4194304 | tf_op jit(solution)/shard_map/send_half/pallas_call | solution.py:437
  76.9 4.0 %send_half.3 = (f32[512,896]{1,0:T(8,128)S(1)}, bf16[512,896]{1,0:T(8,128)(2,1)S(1)}, bf16[1024,896]{1,0:T(8,128)(2,1)S(1)}, bf16[512,256]{1,0:T(8,128)(2,1)S(1)}, bf16[1024,384]{1,0:T(8,128)(2,1)S(1)}) custom-call(bf16[512,128]{1,0:T(8,128)(2,1)S(1)} %embed.1.refs_0_.z, bf16[2048,512]{1,0:T(8,128)(2,1)S(1)} %bitcast.18, bf16[2048,512]{1,0:T(8,128)(2,1)S(1)} %bitcast.9, ...), custom_call_target="tpu_custom_call" | custom-call | flops 1207959552 | bytes 4194304 | tf_op jit(solution)/shard_map/send_half/pallas_call | solution.py:437
  81.6 1.3 collective-permute-start.4
  82.9 1.2 collective-permute-start.5
  84.1 0.7 keep_half.6.refs_0_
  86.0 1.3 collective-permute-start.3
  88.0 1.2 collective-permute-start.7
  90.2 4.7 %collective-permute-done.5.refs_3_.refs_4_ = bf16[512,384]{1,0:T(8,128)(2,1)S(1)} collective-permute-done((bf16[512,384]{1,0:T(8,128)(2,1)S(1)}, bf16[512,384]{1,0:T(8,128)(2,1)S(1)}, u32[]{:S(2)}, u32[]{:S(2)}) %collective-permute-start.5) | collective-permute-done | bytes 393248 | tf_op jit(solution)/shard_map/ppermute | solution.py:484
  94.9 1.5 %collective-permute-done.4.refs_2_ = bf16[512,512]{1,0:T(8,128)(2,1)S(1)} collective-permute-done((bf16[512,512]{1,0:T(8,128)(2,1)S(1)}, bf16[512,512]{1,0:T(8,128)(2,1)S(1)}, u32[]{:S(2)}, u32[]{:S(2)}) %collective-permute-start.4) | collective-permute-done | bytes 524320 | tf_op jit(solution)/shard_map/ppermute | solution.py:484
  96.5 1.3 collective-permute-start.9
  97.9 1.5 %collective-permute-start.6 = (bf16[256,384]{1,0:T(8,128)(2,1)S(1)}, bf16[256,384]{1,0:T(8,128)(2,1)S(1)}, u32[]{:S(2)}, u32[]{:S(2)}) collective-permute-start(bf16[256,384]{1,0:T(8,128)(2,1)S(1)} %fold.15), channel_id=1, source_target_pairs={{0,16},{4,20},{8,24},{12,28},{16,0},{20,4},{24,8},{28,12},{1,17},{... | collective-permute-start | bytes 589832 | tf_op jit(solution)/shard_map/ppermute | solution.py:484
  99.4 1.5 %collective-permute-start.10 = (bf16[256,384]{1,0:T(8,128)(2,1)S(1)}, bf16[256,384]{1,0:T(8,128)(2,1)S(1)}, u32[]{:S(2)}, u32[]{:S(2)}) collective-permute-start(bf16[256,384]{1,0:T(8,128)(2,1)S(1)} %get-tuple-element.97), channel_id=1, source_target_pairs={{0,4},{4,0},{8,12},{12,8},{16,20},{20,16},{24,28},{28,24},{1,5},{5... | collective-permute-start | bytes 589832 | tf_op jit(solution)/shard_map/ppermute | solution.py:484
  100.9 0.7 keep_half.10.refs_0_
  102.1 4.1 %collective-permute-done.8.refs_3_.refs_4_ = bf16[512,512]{1,0:T(8,128)(2,1)S(1)} collective-permute-done((bf16[512,512]{1,0:T(8,128)(2,1)S(1)}, bf16[512,512]{1,0:T(8,128)(2,1)S(1)}, u32[]{:S(2)}, u32[]{:S(2)}) %collective-permute-start.8) | collective-permute-done | bytes 524320 | tf_op jit(solution)/shard_map/ppermute | solution.py:484
  106.3 1.2 collective-permute-start.13
  107.5 0.9 collective-permute-start.14
  109.1 2.6 %collective-permute-done.9.refs_3_ = bf16[256,512]{1,0:T(8,128)(2,1)S(1)} collective-permute-done((bf16[256,512]{1,0:T(8,128)(2,1)S(1)}, bf16[256,512]{1,0:T(8,128)(2,1)S(1)}, u32[]{:S(2)}, u32[]{:S(2)}) %collective-permute-start.9) | collective-permute-done | bytes 262176 | tf_op jit(solution)/shard_map/ppermute | solution.py:484
  111.9 0.9 collective-permute-start.11
  112.8 1.3 collective-permute-start.17
  114.0 0.8 collective-permute-start.18
  114.8 2.5 %collective-permute-done.13.refs_3_ = bf16[256,512]{1,0:T(8,128)(2,1)S(1)} collective-permute-done((bf16[256,512]{1,0:T(8,128)(2,1)S(1)}, bf16[256,512]{1,0:T(8,128)(2,1)S(1)}, u32[]{:S(2)}, u32[]{:S(2)}) %collective-permute-start.13) | collective-permute-done | bytes 262176 | tf_op jit(solution)/shard_map/ppermute | solution.py:484
  117.6 0.9 collective-permute-start.15
  118.5 2.1 %collective-permute-start.12 = (bf16[64,896]{1,0:T(8,128)(2,1)S(1)}, bf16[64,896]{1,0:T(8,128)(2,1)S(1)}, u32[]{:S(2)}, u32[]{:S(2)}) collective-permute-start(bf16[64,896]{1,0:T(8,128)(2,1)S(1)} %slice.43), channel_id=1, source_target_pairs={{0,16},{4,20},{8,24},{12,28},{16,0},{20,4},{24,8},{28,12},{1,17},{... | collective-permute-start | bytes 344072 | tf_op jit(solution)/shard_map/ppermute | solution.py:484
  120.6 5.6 %collective-permute-done.15 = bf16[128,896]{1,0:T(8,128)(2,1)S(1)} collective-permute-done((bf16[128,896]{1,0:T(8,128)(2,1)S(1)}, bf16[128,896]{1,0:T(8,128)(2,1)S(1)}, u32[]{:S(2)}, u32[]{:S(2)}) %collective-permute-start.15) | collective-permute-done | bytes 229408 | tf_op jit(solution)/shard_map/ppermute | solution.py:484
  126.4 0.9 collective-permute-start.20
  127.8 1.0 collective-permute-start.16
  128.8 2.1 %collective-permute-done.19.refs_5_ = bf16[64,128]{1,0:T(8,128)(2,1)S(1)} collective-permute-done((bf16[64,128]{1,0:T(8,128)(2,1)S(1)}, bf16[64,128]{1,0:T(8,128)(2,1)S(1)}, u32[]{:S(2)}, u32[]{:S(2)}) %collective-permute-start.19) | collective-permute-done | bytes 16416 | tf_op jit(solution)/shard_map/ppermute | solution.py:484
  131.7 3.1 %collective-permute-done.16 = bf16[64,896]{1,0:T(8,128)(2,1)S(1)} collective-permute-done((bf16[64,896]{1,0:T(8,128)(2,1)S(1)}, bf16[64,896]{1,0:T(8,128)(2,1)S(1)}, u32[]{:S(2)}, u32[]{:S(2)}) %collective-permute-start.16) | collective-permute-done | bytes 114720 | tf_op jit(solution)/shard_map/ppermute | solution.py:484
  134.7 0.8 pad_maximum_fusion
  (69 shorter events, 8.5 us)
Async XLA Ops:
  15.8 1.6 %copy-start.13 = (bf16[512,2048]{1,0:T(8,128)(2,1)S(1)}, bf16[512,2048]{1,0:T(8,128)(2,1)}, u32[]{:S(2)}) copy-start(bf16[512,2048]{1,0:T(8,128)(2,1)} %refs_1_.1) | copy-start | bytes 6291460
  17.4 13.2 %copy-start.6 = (bf16[2048,128]{1,0:T(8,128)(2,1)S(1)}, bf16[2048,128]{1,0:T(8,128)(2,1)}, u32[]{:S(2)}) copy-start(bf16[2048,128]{1,0:T(8,128)(2,1)} %refs_9_.1) | copy-start | bytes 1572868
  27.7 18.2 %all-to-all-start.1 = ((f32[32,1,4096]{2,1,0:T(1,128)}), f32[32,1,4096]{2,1,0:T(1,128)S(1)}, u32[]{:S(2)}, u32[]{:S(2)}) async-start(f32[32,1,4096]{2,1,0:T(1,128)} %get-tuple-element.63), calls=%async_computation.1 | async-start | bytes 1048576 | tf_op jit(solution)/shard_map/all_to_all | solution.py:606
  41.0 1.3 copy-start
  42.3 1.4 %copy-start.2 = (bf16[2,16,64,512]{3,2,1,0:T(8,128)(2,1)}, bf16[2,16,64,512]{3,2,1,0:T(8,128)(2,1)S(1)}, u32[]{:S(2)}) copy-start(bf16[2,16,64,512]{3,2,1,0:T(8,128)(2,1)S(1)} %get-tuple-element.78) | copy-start | bytes 6291460
  43.7 1.4 %copy-start.4 = (bf16[2,16,64,512]{3,2,1,0:T(8,128)(2,1)}, bf16[2,16,64,512]{3,2,1,0:T(8,128)(2,1)S(1)}, u32[]{:S(2)}) copy-start(bf16[2,16,64,512]{3,2,1,0:T(8,128)(2,1)S(1)} %get-tuple-element.77) | copy-start | bytes 6291460
  46.2 0.8 copy-start.8
  47.0 20.5 %all-to-all-start.2 = ((f32[32,1,4096]{2,1,0:T(1,128)}), f32[32,1,4096]{2,1,0:T(1,128)S(1)}, u32[]{:S(2)}, u32[]{:S(2)}) async-start(f32[32,1,4096]{2,1,0:T(1,128)} %copy-done.8), calls=%async_computation.2 | async-start | bytes 1048576 | tf_op jit(solution)/shard_map/all_to_all | solution.py:626
  51.9 2.2 %copy-start.12 = (bf16[16384,128]{1,0:T(8,128)(2,1)S(1)}, bf16[16384,128]{1,0:T(8,128)(2,1)}, u32[]{:S(2)}) copy-start(bf16[16384,128]{1,0:T(8,128)(2,1)} %bank_ref.1) | copy-start | bytes 12582916
  65.1 0.8 copy-start.10
  67.5 2.2 %copy-start.7 = (f32[512,2048]{1,0:T(8,128)S(1)}, f32[512,2048]{1,0:T(8,128)}, u32[]{:S(2)}) copy-start(f32[512,2048]{1,0:T(8,128)} %get-tuple-element.68.refs_1_) | copy-start | bytes 12582916
  69.7 1.0 copy-start.9
  70.7 1.0 copy-start.11
  71.7 2.8 %copy-start.1 = (bf16[512,2048]{1,0:T(8,128)(2,1)S(1)}, bf16[512,2048]{1,0:T(8,128)(2,1)}, u32[]{:S(2)}) copy-start(bf16[512,2048]{1,0:T(8,128)(2,1)} %copy-done) | copy-start | bytes 6291460
  74.6 2.3 %copy-start.3 = (bf16[2,16,64,512]{3,2,1,0:T(8,128)(2,1)S(1)}, bf16[2,16,64,512]{3,2,1,0:T(8,128)(2,1)}, u32[]{:S(2)}) copy-start(bf16[2,16,64,512]{3,2,1,0:T(8,128)(2,1)} %copy-done.2) | copy-start | bytes 6291460
  74.6 2.3 %copy-start.5 = (bf16[2,16,64,512]{3,2,1,0:T(8,128)(2,1)S(1)}, bf16[2,16,64,512]{3,2,1,0:T(8,128)(2,1)}, u32[]{:S(2)}) copy-start(bf16[2,16,64,512]{3,2,1,0:T(8,128)(2,1)} %copy-done.4) | copy-start | bytes 6291460
  76.8 4.7 %collective-permute-start = (bf16[1024,896]{1,0:T(8,128)(2,1)S(1)}, bf16[1024,896]{1,0:T(8,128)(2,1)S(1)}, u32[]{:S(2)}, u32[]{:S(2)}) collective-permute-start(bf16[1024,896]{1,0:T(8,128)(2,1)S(1)} %get-tuple-element.82), channel_id=1, source_target_pairs={{0,1},{1,0},{2,3},{3,2},{4,5},{5,4},{6,7},{7,6},{8,9},{9,8},{10,11... | collective-permute-start | bytes 5505032 | tf_op jit(solution)/shard_map/ppermute | solution.py:484
  80.8 4.0 %collective-permute-start.1 = (bf16[1024,896]{1,0:T(8,128)(2,1)S(1)}, bf16[1024,896]{1,0:T(8,128)(2,1)S(1)}, u32[]{:S(2)}, u32[]{:S(2)}) collective-permute-start(bf16[1024,896]{1,0:T(8,128)(2,1)S(1)} %get-tuple-element.86), channel_id=1, source_target_pairs={{0,1},{1,0},{2,3},{3,2},{4,5},{5,4},{6,7},{7,6},{8,9},{9,8},{10,11... | collective-permute-start | bytes 5505032 | tf_op jit(solution)/shard_map/ppermute | solution.py:484
  81.4 4.5 %collective-permute-start.2 = (bf16[1024,384]{1,0:T(8,128)(2,1)S(1)}, bf16[1024,384]{1,0:T(8,128)(2,1)S(1)}, u32[]{:S(2)}, u32[]{:S(2)}) collective-permute-start(bf16[1024,384]{1,0:T(8,128)(2,1)S(1)} %get-tuple-element.90), channel_id=1, source_target_pairs={{0,1},{1,0},{2,3},{3,2},{4,5},{5,4},{6,7},{7,6},{8,9},{9,8},{10,11... | collective-permute-start | bytes 2359304 | tf_op jit(solution)/shard_map/ppermute | solution.py:484
  81.6 14.8 %collective-permute-start.4 = (bf16[512,512]{1,0:T(8,128)(2,1)S(1)}, bf16[512,512]{1,0:T(8,128)(2,1)S(1)}, u32[]{:S(2)}, u32[]{:S(2)}) collective-permute-start(bf16[512,512]{1,0:T(8,128)(2,1)S(1)} %get-tuple-element.83), channel_id=1, source_target_pairs={{0,4},{4,0},{8,12},{12,8},{16,20},{20,16},{24,28},{28,24},{1,5},{5... | collective-permute-start | bytes 1572872 | tf_op jit(solution)/shard_map/ppermute | solution.py:484
  82.9 12.0 %collective-permute-start.5 = (bf16[512,384]{1,0:T(8,128)(2,1)S(1)}, bf16[512,384]{1,0:T(8,128)(2,1)S(1)}, u32[]{:S(2)}, u32[]{:S(2)}) collective-permute-start(bf16[512,384]{1,0:T(8,128)(2,1)S(1)} %get-tuple-element.84), channel_id=1, source_target_pairs={{0,2},{1,3},{2,0},{3,1},{4,6},{5,7},{6,4},{7,5},{8,10},{9,11},{10,... | collective-permute-start | bytes 1179656 | tf_op jit(solution)/shard_map/ppermute | solution.py:484
  86.0 11.9 %collective-permute-start.3 = (bf16[512,384]{1,0:T(8,128)(2,1)S(1)}, bf16[512,384]{1,0:T(8,128)(2,1)S(1)}, u32[]{:S(2)}, u32[]{:S(2)}) collective-permute-start(bf16[512,384]{1,0:T(8,128)(2,1)S(1)} %fold.13), channel_id=1, source_target_pairs={{0,8},{4,12},{8,0},{12,4},{16,24},{20,28},{24,16},{28,20},{1,9},{5... | collective-permute-start | bytes 1179656 | tf_op jit(solution)/shard_map/ppermute | solution.py:484
  87.3 18.8 %collective-permute-start.8 = (bf16[512,512]{1,0:T(8,128)(2,1)S(1)}, bf16[512,512]{1,0:T(8,128)(2,1)S(1)}, u32[]{:S(2)}, u32[]{:S(2)}) collective-permute-start(bf16[512,512]{1,0:T(8,128)(2,1)S(1)} %get-tuple-element.88), channel_id=1, source_target_pairs={{0,2},{1,3},{2,0},{3,1},{4,6},{5,7},{6,4},{7,5},{8,10},{9,11},{10,... | collective-permute-start | bytes 1572872 | tf_op jit(solution)/shard_map/ppermute | solution.py:484
  88.0 18.1 %collective-permute-start.7 = (bf16[512,384]{1,0:T(8,128)(2,1)S(1)}, bf16[512,384]{1,0:T(8,128)(2,1)S(1)}, u32[]{:S(2)}, u32[]{:S(2)}) collective-permute-start(bf16[512,384]{1,0:T(8,128)(2,1)S(1)} %get-tuple-element.87), channel_id=1, source_target_pairs={{0,4},{4,0},{8,12},{12,8},{16,20},{20,16},{24,28},{28,24},{1,5},{5... | collective-permute-start | bytes 1179656 | tf_op jit(solution)/shard_map/ppermute | solution.py:484
  96.5 15.2 %collective-permute-start.9 = (bf16[256,512]{1,0:T(8,128)(2,1)S(1)}, bf16[256,512]{1,0:T(8,128)(2,1)S(1)}, u32[]{:S(2)}, u32[]{:S(2)}) collective-permute-start(bf16[256,512]{1,0:T(8,128)(2,1)S(1)} %get-tuple-element.96), channel_id=1, source_target_pairs={{0,2},{1,3},{2,0},{3,1},{4,6},{5,7},{6,4},{7,5},{8,10},{9,11},{10,... | collective-permute-start | bytes 786440 | tf_op jit(solution)/shard_map/ppermute | solution.py:484
  97.9 11.1 %collective-permute-start.6 = (bf16[256,384]{1,0:T(8,128)(2,1)S(1)}, bf16[256,384]{1,0:T(8,128)(2,1)S(1)}, u32[]{:S(2)}, u32[]{:S(2)}) collective-permute-start(bf16[256,384]{1,0:T(8,128)(2,1)S(1)} %fold.15), channel_id=1, source_target_pairs={{0,16},{4,20},{8,24},{12,28},{16,0},{20,4},{24,8},{28,12},{1,17},{... | collective-permute-start | bytes 589832 | tf_op jit(solution)/shard_map/ppermute | solution.py:484
  99.4 9.7 %collective-permute-start.10 = (bf16[256,384]{1,0:T(8,128)(2,1)S(1)}, bf16[256,384]{1,0:T(8,128)(2,1)S(1)}, u32[]{:S(2)}, u32[]{:S(2)}) collective-permute-start(bf16[256,384]{1,0:T(8,128)(2,1)S(1)} %get-tuple-element.97), channel_id=1, source_target_pairs={{0,4},{4,0},{8,12},{12,8},{16,20},{20,16},{24,28},{28,24},{1,5},{5... | collective-permute-start | bytes 589832 | tf_op jit(solution)/shard_map/ppermute | solution.py:484
  106.3 11.0 %collective-permute-start.13 = (bf16[256,512]{1,0:T(8,128)(2,1)S(1)}, bf16[256,512]{1,0:T(8,128)(2,1)S(1)}, u32[]{:S(2)}, u32[]{:S(2)}) collective-permute-start(bf16[256,512]{1,0:T(8,128)(2,1)S(1)} %get-tuple-element.104), channel_id=1, source_target_pairs={{0,2},{1,3},{2,0},{3,1},{4,6},{5,7},{6,4},{7,5},{8,10},{9,11},{10,... | collective-permute-start | bytes 786440 | tf_op jit(solution)/shard_map/ppermute | solution.py:484
  107.5 9.8 %collective-permute-start.14 = (bf16[256,512]{1,0:T(8,128)(2,1)S(1)}, bf16[256,512]{1,0:T(8,128)(2,1)S(1)}, u32[]{:S(2)}, u32[]{:S(2)}) collective-permute-start(bf16[256,512]{1,0:T(8,128)(2,1)S(1)} %get-tuple-element.105), channel_id=1, source_target_pairs={{0,4},{4,0},{8,12},{12,8},{16,20},{20,16},{24,28},{28,24},{1,5},{5... | collective-permute-start | bytes 786440 | tf_op jit(solution)/shard_map/ppermute | solution.py:484
  111.9 6.5 %collective-permute-start.11 = (bf16[128,896]{1,0:T(8,128)(2,1)S(1)}, bf16[128,896]{1,0:T(8,128)(2,1)S(1)}, u32[]{:S(2)}, u32[]{:S(2)}) collective-permute-start(bf16[128,896]{1,0:T(8,128)(2,1)S(1)} %get-tuple-element.113), channel_id=1, source_target_pairs={{0,8},{4,12},{8,0},{12,4},{16,24},{20,28},{24,16},{28,20},{1,9},{5... | collective-permute-start | bytes 688136 | tf_op jit(solution)/shard_map/ppermute | solution.py:484
  112.8 13.5 %collective-permute-start.17 = (bf16[128,128]{1,0:T(8,128)(2,1)S(1)}, bf16[128,128]{1,0:T(8,128)(2,1)S(1)}, u32[]{:S(2)}, u32[]{:S(2)}) collective-permute-start(bf16[128,128]{1,0:T(8,128)(2,1)S(1)} %get-tuple-element.107), channel_id=1, source_target_pairs={{0,4},{4,0},{8,12},{12,8},{16,20},{20,16},{24,28},{28,24},{1,5},{5... | collective-permute-start | bytes 98312 | tf_op jit(solution)/shard_map/ppermute | solution.py:484
  114.0 12.3 %collective-permute-start.18 = (bf16[128,256]{1,0:T(8,128)(2,1)S(1)}, bf16[128,256]{1,0:T(8,128)(2,1)S(1)}, u32[]{:S(2)}, u32[]{:S(2)}) collective-permute-start(bf16[128,256]{1,0:T(8,128)(2,1)S(1)} %get-tuple-element.108), channel_id=1, source_target_pairs={{0,2},{1,3},{2,0},{3,1},{4,6},{5,7},{6,4},{7,5},{8,10},{9,11},{10,... | collective-permute-start | bytes 196616 | tf_op jit(solution)/shard_map/ppermute | solution.py:484
  117.6 8.7 %collective-permute-start.15 = (bf16[128,896]{1,0:T(8,128)(2,1)S(1)}, bf16[128,896]{1,0:T(8,128)(2,1)S(1)}, u32[]{:S(2)}, u32[]{:S(2)}) collective-permute-start(bf16[128,896]{1,0:T(8,128)(2,1)S(1)} %get-tuple-element.118), channel_id=1, source_target_pairs={{0,8},{4,12},{8,0},{12,4},{16,24},{20,28},{24,16},{28,20},{1,9},{5... | collective-permute-start | bytes 688136 | tf_op jit(solution)/shard_map/ppermute | solution.py:484
  118.5 13.1 %collective-permute-start.12 = (bf16[64,896]{1,0:T(8,128)(2,1)S(1)}, bf16[64,896]{1,0:T(8,128)(2,1)S(1)}, u32[]{:S(2)}, u32[]{:S(2)}) collective-permute-start(bf16[64,896]{1,0:T(8,128)(2,1)S(1)} %slice.43), channel_id=1, source_target_pairs={{0,16},{4,20},{8,24},{12,28},{16,0},{20,4},{24,8},{28,12},{1,17},{... | collective-permute-start | bytes 344072 | tf_op jit(solution)/shard_map/ppermute | solution.py:484
  126.4 4.6 %collective-permute-start.20 = (bf16[64,256]{1,0:T(8,128)(2,1)S(1)}, bf16[64,256]{1,0:T(8,128)(2,1)S(1)}, u32[]{:S(2)}, u32[]{:S(2)}) collective-permute-start(bf16[64,256]{1,0:T(8,128)(2,1)S(1)} %get-tuple-element.123), channel_id=1, source_target_pairs={{0,4},{4,0},{8,12},{12,8},{16,20},{20,16},{24,28},{28,24},{1,5},{5... | collective-permute-start | bytes 98312 | tf_op jit(solution)/shard_map/ppermute | solution.py:484
  127.2 3.7 %collective-permute-start.19 = (bf16[64,128]{1,0:T(8,128)(2,1)S(1)}, bf16[64,128]{1,0:T(8,128)(2,1)S(1)}, u32[]{:S(2)}, u32[]{:S(2)}) collective-permute-start(bf16[64,128]{1,0:T(8,128)(2,1)S(1)} %get-tuple-element.122), channel_id=1, source_target_pairs={{0,2},{1,3},{2,0},{3,1},{4,6},{5,7},{6,4},{7,5},{8,10},{9,11},{10,... | collective-permute-start | bytes 49160 | tf_op jit(solution)/shard_map/ppermute | solution.py:484
  127.8 6.9 %collective-permute-start.16 = (bf16[64,896]{1,0:T(8,128)(2,1)S(1)}, bf16[64,896]{1,0:T(8,128)(2,1)S(1)}, u32[]{:S(2)}, u32[]{:S(2)}) collective-permute-start(bf16[64,896]{1,0:T(8,128)(2,1)S(1)} %slice.42), channel_id=1, source_target_pairs={{0,16},{4,20},{8,24},{12,28},{16,0},{20,4},{24,8},{28,12},{1,17},{... | collective-permute-start | bytes 344072 | tf_op jit(solution)/shard_map/ppermute | solution.py:484

commit v10 on v9

--- a/solution.py
+++ b/solution.py
@@ -158,7 +158,7 @@
         cost_estimate=pl.CostEstimate(
             flops=2 * rows * d * (hid + rows), bytes_accessed=2 * d * hid, transcendentals=0
         ),
-        compiler_params=params(50),
+        compiler_params=params(54),
         name="key_hidden",
     )(flat_col, k, w)
 
@@ -697,7 +697,7 @@
     c_2 = two.add(rows, 0, "halves")
     own_1 = lax.optimization_barrier(one.cross_third(c_1))
     own_2 = lax.optimization_barrier(two.cross_third(c_2))
-    three.hold(own_1, own_2)
+    three.hold(own_1)
     line_rows //= 2
     out = three.add(line_rows, 1, "sides")
     three.cross_second(out)

time: 136 us -> 133 us (0.978)
  waiting for transfers between devices: 29.7 us -> 25.6 us
  starting transfers between devices: 28.6 us -> 30.2 us
    ppermute x21, waiting for transfers between devices: 27.2 us -> 23.2 us  [swap(): return lax.ppermute(x, axis, [(i, i ^ bit) for i in range(size)])]
    ppermute x21, starting transfers between devices: 21.1 us -> 22.7 us  [swap(): return lax.ppermute(x, axis, [(i, i ^ bit) for i in range(size)])]
    unnamed x28 -> x26, local copies, waits for them, and re-layouts: 13.7 us -> 12.1 us
  transfers between devices with their start and end apart: 23 -> 23, of which waited for: 12 -> 12; matrix products, arithmetic and copies ran while one was open for 1% -> 1% of each run, Pallas kernels for 22% -> 23%
where the time goes in v10:
time: 133 us
  Pallas kernels  46.2 us (35%)
  starting transfers between devices  30.2 us (23%)
  waiting for transfers between devices  25.6 us (19%)
  blocking collectives  14.2 us (11%)
  local copies, waits for them, and re-layouts  13.9 us (10%)
  other arithmetic  1.74 us (1%)
    ppermute x21, waiting for transfers between devices, swap(): return lax.ppermute(x, axis, [(i, i ^ bit) for i in range(size)])  23.2 us
    ppermute x21, starting transfers between devices, swap(): return lax.ppermute(x, axis, [(i, i ^ bit) for i in range(size)])  22.7 us
    all_to_all x1, blocking collectives, per_device(): lax.all_to_all(wanted, AXES, split_axis=0, concat_axis=0, tiled=True)  14.2 us
    unnamed x26, local copies, waits for them, and re-layouts  12.1 us
    pallas_call x1, Pallas kernels, negatives(): pl.pallas_call(neg_kernel, grid=(bank.shape[0] // tile,), in_specs=[pl.Bl...  11 us
    pallas_call x1, Pallas kernels, key_hidden(): pl.pallas_call(lambda *refs: key_hidden_kernel(groups, *refs), grid=(hid...  11 us
    pallas_call x1, Pallas kernels, query_forward(): pl.pallas_call(lambda *refs: query_kernel(size, *refs), grid_spec=pltpu.P...  10.3 us
    pallas_call x2, Pallas kernels, send_half(): pl.pallas_call(lambda *refs: send_kernel(sizes, old_plain, at is not None...  6.14 us
  transfers between devices with their start and end apart: 23, of which 12 were waited for; matrix products, arithmetic and copies ran while one was open for 1% of the time, Pallas kernels for 23%

profile of v10, /device:TPU:0, one launch (start us, length us, event | category | flops | bytes accessed | tf_op | source)
XLA Modules:
  0.0 132.9 jit_solution(1569876306845894243)
XLA Ops:
  1.4 14.2 %all_to_all.22 = f32[32,1,128]{2,1,0:T(1,128)S(1)} all-to-all(f32[32,1,128]{2,1,0:T(1,128)S(1)} %bitcast.21), channel_id=1, replica_groups=mesh['dp'=8,'crop'=4] {'dp','crop'}, dimensions={0} | all-to-all | bytes 32768 | tf_op jit(solution)/shard_map/all_to_all | solution.py:601
  15.7 0.9 broadcast_in_dim_reshape.8.refs_0_
  16.5 11.0 %key_hidden.1 = (f32[512,2048]{1,0:T(8,128)}, f32[32,1,4096]{2,1,0:T(1,128)}) custom-call(s32[512,1]{1,0:T(8,128)} %broadcast_in_dim_reshape.8.refs_0_, bf16[512,2048]{1,0:T(8,128)(2,1)} %refs_1_.1, bf16[2048,2048]{1,0:T(8,128)(2,1)} %refs_2_.3), custom_call_target="tpu_custom_call" | custom-call | flops 5368709120 | bytes 8388608 | tf_op jit(solution)/shard_map/key_hidden/pallas_call | solution.py:141
  27.5 2.6 %all-to-all-start.1 = ((f32[32,1,4096]{2,1,0:T(1,128)}), f32[32,1,4096]{2,1,0:T(1,128)S(1)}, u32[]{:S(2)}, u32[]{:S(2)}) async-start(f32[32,1,4096]{2,1,0:T(1,128)} %get-tuple-element.63), calls=%async_computation.1 | async-start | bytes 1048576 | tf_op jit(solution)/shard_map/all_to_all | solution.py:606
  30.4 10.3 %query_forward.1 = (bf16[512,2048]{1,0:T(8,128)(2,1)S(1)}, f32[1,2048]{1,0:T(1,128)S(1)}, f32[512,128]{1,0:T(8,128)S(1)}, bf16[512,128]{1,0:T(8,128)(2,1)S(1)}, ...) custom-call(s32[3,16]{1,0:T(4,128)S(1)} %add_add_fusion.refs_0_, ...), custom_call_target="tpu_custom_call" | custom-call | flops 4563402752 | bytes 8388608 | tf_op jit(solution)/shard_map/query_forward/pallas_call | solution.py:239
  40.7 1.3 copy-done
  42.0 1.4 %copy-done.2 = bf16[2,16,64,512]{3,2,1,0:T(8,128)(2,1)} copy-done((bf16[2,16,64,512]{3,2,1,0:T(8,128)(2,1)}, bf16[2,16,64,512]{3,2,1,0:T(8,128)(2,1)S(1)}, u32[]{:S(2)}) %copy-start.2) | copy-done | bytes 2097176
  43.4 1.4 %copy-done.4 = bf16[2,16,64,512]{3,2,1,0:T(8,128)(2,1)} copy-done((bf16[2,16,64,512]{3,2,1,0:T(8,128)(2,1)}, bf16[2,16,64,512]{3,2,1,0:T(8,128)(2,1)S(1)}, u32[]{:S(2)}) %copy-start.4) | copy-done | bytes 2097176
  44.8 0.9 all-to-all-done.1.refs_0_
  45.9 0.8 copy-done.8
  46.7 5.0 %all-to-all-start.2 = ((f32[32,1,4096]{2,1,0:T(1,128)}), f32[32,1,4096]{2,1,0:T(1,128)S(1)}, u32[]{:S(2)}, u32[]{:S(2)}) async-start(f32[32,1,4096]{2,1,0:T(1,128)} %copy-done.8), calls=%async_computation.2 | async-start | bytes 1048576 | tf_op jit(solution)/shard_map/all_to_all | solution.py:626
  51.7 2.2 %copy-done.12 = bf16[16384,128]{1,0:T(8,128)(2,1)S(1)} copy-done((bf16[16384,128]{1,0:T(8,128)(2,1)S(1)}, bf16[16384,128]{1,0:T(8,128)(2,1)}, u32[]{:S(2)}) %copy-start.12) | copy-done | bytes 4194328
  53.9 11.0 %negatives.1.refs_5_ = f32[512,256]{1,0:T(8,128)S(1)} custom-call(bf16[512,128]{1,0:T(8,128)(2,1)S(1)} %get-tuple-element.70.q_ref, bf16[16384,128]{1,0:T(8,128)(2,1)S(1)} %copy-done.12), custom_call_target="tpu_custom_call" | custom-call | flops 4294967296 | bytes 4194304 | tf_op jit(solution)/shard_map/negatives/pallas_call | solution.py:42
  64.9 0.8 copy-done.10
  65.7 1.5 %all-to-all-done.2.refs_2_ = f32[32,1,4096]{2,1,0:T(1,128)S(1)} async-done(((f32[32,1,4096]{2,1,0:T(1,128)}), f32[32,1,4096]{2,1,0:T(1,128)S(1)}, u32[]{:S(2)}, u32[]{:S(2)}) %all-to-all-start.2) | async-done | bytes 524320 | tf_op jit(solution)/shard_map/all_to_all | solution.py:626
  67.2 2.2 %copy-done.7 = f32[512,2048]{1,0:T(8,128)S(1)} copy-done((f32[512,2048]{1,0:T(8,128)S(1)}, f32[512,2048]{1,0:T(8,128)}, u32[]{:S(2)}) %copy-start.7) | copy-done | bytes 4194328
  69.4 1.0 copy-done.9
  70.4 1.0 copy-done.11
  71.5 2.8 %embed.1.refs_0_.z = bf16[512,128]{1,0:T(8,128)(2,1)S(1)} custom-call(s32[1,512]{1,0:T(1,128)S(1)} %broadcast_in_dim_reshape.7.refs_0_, f32[512,2048]{1,0:T(8,128)S(1)} %copy-done.7, f32[32,1,4096]{2,1,0:T(1,128)S(1)} %all-to-all-done.2.refs_2_, bf16[2048,128]{1,0:T(8,128)(2,1)S(1)} %copy-done.9, f32[512,128]{1,0:T(8,128)S(1)} %get-tuple-element.72.refs_4_, ...), custom_call_target="tpu_custom_call" | custom-call | flops 268435456 | bytes 4194304 | tf_op jit(solution)/shard_map/embed/pallas_call | solution.py:325
  74.3 2.2 %send_half.2 = (bf16[512,896]{1,0:T(8,128)(2,1)S(1)}, bf16[1024,896]{1,0:T(8,128)(2,1)S(1)}) custom-call(bf16[512,128]{1,0:T(8,128)(2,1)S(1)} %embed.1.refs_0_.z, bf16[2048,512]{1,0:T(8,128)(2,1)S(1)} %bitcast.8, bf16[2048,128]{1,0:T(8,128)(2,1)S(1)} %copy-done.6, bf16[512,2048]{1,0:T(8,128)(2,1)S(1)} %copy-done.1, ...), custom_call_target="tpu_custom_call" | custom-call | flops 939524096 | bytes 4194304 | tf_op jit(solution)/shard_map/send_half/pallas_call | solution.py:437
  76.6 4.0 %send_half.3 = (f32[512,896]{1,0:T(8,128)S(1)}, bf16[512,896]{1,0:T(8,128)(2,1)S(1)}, bf16[1024,896]{1,0:T(8,128)(2,1)S(1)}, bf16[512,256]{1,0:T(8,128)(2,1)S(1)}, bf16[1024,384]{1,0:T(8,128)(2,1)S(1)}) custom-call(bf16[512,128]{1,0:T(8,128)(2,1)S(1)} %embed.1.refs_0_.z, bf16[2048,512]{1,0:T(8,128)(2,1)S(1)} %bitcast.18, bf16[2048,512]{1,0:T(8,128)(2,1)S(1)} %bitcast.9, ...), custom_call_target="tpu_custom_call" | custom-call | flops 1207959552 | bytes 4194304 | tf_op jit(solution)/shard_map/send_half/pallas_call | solution.py:437
  81.3 1.3 collective-permute-start.4
  82.6 1.2 collective-permute-start.5
  83.8 0.7 keep_half.6.refs_0_
  85.7 1.3 %collective-permute-start.3 = (bf16[512,384]{1,0:T(8,128)(2,1)S(1)}, bf16[512,384]{1,0:T(8,128)(2,1)S(1)}, u32[]{:S(2)}, u32[]{:S(2)}) collective-permute-start(bf16[512,384]{1,0:T(8,128)(2,1)S(1)} %fold.13), channel_id=1, source_target_pairs={{0,8},{4,12},{8,0},{12,4},{16,24},{20,28},{24,16},{28,20},{1,9},{5... | collective-permute-start | bytes 1179656 | tf_op jit(solution)/shard_map/ppermute | solution.py:484
  87.7 1.3 collective-permute-start.7
  90.0 4.6 %collective-permute-done.5.refs_3_.refs_4_ = bf16[512,384]{1,0:T(8,128)(2,1)S(1)} collective-permute-done((bf16[512,384]{1,0:T(8,128)(2,1)S(1)}, bf16[512,384]{1,0:T(8,128)(2,1)S(1)}, u32[]{:S(2)}, u32[]{:S(2)}) %collective-permute-start.5) | collective-permute-done | bytes 393248 | tf_op jit(solution)/shard_map/ppermute | solution.py:484
  94.6 1.5 %collective-permute-done.4.refs_2_ = bf16[512,512]{1,0:T(8,128)(2,1)S(1)} collective-permute-done((bf16[512,512]{1,0:T(8,128)(2,1)S(1)}, bf16[512,512]{1,0:T(8,128)(2,1)S(1)}, u32[]{:S(2)}, u32[]{:S(2)}) %collective-permute-start.4) | collective-permute-done | bytes 524320 | tf_op jit(solution)/shard_map/ppermute | solution.py:484
  96.3 1.4 %collective-permute-start.9 = (bf16[256,512]{1,0:T(8,128)(2,1)S(1)}, bf16[256,512]{1,0:T(8,128)(2,1)S(1)}, u32[]{:S(2)}, u32[]{:S(2)}) collective-permute-start(bf16[256,512]{1,0:T(8,128)(2,1)S(1)} %get-tuple-element.96), channel_id=1, source_target_pairs={{0,2},{1,3},{2,0},{3,1},{4,6},{5,7},{6,4},{7,5},{8,10},{9,11},{10,... | collective-permute-start | bytes 786440 | tf_op jit(solution)/shard_map/ppermute | solution.py:484
  97.7 1.5 %collective-permute-start.6 = (bf16[256,384]{1,0:T(8,128)(2,1)S(1)}, bf16[256,384]{1,0:T(8,128)(2,1)S(1)}, u32[]{:S(2)}, u32[]{:S(2)}) collective-permute-start(bf16[256,384]{1,0:T(8,128)(2,1)S(1)} %fold.15), channel_id=1, source_target_pairs={{0,16},{4,20},{8,24},{12,28},{16,0},{20,4},{24,8},{28,12},{1,17},{... | collective-permute-start | bytes 589832 | tf_op jit(solution)/shard_map/ppermute | solution.py:484
  99.2 1.5 %collective-permute-start.10 = (bf16[256,384]{1,0:T(8,128)(2,1)S(1)}, bf16[256,384]{1,0:T(8,128)(2,1)S(1)}, u32[]{:S(2)}, u32[]{:S(2)}) collective-permute-start(bf16[256,384]{1,0:T(8,128)(2,1)S(1)} %get-tuple-element.97), channel_id=1, source_target_pairs={{0,4},{4,0},{8,12},{12,8},{16,20},{20,16},{24,28},{28,24},{1,5},{5... | collective-permute-start | bytes 589832 | tf_op jit(solution)/shard_map/ppermute | solution.py:484
  100.7 0.7 keep_half.10.refs_0_
  101.8 4.0 %collective-permute-done.8.refs_3_.refs_4_ = bf16[512,512]{1,0:T(8,128)(2,1)S(1)} collective-permute-done((bf16[512,512]{1,0:T(8,128)(2,1)S(1)}, bf16[512,512]{1,0:T(8,128)(2,1)S(1)}, u32[]{:S(2)}, u32[]{:S(2)}) %collective-permute-start.8) | collective-permute-done | bytes 524320 | tf_op jit(solution)/shard_map/ppermute | solution.py:484
  106.0 1.2 collective-permute-start.13
  107.2 0.9 collective-permute-start.14
  108.8 2.6 %collective-permute-done.9.refs_3_ = bf16[256,512]{1,0:T(8,128)(2,1)S(1)} collective-permute-done((bf16[256,512]{1,0:T(8,128)(2,1)S(1)}, bf16[256,512]{1,0:T(8,128)(2,1)S(1)}, u32[]{:S(2)}, u32[]{:S(2)}) %collective-permute-start.9) | collective-permute-done | bytes 262176 | tf_op jit(solution)/shard_map/ppermute | solution.py:484
  111.6 0.9 collective-permute-start.11
  112.5 1.2 collective-permute-start.17
  113.8 0.7 collective-permute-start.18
  114.5 2.5 %collective-permute-done.13.refs_3_ = bf16[256,512]{1,0:T(8,128)(2,1)S(1)} collective-permute-done((bf16[256,512]{1,0:T(8,128)(2,1)S(1)}, bf16[256,512]{1,0:T(8,128)(2,1)S(1)}, u32[]{:S(2)}, u32[]{:S(2)}) %collective-permute-start.13) | collective-permute-done | bytes 262176 | tf_op jit(solution)/shard_map/ppermute | solution.py:484
  117.3 0.9 collective-permute-start.15
  118.3 1.2 collective-permute-start.19
  120.2 2.4 %collective-permute-start.12 = (bf16[64,896]{1,0:T(8,128)(2,1)S(1)}, bf16[64,896]{1,0:T(8,128)(2,1)S(1)}, u32[]{:S(2)}, u32[]{:S(2)}) collective-permute-start(bf16[64,896]{1,0:T(8,128)(2,1)S(1)} %slice.43), channel_id=1, source_target_pairs={{0,16},{4,20},{8,24},{12,28},{16,0},{20,4},{24,8},{28,12},{1,17},{... | collective-permute-start | bytes 344072 | tf_op jit(solution)/shard_map/ppermute | solution.py:484
  122.6 2.1 %collective-permute-done.15 = bf16[128,896]{1,0:T(8,128)(2,1)S(1)} collective-permute-done((bf16[128,896]{1,0:T(8,128)(2,1)S(1)}, bf16[128,896]{1,0:T(8,128)(2,1)S(1)}, u32[]{:S(2)}, u32[]{:S(2)}) %collective-permute-start.15) | collective-permute-done | bytes 229408 | tf_op jit(solution)/shard_map/ppermute | solution.py:484
  124.8 1.6 %collective-permute-start.16 = (bf16[64,896]{1,0:T(8,128)(2,1)S(1)}, bf16[64,896]{1,0:T(8,128)(2,1)S(1)}, u32[]{:S(2)}, u32[]{:S(2)}) collective-permute-start(bf16[64,896]{1,0:T(8,128)(2,1)S(1)} %slice.42), channel_id=1, source_target_pairs={{0,16},{4,20},{8,24},{12,28},{16,0},{20,4},{24,8},{28,12},{1,17},{... | collective-permute-start | bytes 344072 | tf_op jit(solution)/shard_map/ppermute | solution.py:484
  127.1 2.2 %collective-permute-done.12 = bf16[64,896]{1,0:T(8,128)(2,1)S(1)} collective-permute-done((bf16[64,896]{1,0:T(8,128)(2,1)S(1)}, bf16[64,896]{1,0:T(8,128)(2,1)S(1)}, u32[]{:S(2)}, u32[]{:S(2)}) %collective-permute-start.12) | collective-permute-done | bytes 114720 | tf_op jit(solution)/shard_map/ppermute | solution.py:484
  129.4 2.6 %collective-permute-done.16 = bf16[64,896]{1,0:T(8,128)(2,1)S(1)} collective-permute-done((bf16[64,896]{1,0:T(8,128)(2,1)S(1)}, bf16[64,896]{1,0:T(8,128)(2,1)S(1)}, u32[]{:S(2)}, u32[]{:S(2)}) %collective-permute-start.16) | collective-permute-done | bytes 114720 | tf_op jit(solution)/shard_map/ppermute | solution.py:484
  132.1 0.8 pad_maximum_fusion
  (67 shorter events, 8.5 us)
Async XLA Ops:
  16.5 13.9 %copy-start.6 = (bf16[2048,128]{1,0:T(8,128)(2,1)S(1)}, bf16[2048,128]{1,0:T(8,128)(2,1)}, u32[]{:S(2)}) copy-start(bf16[2048,128]{1,0:T(8,128)(2,1)} %refs_9_.1) | copy-start | bytes 1572868
  27.5 18.2 %all-to-all-start.1 = ((f32[32,1,4096]{2,1,0:T(1,128)}), f32[32,1,4096]{2,1,0:T(1,128)S(1)}, u32[]{:S(2)}, u32[]{:S(2)}) async-start(f32[32,1,4096]{2,1,0:T(1,128)} %get-tuple-element.63), calls=%async_computation.1 | async-start | bytes 1048576 | tf_op jit(solution)/shard_map/all_to_all | solution.py:606
  40.7 1.3 copy-start
  42.0 1.4 %copy-start.2 = (bf16[2,16,64,512]{3,2,1,0:T(8,128)(2,1)}, bf16[2,16,64,512]{3,2,1,0:T(8,128)(2,1)S(1)}, u32[]{:S(2)}) copy-start(bf16[2,16,64,512]{3,2,1,0:T(8,128)(2,1)S(1)} %get-tuple-element.78) | copy-start | bytes 6291460
  43.4 1.4 %copy-start.4 = (bf16[2,16,64,512]{3,2,1,0:T(8,128)(2,1)}, bf16[2,16,64,512]{3,2,1,0:T(8,128)(2,1)S(1)}, u32[]{:S(2)}) copy-start(bf16[2,16,64,512]{3,2,1,0:T(8,128)(2,1)S(1)} %get-tuple-element.77) | copy-start | bytes 6291460
  45.9 0.8 copy-start.8
  46.7 20.5 %all-to-all-start.2 = ((f32[32,1,4096]{2,1,0:T(1,128)}), f32[32,1,4096]{2,1,0:T(1,128)S(1)}, u32[]{:S(2)}, u32[]{:S(2)}) async-start(f32[32,1,4096]{2,1,0:T(1,128)} %copy-done.8), calls=%async_computation.2 | async-start | bytes 1048576 | tf_op jit(solution)/shard_map/all_to_all | solution.py:626
  51.7 2.2 %copy-start.12 = (bf16[16384,128]{1,0:T(8,128)(2,1)S(1)}, bf16[16384,128]{1,0:T(8,128)(2,1)}, u32[]{:S(2)}) copy-start(bf16[16384,128]{1,0:T(8,128)(2,1)} %bank_ref.1) | copy-start | bytes 12582916
  64.9 0.8 copy-start.10
  67.2 2.2 %copy-start.7 = (f32[512,2048]{1,0:T(8,128)S(1)}, f32[512,2048]{1,0:T(8,128)}, u32[]{:S(2)}) copy-start(f32[512,2048]{1,0:T(8,128)} %get-tuple-element.68.refs_1_) | copy-start | bytes 12582916
  69.4 1.0 copy-start.9
  70.4 1.0 copy-start.11
  71.5 2.8 %copy-start.1 = (bf16[512,2048]{1,0:T(8,128)(2,1)S(1)}, bf16[512,2048]{1,0:T(8,128)(2,1)}, u32[]{:S(2)}) copy-start(bf16[512,2048]{1,0:T(8,128)(2,1)} %copy-done) | copy-start | bytes 6291460
  74.3 2.3 %copy-start.3 = (bf16[2,16,64,512]{3,2,1,0:T(8,128)(2,1)S(1)}, bf16[2,16,64,512]{3,2,1,0:T(8,128)(2,1)}, u32[]{:S(2)}) copy-start(bf16[2,16,64,512]{3,2,1,0:T(8,128)(2,1)} %copy-done.2) | copy-start | bytes 6291460
  74.3 2.3 %copy-start.5 = (bf16[2,16,64,512]{3,2,1,0:T(8,128)(2,1)S(1)}, bf16[2,16,64,512]{3,2,1,0:T(8,128)(2,1)}, u32[]{:S(2)}) copy-start(bf16[2,16,64,512]{3,2,1,0:T(8,128)(2,1)} %copy-done.4) | copy-start | bytes 6291460
  76.5 4.7 %collective-permute-start = (bf16[1024,896]{1,0:T(8,128)(2,1)S(1)}, bf16[1024,896]{1,0:T(8,128)(2,1)S(1)}, u32[]{:S(2)}, u32[]{:S(2)}) collective-permute-start(bf16[1024,896]{1,0:T(8,128)(2,1)S(1)} %get-tuple-element.82), channel_id=1, source_target_pairs={{0,1},{1,0},{2,3},{3,2},{4,5},{5,4},{6,7},{7,6},{8,9},{9,8},{10,11... | collective-permute-start | bytes 5505032 | tf_op jit(solution)/shard_map/ppermute | solution.py:484
  80.5 4.0 %collective-permute-start.1 = (bf16[1024,896]{1,0:T(8,128)(2,1)S(1)}, bf16[1024,896]{1,0:T(8,128)(2,1)S(1)}, u32[]{:S(2)}, u32[]{:S(2)}) collective-permute-start(bf16[1024,896]{1,0:T(8,128)(2,1)S(1)} %get-tuple-element.86), channel_id=1, source_target_pairs={{0,1},{1,0},{2,3},{3,2},{4,5},{5,4},{6,7},{7,6},{8,9},{9,8},{10,11... | collective-permute-start | bytes 5505032 | tf_op jit(solution)/shard_map/ppermute | solution.py:484
  81.1 4.5 %collective-permute-start.2 = (bf16[1024,384]{1,0:T(8,128)(2,1)S(1)}, bf16[1024,384]{1,0:T(8,128)(2,1)S(1)}, u32[]{:S(2)}, u32[]{:S(2)}) collective-permute-start(bf16[1024,384]{1,0:T(8,128)(2,1)S(1)} %get-tuple-element.90), channel_id=1, source_target_pairs={{0,1},{1,0},{2,3},{3,2},{4,5},{5,4},{6,7},{7,6},{8,9},{9,8},{10,11... | collective-permute-start | bytes 2359304 | tf_op jit(solution)/shard_map/ppermute | solution.py:484
  81.3 14.8 %collective-permute-start.4 = (bf16[512,512]{1,0:T(8,128)(2,1)S(1)}, bf16[512,512]{1,0:T(8,128)(2,1)S(1)}, u32[]{:S(2)}, u32[]{:S(2)}) collective-permute-start(bf16[512,512]{1,0:T(8,128)(2,1)S(1)} %get-tuple-element.83), channel_id=1, source_target_pairs={{0,4},{4,0},{8,12},{12,8},{16,20},{20,16},{24,28},{28,24},{1,5},{5... | collective-permute-start | bytes 1572872 | tf_op jit(solution)/shard_map/ppermute | solution.py:484
  82.6 12.0 %collective-permute-start.5 = (bf16[512,384]{1,0:T(8,128)(2,1)S(1)}, bf16[512,384]{1,0:T(8,128)(2,1)S(1)}, u32[]{:S(2)}, u32[]{:S(2)}) collective-permute-start(bf16[512,384]{1,0:T(8,128)(2,1)S(1)} %get-tuple-element.84), channel_id=1, source_target_pairs={{0,2},{1,3},{2,0},{3,1},{4,6},{5,7},{6,4},{7,5},{8,10},{9,11},{10,... | collective-permute-start | bytes 1179656 | tf_op jit(solution)/shard_map/ppermute | solution.py:484
  85.7 11.9 %collective-permute-start.3 = (bf16[512,384]{1,0:T(8,128)(2,1)S(1)}, bf16[512,384]{1,0:T(8,128)(2,1)S(1)}, u32[]{:S(2)}, u32[]{:S(2)}) collective-permute-start(bf16[512,384]{1,0:T(8,128)(2,1)S(1)} %fold.13), channel_id=1, source_target_pairs={{0,8},{4,12},{8,0},{12,4},{16,24},{20,28},{24,16},{28,20},{1,9},{5... | collective-permute-start | bytes 1179656 | tf_op jit(solution)/shard_map/ppermute | solution.py:484
  87.0 18.8 %collective-permute-start.8 = (bf16[512,512]{1,0:T(8,128)(2,1)S(1)}, bf16[512,512]{1,0:T(8,128)(2,1)S(1)}, u32[]{:S(2)}, u32[]{:S(2)}) collective-permute-start(bf16[512,512]{1,0:T(8,128)(2,1)S(1)} %get-tuple-element.88), channel_id=1, source_target_pairs={{0,2},{1,3},{2,0},{3,1},{4,6},{5,7},{6,4},{7,5},{8,10},{9,11},{10,... | collective-permute-start | bytes 1572872 | tf_op jit(solution)/shard_map/ppermute | solution.py:484
  87.7 18.2 %collective-permute-start.7 = (bf16[512,384]{1,0:T(8,128)(2,1)S(1)}, bf16[512,384]{1,0:T(8,128)(2,1)S(1)}, u32[]{:S(2)}, u32[]{:S(2)}) collective-permute-start(bf16[512,384]{1,0:T(8,128)(2,1)S(1)} %get-tuple-element.87), channel_id=1, source_target_pairs={{0,4},{4,0},{8,12},{12,8},{16,20},{20,16},{24,28},{28,24},{1,5},{5... | collective-permute-start | bytes 1179656 | tf_op jit(solution)/shard_map/ppermute | solution.py:484
  96.3 15.2 %collective-permute-start.9 = (bf16[256,512]{1,0:T(8,128)(2,1)S(1)}, bf16[256,512]{1,0:T(8,128)(2,1)S(1)}, u32[]{:S(2)}, u32[]{:S(2)}) collective-permute-start(bf16[256,512]{1,0:T(8,128)(2,1)S(1)} %get-tuple-element.96), channel_id=1, source_target_pairs={{0,2},{1,3},{2,0},{3,1},{4,6},{5,7},{6,4},{7,5},{8,10},{9,11},{10,... | collective-permute-start | bytes 786440 | tf_op jit(solution)/shard_map/ppermute | solution.py:484
  97.7 11.1 %collective-permute-start.6 = (bf16[256,384]{1,0:T(8,128)(2,1)S(1)}, bf16[256,384]{1,0:T(8,128)(2,1)S(1)}, u32[]{:S(2)}, u32[]{:S(2)}) collective-permute-start(bf16[256,384]{1,0:T(8,128)(2,1)S(1)} %fold.15), channel_id=1, source_target_pairs={{0,16},{4,20},{8,24},{12,28},{16,0},{20,4},{24,8},{28,12},{1,17},{... | collective-permute-start | bytes 589832 | tf_op jit(solution)/shard_map/ppermute | solution.py:484
  99.2 9.6 %collective-permute-start.10 = (bf16[256,384]{1,0:T(8,128)(2,1)S(1)}, bf16[256,384]{1,0:T(8,128)(2,1)S(1)}, u32[]{:S(2)}, u32[]{:S(2)}) collective-permute-start(bf16[256,384]{1,0:T(8,128)(2,1)S(1)} %get-tuple-element.97), channel_id=1, source_target_pairs={{0,4},{4,0},{8,12},{12,8},{16,20},{20,16},{24,28},{28,24},{1,5},{5... | collective-permute-start | bytes 589832 | tf_op jit(solution)/shard_map/ppermute | solution.py:484
  106.0 11.0 %collective-permute-start.13 = (bf16[256,512]{1,0:T(8,128)(2,1)S(1)}, bf16[256,512]{1,0:T(8,128)(2,1)S(1)}, u32[]{:S(2)}, u32[]{:S(2)}) collective-permute-start(bf16[256,512]{1,0:T(8,128)(2,1)S(1)} %get-tuple-element.104), channel_id=1, source_target_pairs={{0,2},{1,3},{2,0},{3,1},{4,6},{5,7},{6,4},{7,5},{8,10},{9,11},{10,... | collective-permute-start | bytes 786440 | tf_op jit(solution)/shard_map/ppermute | solution.py:484
  107.2 9.8 %collective-permute-start.14 = (bf16[256,512]{1,0:T(8,128)(2,1)S(1)}, bf16[256,512]{1,0:T(8,128)(2,1)S(1)}, u32[]{:S(2)}, u32[]{:S(2)}) collective-permute-start(bf16[256,512]{1,0:T(8,128)(2,1)S(1)} %get-tuple-element.105), channel_id=1, source_target_pairs={{0,4},{4,0},{8,12},{12,8},{16,20},{20,16},{24,28},{28,24},{1,5},{5... | collective-permute-start | bytes 786440 | tf_op jit(solution)/shard_map/ppermute | solution.py:484
  111.6 6.5 %collective-permute-start.11 = (bf16[128,896]{1,0:T(8,128)(2,1)S(1)}, bf16[128,896]{1,0:T(8,128)(2,1)S(1)}, u32[]{:S(2)}, u32[]{:S(2)}) collective-permute-start(bf16[128,896]{1,0:T(8,128)(2,1)S(1)} %get-tuple-element.113), channel_id=1, source_target_pairs={{0,8},{4,12},{8,0},{12,4},{16,24},{20,28},{24,16},{28,20},{1,9},{5... | collective-permute-start | bytes 688136 | tf_op jit(solution)/shard_map/ppermute | solution.py:484
  112.5 5.7 %collective-permute-start.17 = (bf16[128,128]{1,0:T(8,128)(2,1)S(1)}, bf16[128,128]{1,0:T(8,128)(2,1)S(1)}, u32[]{:S(2)}, u32[]{:S(2)}) collective-permute-start(bf16[128,128]{1,0:T(8,128)(2,1)S(1)} %get-tuple-element.107), channel_id=1, source_target_pairs={{0,4},{4,0},{8,12},{12,8},{16,20},{20,16},{24,28},{28,24},{1,5},{5... | collective-permute-start | bytes 98312 | tf_op jit(solution)/shard_map/ppermute | solution.py:484
  113.8 4.5 %collective-permute-start.18 = (bf16[128,256]{1,0:T(8,128)(2,1)S(1)}, bf16[128,256]{1,0:T(8,128)(2,1)S(1)}, u32[]{:S(2)}, u32[]{:S(2)}) collective-permute-start(bf16[128,256]{1,0:T(8,128)(2,1)S(1)} %get-tuple-element.108), channel_id=1, source_target_pairs={{0,2},{1,3},{2,0},{3,1},{4,6},{5,7},{6,4},{7,5},{8,10},{9,11},{10,... | collective-permute-start | bytes 196616 | tf_op jit(solution)/shard_map/ppermute | solution.py:484
  117.3 7.4 %collective-permute-start.15 = (bf16[128,896]{1,0:T(8,128)(2,1)S(1)}, bf16[128,896]{1,0:T(8,128)(2,1)S(1)}, u32[]{:S(2)}, u32[]{:S(2)}) collective-permute-start(bf16[128,896]{1,0:T(8,128)(2,1)S(1)} %get-tuple-element.118), channel_id=1, source_target_pairs={{0,8},{4,12},{8,0},{12,4},{16,24},{20,28},{24,16},{28,20},{1,9},{5... | collective-permute-start | bytes 688136 | tf_op jit(solution)/shard_map/ppermute | solution.py:484
  118.3 8.2 %collective-permute-start.19 = (bf16[64,128]{1,0:T(8,128)(2,1)S(1)}, bf16[64,128]{1,0:T(8,128)(2,1)S(1)}, u32[]{:S(2)}, u32[]{:S(2)}) collective-permute-start(bf16[64,128]{1,0:T(8,128)(2,1)S(1)} %get-tuple-element.122), channel_id=1, source_target_pairs={{0,2},{1,3},{2,0},{3,1},{4,6},{5,7},{6,4},{7,5},{8,10},{9,11},{10,... | collective-permute-start | bytes 49160 | tf_op jit(solution)/shard_map/ppermute | solution.py:484
  119.5 6.9 %collective-permute-start.20 = (bf16[64,256]{1,0:T(8,128)(2,1)S(1)}, bf16[64,256]{1,0:T(8,128)(2,1)S(1)}, u32[]{:S(2)}, u32[]{:S(2)}) collective-permute-start(bf16[64,256]{1,0:T(8,128)(2,1)S(1)} %get-tuple-element.123), channel_id=1, source_target_pairs={{0,4},{4,0},{8,12},{12,8},{16,20},{20,16},{24,28},{28,24},{1,5},{5... | collective-permute-start | bytes 98312 | tf_op jit(solution)/shard_map/ppermute | solution.py:484
  120.2 9.2 %collective-permute-start.12 = (bf16[64,896]{1,0:T(8,128)(2,1)S(1)}, bf16[64,896]{1,0:T(8,128)(2,1)S(1)}, u32[]{:S(2)}, u32[]{:S(2)}) collective-permute-start(bf16[64,896]{1,0:T(8,128)(2,1)S(1)} %slice.43), channel_id=1, source_target_pairs={{0,16},{4,20},{8,24},{12,28},{16,0},{20,4},{24,8},{28,12},{1,17},{... | collective-permute-start | bytes 344072 | tf_op jit(solution)/shard_map/ppermute | solution.py:484
  124.8 7.2 %collective-permute-start.16 = (bf16[64,896]{1,0:T(8,128)(2,1)S(1)}, bf16[64,896]{1,0:T(8,128)(2,1)S(1)}, u32[]{:S(2)}, u32[]{:S(2)}) collective-permute-start(bf16[64,896]{1,0:T(8,128)(2,1)S(1)} %slice.42), channel_id=1, source_target_pairs={{0,16},{4,20},{8,24},{12,28},{16,0},{20,4},{24,8},{28,12},{1,17},{... | collective-permute-start | bytes 344072 | tf_op jit(solution)/shard_map/ppermute | solution.py:484
